TPU v7x, 32 devices: a whole 2x2x4 slice. The times are simulated.
32 devices in a mesh: ctx: 4 (over y, x), rep: 8 (over z, core).
Axes of the slice: x: 2, y: 2, z: 4, core: 2. Of those that a mesh axis runs over, the one named last changes fastest.
Arguments:
- queries: bfloat16 [8, 512, 4096], P('rep', 'ctx'), may hold values from -200 to 200
- keys: bfloat16 [8, 512, 512], P('rep', 'ctx'), may hold values from -6 to 6
- values: bfloat16 [8, 512, 512], P('rep', 'ctx'), may hold values from -6 to 6
- mixer_input: bfloat16 [8, 512, 8192], P('rep', 'ctx'), may hold values from -6 to 6
- gate_input: bfloat16 [8, 512, 8192], P('rep', 'ctx'), may hold values from -6 to 6
- segment_ids: int32 [8, 512], P('rep'), may hold values from 0 to 2, never falling along the last dimension, each value on 1 to 256 neighbouring positions
- conv_weight: float32 [4, 8192], replicated, may hold values from -3 to 3
- conv_bias: float32 [8192], replicated, may hold values from -3 to 3
- select_weight: bfloat16 [544, 8192], P(None, 'rep'), may hold values from -0.0625 to 0.0625
- delta_weight: bfloat16 [512, 8192], P(None, 'rep'), may hold values from -0.25 to 0.25
- delta_bias: float32 [8192], replicated, may hold values from -12 to -3
- decay_log: float32 [8192, 16], replicated, may hold values from 0 to 2.77
- skip_gain: float32 [8192], replicated, may hold values from 0.5 to 1.5
Outputs:
- attended: bfloat16 [8, 512, 4096], P('rep', 'ctx')
- mixed: bfloat16 [8, 512, 8192], P('rep', 'ctx')
All inputs are finite; a program needn't handle non-finite values.
Results may differ from a plain program's by a relative error of at most 0.012.
Values may be sent and summed in bfloat16 or wider, within the bound.
No kernel may reach another device: no remote copies, remote signals or barrier semaphores. Data moves between devices by JAX's collectives and lax.ppermute only.
A program may use at most 192 MiB of HBM per device.

v0:
```python
import math

import jax
import jax.numpy as jnp
from jax import lax
from jax.sharding import PartitionSpec as P

QUERY_HEADS = 32
KEY_VALUE_HEADS = 4
HEAD_WIDTH = 128


def shifted(value, axis, by):
    size = lax.axis_size(axis)
    pairs = [(i, i + by) for i in range(size) if 0 <= i + by < size]
    return lax.ppermute(value, axis, pairs)


def combine_pair(early_pair, later_pair):
    return (early_pair[0] * later_pair[0], later_pair[0] * early_pair[1] + later_pair[1])


def local(
    queries,
    keys,
    values,
    mixer_input,
    gate_input,
    segment_ids,
    conv_weight,
    conv_bias,
    select_weight,
    delta_weight,
    delta_bias,
    decay_log,
    skip_gain,
):
    tok_rows = mixer_input.shape[1]
    channels = mixer_input.shape[2]
    low_rank = delta_weight.shape[0]
    state_count = decay_log.shape[1]
    seg_full = segment_ids[0]
    offset = lax.axis_index("ctx") * tok_rows
    mixer_rows = mixer_input[0]
    rim_rows = shifted(mixer_rows[tok_rows - 3 :], "ctx", 1)
    window = jnp.concatenate([rim_rows, mixer_rows], axis=0).astype(jnp.float32)
    seg_pad = jnp.concatenate([jnp.full((3,), -1, jnp.int32), seg_full], axis=0)
    seg_window = lax.dynamic_slice_in_dim(seg_pad, offset, tok_rows + 3, 0)
    seg_query = seg_window[3:]
    running = conv_bias[None, :] + jnp.zeros((tok_rows, channels), jnp.float32)
    for tap_index in range(4):
        match_seg = (seg_window[tap_index : tap_index + tok_rows] == seg_query).astype(jnp.float32)
        running = (
            running
            + conv_weight[tap_index][None, :]
            * window[tap_index : tap_index + tok_rows]
            * match_seg[:, None]
        )
    conv_out = jax.nn.silu(running).astype(jnp.bfloat16)
    select = lax.dot_general(
        conv_out,
        lax.all_gather(select_weight, "rep", axis=1, tiled=True),
        (((1,), (1,)), ((), ())),
        preferred_element_type=jnp.float32,
    )
    low_part = select[:, :low_rank]
    in_map = select[:, low_rank : low_rank + state_count]
    out_map = select[:, low_rank + state_count :]
    low_norm = (
        low_part * lax.rsqrt(jnp.mean(low_part * low_part, axis=-1, keepdims=True) + 1e-06)
    ).astype(jnp.bfloat16)
    delta = jax.nn.softplus(
        jnp.dot(
            low_norm,
            lax.all_gather(delta_weight, "rep", axis=1, tiled=True),
            preferred_element_type=jnp.float32,
        )
        + delta_bias
    ).astype(jnp.bfloat16)
    decay_rates = -jnp.exp(jnp.transpose(decay_log))
    same_seg = (seg_query == seg_window[2 : tok_rows + 2]).astype(jnp.float32)
    delta_f = delta.astype(jnp.float32)
    conv_f = conv_out.astype(jnp.float32)
    drive_term = delta_f * conv_f
    block_count = tok_rows // 16

    def local_block(hidden_state, inputs):
        delta_rows, drive_rows, in_rows, out_rows, keep_rows = inputs
        decay = jnp.exp(delta_rows[:, None, :] * decay_rates[None]) * keep_rows[:, None, None]
        inject = in_rows[:, :, None] * drive_rows[:, None, :]
        decay_prod, input_sum = lax.associative_scan(combine_pair, (decay, inject), axis=0)
        history = decay_prod * hidden_state[None] + input_sum
        result = jnp.sum(history * out_rows[:, :, None], axis=1)
        return (history[-1], result)

    local_inputs = (
        delta_f.reshape(block_count, 16, channels),
        drive_term.reshape(block_count, 16, channels),
        in_map.reshape(block_count, 16, state_count),
        out_map.reshape(block_count, 16, state_count),
        same_seg.reshape(block_count, 16),
    )
    final_state, local_out = lax.scan(
        local_block, jnp.zeros((state_count, channels), jnp.float32), local_inputs
    )
    local_out = local_out.reshape(tok_rows, channels)
    cum_delta = jnp.cumsum(delta_f, axis=0)
    unbroken = (jnp.cumsum(1.0 - same_seg, axis=0) == 0.0).astype(jnp.float32)
    device_decay = jnp.exp(cum_delta[-1][None, :] * decay_rates) * unbroken[-1]
    incoming = jnp.zeros((state_count, channels), jnp.float32)
    for handoff in range(lax.axis_size("ctx") - 1):
        outgoing = device_decay * incoming + final_state
        incoming = shifted(outgoing.astype(jnp.bfloat16), "ctx", 1).astype(outgoing.dtype)
    carry_in = incoming

    def carried_block(inputs):
        cum_rows, unbroken_rows, out_rows = inputs
        factor = jnp.exp(cum_rows[:, None, :] * decay_rates[None]) * unbroken_rows[:, None, None]
        return jnp.sum(factor * carry_in[None] * out_rows[:, :, None], axis=1)

    correction = lax.map(
        carried_block,
        (
            cum_delta.reshape(block_count, 16, channels),
            unbroken.reshape(block_count, 16),
            out_map.reshape(block_count, 16, state_count),
        ),
    )
    correction = correction.reshape(tok_rows, channels)
    mixed = (
        (local_out + correction + skip_gain[None, :] * conv_f)
        * jax.nn.silu(gate_input[0].astype(jnp.float32))
    ).astype(jnp.bfloat16)
    head_size = HEAD_WIDTH
    key_value_heads = KEY_VALUE_HEADS
    query_groups = QUERY_HEADS // KEY_VALUE_HEADS
    score_scale = 1.0 / math.sqrt(head_size)
    query_four = queries[0].reshape(tok_rows, key_value_heads, query_groups, head_size)
    query_pos = offset + jnp.arange(tok_rows)
    running_max = jnp.full((key_value_heads, query_groups, tok_rows), -1e30, jnp.float32)
    key_piece = lax.all_gather(keys, "ctx", axis=1, tiled=True)[0]
    value_piece = lax.all_gather(values, "ctx", axis=1, tiled=True)[0]
    piece_rows = key_piece.shape[0]
    key_three = key_piece.reshape(piece_rows, key_value_heads, head_size)
    value_three = value_piece.reshape(piece_rows, key_value_heads, head_size)
    scores = (
        jnp.einsum("tkgd,pkd->kgtp", query_four, key_three, preferred_element_type=jnp.float32)
        * score_scale
    )
    key_pos = jnp.arange(piece_rows)
    allowed = (key_pos[None, :] <= query_pos[:, None]) & (seg_full[None, :] == seg_query[:, None])
    scores = jnp.where(allowed, scores, -1e30)
    new_max = jnp.maximum(running_max, jnp.max(scores, axis=-1))
    weights = jnp.where(allowed, jnp.exp(scores - new_max[..., None]), 0.0)
    normaliser = jnp.sum(weights, axis=-1)
    accum = jnp.einsum(
        "kgtp,pkd->kgtd",
        weights.astype(jnp.bfloat16),
        value_three,
        preferred_element_type=jnp.float32,
    )
    running_max, normaliser, accum = (new_max, normaliser, accum)
    attended = jnp.transpose(accum / normaliser[..., None], (2, 0, 1, 3)).reshape(
        tok_rows, key_value_heads * query_groups * head_size
    )
    return (attended.astype(jnp.bfloat16)[None], mixed[None])


def solution(mesh):
    placed = (
        P("rep", "ctx", None),
        P("rep", "ctx", None),
        P("rep", "ctx", None),
        P("rep", "ctx", None),
        P("rep", "ctx", None),
        P("rep", None),
        P(),
        P(),
        P(None, "rep"),
        P(None, "rep"),
        P(),
        P(),
        P(),
    )
    return jax.shard_map(
        local,
        mesh=mesh,
        in_specs=placed,
        out_specs=(P("rep", "ctx", None), P("rep", "ctx", None)),
        check_vma=False,
    )
```

profile of v0, /device:TPU:0, one launch (start us, length us, event | category | flops | bytes accessed | tf_op | source)
XLA Modules:
  0.0 1762.3 jit_solution(7607810786430474079)
XLA Ops:
  23.5 10.6 all_gather.12
  43.8 54.9 %all-gather.3.cloned.1.call-done = bf16[544,8192]{1,0:T(8,128)(2,1)} async-done(((bf16[544,1024]{1,0:T(8,128)(2,1)}), bf16[544,8192]{1,0:T(8,128)(2,1)}) %all-gather.3.cloned.1.call-update) | async-done | bytes 8912912 | tf_op jit(solution)/shard_map/all_gather | solution.py:62
  105.1 75.8 %all-gather.5.cloned.1.call-done = bf16[512,8192]{1,0:T(8,128)(2,1)} async-done(((bf16[512,1024]{1,0:T(8,128)(2,1)}), bf16[512,8192]{1,0:T(8,128)(2,1)}) %all-gather.5.cloned.1.call-update) | async-done | bytes 8388624 | tf_op jit(solution)/shard_map/all_gather | solution.py:75
  180.9 10.4 convert_multiply_fusion.2
  194.6 1315.5 %while.22 = (s32[]{:T(128)}, f32[16,8192]{1,0:T(8,128)}, f32[8,16,8192]{2,1,0:T(8,128)}, f32[8,16,8192]{2,1,0:T(8,128)}, f32[16,8192]{1,0:T(8,128)}, /*index=5*/...) while((s32[]{:T(128)}, f32[16,8192]{1,0:T(8,128)}, ...), condition=%wide.region_5.6_spmd, body=%wide.region_3.5_spmd.sunk | while | flops 39190528 | bytes 358095392 | solution.py:103
  303.8 9.9 pad.156
  318.2 9.9 pad.157
  343.9 13.6 multiply_reduce_fusion.5
  468.2 9.9 pad.156
  482.5 9.9 pad.157
  508.3 13.6 multiply_reduce_fusion.5
  632.6 9.9 pad.156
  646.9 9.9 pad.157
  672.6 13.6 multiply_reduce_fusion.5
  797.0 9.9 pad.156
  811.3 9.9 pad.157
  837.1 13.6 multiply_reduce_fusion.5
  961.4 9.9 pad.156
  975.7 9.9 pad.157
  1001.4 13.6 multiply_reduce_fusion.5
  1125.7 9.9 pad.156
  1140.1 9.9 pad.157
  1165.8 13.6 multiply_reduce_fusion.5
  1290.1 9.9 pad.156
  1304.5 9.9 pad.157
  1330.2 13.6 multiply_reduce_fusion.5
  1454.5 9.9 pad.156
  1468.9 9.9 pad.157
  1494.6 13.6 multiply_reduce_fusion.5
  1510.1 144.3 %reduce_window_sum.18 = f32[128,8192]{1,0:T(8,128)} reduce-window(f32[128,8192]{1,0:T(8,128)} %bitcast.112, f32[]{:T(128)} %constant.69.clone.1), window={size=128x1 pad=127_0x0_0}, to_apply=%region_6.7 | reduce-window | flops 133169152 | bytes 8388612 | tf_op jit(solution)/shard_map/jit(cumsum)/reduce_window_sum | solution.py:107
  1672.1 11.4 all_gather.13
  1695.8 47.7 %while.23 = (s32[]{:T(128)}, f32[8,16,8192]{2,1,0:T(8,128)}, f32[8,16,8192]{2,1,0:T(8,128)}, f32[16,8192]{1,0:T(8,128)}, f32[8,16]{1,0:T(8,128)S(1)}, /*index=5*...) while((s32[]{:T(128)}, f32[8,16,8192]{2,1,0:T(8,128)}, f32[8,16,8192]{2,1,0:T(8,128)}, ...), condition=%wide.region_10.11_spmd, body=%wide.region_8.10_spmd.sunk | while | flops 10354690 | bytes 4197677 | solution.py:121
  (574 shorter events, 1170.0 us)
Async XLA Ops:
  7.2 30.7 %copy-start.11 = (bf16[1,128,8192]{2,1,0:T(8,128)(2,1)S(1)}, bf16[1,128,8192]{2,1,0:T(8,128)(2,1)}, u32[]{:S(2)}) copy-start(bf16[1,128,8192]{2,1,0:T(8,128)(2,1)} %param.20) | copy-start | bytes 6291460
  7.2 26.9 %copy-start.14 = (bf16[1,128,4096]{2,1,0:T(8,128)(2,1)S(1)}, bf16[1,128,4096]{2,1,0:T(8,128)(2,1)}, u32[]{:S(2)}) copy-start(bf16[1,128,4096]{2,1,0:T(8,128)(2,1)} %param.17) | copy-start | bytes 3145732
  7.2 91.6 %all-gather.3.cloned.1.call-start = ((), (), s32[]{:S(2)}) async-start(), calls=%async_computation | async-start | bytes 10027008 | tf_op jit(solution)/shard_map/all_gather | solution.py:62
  7.9 173.0 %all-gather.5.cloned.1.call-start = ((), (), s32[]{:S(2)}) async-start(), calls=%async_computation.1 | async-start | bytes 9437184 | tf_op jit(solution)/shard_map/all_gather | solution.py:75
  9.6 28.2 %collective-permute-start = (bf16[3,8192]{1,0:T(4,128)(2,1)S(1)}, bf16[3,8192]{1,0:T(4,128)(2,1)S(1)}, u32[]{:S(2)}, u32[]{:S(2)}) collective-permute-start(bf16[3,8192]{1,0:T(4,128)(2,1)S(1)} %slice_bitcast_fusion.1), channel_id=1, source_target_pairs={{0,8},{8,16},{16,24},{1,9},{9,17},{17,25},{2,10},{10,18},{18,26},{... | collective-permute-start | bytes 147464 | tf_op jit(solution)/shard_map/ppermute | solution.py:16
  21.4 17.1 copy-start.15
  21.4 17.1 copy-start.17
  21.4 17.1 copy-start.19
  21.4 17.1 copy-start.21
  43.8 137.1 %copy-start.26 = (f32[8192]{0:T(1024)S(1)}, f32[8192]{0:T(1024)}, u32[]{:S(2)}) copy-start(f32[8192]{0:T(1024)} %param.27) | copy-start | bytes 98308
  303.8 9.9 slice-start.1
  440.0 9.9 slice-start
  468.2 9.9 slice-start.1
  632.6 9.9 slice-start.1
  768.8 9.9 slice-start
  797.0 9.9 slice-start.1
  933.2 9.9 slice-start
  961.4 9.9 slice-start.1
  1097.6 9.9 slice-start
  1125.7 9.9 slice-start.1
  1290.1 9.9 slice-start.1
  1426.4 9.9 slice-start
  1454.5 9.9 slice-start.1
  1510.1 145.4 %copy-start.7 = (f32[16,8192]{1,0:T(8,128)S(1)}, f32[16,8192]{1,0:T(8,128)}, u32[]{:S(2)}) copy-start(f32[16,8192]{1,0:T(8,128)} %get-tuple-element.88) | copy-start | bytes 1572868
  1510.1 145.4 %copy-start.8 = (f32[8192,16]{0,1:T(8,128)S(1)}, f32[8192,16]{0,1:T(8,128)}, u32[]{:S(2)}) copy-start(f32[8192,16]{0,1:T(8,128)} %param.28) | copy-start | bytes 1572868
  1510.1 149.0 %copy-start.9 = (bf16[16,8,32,128]{3,2,1,0:T(8,128)(2,1)S(1)}, bf16[16,8,32,128]{3,2,1,0:T(8,128)(2,1)}, u32[]{:S(2)}) copy-start(bf16[16,8,32,128]{3,2,1,0:T(8,128)(2,1)} %copy.50) | copy-start | bytes 3145732
  1510.1 149.0 %copy-start.10 = (bf16[1,512,512]{1,2,0:T(8,128)(2,1)S(1)}, bf16[1,512,512]{1,2,0:T(8,128)(2,1)}, u32[]{:S(2)}) copy-start(bf16[1,512,512]{1,2,0:T(8,128)(2,1)} %all_gather.12) | copy-start | bytes 1572868
  1510.1 149.0 %copy-start.13 = (pred[128,512]{0,1:T(8,128)(4,1)S(1)}, pred[128,512]{0,1:T(8,128)(4,1)}, u32[]{:S(2)}) copy-start(pred[128,512]{0,1:T(8,128)(4,1)} %fusion.35) | copy-start | bytes 196612
  1655.7 9.3 collective-permute-start.1
  1661.1 10.9 copy-start.5
  1665.2 18.5 %collective-permute-start.2 = (bf16[16,8192]{1,0:T(8,128)(2,1)S(1)}, bf16[16,8192]{1,0:T(8,128)(2,1)S(1)}, u32[]{:S(2)}, u32[]{:S(2)}) collective-permute-start(bf16[16,8192]{1,0:T(8,128)(2,1)S(1)} %add_convert_fusion.1), channel_id=1, source_target_pairs={{0,8},{8,16},{16,24},{1,9},{9,17},{17,25},{2,10},{10,18},{18,26},{... | collective-permute-start | bytes 786440 | tf_op jit(solution)/shard_map/ppermute | solution.py:16
  1683.9 9.4 collective-permute-start.3
  (62 other events, 313.3 us)
Sparse Core Ops, SparseCore 0:
  9.6 89.0 all-gather.2
  100.4 80.4 all-gather.4
where the time goes:
time: 1780 us; the launch traced here: 1760 us
  other arithmetic  893 us (50%)
  local copies, waits for them, and re-layouts  655 us (37%)
  waiting for transfers between devices  136 us (8%)
  matrix products  24 us (1%)
  blocking collectives  22 us (1%)
    pad x96, local copies, waits for them, and re-layouts, local_block(): lax.associative_scan(combine_pair, (decay, inject), axis=0)  574 us
    mul x40, other arithmetic, combine_pair(): early_pair[0] * later_pair[0]  226 us
    add x48, other arithmetic, local_block(): lax.associative_scan(combine_pair, (decay, inject), axis=0)  172 us
    another operation x1, other arithmetic, local(): cum_delta = jnp.cumsum(delta_f, axis=0)  144 us
    reduce_sum x8, other arithmetic, local_block(): result = jnp.sum(history * out_rows[:, :, None], axis=1)  109 us
    concatenate x48, other arithmetic, local_block(): lax.associative_scan(combine_pair, (decay, inject), axis=0)  97.6 us
    all_gather x1, waiting for transfers between devices, local(): lax.all_gather(delta_weight, 'rep', axis=1, tiled=True)  75.8 us
    all_gather x1, waiting for transfers between devices, local(): lax.all_gather(select_weight, 'rep', axis=1, tiled=True)  54.9 us
  transfers between devices with their start and end apart: 6, of which 3 were waited for; matrix products, arithmetic and copies ran while one was open for 2% of the time, Pallas kernels for 0%

commit v1 on v0

v1 whole, which is shorter than its diff:
```python
import functools
import math

import jax
import jax.numpy as jnp
from jax import lax
from jax.experimental import pallas as pl
from jax.experimental.pallas import tpu as pltpu
from jax.sharding import PartitionSpec as P

QUERY_HEADS = 32
KEY_VALUE_HEADS = 4
HEAD_WIDTH = 128
LANES = 128
SUBLANES = 8
LOG2E = 1.0 / math.log(2.0)
FAR = 1e30


def silu(value):
    return 0.5 * value * (1.0 + jnp.tanh(0.5 * value))


def attention_kernel(seg_q_ref, seg_k_ref, q_ref, *refs):
    key_refs, value_refs, out_ref = refs[0:-1:2], refs[1:-1:2], refs[-1]
    rows = q_ref.shape[0]
    span = seg_k_ref.shape[1]
    groups = QUERY_HEADS // KEY_VALUE_HEADS
    row = lax.broadcasted_iota(jnp.int32, (rows, span), 0) + (span - rows)
    col = lax.broadcasted_iota(jnp.int32, (rows, span), 1)
    allowed = (col <= row) & (seg_q_ref[...] == seg_k_ref[...])
    keys = jnp.concatenate([ref[...] for ref in key_refs], axis=0)
    vals = jnp.concatenate([ref[...] for ref in value_refs], axis=0)
    factor = LOG2E / math.sqrt(HEAD_WIDTH)
    for head in range(groups):
        lanes = slice(head * HEAD_WIDTH, (head + 1) * HEAD_WIDTH)
        scores = lax.dot_general(
            q_ref[:, lanes], keys, (((1,), (1,)), ((), ())), preferred_element_type=jnp.float32
        )
        scores = jnp.where(allowed, scores, -FAR)
        top = jnp.max(scores, axis=-1, keepdims=True)
        weights = jnp.exp2((scores - top) * factor)
        norm = jnp.sum(weights, axis=-1, keepdims=True)
        total = jnp.dot(weights.astype(jnp.bfloat16), vals, preferred_element_type=jnp.float32)
        out_ref[:, lanes] = (total / norm).astype(out_ref.dtype)


def attention(queries, blocks, seg_q, seg_k):
    rows = queries.shape[0]
    span = seg_k.shape[1]
    group_width = QUERY_HEADS // KEY_VALUE_HEADS * HEAD_WIDTH
    key_spec = pl.BlockSpec((rows, HEAD_WIDTH), lambda h: (0, h))
    value_spec = pl.BlockSpec((rows, HEAD_WIDTH), lambda h: (0, KEY_VALUE_HEADS + h))
    wide = pl.BlockSpec((rows, group_width), lambda h: (0, h))
    return pl.pallas_call(
        attention_kernel,
        grid=(KEY_VALUE_HEADS,),
        in_specs=[
            pl.BlockSpec((rows, 1), lambda h: (0, 0)),
            pl.BlockSpec((1, span), lambda h: (0, 0)),
            wide,
            *([key_spec, value_spec] * len(blocks)),
        ],
        out_specs=wide,
        out_shape=jax.ShapeDtypeStruct(queries.shape, jnp.bfloat16),
        compiler_params=pltpu.CompilerParams(vmem_limit_bytes=32 << 20),
        cost_estimate=pl.CostEstimate(
            flops=4 * rows * span * QUERY_HEADS * HEAD_WIDTH,
            bytes_accessed=4 * queries.size,
            transcendentals=rows * span * QUERY_HEADS,
        ),
        name="attention",
    )(seg_q, seg_k, queries, *[block for block in blocks for _ in range(2)])


def conv_select_kernel(place_ref, seg_ref, x_ref, weight_ref, bias_ref, select_ref, conv_ref, part_ref, masks, padded, total):
    step = pl.program_id(0)
    toks = seg_ref.shape[0]
    width = x_ref.shape[2]
    pieces = x_ref.shape[0]
    rows = x_ref.shape[1]

    @pl.when(step == 0)
    def _():
        seg = seg_ref[...]
        wide_seg = jnp.broadcast_to(seg, (toks, LANES)).astype(jnp.float32)
        padded[0:SUBLANES, 0:LANES] = jnp.full((SUBLANES, LANES), -1.0, jnp.float32)
        padded[SUBLANES : SUBLANES + toks, 0:LANES] = wide_seg
        for tap in range(3):
            before = padded[SUBLANES - 3 + tap : SUBLANES - 3 + tap + toks, 0:LANES]
            masks[tap] = jnp.where(before == wide_seg, 1.0, 0.0)
        padded[0:SUBLANES, :] = jnp.zeros((SUBLANES, width), jnp.float32)
        total[...] = jnp.zeros_like(total)

    for piece in range(pieces):
        padded[SUBLANES + piece * rows : SUBLANES + (piece + 1) * rows, :] = x_ref[piece].astype(jnp.float32)
    outs = []
    for tile in range(width // LANES):
        lanes = slice(tile * LANES, (tile + 1) * LANES)
        running = jnp.broadcast_to(bias_ref[0:1, lanes], (toks, LANES))
        for tap in range(4):
            moved = padded[SUBLANES - 3 + tap : SUBLANES - 3 + tap + toks, lanes]
            term = weight_ref[tap : tap + 1, lanes] * moved
            running = running + (term * masks[tap] if tap < 3 else term)
        conv = silu(running).astype(jnp.bfloat16)
        conv_ref[tile] = conv
        outs.append(conv)
    conv_all = jnp.concatenate(outs, axis=1) if len(outs) > 1 else outs[0]
    total[...] += lax.dot_general(
        conv_all, select_ref[0], (((1,), (1,)), ((), ())), preferred_element_type=jnp.float32
    )

    @pl.when(step == pl.num_programs(0) - 1)
    def _():
        for piece in range(pieces):
            part_ref[piece] = total[piece * rows : (piece + 1) * rows, :].astype(part_ref.dtype)


def conv_select(place, seg_col, pieces, conv_weight, conv_bias, select_parts):
    shards, outputs, width = select_parts.shape
    ctx, rows, _ = pieces.shape
    toks = ctx * rows
    tiles = width // LANES
    return pl.pallas_call(
        conv_select_kernel,
        grid_spec=pltpu.PrefetchScalarGridSpec(
            num_scalar_prefetch=1,
            grid=(shards,),
            in_specs=[
                pl.BlockSpec((toks, 1), lambda s, p: (0, 0)),
                pl.BlockSpec((ctx, rows, width), lambda s, p: (0, 0, s)),
                pl.BlockSpec((4, width), lambda s, p: (0, s * ctx + p[0])),
                pl.BlockSpec((1, width), lambda s, p: (0, s * ctx + p[0])),
                pl.BlockSpec((1, outputs, width), lambda s, p: (s, 0, 0)),
            ],
            out_specs=[
                pl.BlockSpec((tiles, toks, LANES), lambda s, p: (s, 0, 0)),
                pl.BlockSpec((ctx, rows, outputs), lambda s, p: (0, 0, 0)),
            ],
            scratch_shapes=[
                pltpu.VMEM((3, toks, LANES), jnp.float32),
                pltpu.VMEM((SUBLANES + toks, width), jnp.float32),
                pltpu.VMEM((toks, outputs), jnp.float32),
            ],
        ),
        out_shape=[
            jax.ShapeDtypeStruct((shards * tiles, toks, LANES), jnp.bfloat16),
            jax.ShapeDtypeStruct((ctx, rows, outputs), jnp.bfloat16),
        ],
        compiler_params=pltpu.CompilerParams(vmem_limit_bytes=40 << 20),
        cost_estimate=pl.CostEstimate(
            flops=2 * toks * shards * width * outputs,
            bytes_accessed=2 * pieces.size * 2 + 2 * select_parts.size,
            transcendentals=pieces.size,
        ),
        name="conv_select",
    )(place, seg_col, pieces, conv_weight, conv_bias, select_parts)


def normalise_kernel(rank, part_ref, out_ref):
    total = part_ref[0].astype(jnp.float32)
    for piece in range(1, part_ref.shape[0]):
        total = total + part_ref[piece].astype(jnp.float32)
    low = total[:, :rank]
    scale = lax.rsqrt(jnp.mean(low * low, axis=-1, keepdims=True) + 1e-06)
    out_ref[:, :rank] = (low * scale).astype(out_ref.dtype)
    out_ref[:, rank:] = total[:, rank:].astype(out_ref.dtype)


def normalise(parts, rank):
    return pl.pallas_call(
        functools.partial(normalise_kernel, rank),
        out_shape=jax.ShapeDtypeStruct(parts.shape[1:], jnp.bfloat16),
        name="normalise",
    )(parts)


def scan_kernel(rank, seg_ref, low_ref, weight_ref, bias_ref, decay_ref, gain_ref, conv_ref, out_ref,
                reset, maps, delta_rows, drive_rows, mixed_rows):
    toks = seg_ref.shape[0]
    states = decay_ref.shape[0]
    tiles = conv_ref.shape[0]
    per_shard = weight_ref.shape[2] // LANES
    ctx = out_ref.shape[0]
    rows = out_ref.shape[1]

    @pl.when(pl.program_id(0) == 0)
    def _():
        seg = jnp.broadcast_to(seg_ref[...], (toks, LANES)).astype(jnp.float32)
        reset[0:SUBLANES, :] = jnp.full((SUBLANES, LANES), -1.0, jnp.float32)
        reset[SUBLANES : SUBLANES + toks, :] = seg
        before = reset[SUBLANES - 1 : SUBLANES - 1 + toks, :]
        reset[0:toks, :] = jnp.where(before == seg, 0.0, FAR)
        for index in range(2 * states):
            column = low_ref[:, rank + index : rank + index + 1].astype(jnp.float32)
            maps[index] = jnp.broadcast_to(column, (toks, LANES))

    low = low_ref[:, 0:rank]
    for shard in range(tiles // per_shard):
        pre = jnp.dot(low, weight_ref[shard], preferred_element_type=jnp.float32)
        for part in range(per_shard):
            tile = shard * per_shard + part
            value = pre[:, part * LANES : (part + 1) * LANES] + bias_ref[tile : tile + 1, :]
            raised = jnp.exp(-jnp.abs(value))
            log_part = jnp.where(
                raised < 0.01,
                raised * (1.0 - raised * (0.5 - raised * (1.0 / 3.0))),
                jnp.log(1.0 + raised),
            )
            delta = (jnp.maximum(value, 0.0) + log_part).astype(jnp.bfloat16).astype(jnp.float32)
            delta_rows[tile * toks : (tile + 1) * toks, :] = delta
            drive_rows[tile * toks : (tile + 1) * toks, :] = delta * conv_ref[tile].astype(jnp.float32)

    rates = [-LOG2E * jnp.exp(decay_ref[n]) for n in range(states)]

    def block(index, held):
        held = list(held)
        for inner in range(SUBLANES):
            t = index * SUBLANES + inner
            delta = delta_rows[pl.ds(t, tiles, stride=toks), :]
            drive = drive_rows[pl.ds(t, tiles, stride=toks), :]
            far = delta + reset[pl.ds(t, 1), :]
            result = None
            for n in range(states):
                grow = jnp.exp2(far * rates[n])
                held[n] = grow * held[n] + drive * maps[n, pl.ds(t, 1), :]
                term = held[n] * maps[states + n, pl.ds(t, 1), :]
                result = term if result is None else result + term
            mixed_rows[pl.ds(t, tiles, stride=toks), :] = result
        return tuple(held)

    start = tuple(jnp.zeros((tiles, LANES), jnp.float32) for _ in range(states))
    lax.fori_loop(0, toks // SUBLANES, block, start)

    for tile in range(tiles):
        full = mixed_rows[tile * toks : (tile + 1) * toks, :] + gain_ref[tile : tile + 1, :] * conv_ref[tile].astype(
            jnp.float32
        )
        full = full.astype(out_ref.dtype)
        for piece in range(ctx):
            out_ref[piece, :, tile * LANES : (tile + 1) * LANES] = full[piece * rows : (piece + 1) * rows, :]


def state_scan(seg_col, low, delta_parts, bias, decay, gain, conv, ctx):
    toks = low.shape[0]
    shards, rank, width = delta_parts.shape
    states = decay.shape[0]
    tiles = SUBLANES
    groups = conv.shape[0] // tiles
    rows = toks // ctx
    steps = toks * conv.shape[0] * LANES * states
    return pl.pallas_call(
        functools.partial(scan_kernel, rank),
        grid=(groups,),
        in_specs=[
            pl.BlockSpec((toks, 1), lambda g: (0, 0)),
            pl.BlockSpec(low.shape, lambda g: (0, 0)),
            pl.BlockSpec((shards // groups, rank, width), lambda g: (g, 0, 0)),
            pl.BlockSpec((tiles, LANES), lambda g: (g, 0)),
            pl.BlockSpec((states, tiles, LANES), lambda g: (0, g, 0)),
            pl.BlockSpec((tiles, LANES), lambda g: (g, 0)),
            pl.BlockSpec((tiles, toks, LANES), lambda g: (g, 0, 0)),
        ],
        out_specs=pl.BlockSpec((ctx, rows, tiles * LANES), lambda g: (0, 0, g)),
        out_shape=jax.ShapeDtypeStruct((ctx, rows, conv.shape[0] * LANES), jnp.bfloat16),
        scratch_shapes=[
            pltpu.VMEM((toks + SUBLANES, LANES), jnp.float32),
            pltpu.VMEM((2 * states, toks, LANES), jnp.float32),
            pltpu.VMEM((tiles * toks, LANES), jnp.float32),
            pltpu.VMEM((tiles * toks, LANES), jnp.float32),
            pltpu.VMEM((tiles * toks, LANES), jnp.float32),
        ],
        compiler_params=pltpu.CompilerParams(vmem_limit_bytes=56 << 20),
        cost_estimate=pl.CostEstimate(
            flops=6 * steps, bytes_accessed=2 * delta_parts.size + 4 * conv.size, transcendentals=steps
        ),
        name="state_scan",
    )(seg_col, low, delta_parts, bias, decay, gain, conv)


def gate_kernel(fold, y_ref, gate_ref, out_ref):
    ctx, _, width = y_ref.shape
    for piece in range(ctx):
        place = piece % fold * (ctx // fold) + piece // fold
        lanes = slice(place * width, (place + 1) * width)
        gate = gate_ref[:, lanes].astype(jnp.float32)
        out_ref[:, lanes] = (y_ref[piece].astype(jnp.float32) * silu(gate)).astype(out_ref.dtype)


def apply_gate(pieces, gate, shards, fold):
    ctx, rows, total = pieces.shape
    width = total // shards
    return pl.pallas_call(
        functools.partial(gate_kernel, fold),
        grid=(shards,),
        in_specs=[
            pl.BlockSpec((ctx, rows, width), lambda s: (0, 0, s)),
            pl.BlockSpec((rows, ctx * width), lambda s: (0, s)),
        ],
        out_specs=pl.BlockSpec((rows, ctx * width), lambda s: (0, s)),
        out_shape=jax.ShapeDtypeStruct(gate.shape, jnp.bfloat16),
        cost_estimate=pl.CostEstimate(
            flops=4 * gate.size, bytes_accessed=6 * gate.size, transcendentals=gate.size
        ),
        name="gate",
    )(pieces, gate)


def shifted(value, axis, by):
    size = lax.axis_size(axis)
    pairs = [(i, i + by) for i in range(size) if 0 <= i + by < size]
    return lax.ppermute(value, axis, pairs)


def exchange(value):
    return lax.all_to_all(value, "ctx", 0, 0, tiled=True)


def local(
    queries,
    keys,
    values,
    mixer_input,
    gate_input,
    segment_ids,
    conv_weight,
    conv_bias,
    select_weight,
    delta_weight,
    delta_bias,
    decay_log,
    skip_gain,
):
    ctx = lax.axis_size("ctx")
    shards = lax.axis_size("rep")
    place = lax.axis_index("ctx")
    rows, channels = mixer_input.shape[1:]
    rank = delta_weight.shape[0]
    states = decay_log.shape[1]
    width = max(channels // (shards * ctx), LANES)
    fold = width * shards * ctx // channels
    tiles = channels // ctx // LANES
    seg = segment_ids[0]
    toks = seg.shape[0]
    seg_col = seg[:, None]
    back = min(ctx - 1, -(-(toks // 2 - 1) // rows))

    def own_part(array):
        cut = array.reshape(array.shape[:-1] + (shards // fold, fold, ctx // fold, width))
        cut = lax.dynamic_index_in_dim(cut, place // fold, cut.ndim - 2, keepdims=False)
        cut = lax.dynamic_index_in_dim(cut, place % fold, cut.ndim - 2, keepdims=False)
        return cut.reshape(array.shape[:-1] + (tiles, LANES))

    def gathered(weight):
        own = lax.dynamic_slice_in_dim(weight, place // fold * width, width, 1)
        parts = lax.all_gather(own, "rep", axis=0)
        if fold > 1:
            parts = parts.reshape((shards // fold, fold) + own.shape)
            parts = lax.dynamic_index_in_dim(parts, place % fold, 1, keepdims=False)
        return parts

    select_parts = gathered(select_weight)
    delta_parts = gathered(delta_weight)

    both = jnp.concatenate([keys[0], values[0]], axis=1)
    blocks = [shifted(both, "ctx", by) for by in range(back, 0, -1)] + [both]

    pieces = mixer_input[0].reshape(rows, shards // fold, fold, ctx // fold, width)
    pieces = jnp.transpose(pieces, (3, 2, 0, 1, 4)).reshape(ctx, rows, channels // ctx)
    pieces = exchange(pieces)

    seg_pad = jnp.concatenate([jnp.full((back * rows,), -1, jnp.int32), seg])
    seg_k = lax.dynamic_slice_in_dim(seg_pad, place * rows, (back + 1) * rows, 0)
    attended = attention(queries[0], blocks, seg_k[back * rows :, None], seg_k[None, :])

    lead = jnp.reshape(place % fold * (ctx // fold) + place // fold, (1,)).astype(jnp.int32)
    conv, parts = conv_select(lead, seg_col, pieces, conv_weight, conv_bias[None, :], select_parts)
    low_own = normalise(exchange(parts), rank)
    low = lax.all_gather(low_own, "ctx", axis=0, tiled=True)

    scanned = state_scan(
        seg_col,
        low,
        delta_parts,
        own_part(delta_bias),
        own_part(jnp.transpose(decay_log)),
        own_part(skip_gain),
        conv,
        ctx,
    )
    mixed = apply_gate(exchange(scanned), gate_input[0], shards // fold, fold)
    return (attended[None], mixed[None])


def solution(mesh):
    placed = (
        P("rep", "ctx", None),
        P("rep", "ctx", None),
        P("rep", "ctx", None),
        P("rep", "ctx", None),
        P("rep", "ctx", None),
        P("rep", None),
        P(),
        P(),
        P(None, "rep"),
        P(None, "rep"),
        P(),
        P(),
        P(),
    )
    return jax.shard_map(
        local,
        mesh=mesh,
        in_specs=placed,
        out_specs=(P("rep", "ctx", None), P("rep", "ctx", None)),
        check_vma=False,
    )
```

time: 1780 us -> 182 us (0.10)
  other arithmetic: 893 us -> 0.02 us
  local copies, waits for them, and re-layouts: 655 us -> 22.5 us
  waiting for transfers between devices: 136 us -> 54.4 us
  Pallas kernels: 0 us -> 58.2 us
  matrix products: 24 us -> 0 us
    pad x96 -> x0, local copies, waits for them, and re-layouts: 574 us -> none  [local_block(): lax.associative_scan(combine_pair, (decay, inject), axis=0)]
    mul x56 -> x0, other arithmetic: 304 us -> none  [the longest x40 226 us: combine_pair(): early_pair[0] * later_pair[0]]
    add x50 -> x0, other arithmetic: 176 us -> none  [the longest x48 172 us: local_block(): lax.associative_scan(combine_pair, (decay, inject), axis=0)]
    another operation x3 -> x0, other arithmetic: 145 us -> none  [the longest x1 144 us: local(): cum_delta = jnp.cumsum(delta_f, axis=0)]
    reduce_sum x18 -> x0, other arithmetic: 143 us -> none  [the longest x8 109 us: local_block(): result = jnp.sum(history * out_rows[:, :, None], axis=1)]
    all_gather x2, waiting for transfers between devices: 131 us -> 0.01 us  [gathered(): parts = lax.all_gather(own, 'rep', axis=0)]
    concatenate x48 -> x1, other arithmetic: 97.6 us -> 0.02 us  [local(): both = jnp.concatenate([keys[0], values[0]], axis=1)]
    pallas_call x0 -> x5, Pallas kernels: none -> 58.2 us  [the longest x1 31.3 us: state_scan(): pl.pallas_call(functools.partial(scan_kernel, rank), grid=(groups,), in_s...]
  transfers between devices with their start and end apart: 6 -> 7, of which waited for: 3 -> 3; matrix products, arithmetic and copies ran while one was open for 2% -> 9% of each run, Pallas kernels for 0% -> 11%
where the time goes in v1:
time: 182 us
  Pallas kernels  58.2 us (32%)
  waiting for transfers between devices  54.4 us (30%)
  local copies, waits for them, and re-layouts  22.5 us (12%)
  starting transfers between devices  20.7 us (11%)
  between operations  14.2 us (8%)
  blocking collectives  11.4 us (6%)
    pallas_call x1, Pallas kernels, state_scan(): pl.pallas_call(functools.partial(scan_kernel, rank), grid=(groups,), in_s...  31.3 us
    all_to_all x3, waiting for transfers between devices, exchange(): return lax.all_to_all(value, 'ctx', 0, 0, tiled=True)  30.6 us
    ppermute x2, waiting for transfers between devices, shifted(): return lax.ppermute(value, axis, pairs)  23.8 us
    all_to_all x3, starting transfers between devices, exchange(): return lax.all_to_all(value, 'ctx', 0, 0, tiled=True)  13.4 us
    all_gather x1, blocking collectives, local(): low = lax.all_gather(low_own, 'ctx', axis=0, tiled=True)  11.4 us
    pallas_call x1, Pallas kernels, attention(): pl.pallas_call(attention_kernel, grid=(KEY_VALUE_HEADS,), in_specs=[pl.Bl...  9.95 us
    pallas_call x1, Pallas kernels, conv_select(): pl.pallas_call(conv_select_kernel, grid_spec=pltpu.PrefetchScalarGridSpec...  8.53 us
    ppermute x2, starting transfers between devices, shifted(): return lax.ppermute(value, axis, pairs)  7.27 us
  transfers between devices with their start and end apart: 7, of which 3 were waited for; matrix products, arithmetic and copies ran while one was open for 9% of the time, Pallas kernels for 11%

profile of v1, /device:TPU:0, one launch (start us, length us, event | category | flops | bytes accessed | tf_op | source)
XLA Modules:
  0.0 181.5 jit_solution(319862642715351518)
XLA Ops:
  7.2 1.2 copy-done
  8.4 0.7 constant_dynamic-slice_fusion.4
  9.2 1.7 constant_dynamic-slice_fusion.3
  10.9 4.5 %reshape_squeeze.3 = bf16[128,8,1,4,256]{4,3,1,0,2:T(4,128)(2,1)} reshape(bf16[1,128,8192]{2,1,0:T(8,128)(2,1)} %param.16) | data formatting | bytes 4194304 | tf_op jit(solution)/shard_map/reshape;squeeze | solution.py:368
  15.4 1.9 %copy.32 = bf16[128,8,1,4,256]{4,1,0,3,2:T(8,128)(2,1)S(1)} copy(bf16[128,8,1,4,256]{4,3,1,0,2:T(4,128)(2,1)} %reshape_squeeze.3) | data formatting | bytes 4194304 | tf_op jit(solution)/shard_map/reshape;squeeze | solution.py:368
  17.3 2.3 %reshape.35 = bf16[4,128,2048]{2,1,0:T(8,128)(2,1)} reshape(bf16[4,1,128,8,256]{4,3,2,0,1:T(8,128)(2,1)S(1)} %bitcast.28) | data formatting | bytes 4194304 | tf_op jit(solution)/shard_map/reshape | solution.py:369
  19.6 5.3 %all-to-all-start = ((bf16[4,128,2048]{2,1,0:T(8,128)(2,1)}), bf16[4,128,2048]{2,1,0:T(8,128)(2,1)S(1)}, u32[]{:S(2)}, u32[]{:S(2)}) async-start(bf16[4,128,2048]{2,1,0:T(8,128)(2,1)} %reshape.35), calls=%async_computation | async-start | bytes 4194304 | tf_op jit(solution)/shard_map/all_to_all | solution.py:316
  24.9 0.1 copy.29.seg_ref
  25.1 24.7 %all-to-all-done.x_ref = bf16[4,128,2048]{2,1,0:T(8,128)(2,1)S(1)} async-done(((bf16[4,128,2048]{2,1,0:T(8,128)(2,1)}), bf16[4,128,2048]{2,1,0:T(8,128)(2,1)S(1)}, u32[]{:S(2)}, u32[]{:S(2)}) %all-to-all-start) | async-done | bytes 2097184 | tf_op jit(solution)/shard_map/all_to_all | solution.py:316
  49.8 1.7 copy-done.1
  51.5 0.9 copy-done.5
  52.4 8.5 %conv_select.1 = (bf16[16,512,128]{2,1,0:T(8,128)(2,1)S(1)}, bf16[4,128,544]{2,1,0:T(8,128)(2,1)S(1)}) custom-call(s32[1]{0:T(128)} %bitcast.7.place_ref, s32[512,1]{1,0:T(8,128)S(1)} %copy.29.seg_ref, bf16[4,128,2048]{2,1,0:T(8,128)(2,1)S(1)} %all-to-all-done.x_ref, f32[4,8192]{1,0:T(4,128)S(1)} %copy-done.5, f32[1,8192]{1,0:T(1,128)S(1)} %bitcast.27, ...), custom_call_target="tpu_custom_call" | custom-call | flops 1140850688 | bytes 6422528 | tf_op jit(solution)/shard_map/conv_select/pallas_call | solution.py:124
  61.0 0.8 copy-done.4
  61.8 1.3 copy-done.7
  63.1 2.2 %copy.26 = bf16[4,128,544]{1,2,0:T(8,128)(2,1)} copy(bf16[4,128,544]{2,1,0:T(8,128)(2,1)} %copy-done.4) | data formatting | bytes 1114112 | tf_op jit(solution)/shard_map/conv_select/pallas_call | solution.py:124
  65.4 3.5 %all-to-all-start.1 = ((bf16[4,128,544]{1,2,0:T(8,128)(2,1)}), bf16[4,128,544]{1,2,0:T(8,128)(2,1)S(1)}, u32[]{:S(2)}, u32[]{:S(2)}) async-start(bf16[4,128,544]{1,2,0:T(8,128)(2,1)} %copy.26), calls=%async_computation.1 | async-start | bytes 1114112 | tf_op jit(solution)/shard_map/all_to_all | solution.py:316
  68.9 0.4 reshape.38
  69.3 0.6 constant_dynamic-slice_fusion
  69.9 0.8 constant_dynamic-slice_fusion.1
  70.7 5.9 %all-to-all-done.1 = bf16[4,128,544]{1,2,0:T(8,128)(2,1)S(1)} async-done(((bf16[4,128,544]{1,2,0:T(8,128)(2,1)}), bf16[4,128,544]{1,2,0:T(8,128)(2,1)S(1)}, u32[]{:S(2)}, u32[]{:S(2)}) %all-to-all-start.1) | async-done | bytes 557088 | tf_op jit(solution)/shard_map/all_to_all | solution.py:316
  76.6 1.1 copy.27.part_ref
  77.7 1.9 %normalise.1 = bf16[128,544]{1,0:T(8,128)(2,1)} custom-call(bf16[4,128,544]{2,1,0:T(8,128)(2,1)} %copy.27.part_ref), custom_call_target="tpu_custom_call" | custom-call | tf_op jit(solution)/shard_map/normalise/pallas_call | solution.py:171
  79.6 11.4 %all_gather.17.low_ref = bf16[512,544]{1,0:T(8,128)(2,1)} all-gather(bf16[128,544]{1,0:T(8,128)(2,1)} %normalise.1), channel_id=1, replica_groups=mesh['ctx'=4,'rep'=8] {'ctx'}, dimensions={0}, use_global_device_ids=true | all-gather | bytes 696320 | tf_op jit(solution)/shard_map/all_gather | solution.py:379
  91.0 31.3 %state_scan.1 = bf16[4,128,2048]{2,1,0:T(8,128)(2,1)} custom-call(s32[512,1]{1,0:T(8,128)} %copy-done.3, bf16[512,544]{1,0:T(8,128)(2,1)} %all_gather.17.low_ref, bf16[8,512,256]{2,1,0:T(8,128)(2,1)} %bitcast.40, f32[16,128]{1,0:T(8,128)} %bitcast.39, f32[16,16,128]{2,1,0:T(8,128)} %bitcast.33, f32[16,128]{1,0:T(8,128)} %bitcast.38, ...), custom_call_target="tpu_custom_call" | custom-call | flops 100663296 | bytes 6291456 | tf_op jit(solution)/shard_map/state_scan/pallas_call | solution.py:252
  122.3 4.6 %all-to-all-start.2 = ((bf16[4,128,2048]{2,1,0:T(8,128)(2,1)}), bf16[4,128,2048]{2,1,0:T(8,128)(2,1)}, u32[]{:S(2)}, u32[]{:S(2)}) async-start(bf16[4,128,2048]{2,1,0:T(8,128)(2,1)} %state_scan.1), calls=%async_computation.2 | async-start | bytes 4194304 | tf_op jit(solution)/shard_map/all_to_all | solution.py:316
  127.0 4.1 %collective-permute-start = (bf16[128,1024]{1,0:T(8,128)(2,1)S(1)}, bf16[128,1024]{1,0:T(8,128)(2,1)S(1)}, u32[]{:S(2)}, u32[]{:S(2)}) collective-permute-start(bf16[128,1024]{1,0:T(8,128)(2,1)S(1)} %pad_maximum_fusion.refs_4_.refs_5_), channel_id=1, source_target_pairs={{0,16},{8,24},{1,17},{9,25},{2,18},{10,26},{3,19},{11,27},{4,20},{... | collective-permute-start | bytes 786440 | tf_op jit(solution)/shard_map/ppermute | solution.py:312
  131.1 3.2 %collective-permute-start.1 = (bf16[128,1024]{1,0:T(8,128)(2,1)S(1)}, bf16[128,1024]{1,0:T(8,128)(2,1)S(1)}, u32[]{:S(2)}, u32[]{:S(2)}) collective-permute-start(bf16[128,1024]{1,0:T(8,128)(2,1)S(1)} %pad_maximum_fusion.refs_4_.refs_5_), channel_id=1, source_target_pairs={{0,8},{8,16},{16,24},{1,9},{9,17},{17,25},{2,10},{10,18},{18,26},{... | collective-permute-start | bytes 786440 | tf_op jit(solution)/shard_map/ppermute | solution.py:312
  134.3 0.1 pad_dynamic-slice_fusion
  134.4 0.1 copy.23.seg_q_ref
  134.5 23.8 %collective-permute-done.refs_0_.refs_1_ = bf16[128,1024]{1,0:T(8,128)(2,1)S(1)} collective-permute-done((bf16[128,1024]{1,0:T(8,128)(2,1)S(1)}, bf16[128,1024]{1,0:T(8,128)(2,1)S(1)}, u32[]{:S(2)}, u32[]{:S(2)}) %collective-permute-start) | collective-permute-done | bytes 262176 | tf_op jit(solution)/shard_map/ppermute | solution.py:312
  158.3 9.9 %attention.1 = bf16[128,4096]{1,0:T(8,128)(2,1)} custom-call(s32[128,1]{1,0:T(8,128)S(1)} %copy.23.seg_q_ref, s32[1,384]{1,0:T(1,128)S(1)} %broadcast_in_dim.17.seg_k_ref, bf16[128,4096]{1,0:T(8,128)(2,1)S(1)} %bitcast.26, bf16[128,1024]{1,0:T(8,128)(2,1)S(1)} %collective-permute-done.refs_0_.refs_1_, ...), custom_call_target="tpu_custom_call" | custom-call | flops 805306368 | bytes 2097152 | tf_op jit(solution)/shard_map/attention/pallas_call | solution.py:55
  168.2 6.5 %gate.1 = bf16[128,8192]{1,0:T(8,128)(2,1)} custom-call(bf16[4,128,2048]{2,1,0:T(8,128)(2,1)} %all-to-all-done.2.y_ref, bf16[128,8192]{1,0:T(8,128)(2,1)} %bitcast.29), custom_call_target="tpu_custom_call" | custom-call | flops 4194304 | bytes 6291456 | tf_op jit(solution)/shard_map/gate/pallas_call | solution.py:293
  (36 shorter events, 0.2 us)
Async XLA Ops:
  7.2 1.3 copy-start
  7.2 42.6 %all-gather.5.cloned.1.call-start = ((), (), s32[]{:S(2)}) async-start(), calls=%async_computation.3 | async-start | bytes 2506752 | tf_op jit(solution)/shard_map/all_gather | solution.py:356
  9.2 81.8 %all-gather.7.cloned.1.call-start = ((), (), s32[]{:S(2)}) async-start(), calls=%async_computation.4 | async-start | bytes 2359296 | tf_op jit(solution)/shard_map/all_gather | solution.py:356
  19.6 5.3 %copy-start.13 = (s32[1,512]{1,0:T(1,128)S(1)}, s32[1,512]{1,0:T(1,128)}, u32[]{:S(2)}) copy-start(s32[1,512]{1,0:T(1,128)} %param.18) | copy-start | bytes 6148
  19.6 30.2 %copy-start.6 = (f32[8192]{0:T(1024)S(1)}, f32[8192]{0:T(1024)}, u32[]{:S(2)}) copy-start(f32[8192]{0:T(1024)} %param.20) | copy-start | bytes 98308
  19.6 30.2 %all-to-all-start = ((bf16[4,128,2048]{2,1,0:T(8,128)(2,1)}), bf16[4,128,2048]{2,1,0:T(8,128)(2,1)S(1)}, u32[]{:S(2)}, u32[]{:S(2)}) async-start(bf16[4,128,2048]{2,1,0:T(8,128)(2,1)} %reshape.35), calls=%async_computation | async-start | bytes 4194304 | tf_op jit(solution)/shard_map/all_to_all | solution.py:316
  25.1 35.9 %copy-start.3 = (s32[512,1]{1,0:T(8,128)}, s32[512,1]{1,0:T(8,128)S(1)}, u32[]{:S(2)}) copy-start(s32[512,1]{1,0:T(8,128)S(1)} %copy.29.seg_ref) | copy-start | bytes 6148
  49.8 1.7 copy-start.1
  51.5 0.9 copy-start.5
  61.0 0.8 copy-start.4
  61.8 1.3 copy-start.7
  63.1 5.7 %copy-start.11 = (f32[8192]{0:T(1024)S(1)}, f32[8192]{0:T(1024)}, u32[]{:S(2)}) copy-start(f32[8192]{0:T(1024)} %param.23) | copy-start | bytes 98308
  63.1 5.7 %copy-start.12 = (f32[8192]{0:T(1024)S(1)}, f32[8192]{0:T(1024)}, u32[]{:S(2)}) copy-start(f32[8192]{0:T(1024)} %param.25) | copy-start | bytes 98308
  63.1 5.8 %copy-start.8 = (f32[8192,16]{0,1:T(8,128)S(1)}, f32[8192,16]{0,1:T(8,128)}, u32[]{:S(2)}) copy-start(f32[8192,16]{0,1:T(8,128)} %param.24) | copy-start | bytes 1572868
  65.4 11.2 %all-to-all-start.1 = ((bf16[4,128,544]{1,2,0:T(8,128)(2,1)}), bf16[4,128,544]{1,2,0:T(8,128)(2,1)S(1)}, u32[]{:S(2)}, u32[]{:S(2)}) async-start(bf16[4,128,544]{1,2,0:T(8,128)(2,1)} %copy.26), calls=%async_computation.1 | async-start | bytes 1114112 | tf_op jit(solution)/shard_map/all_to_all | solution.py:316
  122.3 4.6 %copy-start.9 = (bf16[1,128,512]{2,1,0:T(8,128)(2,1)S(1)}, bf16[1,128,512]{2,1,0:T(8,128)(2,1)}, u32[]{:S(2)}) copy-start(bf16[1,128,512]{2,1,0:T(8,128)(2,1)} %param.15) | copy-start | bytes 393220
  122.3 4.6 %copy-start.10 = (bf16[1,128,512]{2,1,0:T(8,128)(2,1)S(1)}, bf16[1,128,512]{2,1,0:T(8,128)(2,1)}, u32[]{:S(2)}) copy-start(bf16[1,128,512]{2,1,0:T(8,128)(2,1)} %param.14) | copy-start | bytes 393220
  122.3 36.0 %copy-start.2 = (bf16[1,128,4096]{2,1,0:T(8,128)(2,1)S(1)}, bf16[1,128,4096]{2,1,0:T(8,128)(2,1)}, u32[]{:S(2)}) copy-start(bf16[1,128,4096]{2,1,0:T(8,128)(2,1)} %param.13) | copy-start | bytes 3145732
  122.3 45.9 %all-to-all-start.2 = ((bf16[4,128,2048]{2,1,0:T(8,128)(2,1)}), bf16[4,128,2048]{2,1,0:T(8,128)(2,1)}, u32[]{:S(2)}, u32[]{:S(2)}) async-start(bf16[4,128,2048]{2,1,0:T(8,128)(2,1)} %state_scan.1), calls=%async_computation.2 | async-start | bytes 4194304 | tf_op jit(solution)/shard_map/all_to_all | solution.py:316
  127.0 31.3 %collective-permute-start = (bf16[128,1024]{1,0:T(8,128)(2,1)S(1)}, bf16[128,1024]{1,0:T(8,128)(2,1)S(1)}, u32[]{:S(2)}, u32[]{:S(2)}) collective-permute-start(bf16[128,1024]{1,0:T(8,128)(2,1)S(1)} %pad_maximum_fusion.refs_4_.refs_5_), channel_id=1, source_target_pairs={{0,16},{8,24},{1,17},{9,25},{2,18},{10,26},{3,19},{11,27},{4,20},{... | collective-permute-start | bytes 786440 | tf_op jit(solution)/shard_map/ppermute | solution.py:312
  131.1 27.2 %collective-permute-start.1 = (bf16[128,1024]{1,0:T(8,128)(2,1)S(1)}, bf16[128,1024]{1,0:T(8,128)(2,1)S(1)}, u32[]{:S(2)}, u32[]{:S(2)}) collective-permute-start(bf16[128,1024]{1,0:T(8,128)(2,1)S(1)} %pad_maximum_fusion.refs_4_.refs_5_), channel_id=1, source_target_pairs={{0,8},{8,16},{16,24},{1,9},{9,17},{17,25},{2,10},{10,18},{18,26},{... | collective-permute-start | bytes 786440 | tf_op jit(solution)/shard_map/ppermute | solution.py:312
Sparse Core Ops, SparseCore 0:
  10.2 32.8 all-gather.4
  44.7 28.5 all-gather.6

commit v2 on v1

v2 whole, which is shorter than its diff:
```python
import functools
import math

import jax
import jax.numpy as jnp
from jax import lax
from jax.experimental import pallas as pl
from jax.experimental.pallas import tpu as pltpu
from jax.sharding import PartitionSpec as P

QUERY_HEADS = 32
KEY_VALUE_HEADS = 4
HEAD_WIDTH = 128
LANES = 128
SUBLANES = 8
LOG2E = 1.0 / math.log(2.0)
FAR = 1e30


def silu(value):
    return 0.5 * value * (1.0 + jnp.tanh(0.5 * value))


def attention_kernel(begin, seg_q_ref, seg_k_ref, q_ref, *refs):
    out_ref = refs[-1]
    refs = refs[: -1 if begin == 0 else -2]
    rows = q_ref.shape[0]
    span = seg_k_ref.shape[1]
    groups = QUERY_HEADS // KEY_VALUE_HEADS
    row = lax.broadcasted_iota(jnp.int32, (rows, span), 0) + (span - rows)
    col = lax.broadcasted_iota(jnp.int32, (rows, span), 1)
    allowed = (col <= row) & (seg_q_ref[...] == seg_k_ref[...])
    shift = jnp.where(allowed, 0.0, -FAR)
    keys = jnp.concatenate([ref[...] for ref in refs[0::2]], axis=0)
    vals = jnp.concatenate([ref[...] for ref in refs[1::2]], axis=0)
    factor = LOG2E / math.sqrt(HEAD_WIDTH)
    batch = 4
    for first in range(0, groups, batch):
        cuts = [slice(head * HEAD_WIDTH, (head + 1) * HEAD_WIDTH) for head in range(first, first + batch)]
        scores = [
            lax.dot_general(q_ref[:, cut], keys, (((1,), (1,)), ((), ())), preferred_element_type=jnp.float32)
            for cut in cuts
        ]
        scores = [score + shift for score in scores]
        tops = [jnp.max(score, axis=-1, keepdims=True) for score in scores]
        weights = [jnp.exp2((score - top) * factor) for score, top in zip(scores, tops)]
        norms = [jnp.sum(weight, axis=-1, keepdims=True) for weight in weights]
        totals = [jnp.dot(weight.astype(jnp.bfloat16), vals, preferred_element_type=jnp.float32) for weight in weights]
        for cut, total, norm in zip(cuts, totals, norms):
            out_ref[:, cut] = (total / norm).astype(out_ref.dtype)


def attention(queries, blocks, seg_q, seg_k, begin, end, before=None):
    rows = queries.shape[0]
    span = seg_k.shape[1]
    group_width = QUERY_HEADS // KEY_VALUE_HEADS * HEAD_WIDTH
    key_spec = pl.BlockSpec((rows, HEAD_WIDTH), lambda h: (0, begin + h))
    value_spec = pl.BlockSpec((rows, HEAD_WIDTH), lambda h: (0, KEY_VALUE_HEADS + begin + h))
    wide = pl.BlockSpec((rows, group_width), lambda h: (0, begin + h))
    operands = [seg_q, seg_k, queries] + [block for block in blocks for _ in range(2)]
    in_specs = [
        pl.BlockSpec((rows, 1), lambda h: (0, 0)),
        pl.BlockSpec((1, span), lambda h: (0, 0)),
        wide,
        *([key_spec, value_spec] * len(blocks)),
    ]
    aliases = {}
    if before is not None:
        aliases = {len(operands): 0}
        operands.append(before)
        in_specs.append(pl.BlockSpec(memory_space=pl.ANY))
    return pl.pallas_call(
        functools.partial(attention_kernel, begin),
        grid=(end - begin,),
        in_specs=in_specs,
        out_specs=wide,
        out_shape=jax.ShapeDtypeStruct(queries.shape, jnp.bfloat16),
        input_output_aliases=aliases,
        compiler_params=pltpu.CompilerParams(vmem_limit_bytes=32 << 20),
        cost_estimate=pl.CostEstimate(
            flops=4 * rows * span * group_width * (end - begin),
            bytes_accessed=4 * rows * group_width * (end - begin),
            transcendentals=rows * span * group_width // HEAD_WIDTH * (end - begin),
        ),
        name=f"attention_{begin}",
    )(*operands)


def pack_kernel(order, fold, x_ref, out_ref):
    ctx, _, width = out_ref.shape
    for piece in range(ctx):
        place = piece % fold * (ctx // fold) + piece // fold
        out_ref[piece] = x_ref[:, place * width : (place + 1) * width]


def pack(value, ctx, shards, order, fold):
    rows, channels = value.shape
    width = channels // shards // ctx
    return pl.pallas_call(
        functools.partial(pack_kernel, order, fold),
        grid=(shards,),
        in_specs=[pl.BlockSpec((rows, ctx * width), lambda s: (0, order(s)))],
        out_specs=pl.BlockSpec((ctx, rows, width), lambda s: (0, 0, s)),
        out_shape=jax.ShapeDtypeStruct((ctx, rows, shards * width), value.dtype),
        name="pack",
    )(value)


def conv_select_kernel(lead_ref, seg_ref, x_ref, weight_ref, bias_ref, select_ref, conv_ref, part_ref, masks, padded, total):
    step = pl.program_id(0)
    toks = seg_ref.shape[0]
    width = x_ref.shape[2]
    pieces = x_ref.shape[0]
    rows = x_ref.shape[1]
    outputs = select_ref.shape[1]

    @pl.when(step == 0)
    def _():
        wide_seg = jnp.broadcast_to(seg_ref[...], (toks, LANES)).astype(jnp.float32)
        padded[0:SUBLANES, 0:LANES] = jnp.full((SUBLANES, LANES), -1.0, jnp.float32)
        padded[SUBLANES : SUBLANES + toks, 0:LANES] = wide_seg
        for tap in range(3):
            before = padded[SUBLANES - 3 + tap : SUBLANES - 3 + tap + toks, 0:LANES]
            masks[tap] = jnp.where(before == wide_seg, 1.0, 0.0)
        padded[0:SUBLANES, :] = jnp.zeros((SUBLANES, width), jnp.float32)
        total[...] = jnp.zeros_like(total)

    for piece in range(pieces):
        padded[SUBLANES + piece * rows : SUBLANES + (piece + 1) * rows, :] = x_ref[piece].astype(jnp.float32)
    outs = []
    for tile in range(width // LANES):
        lanes = slice(tile * LANES, (tile + 1) * LANES)
        running = jnp.broadcast_to(bias_ref[0:1, lanes], (toks, LANES))
        for tap in range(4):
            moved = padded[SUBLANES - 3 + tap : SUBLANES - 3 + tap + toks, lanes]
            term = weight_ref[tap : tap + 1, lanes] * moved
            running = running + (term * masks[tap] if tap < 3 else term)
        conv = silu(running).astype(jnp.bfloat16)
        conv_ref[:, lanes] = conv
        outs.append(conv)
    conv_all = jnp.concatenate(outs, axis=1) if len(outs) > 1 else outs[0]
    total[...] += lax.dot_general(
        conv_all, select_ref[0], (((1,), (1,)), ((), ())), preferred_element_type=jnp.float32
    )

    @pl.when(step == pl.num_programs(0) - 1)
    def _():
        spare = part_ref.shape[2] - outputs
        for piece in range(pieces):
            part_ref[piece, :, 0:outputs] = total[piece * rows : (piece + 1) * rows, :].astype(part_ref.dtype)
            part_ref[piece, :, outputs:] = jnp.zeros((rows, spare), part_ref.dtype)


def conv_select(lead, seg_col, pieces, conv_weight, conv_bias, select_parts, order):
    shards, outputs, width = select_parts.shape
    ctx, rows, _ = pieces.shape
    toks = ctx * rows
    padded_outputs = -(-outputs // LANES) * LANES
    return pl.pallas_call(
        conv_select_kernel,
        grid_spec=pltpu.PrefetchScalarGridSpec(
            num_scalar_prefetch=1,
            grid=(shards,),
            in_specs=[
                pl.BlockSpec((toks, 1), lambda s, p: (0, 0)),
                pl.BlockSpec((ctx, rows, width), lambda s, p: (0, 0, s)),
                pl.BlockSpec((4, width), lambda s, p: (0, order(s) * ctx + p[0])),
                pl.BlockSpec((1, width), lambda s, p: (0, order(s) * ctx + p[0])),
                pl.BlockSpec((1, outputs, width), lambda s, p: (s, 0, 0)),
            ],
            out_specs=[
                pl.BlockSpec((toks, width), lambda s, p: (0, s)),
                pl.BlockSpec((ctx, rows, padded_outputs), lambda s, p: (0, 0, 0)),
            ],
            scratch_shapes=[
                pltpu.VMEM((3, toks, LANES), jnp.float32),
                pltpu.VMEM((SUBLANES + toks, width), jnp.float32),
                pltpu.VMEM((toks, outputs), jnp.float32),
            ],
        ),
        out_shape=[
            jax.ShapeDtypeStruct((toks, shards * width), jnp.bfloat16),
            jax.ShapeDtypeStruct((ctx, rows, padded_outputs), jnp.bfloat16),
        ],
        compiler_params=pltpu.CompilerParams(vmem_limit_bytes=40 << 20),
        cost_estimate=pl.CostEstimate(
            flops=2 * toks * shards * width * outputs,
            bytes_accessed=2 * pieces.size * 2 + 2 * select_parts.size,
            transcendentals=pieces.size,
        ),
        name="conv_select",
    )(lead, seg_col, pieces, conv_weight, conv_bias, select_parts)


def normalise_kernel(rank, part_ref, out_ref):
    pieces = part_ref.shape[0]
    total = part_ref[0].astype(jnp.float32)
    for piece in range(1, pieces):
        total = total + part_ref[piece].astype(jnp.float32)
    low = total[:, :rank]
    scale = lax.rsqrt(jnp.mean(low * low, axis=-1, keepdims=True) + 1e-06)
    low = (low * scale).astype(out_ref.dtype)
    maps = total[:, rank:].astype(out_ref.dtype)
    for piece in range(pieces):
        out_ref[piece, :, :rank] = low
        out_ref[piece, :, rank:] = maps


def normalise(parts, rank):
    return pl.pallas_call(
        functools.partial(normalise_kernel, rank),
        out_shape=jax.ShapeDtypeStruct(parts.shape, jnp.bfloat16),
        name="normalise",
    )(parts)


def scan_kernel(rank, seg_ref, low_ref, weight_ref, bias_ref, decay_ref, gain_ref, conv_ref, out_ref,
                in_wide, out_diag, delta_rows, drive_rows, held_even, held_odd):
    toks = seg_ref.shape[0]
    states = decay_ref.shape[0]
    shards = weight_ref.shape[0]
    width = weight_ref.shape[2]
    tiles = shards * width // LANES
    rows = out_ref.shape[1]
    block = 16
    span = block * states

    for n in range(states):
        column = low_ref[:, rank + n : rank + n + 1].astype(jnp.float32)
        in_wide[:, n, :] = jnp.broadcast_to(column, (toks, LANES))
    lane = lax.broadcasted_iota(jnp.int32, (states, span), 1)
    spread = jnp.where(lane % states == lax.broadcasted_iota(jnp.int32, (states, span), 0), 1.0, 0.0)
    copies = jnp.dot(
        low_ref[:, rank + states : rank + 2 * states], spread.astype(jnp.bfloat16), preferred_element_type=jnp.float32
    )
    here = lax.broadcasted_iota(jnp.int32, (toks, span), 1) // states
    there = lax.broadcasted_iota(jnp.int32, (toks, span), 0) % block
    out_diag[...] = jnp.where(here == there, copies, 0.0).astype(jnp.bfloat16)

    seg = jnp.broadcast_to(seg_ref[...], (toks, LANES)).astype(jnp.float32)
    drive_rows[0, 0:SUBLANES, :] = jnp.full((SUBLANES, LANES), -1.0, jnp.float32)
    drive_rows[0, SUBLANES : SUBLANES + toks, :] = seg
    before = drive_rows[0, SUBLANES - 1 : SUBLANES - 1 + toks, :]
    reset = jnp.where(before == seg, 0.0, FAR)
    low = low_ref[:, 0:rank]
    for shard in range(shards):
        pre = jnp.dot(low, weight_ref[shard], preferred_element_type=jnp.float32)
        for part in range(width // LANES):
            tile = shard * (width // LANES) + part
            lanes = slice(tile * LANES, (tile + 1) * LANES)
            value = pre[:, part * LANES : (part + 1) * LANES] + bias_ref[:, lanes]
            raised = jnp.exp(-jnp.abs(value))
            log_part = jnp.where(
                raised < 0.01,
                raised * (1.0 - raised * (0.5 - raised * (1.0 / 3.0))),
                jnp.log(1.0 + raised),
            )
            delta = (jnp.maximum(value, 0.0) + log_part).astype(jnp.bfloat16).astype(jnp.float32)
            delta_rows[tile] = delta + reset
            drive_rows[tile, 0:toks, :] = delta * conv_ref[:, lanes].astype(jnp.float32)

    rates = [-LOG2E * jnp.exp(decay_ref[:, tile * LANES : (tile + 1) * LANES]) for tile in range(tiles)]

    def advance(index, held, history):
        held = list(held)
        for inner in range(block):
            t = index * block + inner
            into = in_wide[t]
            for tile in range(tiles):
                lanes = slice(tile * LANES, (tile + 1) * LANES)
                grow = jnp.exp2(delta_rows[tile, pl.ds(t, 1), :] * rates[tile])
                held[tile] = grow * held[tile] + into * drive_rows[tile, pl.ds(t, 1), :]
                history[inner * states : (inner + 1) * states, lanes] = held[tile].astype(jnp.bfloat16)
        return tuple(held)

    def finish(index, history):
        first = pl.multiple_of(index * block, block)
        mixed = jnp.dot(out_diag[pl.ds(first, block), :], history[...], preferred_element_type=jnp.float32)
        full = mixed + gain_ref[...] * conv_ref[pl.ds(first, block), :].astype(jnp.float32)
        place = pl.multiple_of(lax.rem(first, rows), block)
        out_ref[lax.div(first, rows), pl.ds(place, block), :] = full.astype(out_ref.dtype)

    held_odd[...] = jnp.zeros_like(held_odd)

    def pair(index, held):
        held = advance(2 * index, held, held_even)
        finish(jnp.maximum(2 * index - 1, 0), held_odd)
        held = advance(2 * index + 1, held, held_odd)
        finish(2 * index, held_even)
        return held

    start = tuple(jnp.zeros((states, LANES), jnp.float32) for _ in range(tiles))
    count = toks // block
    lax.fori_loop(0, count // 2, pair, start)
    finish(count - 1, held_odd)


def state_scan(seg_col, low, delta_parts, bias, decay, gain, conv, ctx, call, calls):
    toks = low.shape[0]
    shards, rank, width = delta_parts.shape
    shards = shards // calls
    states = decay.shape[0]
    rows = toks // ctx
    wide = shards * width
    steps = toks * wide * states
    return pl.pallas_call(
        functools.partial(scan_kernel, rank),
        grid=(1,),
        in_specs=[
            pl.BlockSpec((toks, 1), lambda g: (0, 0)),
            pl.BlockSpec(low.shape, lambda g: (0, 0)),
            pl.BlockSpec((shards, rank, width), lambda g: (call, 0, 0)),
            pl.BlockSpec((1, wide), lambda g: (0, call)),
            pl.BlockSpec((states, wide), lambda g: (0, call)),
            pl.BlockSpec((1, wide), lambda g: (0, call)),
            pl.BlockSpec((toks, wide), lambda g: (0, call)),
        ],
        out_specs=pl.BlockSpec((ctx, rows, wide), lambda g: (0, 0, 0)),
        out_shape=jax.ShapeDtypeStruct((ctx, rows, wide), jnp.bfloat16),
        scratch_shapes=[
            pltpu.VMEM((toks, states, LANES), jnp.float32),
            pltpu.VMEM((toks, 16 * states), jnp.bfloat16),
            pltpu.VMEM((wide // LANES, toks, LANES), jnp.float32),
            pltpu.VMEM((wide // LANES, toks + SUBLANES, LANES), jnp.float32),
            pltpu.VMEM((16 * states, wide), jnp.bfloat16),
            pltpu.VMEM((16 * states, wide), jnp.bfloat16),
        ],
        compiler_params=pltpu.CompilerParams(vmem_limit_bytes=56 << 20),
        cost_estimate=pl.CostEstimate(
            flops=6 * steps, bytes_accessed=2 * delta_parts.size // calls + 4 * toks * wide, transcendentals=steps
        ),
        name=f"state_scan_{call}",
    )(seg_col, low, delta_parts, bias, decay, gain, conv)


def gate_kernel(fold, y_ref, gate_ref, *refs):
    out_ref = refs[-1]
    ctx, _, width = y_ref.shape
    for piece in range(ctx):
        place = piece % fold * (ctx // fold) + piece // fold
        lanes = slice(place * width, (place + 1) * width)
        gate = gate_ref[:, lanes].astype(jnp.float32)
        out_ref[:, lanes] = (y_ref[piece].astype(jnp.float32) * silu(gate)).astype(out_ref.dtype)


def apply_gate(pieces, gate, width, order, fold, first, before=None):
    ctx, rows, total = pieces.shape
    wide = pl.BlockSpec((rows, ctx * width), lambda s: (0, order(first + s)))
    operands = [pieces, gate]
    in_specs = [pl.BlockSpec((ctx, rows, width), lambda s: (0, 0, s)), wide]
    aliases = {}
    if before is not None:
        aliases = {2: 0}
        operands.append(before)
        in_specs.append(pl.BlockSpec(memory_space=pl.ANY))
    return pl.pallas_call(
        functools.partial(gate_kernel, fold),
        grid=(total // width,),
        in_specs=in_specs,
        out_specs=wide,
        out_shape=jax.ShapeDtypeStruct(gate.shape, jnp.bfloat16),
        input_output_aliases=aliases,
        cost_estimate=pl.CostEstimate(
            flops=4 * pieces.size, bytes_accessed=6 * pieces.size, transcendentals=pieces.size
        ),
        name=f"gate_{first}",
    )(*operands)


def shifted(value, axis, by):
    size = lax.axis_size(axis)
    pairs = [(i, i + by) for i in range(size) if 0 <= i + by < size]
    return lax.ppermute(value, axis, pairs)


def exchange(value):
    return lax.all_to_all(value, "ctx", 0, 0, tiled=True)


def local(
    queries,
    keys,
    values,
    mixer_input,
    gate_input,
    segment_ids,
    conv_weight,
    conv_bias,
    select_weight,
    delta_weight,
    delta_bias,
    decay_log,
    skip_gain,
):
    ctx = lax.axis_size("ctx")
    shards = lax.axis_size("rep")
    place = lax.axis_index("ctx")
    rows, channels = mixer_input.shape[1:]
    rank = delta_weight.shape[0]
    states = decay_log.shape[1]
    width = max(channels // (shards * ctx), LANES)
    fold = width * shards * ctx // channels
    seg = segment_ids[0]
    toks = seg.shape[0]
    seg_col = seg[:, None]
    back = min(ctx - 1, -(-(toks // 2 - 1) // rows))

    slots = shards // fold
    half = slots // 2

    def order(slot):
        return slot % half * 2 + slot // half if fold == 1 else slot

    def own_part(array):
        cut = array.reshape(array.shape[:-1] + (slots, fold, ctx // fold, width))
        cut = lax.dynamic_index_in_dim(cut, place // fold, cut.ndim - 2, keepdims=False)
        cut = lax.dynamic_index_in_dim(cut, place % fold, cut.ndim - 2, keepdims=False)
        if fold == 1:
            cut = cut.reshape(array.shape[:-1] + (half, 2, width))
            cut = jnp.swapaxes(cut, -3, -2)
        return cut.reshape(array.shape[:-1] + (slots * width,))

    def gathered(weight):
        own = lax.dynamic_slice_in_dim(weight, place // fold * width, width, 1)
        if fold == 1:
            same_core = [list(range(core, shards, 2)) for core in range(2)]
            same_chip = [[chip, chip + 1] for chip in range(0, shards, 2)]
            parts = lax.all_gather(own, "rep", axis=0, axis_index_groups=same_core)
            return lax.all_gather(parts, "rep", axis=0, axis_index_groups=same_chip, tiled=True)
        parts = lax.all_gather(own, "rep", axis=0).reshape((slots, fold) + own.shape)
        return lax.dynamic_index_in_dim(parts, place % fold, 1, keepdims=False)

    select_parts = gathered(select_weight)
    delta_parts = gathered(delta_weight)

    both = jnp.concatenate([keys[0], values[0]], axis=1)
    blocks = [shifted(both, "ctx", by) for by in range(back, 0, -1)] + [both]

    pieces = exchange(pack(mixer_input[0], ctx, slots, order, fold))
    pieces, blocks = lax.optimization_barrier((pieces, blocks))

    lead = jnp.reshape(place % fold * (ctx // fold) + place // fold, (1,)).astype(jnp.int32)
    conv, parts = conv_select(lead, seg_col, pieces, conv_weight, conv_bias[None, :], select_parts, order)

    seg_pad = jnp.concatenate([jnp.full((back * rows,), -1, jnp.int32), seg])
    seg_k = lax.dynamic_slice_in_dim(seg_pad, place * rows, (back + 1) * rows, 0)
    seg_q = seg_k[back * rows :, None]
    parts, blocks = lax.optimization_barrier((parts, blocks))
    middle = KEY_VALUE_HEADS // 2
    attended = attention(queries[0], blocks, seg_q, seg_k[None, :], 0, middle)
    parts, attended = lax.optimization_barrier((exchange(parts), attended))
    low_own = normalise(parts, rank)
    low_own, attended = lax.optimization_barrier((low_own, attended))
    attended = attention(queries[0], blocks, seg_q, seg_k[None, :], middle, KEY_VALUE_HEADS, attended)
    low, attended = lax.optimization_barrier((exchange(low_own), attended))
    low = low.reshape(toks, low.shape[2])

    calls = 2
    bias = own_part(delta_bias)[None, :]
    gain = own_part(skip_gain)[None, :]
    decay = own_part(jnp.transpose(decay_log))
    scanned = [
        exchange(state_scan(seg_col, low, delta_parts, bias, decay, gain, conv, ctx, call, calls))
        for call in range(calls)
    ]
    mixed = None
    for call in range(calls):
        mixed = apply_gate(scanned[call], gate_input[0], width, order, fold, call * slots // calls, mixed)
    return (attended[None], mixed[None])


def solution(mesh):
    placed = (
        P("rep", "ctx", None),
        P("rep", "ctx", None),
        P("rep", "ctx", None),
        P("rep", "ctx", None),
        P("rep", "ctx", None),
        P("rep", None),
        P(),
        P(),
        P(None, "rep"),
        P(None, "rep"),
        P(),
        P(),
        P(),
    )
    return jax.shard_map(
        local,
        mesh=mesh,
        in_specs=placed,
        out_specs=(P("rep", "ctx", None), P("rep", "ctx", None)),
        check_vma=False,
    )
```

time: 182 us -> 201 us (1.10)
  waiting for transfers between devices: 54.4 us -> 72.7 us
  blocking collectives: 11.4 us -> 0 us
  Pallas kernels: 58.2 us -> 68.6 us
  starting transfers between devices: 20.7 us -> 28 us
  local copies, waits for them, and re-layouts: 22.5 us -> 15.9 us
    all_gather x2 -> x4, waiting for transfers between devices: 0.01 us -> 50.4 us  [the longest x2 50.4 us: gathered(): parts = lax.all_gather(own, 'rep', axis=0, axis_index_groups=same_core)]
    ppermute x2, waiting for transfers between devices: 23.8 us -> 5.36 us  [shifted(): return lax.ppermute(value, axis, pairs)]
    all_to_all x3 -> x5, waiting for transfers between devices: 30.6 us -> 16.9 us  [exchange(): return lax.all_to_all(value, 'ctx', 0, 0, tiled=True)]
    all_gather x1 -> x0, blocking collectives: 11.4 us -> none  [local(): low = lax.all_gather(low_own, 'ctx', axis=0, tiled=True)]
    pallas_call x3 -> x7, Pallas kernels: 47.7 us -> 57.8 us  [the longest x2 37.7 us: state_scan(): pl.pallas_call(functools.partial(scan_kernel, rank), grid=(1,), in_specs=...]
    all_to_all x3 -> x5, starting transfers between devices: 13.4 us -> 19.7 us  [exchange(): return lax.all_to_all(value, 'ctx', 0, 0, tiled=True)]
    another operation x2, local copies, waits for them, and re-layouts: 6.35 us -> 1.23 us  [the longest x1 0.62 us: local(): bias = own_part(delta_bias)[None, :]]
    unnamed x28, local copies, waits for them, and re-layouts: 5.98 us -> 8.68 us
  transfers between devices with their start and end apart: 7 -> 11, of which waited for: 3 -> 6; matrix products, arithmetic and copies ran while one was open for 9% -> 4% of each run, Pallas kernels for 11% -> 23%
where the time goes in v2:
time: 201 us; the launch traced here: 200 us
  waiting for transfers between devices  72.7 us (36%)
  Pallas kernels  68.6 us (34%)
  starting transfers between devices  28 us (14%)
  local copies, waits for them, and re-layouts  15.9 us (8%)
  between operations  13.9 us (7%)
    all_gather x2, waiting for transfers between devices, gathered(): parts = lax.all_gather(own, 'rep', axis=0, axis_index_groups=same_core)  50.4 us
    pallas_call x2, Pallas kernels, state_scan(): pl.pallas_call(functools.partial(scan_kernel, rank), grid=(1,), in_specs=...  37.7 us
    all_to_all x5, starting transfers between devices, exchange(): return lax.all_to_all(value, 'ctx', 0, 0, tiled=True)  19.7 us
    all_to_all x5, waiting for transfers between devices, exchange(): return lax.all_to_all(value, 'ctx', 0, 0, tiled=True)  16.9 us
    pallas_call x1, Pallas kernels, conv_select(): pl.pallas_call(conv_select_kernel, grid_spec=pltpu.PrefetchScalarGridSpec...  8.76 us
    unnamed x28, local copies, waits for them, and re-layouts  8.68 us
    ppermute x2, starting transfers between devices, shifted(): return lax.ppermute(value, axis, pairs)  8.18 us
    pallas_call x2, Pallas kernels, apply_gate(): pl.pallas_call(functools.partial(gate_kernel, fold), grid=(total // width...  7.56 us
  transfers between devices with their start and end apart: 11, of which 6 were waited for; matrix products, arithmetic and copies ran while one was open for 4% of the time, Pallas kernels for 23%

profile of v2, /device:TPU:0, one launch (start us, length us, event | category | flops | bytes accessed | tf_op | source)
XLA Modules:
  0.0 200.2 jit_solution(12134791337563626372)
XLA Ops:
  7.2 1.2 copy-done
  9.2 1.7 constant_dynamic-slice_fusion.1
  11.0 30.9 %all-gather.11.cloned.1.call-done = bf16[2176,256]{1,0:T(8,128)(2,1)} async-done(((bf16[544,256]{1,0:T(8,128)(2,1)}), bf16[2176,256]{1,0:T(8,128)(2,1)}) %all-gather.11.cloned.1.call-update) | async-done | bytes 1114128 | tf_op jit(solution)/shard_map/all_gather | solution.py:428
  41.9 5.7 %pack.1 = bf16[4,128,2048]{2,1,0:T(8,128)(2,1)} custom-call(bf16[128,8192]{1,0:T(8,128)(2,1)} %bitcast.29), custom_call_target="tpu_custom_call" | custom-call | tf_op jit(solution)/shard_map/pack/pallas_call | solution.py:99
  47.6 3.8 %all-to-all-start = ((bf16[4,128,2048]{2,1,0:T(8,128)(2,1)}), bf16[4,128,2048]{2,1,0:T(8,128)(2,1)S(1)}, u32[]{:S(2)}, u32[]{:S(2)}) async-start(bf16[4,128,2048]{2,1,0:T(8,128)(2,1)} %pack.1), calls=%async_computation | async-start | bytes 4194304 | tf_op jit(solution)/shard_map/all_to_all | solution.py:377
  51.4 19.5 %all-gather.13.cloned.1.call-done = bf16[2048,256]{1,0:T(8,128)(2,1)} async-done(((bf16[512,256]{1,0:T(8,128)(2,1)}), bf16[2048,256]{1,0:T(8,128)(2,1)}) %all-gather.13.cloned.1.call-update) | async-done | bytes 1048592 | tf_op jit(solution)/shard_map/all_gather | solution.py:428
  70.9 1.0 pad_maximum_fusion.refs_4_.refs_5_
  71.9 4.1 %collective-permute-start = (bf16[128,1024]{1,0:T(8,128)(2,1)S(1)}, bf16[128,1024]{1,0:T(8,128)(2,1)}, u32[]{:S(2)}, u32[]{:S(2)}) collective-permute-start(bf16[128,1024]{1,0:T(8,128)(2,1)S(1)} %pad_maximum_fusion.refs_4_.refs_5_), channel_id=1, source_target_pairs={{0,16},{8,24},{1,17},{9,25},{2,18},{10,26},{3,19},{11,27},{4,20},{... | collective-permute-start | bytes 786440 | tf_op jit(solution)/shard_map/ppermute | solution.py:373
  76.0 4.1 %collective-permute-start.1 = (bf16[128,1024]{1,0:T(8,128)(2,1)S(1)}, bf16[128,1024]{1,0:T(8,128)(2,1)}, u32[]{:S(2)}, u32[]{:S(2)}) collective-permute-start(bf16[128,1024]{1,0:T(8,128)(2,1)S(1)} %pad_maximum_fusion.refs_4_.refs_5_), channel_id=1, source_target_pairs={{0,8},{8,16},{16,24},{1,9},{9,17},{17,25},{2,10},{10,18},{18,26},{... | collective-permute-start | bytes 786440 | tf_op jit(solution)/shard_map/ppermute | solution.py:373
  80.1 0.9 copy.36.seg_ref
  81.0 5.4 %collective-permute-done.refs_0_.refs_1_ = bf16[128,1024]{1,0:T(8,128)(2,1)} collective-permute-done((bf16[128,1024]{1,0:T(8,128)(2,1)S(1)}, bf16[128,1024]{1,0:T(8,128)(2,1)}, u32[]{:S(2)}, u32[]{:S(2)}) %collective-permute-start) | collective-permute-done | bytes 262176 | tf_op jit(solution)/shard_map/ppermute | solution.py:373
  86.4 1.6 copy-done.2
  88.0 0.9 copy-done.3
  88.9 0.9 copy-done.5
  89.8 8.8 %conv_select.1 = (bf16[512,2048]{1,0:T(8,128)(2,1)S(1)}, bf16[4,128,640]{2,1,0:T(8,128)(2,1)S(1)}) custom-call(s32[1]{0:T(128)} %bitcast.lead_ref, s32[512,1]{1,0:T(8,128)S(1)} %copy-done.3, bf16[4,128,2048]{2,1,0:T(8,128)(2,1)S(1)} %all-to-all-done.x_ref, f32[4,8192]{1,0:T(4,128)S(1)} %copy-done.5, f32[1,8192]{1,0:T(1,128)S(1)} %bitcast.24, ...), custom_call_target="tpu_custom_call" | custom-call | flops 1140850688 | bytes 6422528 | tf_op jit(solution)/shard_map/conv_select/pallas_call | solution.py:159
  99.5 1.3 copy-done.7
  100.8 4.0 %all-to-all-start.1 = ((bf16[4,128,640]{2,1,0:T(8,128)(2,1)}), bf16[4,128,640]{2,1,0:T(8,128)(2,1)S(1)}, u32[]{:S(2)}, u32[]{:S(2)}) async-start(bf16[4,128,640]{2,1,0:T(8,128)(2,1)} %copy-done.4), calls=%async_computation.1 | async-start | bytes 1310720 | tf_op jit(solution)/shard_map/all_to_all | solution.py:377
  105.0 3.4 %attention_0.1.refs_6_ = bf16[128,4096]{1,0:T(8,128)(2,1)} custom-call(s32[128,1]{1,0:T(8,128)S(1)} %copy.37.seg_q_ref, s32[1,384]{1,0:T(1,128)S(1)} %broadcast_in_dim.19.seg_k_ref, bf16[128,4096]{1,0:T(8,128)(2,1)S(1)} %bitcast.22, bf16[128,1024]{1,0:T(8,128)(2,1)} %collective-permute-done.refs_0_.refs_1_, ...), custom_call_target="tpu_custom_call" | custom-call | flops 402653184 | bytes 1048576 | tf_op jit(solution)/shard_map/attention_0/pallas_call | solution.py:72
  108.5 5.4 %all-to-all-done.1.part_ref = bf16[4,128,640]{2,1,0:T(8,128)(2,1)S(1)} async-done(((bf16[4,128,640]{2,1,0:T(8,128)(2,1)}), bf16[4,128,640]{2,1,0:T(8,128)(2,1)S(1)}, u32[]{:S(2)}, u32[]{:S(2)}) %all-to-all-start.1) | async-done | bytes 655392 | tf_op jit(solution)/shard_map/all_to_all | solution.py:377
  114.7 2.1 %normalise.1 = bf16[4,128,640]{2,1,0:T(8,128)(2,1)} custom-call(bf16[4,128,640]{2,1,0:T(8,128)(2,1)} %copy-done.10), custom_call_target="tpu_custom_call" | custom-call | tf_op jit(solution)/shard_map/normalise/pallas_call | solution.py:210
  116.8 4.2 %all-to-all-start.2 = ((bf16[4,128,640]{2,1,0:T(8,128)(2,1)}), bf16[4,128,640]{2,1,0:T(8,128)(2,1)}, u32[]{:S(2)}, u32[]{:S(2)}) async-start(bf16[4,128,640]{2,1,0:T(8,128)(2,1)} %normalise.1), calls=%async_computation.2 | async-start | bytes 1310720 | tf_op jit(solution)/shard_map/all_to_all | solution.py:377
  121.8 1.4 reshape.41
  124.8 3.4 %attention_2.1 = bf16[128,4096]{1,0:T(8,128)(2,1)} custom-call(s32[128,1]{1,0:T(8,128)S(1)} %copy.37.seg_q_ref, s32[1,384]{1,0:T(1,128)S(1)} %broadcast_in_dim.19.seg_k_ref, bf16[128,4096]{1,0:T(8,128)(2,1)S(1)} %bitcast.23, bf16[128,1024]{1,0:T(8,128)(2,1)} %collective-permute-done.refs_0_.refs_1_, ...), custom_call_target="tpu_custom_call", output_to_operand_aliasing={{}: (9, {})} | custom-call | flops 402653184 | bytes 1048576 | tf_op jit(solution)/shard_map/attention_2/pallas_call | solution.py:72
  128.3 2.5 %all-to-all-done.2 = bf16[4,128,640]{2,1,0:T(8,128)(2,1)} async-done(((bf16[4,128,640]{2,1,0:T(8,128)(2,1)}), bf16[4,128,640]{2,1,0:T(8,128)(2,1)}, u32[]{:S(2)}, u32[]{:S(2)}) %all-to-all-start.2) | async-done | bytes 655392 | tf_op jit(solution)/shard_map/all_to_all | solution.py:377
  130.8 18.9 %state_scan_0.1 = bf16[4,128,1024]{2,1,0:T(8,128)(2,1)} custom-call(s32[512,1]{1,0:T(8,128)} %copy.36.seg_ref, bf16[512,640]{1,0:T(8,128)(2,1)} %bitcast.11.low_ref, bf16[8,512,256]{2,1,0:T(8,128)(2,1)} %all-gather.9.cloned.1.call-done.weight_ref, f32[1,2048]{1,0:T(1,128)} %broadcast_in_dim_reshape.6.bias_ref, f32[16,2048]{1,0:T(8,128)} %reshape.43.decay_ref, ...), custom_call_target="tpu_custom_call" | custom-call | flops 50331648 | bytes 3145728 | tf_op jit(solution)/shard_map/state_scan_0/pallas_call | solution.py:306
  149.7 3.7 %all-to-all-start.4 = ((bf16[4,128,1024]{2,1,0:T(8,128)(2,1)}), bf16[4,128,1024]{2,1,0:T(8,128)(2,1)S(1)}, u32[]{:S(2)}, u32[]{:S(2)}) async-start(bf16[4,128,1024]{2,1,0:T(8,128)(2,1)} %state_scan_0.1), calls=%async_computation.4 | async-start | bytes 2097152 | tf_op jit(solution)/shard_map/all_to_all | solution.py:377
  153.4 18.9 %state_scan_1.1 = bf16[4,128,1024]{2,1,0:T(8,128)(2,1)} custom-call(s32[512,1]{1,0:T(8,128)} %copy.36.seg_ref, bf16[512,640]{1,0:T(8,128)(2,1)} %bitcast.11.low_ref, bf16[8,512,256]{2,1,0:T(8,128)(2,1)} %all-gather.9.cloned.1.call-done.weight_ref, f32[1,2048]{1,0:T(1,128)} %broadcast_in_dim_reshape.6.bias_ref, f32[16,2048]{1,0:T(8,128)} %reshape.43.decay_ref, ...), custom_call_target="tpu_custom_call" | custom-call | flops 50331648 | bytes 3145728 | tf_op jit(solution)/shard_map/state_scan_1/pallas_call | solution.py:306
  172.2 4.0 %all-to-all-start.3 = ((bf16[4,128,1024]{2,1,0:T(8,128)(2,1)}), bf16[4,128,1024]{2,1,0:T(8,128)(2,1)S(1)}, u32[]{:S(2)}, u32[]{:S(2)}) async-start(bf16[4,128,1024]{2,1,0:T(8,128)(2,1)} %state_scan_1.1), calls=%async_computation.3 | async-start | bytes 2097152 | tf_op jit(solution)/shard_map/all_to_all | solution.py:377
  176.2 3.8 %gate_0.1.refs_0_ = bf16[128,8192]{1,0:T(8,128)(2,1)} custom-call(bf16[4,128,1024]{2,1,0:T(8,128)(2,1)} %copy-done.8, bf16[128,8192]{1,0:T(8,128)(2,1)} %bitcast.25), custom_call_target="tpu_custom_call" | custom-call | flops 2097152 | bytes 3145728 | tf_op jit(solution)/shard_map/gate_0/pallas_call | solution.py:356
  180.0 8.9 %all-to-all-done.3.y_ref = bf16[4,128,1024]{2,1,0:T(8,128)(2,1)S(1)} async-done(((bf16[4,128,1024]{2,1,0:T(8,128)(2,1)}), bf16[4,128,1024]{2,1,0:T(8,128)(2,1)S(1)}, u32[]{:S(2)}, u32[]{:S(2)}) %all-to-all-start.3) | async-done | bytes 1048608 | tf_op jit(solution)/shard_map/all_to_all | solution.py:377
  188.9 1.0 copy-done.9
  189.9 3.8 %gate_4.1 = bf16[128,8192]{1,0:T(8,128)(2,1)} custom-call(bf16[4,128,1024]{2,1,0:T(8,128)(2,1)} %copy-done.9, bf16[128,8192]{1,0:T(8,128)(2,1)} %bitcast.26, bf16[128,8192]{1,0:T(8,128)(2,1)} %gate_0.1.refs_0_), custom_call_target="tpu_custom_call", output_to_operand_aliasing={{}: (2, {})} | custom-call | flops 2097152 | bytes 3145728 | tf_op jit(solution)/shard_map/gate_4/pallas_call | solution.py:356
  (53 shorter events, 5.2 us)
Async XLA Ops:
  7.2 1.3 copy-start
  7.2 34.7 %all-gather.11.cloned.1.call-start = ((), (), s32[]{:S(2)}) async-start(), calls=%async_computation.7 | async-start | bytes 1392640 | tf_op jit(solution)/shard_map/all_gather | solution.py:428
  9.2 61.7 %all-gather.13.cloned.1.call-start = ((), (), s32[]{:S(2)}) async-start(), calls=%async_computation.8 | async-start | bytes 1310720 | tf_op jit(solution)/shard_map/all_gather | solution.py:428
  10.9 75.4 %all-gather.7.cloned.1.call-start = ((), (), s32[]{:S(2)}) async-start(), calls=%async_computation.5 | async-start | bytes 3342336 | tf_op jit(solution)/shard_map/all_gather | solution.py:429
  47.6 32.5 %copy-start.13 = (s32[1,512]{1,0:T(1,128)S(1)}, s32[1,512]{1,0:T(1,128)}, u32[]{:S(2)}) copy-start(s32[1,512]{1,0:T(1,128)} %param.18) | copy-start | bytes 6148
  47.6 38.8 %copy-start.6 = (f32[8192]{0:T(1024)S(1)}, f32[8192]{0:T(1024)}, u32[]{:S(2)}) copy-start(f32[8192]{0:T(1024)} %param.20) | copy-start | bytes 98308
  47.6 38.8 %all-to-all-start = ((bf16[4,128,2048]{2,1,0:T(8,128)(2,1)}), bf16[4,128,2048]{2,1,0:T(8,128)(2,1)S(1)}, u32[]{:S(2)}, u32[]{:S(2)}) async-start(bf16[4,128,2048]{2,1,0:T(8,128)(2,1)} %pack.1), calls=%async_computation | async-start | bytes 4194304 | tf_op jit(solution)/shard_map/all_to_all | solution.py:377
  51.4 79.4 %all-gather.9.cloned.1.call-start = ((), (), s32[]{:S(2)}) async-start(), calls=%async_computation.6 | async-start | bytes 3145728 | tf_op jit(solution)/shard_map/all_gather | solution.py:429
  71.9 14.4 %collective-permute-start = (bf16[128,1024]{1,0:T(8,128)(2,1)S(1)}, bf16[128,1024]{1,0:T(8,128)(2,1)}, u32[]{:S(2)}, u32[]{:S(2)}) collective-permute-start(bf16[128,1024]{1,0:T(8,128)(2,1)S(1)} %pad_maximum_fusion.refs_4_.refs_5_), channel_id=1, source_target_pairs={{0,16},{8,24},{1,17},{9,25},{2,18},{10,26},{3,19},{11,27},{4,20},{... | collective-permute-start | bytes 786440 | tf_op jit(solution)/shard_map/ppermute | solution.py:373
  76.0 10.3 %collective-permute-start.1 = (bf16[128,1024]{1,0:T(8,128)(2,1)S(1)}, bf16[128,1024]{1,0:T(8,128)(2,1)}, u32[]{:S(2)}, u32[]{:S(2)}) collective-permute-start(bf16[128,1024]{1,0:T(8,128)(2,1)S(1)} %pad_maximum_fusion.refs_4_.refs_5_), channel_id=1, source_target_pairs={{0,8},{8,16},{16,24},{1,9},{9,17},{17,25},{2,10},{10,18},{18,26},{... | collective-permute-start | bytes 786440 | tf_op jit(solution)/shard_map/ppermute | solution.py:373
  86.4 1.6 copy-start.2
  88.0 0.9 copy-start.3
  88.9 0.9 copy-start.5
  98.6 0.8 copy-start.4
  99.5 1.3 copy-start.7
  100.8 4.2 %copy-start.1 = (bf16[1,128,4096]{2,1,0:T(8,128)(2,1)S(1)}, bf16[1,128,4096]{2,1,0:T(8,128)(2,1)}, u32[]{:S(2)}) copy-start(bf16[1,128,4096]{2,1,0:T(8,128)(2,1)} %param.13) | copy-start | bytes 3145732
  100.8 13.1 %all-to-all-start.1 = ((bf16[4,128,640]{2,1,0:T(8,128)(2,1)}), bf16[4,128,640]{2,1,0:T(8,128)(2,1)S(1)}, u32[]{:S(2)}, u32[]{:S(2)}) async-start(bf16[4,128,640]{2,1,0:T(8,128)(2,1)} %copy-done.4), calls=%async_computation.1 | async-start | bytes 1310720 | tf_op jit(solution)/shard_map/all_to_all | solution.py:377
  108.5 12.6 %copy-start.11 = (f32[8192]{0:T(1024)S(1)}, f32[8192]{0:T(1024)}, u32[]{:S(2)}) copy-start(f32[8192]{0:T(1024)} %param.25) | copy-start | bytes 98308
  108.5 12.6 %copy-start.12 = (f32[8192]{0:T(1024)S(1)}, f32[8192]{0:T(1024)}, u32[]{:S(2)}) copy-start(f32[8192]{0:T(1024)} %param.23) | copy-start | bytes 98308
  113.9 0.8 copy-start.10
  116.8 14.0 %all-to-all-start.2 = ((bf16[4,128,640]{2,1,0:T(8,128)(2,1)}), bf16[4,128,640]{2,1,0:T(8,128)(2,1)}, u32[]{:S(2)}, u32[]{:S(2)}) async-start(bf16[4,128,640]{2,1,0:T(8,128)(2,1)} %normalise.1), calls=%async_computation.2 | async-start | bytes 1310720 | tf_op jit(solution)/shard_map/all_to_all | solution.py:377
  149.7 22.6 %all-to-all-start.4 = ((bf16[4,128,1024]{2,1,0:T(8,128)(2,1)}), bf16[4,128,1024]{2,1,0:T(8,128)(2,1)S(1)}, u32[]{:S(2)}, u32[]{:S(2)}) async-start(bf16[4,128,1024]{2,1,0:T(8,128)(2,1)} %state_scan_0.1), calls=%async_computation.4 | async-start | bytes 2097152 | tf_op jit(solution)/shard_map/all_to_all | solution.py:377
  172.2 4.0 %copy-start.8 = (bf16[4,128,1024]{2,1,0:T(8,128)(2,1)}, bf16[4,128,1024]{2,1,0:T(8,128)(2,1)S(1)}, u32[]{:S(2)}) copy-start(bf16[4,128,1024]{2,1,0:T(8,128)(2,1)S(1)} %all-to-all-done.4.y_ref) | copy-start | bytes 3145732
  172.2 16.6 %all-to-all-start.3 = ((bf16[4,128,1024]{2,1,0:T(8,128)(2,1)}), bf16[4,128,1024]{2,1,0:T(8,128)(2,1)S(1)}, u32[]{:S(2)}, u32[]{:S(2)}) async-start(bf16[4,128,1024]{2,1,0:T(8,128)(2,1)} %state_scan_1.1), calls=%async_computation.3 | async-start | bytes 2097152 | tf_op jit(solution)/shard_map/all_to_all | solution.py:377
  188.9 1.0 copy-start.9
Sparse Core Ops, SparseCore 0:
  10.2 31.6 all-gather.10
  43.5 27.3 all-gather.12
  72.5 10.2 all-gather.6
  84.2 11.7 all-gather.8

commit v3 on v2

--- a/solution.py
+++ b/solution.py
@@ -86,62 +86,72 @@
     )(*operands)
 
 
-def pack_kernel(order, fold, x_ref, out_ref):
-    ctx, _, width = out_ref.shape
+def piece_lanes(slot, piece, ctx, fold, width):
+    start = (slot * ctx + piece % fold * (ctx // fold) + piece // fold) * width
+    return slice(start, start + width)
+
+
+def pack_kernel(fold, width, x_ref, out_ref):
+    ctx = out_ref.shape[0]
     for piece in range(ctx):
-        place = piece % fold * (ctx // fold) + piece // fold
-        out_ref[piece] = x_ref[:, place * width : (place + 1) * width]
-
-
-def pack(value, ctx, shards, order, fold):
+        for slot in range(out_ref.shape[2] // width):
+            out_ref[piece, :, slot * width : (slot + 1) * width] = x_ref[:, piece_lanes(slot, piece, ctx, fold, width)]
+
+
+def pack(value, ctx, fold, width):
     rows, channels = value.shape
-    width = channels // shards // ctx
-    return pl.pallas_call(
-        functools.partial(pack_kernel, order, fold),
-        grid=(shards,),
-        in_specs=[pl.BlockSpec((rows, ctx * width), lambda s: (0, order(s)))],
-        out_specs=pl.BlockSpec((ctx, rows, width), lambda s: (0, 0, s)),
-        out_shape=jax.ShapeDtypeStruct((ctx, rows, shards * width), value.dtype),
+    part = min(rows, 32)
+    return pl.pallas_call(
+        functools.partial(pack_kernel, fold, width),
+        grid=(rows // part,),
+        in_specs=[pl.BlockSpec((part, channels), lambda r: (r, 0))],
+        out_specs=pl.BlockSpec((ctx, part, channels // ctx), lambda r: (0, r, 0)),
+        out_shape=jax.ShapeDtypeStruct((ctx, rows, channels // ctx), value.dtype),
         name="pack",
     )(value)
 
 
-def conv_select_kernel(lead_ref, seg_ref, x_ref, weight_ref, bias_ref, select_ref, conv_ref, part_ref, masks, padded, total):
+def conv_select_kernel(seg_ref, x_ref, weight_ref, bias_ref, select_ref, conv_ref, part_ref, masks, padded, total):
     step = pl.program_id(0)
     toks = seg_ref.shape[0]
-    width = x_ref.shape[2]
-    pieces = x_ref.shape[0]
-    rows = x_ref.shape[1]
-    outputs = select_ref.shape[1]
+    pieces, rows, wide = x_ref.shape
+    tiles = wide // LANES
+    slots, outputs, width = select_ref.shape
 
     @pl.when(step == 0)
     def _():
         wide_seg = jnp.broadcast_to(seg_ref[...], (toks, LANES)).astype(jnp.float32)
-        padded[0:SUBLANES, 0:LANES] = jnp.full((SUBLANES, LANES), -1.0, jnp.float32)
-        padded[SUBLANES : SUBLANES + toks, 0:LANES] = wide_seg
+        padded[0, 0:SUBLANES, :] = jnp.full((SUBLANES, LANES), -1.0, jnp.float32)
+        padded[0, SUBLANES : SUBLANES + toks, :] = wide_seg
         for tap in range(3):
-            before = padded[SUBLANES - 3 + tap : SUBLANES - 3 + tap + toks, 0:LANES]
+            before = padded[0, SUBLANES - 3 + tap : SUBLANES - 3 + tap + toks, :]
             masks[tap] = jnp.where(before == wide_seg, 1.0, 0.0)
-        padded[0:SUBLANES, :] = jnp.zeros((SUBLANES, width), jnp.float32)
+        for tile in range(tiles):
+            padded[tile, 0:SUBLANES, :] = jnp.zeros((SUBLANES, LANES), jnp.float32)
         total[...] = jnp.zeros_like(total)
 
-    for piece in range(pieces):
-        padded[SUBLANES + piece * rows : SUBLANES + (piece + 1) * rows, :] = x_ref[piece].astype(jnp.float32)
     outs = []
-    for tile in range(width // LANES):
+    for tile in range(tiles):
         lanes = slice(tile * LANES, (tile + 1) * LANES)
+        for piece in range(pieces):
+            first = SUBLANES + piece * rows
+            padded[tile, first : first + rows, :] = x_ref[piece, :, lanes].astype(jnp.float32)
         running = jnp.broadcast_to(bias_ref[0:1, lanes], (toks, LANES))
         for tap in range(4):
-            moved = padded[SUBLANES - 3 + tap : SUBLANES - 3 + tap + toks, lanes]
+            moved = padded[tile, SUBLANES - 3 + tap : SUBLANES - 3 + tap + toks, :]
             term = weight_ref[tap : tap + 1, lanes] * moved
             running = running + (term * masks[tap] if tap < 3 else term)
         conv = silu(running).astype(jnp.bfloat16)
         conv_ref[:, lanes] = conv
         outs.append(conv)
-    conv_all = jnp.concatenate(outs, axis=1) if len(outs) > 1 else outs[0]
-    total[...] += lax.dot_general(
-        conv_all, select_ref[0], (((1,), (1,)), ((), ())), preferred_element_type=jnp.float32
-    )
+    per_slot = width // LANES
+    added = total[...]
+    for slot in range(slots):
+        conv = jnp.concatenate(outs[slot * per_slot : (slot + 1) * per_slot], axis=1) if per_slot > 1 else outs[slot]
+        added = added + lax.dot_general(
+            conv, select_ref[slot], (((1,), (1,)), ((), ())), preferred_element_type=jnp.float32
+        )
+    total[...] = added
 
     @pl.when(step == pl.num_programs(0) - 1)
     def _():
@@ -151,45 +161,44 @@
             part_ref[piece, :, outputs:] = jnp.zeros((rows, spare), part_ref.dtype)
 
 
-def conv_select(lead, seg_col, pieces, conv_weight, conv_bias, select_parts, order):
-    shards, outputs, width = select_parts.shape
+def conv_select(seg_col, pieces, conv_weight, conv_bias, select_parts):
+    slots, outputs, width = select_parts.shape
     ctx, rows, _ = pieces.shape
     toks = ctx * rows
     padded_outputs = -(-outputs // LANES) * LANES
+    batch = 2
+    wide = batch * width
     return pl.pallas_call(
         conv_select_kernel,
-        grid_spec=pltpu.PrefetchScalarGridSpec(
-            num_scalar_prefetch=1,
-            grid=(shards,),
-            in_specs=[
-                pl.BlockSpec((toks, 1), lambda s, p: (0, 0)),
-                pl.BlockSpec((ctx, rows, width), lambda s, p: (0, 0, s)),
-                pl.BlockSpec((4, width), lambda s, p: (0, order(s) * ctx + p[0])),
-                pl.BlockSpec((1, width), lambda s, p: (0, order(s) * ctx + p[0])),
-                pl.BlockSpec((1, outputs, width), lambda s, p: (s, 0, 0)),
-            ],
-            out_specs=[
-                pl.BlockSpec((toks, width), lambda s, p: (0, s)),
-                pl.BlockSpec((ctx, rows, padded_outputs), lambda s, p: (0, 0, 0)),
-            ],
-            scratch_shapes=[
-                pltpu.VMEM((3, toks, LANES), jnp.float32),
-                pltpu.VMEM((SUBLANES + toks, width), jnp.float32),
-                pltpu.VMEM((toks, outputs), jnp.float32),
-            ],
-        ),
+        grid=(slots // batch,),
+        in_specs=[
+            pl.BlockSpec((toks, 1), lambda s: (0, 0)),
+            pl.BlockSpec((ctx, rows, wide), lambda s: (0, 0, s)),
+            pl.BlockSpec((4, wide), lambda s: (0, s)),
+            pl.BlockSpec((1, wide), lambda s: (0, s)),
+            pl.BlockSpec((batch, outputs, width), lambda s: (s, 0, 0)),
+        ],
+        out_specs=[
+            pl.BlockSpec((toks, wide), lambda s: (0, s)),
+            pl.BlockSpec((ctx, rows, padded_outputs), lambda s: (0, 0, 0)),
+        ],
+        scratch_shapes=[
+            pltpu.VMEM((3, toks, LANES), jnp.float32),
+            pltpu.VMEM((wide // LANES, SUBLANES + toks, LANES), jnp.float32),
+            pltpu.VMEM((toks, outputs), jnp.float32),
+        ],
         out_shape=[
-            jax.ShapeDtypeStruct((toks, shards * width), jnp.bfloat16),
+            jax.ShapeDtypeStruct((toks, slots * width), jnp.bfloat16),
             jax.ShapeDtypeStruct((ctx, rows, padded_outputs), jnp.bfloat16),
         ],
         compiler_params=pltpu.CompilerParams(vmem_limit_bytes=40 << 20),
         cost_estimate=pl.CostEstimate(
-            flops=2 * toks * shards * width * outputs,
+            flops=2 * toks * slots * width * outputs,
             bytes_accessed=2 * pieces.size * 2 + 2 * select_parts.size,
             transcendentals=pieces.size,
         ),
         name="conv_select",
-    )(lead, seg_col, pieces, conv_weight, conv_bias, select_parts)
+    )(seg_col, pieces, conv_weight, conv_bias, select_parts)
 
 
 def normalise_kernel(rank, part_ref, out_ref):
@@ -214,9 +223,9 @@
     )(parts)
 
 
-def scan_kernel(rank, seg_ref, low_ref, weight_ref, bias_ref, decay_ref, gain_ref, conv_ref, out_ref,
-                in_wide, out_diag, delta_rows, drive_rows, held_even, held_odd):
-    toks = seg_ref.shape[0]
+def scan_kernel(rank, reset_ref, low_ref, weight_ref, bias_ref, decay_ref, gain_ref, conv_ref, out_ref,
+                in_cols, out_diag, delta_rows, drive_rows, held_even, held_odd):
+    toks = reset_ref.shape[0]
     states = decay_ref.shape[0]
     shards = weight_ref.shape[0]
     width = weight_ref.shape[2]
@@ -224,10 +233,9 @@
     rows = out_ref.shape[1]
     block = 16
     span = block * states
-
-    for n in range(states):
-        column = low_ref[:, rank + n : rank + n + 1].astype(jnp.float32)
-        in_wide[:, n, :] = jnp.broadcast_to(column, (toks, LANES))
+    count = toks // block
+
+    in_cols[...] = jnp.transpose(low_ref[:, rank : rank + LANES].astype(jnp.float32))[0:states, :]
     lane = lax.broadcasted_iota(jnp.int32, (states, span), 1)
     spread = jnp.where(lane % states == lax.broadcasted_iota(jnp.int32, (states, span), 0), 1.0, 0.0)
     copies = jnp.dot(
@@ -237,11 +245,7 @@
     there = lax.broadcasted_iota(jnp.int32, (toks, span), 0) % block
     out_diag[...] = jnp.where(here == there, copies, 0.0).astype(jnp.bfloat16)
 
-    seg = jnp.broadcast_to(seg_ref[...], (toks, LANES)).astype(jnp.float32)
-    drive_rows[0, 0:SUBLANES, :] = jnp.full((SUBLANES, LANES), -1.0, jnp.float32)
-    drive_rows[0, SUBLANES : SUBLANES + toks, :] = seg
-    before = drive_rows[0, SUBLANES - 1 : SUBLANES - 1 + toks, :]
-    reset = jnp.where(before == seg, 0.0, FAR)
+    reset = jnp.broadcast_to(reset_ref[...], (toks, LANES))
     low = low_ref[:, 0:rank]
     for shard in range(shards):
         pre = jnp.dot(low, weight_ref[shard], preferred_element_type=jnp.float32)
@@ -256,20 +260,24 @@
                 jnp.log(1.0 + raised),
             )
             delta = (jnp.maximum(value, 0.0) + log_part).astype(jnp.bfloat16).astype(jnp.float32)
-            delta_rows[tile] = delta + reset
-            drive_rows[tile, 0:toks, :] = delta * conv_ref[:, lanes].astype(jnp.float32)
+            delta_rows[:, tile] = (delta + reset).reshape(count, block, LANES)
+            drive_rows[:, tile] = (delta * conv_ref[:, lanes].astype(jnp.float32)).reshape(count, block, LANES)
 
     rates = [-LOG2E * jnp.exp(decay_ref[:, tile * LANES : (tile + 1) * LANES]) for tile in range(tiles)]
 
     def advance(index, held, history):
         held = list(held)
+        per_row = LANES // block
+        columns = in_cols[:, pl.ds(pl.multiple_of(lax.div(index, per_row) * LANES, LANES), LANES)]
+        columns = pltpu.roll(columns, lax.rem(LANES - lax.rem(index, per_row) * block, LANES), 1)
+        delta_now = delta_rows.at[index]
+        drive_now = drive_rows.at[index]
         for inner in range(block):
-            t = index * block + inner
-            into = in_wide[t]
+            into = jnp.broadcast_to(columns[:, inner : inner + 1], (states, LANES))
             for tile in range(tiles):
                 lanes = slice(tile * LANES, (tile + 1) * LANES)
-                grow = jnp.exp2(delta_rows[tile, pl.ds(t, 1), :] * rates[tile])
-                held[tile] = grow * held[tile] + into * drive_rows[tile, pl.ds(t, 1), :]
+                grow = jnp.exp2(delta_now[tile, inner : inner + 1, :] * rates[tile])
+                held[tile] = grow * held[tile] + into * drive_now[tile, inner : inner + 1, :]
                 history[inner * states : (inner + 1) * states, lanes] = held[tile].astype(jnp.bfloat16)
         return tuple(held)
 
@@ -290,12 +298,11 @@
         return held
 
     start = tuple(jnp.zeros((states, LANES), jnp.float32) for _ in range(tiles))
-    count = toks // block
     lax.fori_loop(0, count // 2, pair, start)
     finish(count - 1, held_odd)
 
 
-def state_scan(seg_col, low, delta_parts, bias, decay, gain, conv, ctx, call, calls):
+def state_scan(reset_col, low, delta_parts, bias, decay, gain, conv, ctx, call, calls):
     toks = low.shape[0]
     shards, rank, width = delta_parts.shape
     shards = shards // calls
@@ -318,10 +325,10 @@
         out_specs=pl.BlockSpec((ctx, rows, wide), lambda g: (0, 0, 0)),
         out_shape=jax.ShapeDtypeStruct((ctx, rows, wide), jnp.bfloat16),
         scratch_shapes=[
-            pltpu.VMEM((toks, states, LANES), jnp.float32),
+            pltpu.VMEM((states, toks), jnp.float32),
             pltpu.VMEM((toks, 16 * states), jnp.bfloat16),
-            pltpu.VMEM((wide // LANES, toks, LANES), jnp.float32),
-            pltpu.VMEM((wide // LANES, toks + SUBLANES, LANES), jnp.float32),
+            pltpu.VMEM((toks // 16, wide // LANES, 16, LANES), jnp.float32),
+            pltpu.VMEM((toks // 16, wide // LANES, 16, LANES), jnp.float32),
             pltpu.VMEM((16 * states, wide), jnp.bfloat16),
             pltpu.VMEM((16 * states, wide), jnp.bfloat16),
         ],
@@ -330,40 +337,41 @@
             flops=6 * steps, bytes_accessed=2 * delta_parts.size // calls + 4 * toks * wide, transcendentals=steps
         ),
         name=f"state_scan_{call}",
-    )(seg_col, low, delta_parts, bias, decay, gain, conv)
-
-
-def gate_kernel(fold, y_ref, gate_ref, *refs):
+    )(reset_col, low, delta_parts, bias, decay, gain, conv)
+
+
+def gate_kernel(fold, width, y_ref, gate_ref, *refs):
     out_ref = refs[-1]
-    ctx, _, width = y_ref.shape
-    for piece in range(ctx):
-        place = piece % fold * (ctx // fold) + piece // fold
-        lanes = slice(place * width, (place + 1) * width)
-        gate = gate_ref[:, lanes].astype(jnp.float32)
-        out_ref[:, lanes] = (y_ref[piece].astype(jnp.float32) * silu(gate)).astype(out_ref.dtype)
-
-
-def apply_gate(pieces, gate, width, order, fold, first, before=None):
-    ctx, rows, total = pieces.shape
-    wide = pl.BlockSpec((rows, ctx * width), lambda s: (0, order(first + s)))
+    ctx, _, wide = y_ref.shape
+    for slot in range(wide // width):
+        for piece in range(ctx):
+            lanes = piece_lanes(slot, piece, ctx, fold, width)
+            value = y_ref[piece, :, slot * width : (slot + 1) * width].astype(jnp.float32)
+            out_ref[:, lanes] = (value * silu(gate_ref[:, lanes].astype(jnp.float32))).astype(out_ref.dtype)
+
+
+def apply_gate(pieces, gate, fold, width, call, before=None):
+    ctx, rows, wide = pieces.shape
+    part = min(rows, 32)
+    columns = pl.BlockSpec((part, ctx * wide), lambda r: (r, call))
     operands = [pieces, gate]
-    in_specs = [pl.BlockSpec((ctx, rows, width), lambda s: (0, 0, s)), wide]
+    in_specs = [pl.BlockSpec((ctx, part, wide), lambda r: (0, r, 0)), columns]
     aliases = {}
     if before is not None:
         aliases = {2: 0}
         operands.append(before)
         in_specs.append(pl.BlockSpec(memory_space=pl.ANY))
     return pl.pallas_call(
-        functools.partial(gate_kernel, fold),
-        grid=(total // width,),
+        functools.partial(gate_kernel, fold, width),
+        grid=(rows // part,),
         in_specs=in_specs,
-        out_specs=wide,
+        out_specs=columns,
         out_shape=jax.ShapeDtypeStruct(gate.shape, jnp.bfloat16),
         input_output_aliases=aliases,
         cost_estimate=pl.CostEstimate(
             flops=4 * pieces.size, bytes_accessed=6 * pieces.size, transcendentals=pieces.size
         ),
-        name=f"gate_{first}",
+        name=f"gate_{call}",
     )(*operands)
 
 
@@ -406,29 +414,20 @@
     back = min(ctx - 1, -(-(toks // 2 - 1) // rows))
 
     slots = shards // fold
-    half = slots // 2
-
-    def order(slot):
-        return slot % half * 2 + slot // half if fold == 1 else slot
 
     def own_part(array):
         cut = array.reshape(array.shape[:-1] + (slots, fold, ctx // fold, width))
         cut = lax.dynamic_index_in_dim(cut, place // fold, cut.ndim - 2, keepdims=False)
         cut = lax.dynamic_index_in_dim(cut, place % fold, cut.ndim - 2, keepdims=False)
-        if fold == 1:
-            cut = cut.reshape(array.shape[:-1] + (half, 2, width))
-            cut = jnp.swapaxes(cut, -3, -2)
         return cut.reshape(array.shape[:-1] + (slots * width,))
 
     def gathered(weight):
         own = lax.dynamic_slice_in_dim(weight, place // fold * width, width, 1)
-        if fold == 1:
-            same_core = [list(range(core, shards, 2)) for core in range(2)]
-            same_chip = [[chip, chip + 1] for chip in range(0, shards, 2)]
-            parts = lax.all_gather(own, "rep", axis=0, axis_index_groups=same_core)
-            return lax.all_gather(parts, "rep", axis=0, axis_index_groups=same_chip, tiled=True)
-        parts = lax.all_gather(own, "rep", axis=0).reshape((slots, fold) + own.shape)
-        return lax.dynamic_index_in_dim(parts, place % fold, 1, keepdims=False)
+        parts = lax.all_gather(own, "rep", axis=0)
+        if fold > 1:
+            parts = parts.reshape((slots, fold) + own.shape)
+            parts = lax.dynamic_index_in_dim(parts, place % fold, 1, keepdims=False)
+        return parts
 
     select_parts = gathered(select_weight)
     delta_parts = gathered(delta_weight)
@@ -436,11 +435,10 @@
     both = jnp.concatenate([keys[0], values[0]], axis=1)
     blocks = [shifted(both, "ctx", by) for by in range(back, 0, -1)] + [both]
 
-    pieces = exchange(pack(mixer_input[0], ctx, slots, order, fold))
+    pieces = exchange(pack(mixer_input[0], ctx, fold, width))
     pieces, blocks = lax.optimization_barrier((pieces, blocks))
 
-    lead = jnp.reshape(place % fold * (ctx // fold) + place // fold, (1,)).astype(jnp.int32)
-    conv, parts = conv_select(lead, seg_col, pieces, conv_weight, conv_bias[None, :], select_parts, order)
+    conv, parts = conv_select(seg_col, pieces, own_part(conv_weight), own_part(conv_bias)[None, :], select_parts)
 
     seg_pad = jnp.concatenate([jnp.full((back * rows,), -1, jnp.int32), seg])
     seg_k = lax.dynamic_slice_in_dim(seg_pad, place * rows, (back + 1) * rows, 0)
@@ -459,13 +457,15 @@
     bias = own_part(delta_bias)[None, :]
     gain = own_part(skip_gain)[None, :]
     decay = own_part(jnp.transpose(decay_log))
+    same = jnp.concatenate([jnp.zeros((1,), bool), seg[1:] == seg[:-1]])
+    reset_col = jnp.where(same, 0.0, FAR)[:, None]
     scanned = [
-        exchange(state_scan(seg_col, low, delta_parts, bias, decay, gain, conv, ctx, call, calls))
+        exchange(state_scan(reset_col, low, delta_parts, bias, decay, gain, conv, ctx, call, calls))
         for call in range(calls)
     ]
     mixed = None
     for call in range(calls):
-        mixed = apply_gate(scanned[call], gate_input[0], width, order, fold, call * slots // calls, mixed)
+        mixed = apply_gate(scanned[call], gate_input[0], fold, width, call, mixed)
     return (attended[None], mixed[None])
 
 

time: 201 us -> 157 us (0.78)
  waiting for transfers between devices: 72.7 us -> 36.3 us
  Pallas kernels: 68.6 us -> 55.7 us
  local copies, waits for them, and re-layouts: 15.9 us -> 18.1 us
    all_gather x4 -> x2, waiting for transfers between devices: 50.4 us -> 0.01 us  [gathered(): parts = lax.all_gather(own, 'rep', axis=0)]
    ppermute x2, waiting for transfers between devices: 5.36 us -> 19.8 us  [shifted(): return lax.ppermute(value, axis, pairs)]
    pallas_call x2, Pallas kernels: 37.7 us -> 30.5 us  [state_scan(): pl.pallas_call(functools.partial(scan_kernel, rank), grid=(1,), in_specs=...]
    pallas_call x4, Pallas kernels: 22 us -> 16.2 us  [the longest x2 7.55 us: apply_gate(): pl.pallas_call(functools.partial(gate_kernel, fold, width), grid=(rows //...]
    reshape x3 -> x5, local copies, waits for them, and re-layouts: 1.43 us -> 3.88 us  [own_part(): cut = array.reshape(array.shape[:-1] + (slots, fold, ctx // fold, width))]
    unnamed x28 -> x26, local copies, waits for them, and re-layouts: 8.68 us -> 8.55 us
  transfers between devices with their start and end apart: 11 -> 9, of which waited for: 6 -> 4; matrix products, arithmetic and copies ran while one was open for 4% -> 7% of each run, Pallas kernels for 23% -> 23%
where the time goes in v3:
time: 157 us; the launch traced here: 156 us
  Pallas kernels  55.7 us (35%)
  waiting for transfers between devices  36.3 us (23%)
  starting transfers between devices  29.9 us (19%)
  local copies, waits for them, and re-layouts  18.1 us (12%)
  between operations  14.2 us (9%)
  other arithmetic  1.87 us (1%)
    pallas_call x2, Pallas kernels, state_scan(): pl.pallas_call(functools.partial(scan_kernel, rank), grid=(1,), in_specs=...  30.5 us
    all_to_all x5, starting transfers between devices, exchange(): return lax.all_to_all(value, 'ctx', 0, 0, tiled=True)  21.1 us
    ppermute x2, waiting for transfers between devices, shifted(): return lax.ppermute(value, axis, pairs)  19.8 us
    all_to_all x5, waiting for transfers between devices, exchange(): return lax.all_to_all(value, 'ctx', 0, 0, tiled=True)  16.5 us
    ppermute x2, starting transfers between devices, shifted(): return lax.ppermute(value, axis, pairs)  8.73 us
    unnamed x26, local copies, waits for them, and re-layouts  8.55 us
    pallas_call x2, Pallas kernels, apply_gate(): pl.pallas_call(functools.partial(gate_kernel, fold, width), grid=(rows //...  7.55 us
    pallas_call x2, Pallas kernels, attention(): pl.pallas_call(functools.partial(attention_kernel, begin), grid=(end - be...  6.85 us
  transfers between devices with their start and end apart: 9, of which 4 were waited for; matrix products, arithmetic and copies ran while one was open for 7% of the time, Pallas kernels for 23%

profile of v3, /device:TPU:0, one launch (start us, length us, event | category | flops | bytes accessed | tf_op | source)
XLA Modules:
  0.0 156.1 jit_solution(16058780520028553450)
XLA Ops:
  7.2 1.2 copy-done
  9.2 1.7 %constant_dynamic-slice_fusion.2 = bf16[512,256]{1,0:T(8,128)(2,1)} fusion(bf16[512,1024]{1,0:T(8,128)(2,1)} %param.22, s32[]{:T(128)S(6)} %select_n.58), kind=kLoop, calls=%fused_computation.9 | loop fusion | bytes 524292 | tf_op jit(solution)/shard_map/dynamic_slice | solution.py:425
  11.0 3.8 %pack.1 = bf16[4,128,2048]{2,1,0:T(8,128)(2,1)} custom-call(bf16[128,8192]{1,0:T(8,128)(2,1)} %bitcast.33), custom_call_target="tpu_custom_call" | custom-call | tf_op jit(solution)/shard_map/pack/pallas_call | solution.py:104
  14.7 5.3 %all-to-all-start = ((bf16[4,128,2048]{2,1,0:T(8,128)(2,1)}), bf16[4,128,2048]{2,1,0:T(8,128)(2,1)S(1)}, u32[]{:S(2)}, u32[]{:S(2)}) async-start(bf16[4,128,2048]{2,1,0:T(8,128)(2,1)} %pack.1), calls=%async_computation | async-start | bytes 4194304 | tf_op jit(solution)/shard_map/all_to_all | solution.py:385
  20.0 1.0 pad_maximum_fusion.refs_4_.refs_5_
  21.0 4.6 %collective-permute-start = (bf16[128,1024]{1,0:T(8,128)(2,1)S(1)}, bf16[128,1024]{1,0:T(8,128)(2,1)}, u32[]{:S(2)}, u32[]{:S(2)}) collective-permute-start(bf16[128,1024]{1,0:T(8,128)(2,1)S(1)} %pad_maximum_fusion.refs_4_.refs_5_), channel_id=1, source_target_pairs={{0,16},{8,24},{1,17},{9,25},{2,18},{10,26},{3,19},{11,27},{4,20},{... | collective-permute-start | bytes 786440 | tf_op jit(solution)/shard_map/ppermute | solution.py:381
  25.7 4.1 %collective-permute-start.1 = (bf16[128,1024]{1,0:T(8,128)(2,1)S(1)}, bf16[128,1024]{1,0:T(8,128)(2,1)}, u32[]{:S(2)}, u32[]{:S(2)}) collective-permute-start(bf16[128,1024]{1,0:T(8,128)(2,1)S(1)} %pad_maximum_fusion.refs_4_.refs_5_), channel_id=1, source_target_pairs={{0,8},{8,16},{16,24},{1,9},{9,17},{17,25},{2,10},{10,18},{18,26},{... | collective-permute-start | bytes 786440 | tf_op jit(solution)/shard_map/ppermute | solution.py:381
  29.8 0.8 copy.28.seg_ref
  30.6 1.7 %reshape.74 = f32[4,8,1,4,256]{4,3,1,0,2:T(4,128)} reshape(f32[4,8192]{1,0:T(4,128)} %param.19) | data formatting | bytes 262144 | tf_op jit(solution)/shard_map/reshape | solution.py:419
  32.3 1.0 dynamic-slice_reduce_fusion.1
  34.1 19.8 %collective-permute-done.refs_0_.refs_1_ = bf16[128,1024]{1,0:T(8,128)(2,1)} collective-permute-done((bf16[128,1024]{1,0:T(8,128)(2,1)S(1)}, bf16[128,1024]{1,0:T(8,128)(2,1)}, u32[]{:S(2)}, u32[]{:S(2)}) %collective-permute-start) | collective-permute-done | bytes 262176 | tf_op jit(solution)/shard_map/ppermute | solution.py:381
  53.9 1.6 %copy-done.2 = bf16[4352,256]{1,0:T(8,128)(2,1)S(1)} copy-done((bf16[4352,256]{1,0:T(8,128)(2,1)S(1)}, bf16[4352,256]{1,0:T(8,128)(2,1)}, u32[]{:S(2)}) %copy-start.2) | copy-done | bytes 2228248
  55.5 0.9 copy-done.3
  56.5 4.9 %conv_select.1 = (bf16[512,2048]{1,0:T(8,128)(2,1)S(1)}, bf16[4,128,640]{2,1,0:T(8,128)(2,1)S(1)}) custom-call(s32[512,1]{1,0:T(8,128)S(1)} %copy-done.3, bf16[4,128,2048]{2,1,0:T(8,128)(2,1)S(1)} %all-to-all-done.x_ref, f32[4,2048]{1,0:T(4,128)S(1)} %bitcast.27, f32[1,2048]{1,0:T(1,128)S(1)} %bitcast.28, bf16[8,544,256]{2,1,0:T(8,128)(2,1)S(1)} %bitcast.26), custom_call_target="tpu_custom_call" | custom-call | flops 1140850688 | bytes 6422528 | tf_op jit(solution)/shard_map/conv_select/pallas_call | solution.py:171
  62.2 1.3 copy-done.5
  63.5 4.0 %all-to-all-start.1 = ((bf16[4,128,640]{2,1,0:T(8,128)(2,1)}), bf16[4,128,640]{2,1,0:T(8,128)(2,1)S(1)}, u32[]{:S(2)}, u32[]{:S(2)}) async-start(bf16[4,128,640]{2,1,0:T(8,128)(2,1)} %copy-done.4), calls=%async_computation.1 | async-start | bytes 1310720 | tf_op jit(solution)/shard_map/all_to_all | solution.py:385
  67.8 3.4 %attention_0.1.refs_6_ = bf16[128,4096]{1,0:T(8,128)(2,1)} custom-call(s32[128,1]{1,0:T(8,128)S(1)} %copy.29.seg_q_ref, s32[1,384]{1,0:T(1,128)S(1)} %broadcast_in_dim.24.seg_k_ref, bf16[128,4096]{1,0:T(8,128)(2,1)S(1)} %bitcast.24, bf16[128,1024]{1,0:T(8,128)(2,1)} %collective-permute-done.refs_0_.refs_1_, ...), custom_call_target="tpu_custom_call" | custom-call | flops 402653184 | bytes 1048576 | tf_op jit(solution)/shard_map/attention_0/pallas_call | solution.py:72
  71.3 5.5 %all-to-all-done.1.part_ref = bf16[4,128,640]{2,1,0:T(8,128)(2,1)S(1)} async-done(((bf16[4,128,640]{2,1,0:T(8,128)(2,1)}), bf16[4,128,640]{2,1,0:T(8,128)(2,1)S(1)}, u32[]{:S(2)}, u32[]{:S(2)}) %all-to-all-start.1) | async-done | bytes 655392 | tf_op jit(solution)/shard_map/all_to_all | solution.py:385
  76.8 0.9 copy-done.8
  77.7 2.1 %normalise.1 = bf16[4,128,640]{2,1,0:T(8,128)(2,1)} custom-call(bf16[4,128,640]{2,1,0:T(8,128)(2,1)} %copy-done.8), custom_call_target="tpu_custom_call" | custom-call | tf_op jit(solution)/shard_map/normalise/pallas_call | solution.py:219
  79.8 4.2 %all-to-all-start.2 = ((bf16[4,128,640]{2,1,0:T(8,128)(2,1)}), bf16[4,128,640]{2,1,0:T(8,128)(2,1)}, u32[]{:S(2)}, u32[]{:S(2)}) async-start(bf16[4,128,640]{2,1,0:T(8,128)(2,1)} %normalise.1), calls=%async_computation.2 | async-start | bytes 1310720 | tf_op jit(solution)/shard_map/all_to_all | solution.py:385
  84.3 1.4 reshape.79
  88.1 3.4 %attention_2.1 = bf16[128,4096]{1,0:T(8,128)(2,1)} custom-call(s32[128,1]{1,0:T(8,128)S(1)} %copy.29.seg_q_ref, s32[1,384]{1,0:T(1,128)S(1)} %broadcast_in_dim.24.seg_k_ref, bf16[128,4096]{1,0:T(8,128)(2,1)S(1)} %bitcast.25, bf16[128,1024]{1,0:T(8,128)(2,1)} %collective-permute-done.refs_0_.refs_1_, ...), custom_call_target="tpu_custom_call", output_to_operand_aliasing={{}: (9, {})} | custom-call | flops 402653184 | bytes 1048576 | tf_op jit(solution)/shard_map/attention_2/pallas_call | solution.py:72
  91.5 2.2 %all-to-all-done.2 = bf16[4,128,640]{2,1,0:T(8,128)(2,1)} async-done(((bf16[4,128,640]{2,1,0:T(8,128)(2,1)}), bf16[4,128,640]{2,1,0:T(8,128)(2,1)}, u32[]{:S(2)}, u32[]{:S(2)}) %all-to-all-start.2) | async-done | bytes 655392 | tf_op jit(solution)/shard_map/all_to_all | solution.py:385
  93.7 15.2 %state_scan_0.1 = bf16[4,128,1024]{2,1,0:T(8,128)(2,1)} custom-call(f32[512,1]{1,0:T(8,128)} %broadcast_select_fusion.reset_ref, bf16[512,640]{1,0:T(8,128)(2,1)} %bitcast.11.low_ref, bf16[8,512,256]{2,1,0:T(8,128)(2,1)} %bitcast.47, f32[1,2048]{1,0:T(1,128)} %bitcast.45, f32[16,2048]{1,0:T(8,128)} %bitcast.36, f32[1,2048]{1,0:T(1,128)} %bitcast.43, ...), custom_call_target="tpu_custom_call" | custom-call | flops 50331648 | bytes 3145728 | tf_op jit(solution)/shard_map/state_scan_0/pallas_call | solution.py:313
  109.0 3.5 %all-to-all-start.4 = ((bf16[4,128,1024]{2,1,0:T(8,128)(2,1)}), bf16[4,128,1024]{2,1,0:T(8,128)(2,1)S(1)}, u32[]{:S(2)}, u32[]{:S(2)}) async-start(bf16[4,128,1024]{2,1,0:T(8,128)(2,1)} %state_scan_0.1), calls=%async_computation.4 | async-start | bytes 2097152 | tf_op jit(solution)/shard_map/all_to_all | solution.py:385
  112.5 15.3 %state_scan_1.1 = bf16[4,128,1024]{2,1,0:T(8,128)(2,1)} custom-call(f32[512,1]{1,0:T(8,128)} %broadcast_select_fusion.reset_ref, bf16[512,640]{1,0:T(8,128)(2,1)} %bitcast.11.low_ref, bf16[8,512,256]{2,1,0:T(8,128)(2,1)} %bitcast.48, f32[1,2048]{1,0:T(1,128)} %bitcast.46, f32[16,2048]{1,0:T(8,128)} %bitcast.37, f32[1,2048]{1,0:T(1,128)} %bitcast.44, ...), custom_call_target="tpu_custom_call" | custom-call | flops 50331648 | bytes 3145728 | tf_op jit(solution)/shard_map/state_scan_1/pallas_call | solution.py:313
  127.8 4.2 %all-to-all-start.3 = ((bf16[4,128,1024]{2,1,0:T(8,128)(2,1)}), bf16[4,128,1024]{2,1,0:T(8,128)(2,1)S(1)}, u32[]{:S(2)}, u32[]{:S(2)}) async-start(bf16[4,128,1024]{2,1,0:T(8,128)(2,1)} %state_scan_1.1), calls=%async_computation.3 | async-start | bytes 2097152 | tf_op jit(solution)/shard_map/all_to_all | solution.py:385
  131.9 3.8 %gate_0.1.refs_0_ = bf16[128,8192]{1,0:T(8,128)(2,1)} custom-call(bf16[4,128,1024]{2,1,0:T(8,128)(2,1)} %copy-done.6, bf16[128,8192]{1,0:T(8,128)(2,1)} %bitcast.29), custom_call_target="tpu_custom_call" | custom-call | flops 2097152 | bytes 3145728 | tf_op jit(solution)/shard_map/gate_0/pallas_call | solution.py:364
  135.7 8.8 %all-to-all-done.3.y_ref = bf16[4,128,1024]{2,1,0:T(8,128)(2,1)S(1)} async-done(((bf16[4,128,1024]{2,1,0:T(8,128)(2,1)}), bf16[4,128,1024]{2,1,0:T(8,128)(2,1)S(1)}, u32[]{:S(2)}, u32[]{:S(2)}) %all-to-all-start.3) | async-done | bytes 1048608 | tf_op jit(solution)/shard_map/all_to_all | solution.py:385
  144.5 1.0 copy-done.7
  145.5 3.8 %gate_1.1 = bf16[128,8192]{1,0:T(8,128)(2,1)} custom-call(bf16[4,128,1024]{2,1,0:T(8,128)(2,1)} %copy-done.7, bf16[128,8192]{1,0:T(8,128)(2,1)} %bitcast.30, bf16[128,8192]{1,0:T(8,128)(2,1)} %gate_0.1.refs_0_), custom_call_target="tpu_custom_call", output_to_operand_aliasing={{}: (2, {})} | custom-call | flops 2097152 | bytes 3145728 | tf_op jit(solution)/shard_map/gate_1/pallas_call | solution.py:364
  (44 shorter events, 5.5 us)
Async XLA Ops:
  7.2 1.3 copy-start
  7.2 46.7 %all-gather.5.cloned.1.call-start = ((), (), s32[]{:S(2)}) async-start(), calls=%async_computation.5 | async-start | bytes 2506752 | tf_op jit(solution)/shard_map/all_gather | solution.py:426
  9.2 84.5 %all-gather.7.cloned.1.call-start = ((), (), s32[]{:S(2)}) async-start(), calls=%async_computation.6 | async-start | bytes 2359296 | tf_op jit(solution)/shard_map/all_gather | solution.py:426
  14.7 15.0 %copy-start.9 = (s32[1,512]{1,0:T(1,128)S(1)}, s32[1,512]{1,0:T(1,128)}, u32[]{:S(2)}) copy-start(s32[1,512]{1,0:T(1,128)} %param.18) | copy-start | bytes 6148
  14.7 39.2 %all-to-all-start = ((bf16[4,128,2048]{2,1,0:T(8,128)(2,1)}), bf16[4,128,2048]{2,1,0:T(8,128)(2,1)S(1)}, u32[]{:S(2)}, u32[]{:S(2)}) async-start(bf16[4,128,2048]{2,1,0:T(8,128)(2,1)} %pack.1), calls=%async_computation | async-start | bytes 4194304 | tf_op jit(solution)/shard_map/all_to_all | solution.py:385
  21.0 32.9 %collective-permute-start = (bf16[128,1024]{1,0:T(8,128)(2,1)S(1)}, bf16[128,1024]{1,0:T(8,128)(2,1)}, u32[]{:S(2)}, u32[]{:S(2)}) collective-permute-start(bf16[128,1024]{1,0:T(8,128)(2,1)S(1)} %pad_maximum_fusion.refs_4_.refs_5_), channel_id=1, source_target_pairs={{0,16},{8,24},{1,17},{9,25},{2,18},{10,26},{3,19},{11,27},{4,20},{... | collective-permute-start | bytes 786440 | tf_op jit(solution)/shard_map/ppermute | solution.py:381
  25.7 28.2 %collective-permute-start.1 = (bf16[128,1024]{1,0:T(8,128)(2,1)S(1)}, bf16[128,1024]{1,0:T(8,128)(2,1)}, u32[]{:S(2)}, u32[]{:S(2)}) collective-permute-start(bf16[128,1024]{1,0:T(8,128)(2,1)S(1)} %pad_maximum_fusion.refs_4_.refs_5_), channel_id=1, source_target_pairs={{0,8},{8,16},{16,24},{1,9},{9,17},{17,25},{2,10},{10,18},{18,26},{... | collective-permute-start | bytes 786440 | tf_op jit(solution)/shard_map/ppermute | solution.py:381
  53.9 1.6 %copy-start.2 = (bf16[4352,256]{1,0:T(8,128)(2,1)S(1)}, bf16[4352,256]{1,0:T(8,128)(2,1)}, u32[]{:S(2)}) copy-start(bf16[4352,256]{1,0:T(8,128)(2,1)} %all-gather.5.cloned.1.call-done) | copy-start | bytes 6684676
  55.5 0.9 copy-start.3
  61.4 0.9 copy-start.4
  62.2 1.3 copy-start.5
  63.5 4.3 %copy-start.1 = (bf16[1,128,4096]{2,1,0:T(8,128)(2,1)S(1)}, bf16[1,128,4096]{2,1,0:T(8,128)(2,1)}, u32[]{:S(2)}) copy-start(bf16[1,128,4096]{2,1,0:T(8,128)(2,1)} %param.13) | copy-start | bytes 3145732
  63.5 13.2 %all-to-all-start.1 = ((bf16[4,128,640]{2,1,0:T(8,128)(2,1)}), bf16[4,128,640]{2,1,0:T(8,128)(2,1)S(1)}, u32[]{:S(2)}, u32[]{:S(2)}) async-start(bf16[4,128,640]{2,1,0:T(8,128)(2,1)} %copy-done.4), calls=%async_computation.1 | async-start | bytes 1310720 | tf_op jit(solution)/shard_map/all_to_all | solution.py:385
  71.3 13.0 %copy-start.10 = (f32[8192]{0:T(1024)S(1)}, f32[8192]{0:T(1024)}, u32[]{:S(2)}) copy-start(f32[8192]{0:T(1024)} %param.25) | copy-start | bytes 98308
  71.3 13.0 %copy-start.11 = (f32[8192]{0:T(1024)S(1)}, f32[8192]{0:T(1024)}, u32[]{:S(2)}) copy-start(f32[8192]{0:T(1024)} %param.23) | copy-start | bytes 98308
  76.8 0.9 copy-start.8
  79.8 13.9 %all-to-all-start.2 = ((bf16[4,128,640]{2,1,0:T(8,128)(2,1)}), bf16[4,128,640]{2,1,0:T(8,128)(2,1)}, u32[]{:S(2)}, u32[]{:S(2)}) async-start(bf16[4,128,640]{2,1,0:T(8,128)(2,1)} %normalise.1), calls=%async_computation.2 | async-start | bytes 1310720 | tf_op jit(solution)/shard_map/all_to_all | solution.py:385
  109.0 18.8 %all-to-all-start.4 = ((bf16[4,128,1024]{2,1,0:T(8,128)(2,1)}), bf16[4,128,1024]{2,1,0:T(8,128)(2,1)S(1)}, u32[]{:S(2)}, u32[]{:S(2)}) async-start(bf16[4,128,1024]{2,1,0:T(8,128)(2,1)} %state_scan_0.1), calls=%async_computation.4 | async-start | bytes 2097152 | tf_op jit(solution)/shard_map/all_to_all | solution.py:385
  127.8 4.2 %copy-start.6 = (bf16[4,128,1024]{2,1,0:T(8,128)(2,1)}, bf16[4,128,1024]{2,1,0:T(8,128)(2,1)S(1)}, u32[]{:S(2)}) copy-start(bf16[4,128,1024]{2,1,0:T(8,128)(2,1)S(1)} %all-to-all-done.4.y_ref) | copy-start | bytes 3145732
  127.8 16.7 %all-to-all-start.3 = ((bf16[4,128,1024]{2,1,0:T(8,128)(2,1)}), bf16[4,128,1024]{2,1,0:T(8,128)(2,1)S(1)}, u32[]{:S(2)}, u32[]{:S(2)}) async-start(bf16[4,128,1024]{2,1,0:T(8,128)(2,1)} %state_scan_1.1), calls=%async_computation.3 | async-start | bytes 2097152 | tf_op jit(solution)/shard_map/all_to_all | solution.py:385
  144.5 1.0 copy-start.7
Sparse Core Ops, SparseCore 0:
  10.2 32.8 all-gather.4
  44.7 28.5 all-gather.6

commit v4 on v3

--- a/solution.py
+++ b/solution.py
@@ -76,7 +76,7 @@
         out_specs=wide,
         out_shape=jax.ShapeDtypeStruct(queries.shape, jnp.bfloat16),
         input_output_aliases=aliases,
-        compiler_params=pltpu.CompilerParams(vmem_limit_bytes=32 << 20),
+        compiler_params=pltpu.CompilerParams(vmem_limit_bytes=16 << 20),
         cost_estimate=pl.CostEstimate(
             flops=4 * rows * span * group_width * (end - begin),
             bytes_accessed=4 * rows * group_width * (end - begin),
@@ -107,6 +107,7 @@
         in_specs=[pl.BlockSpec((part, channels), lambda r: (r, 0))],
         out_specs=pl.BlockSpec((ctx, part, channels // ctx), lambda r: (0, r, 0)),
         out_shape=jax.ShapeDtypeStruct((ctx, rows, channels // ctx), value.dtype),
+        compiler_params=pltpu.CompilerParams(vmem_limit_bytes=12 << 20),
         name="pack",
     )(value)
 
@@ -191,7 +192,7 @@
             jax.ShapeDtypeStruct((toks, slots * width), jnp.bfloat16),
             jax.ShapeDtypeStruct((ctx, rows, padded_outputs), jnp.bfloat16),
         ],
-        compiler_params=pltpu.CompilerParams(vmem_limit_bytes=40 << 20),
+        compiler_params=pltpu.CompilerParams(vmem_limit_bytes=20 << 20),
         cost_estimate=pl.CostEstimate(
             flops=2 * toks * slots * width * outputs,
             bytes_accessed=2 * pieces.size * 2 + 2 * select_parts.size,
@@ -219,6 +220,7 @@
     return pl.pallas_call(
         functools.partial(normalise_kernel, rank),
         out_shape=jax.ShapeDtypeStruct(parts.shape, jnp.bfloat16),
+        compiler_params=pltpu.CompilerParams(vmem_limit_bytes=12 << 20),
         name="normalise",
     )(parts)
 
@@ -265,7 +267,18 @@
 
     rates = [-LOG2E * jnp.exp(decay_ref[:, tile * LANES : (tile + 1) * LANES]) for tile in range(tiles)]
 
-    def advance(index, held, history):
+    quarter = min(2 * LANES, tiles * LANES)
+    quarters = tiles * LANES // quarter
+
+    def finish(index, history, part):
+        first = pl.multiple_of(index * block, block)
+        lanes = slice(part * quarter, (part + 1) * quarter)
+        mixed = jnp.dot(out_diag[pl.ds(first, block), :], history[:, lanes], preferred_element_type=jnp.float32)
+        full = mixed + gain_ref[:, lanes] * conv_ref[pl.ds(first, block), lanes].astype(jnp.float32)
+        place = pl.multiple_of(lax.rem(first, rows), block)
+        out_ref[lax.div(first, rows), pl.ds(place, block), lanes] = full.astype(out_ref.dtype)
+
+    def advance(index, held, history, before, before_history):
         held = list(held)
         per_row = LANES // block
         columns = in_cols[:, pl.ds(pl.multiple_of(lax.div(index, per_row) * LANES, LANES), LANES)]
@@ -279,27 +292,20 @@
                 grow = jnp.exp2(delta_now[tile, inner : inner + 1, :] * rates[tile])
                 held[tile] = grow * held[tile] + into * drive_now[tile, inner : inner + 1, :]
                 history[inner * states : (inner + 1) * states, lanes] = held[tile].astype(jnp.bfloat16)
+            if inner % (block // quarters) == 0:
+                finish(before, before_history, inner // (block // quarters))
         return tuple(held)
 
-    def finish(index, history):
-        first = pl.multiple_of(index * block, block)
-        mixed = jnp.dot(out_diag[pl.ds(first, block), :], history[...], preferred_element_type=jnp.float32)
-        full = mixed + gain_ref[...] * conv_ref[pl.ds(first, block), :].astype(jnp.float32)
-        place = pl.multiple_of(lax.rem(first, rows), block)
-        out_ref[lax.div(first, rows), pl.ds(place, block), :] = full.astype(out_ref.dtype)
-
     held_odd[...] = jnp.zeros_like(held_odd)
 
     def pair(index, held):
-        held = advance(2 * index, held, held_even)
-        finish(jnp.maximum(2 * index - 1, 0), held_odd)
-        held = advance(2 * index + 1, held, held_odd)
-        finish(2 * index, held_even)
-        return held
+        held = advance(2 * index, held, held_even, jnp.maximum(2 * index - 1, 0), held_odd)
+        return advance(2 * index + 1, held, held_odd, 2 * index, held_even)
 
     start = tuple(jnp.zeros((states, LANES), jnp.float32) for _ in range(tiles))
     lax.fori_loop(0, count // 2, pair, start)
-    finish(count - 1, held_odd)
+    for part in range(quarters):
+        finish(count - 1, held_odd, part)
 
 
 def state_scan(reset_col, low, delta_parts, bias, decay, gain, conv, ctx, call, calls):
@@ -332,7 +338,7 @@
             pltpu.VMEM((16 * states, wide), jnp.bfloat16),
             pltpu.VMEM((16 * states, wide), jnp.bfloat16),
         ],
-        compiler_params=pltpu.CompilerParams(vmem_limit_bytes=56 << 20),
+        compiler_params=pltpu.CompilerParams(vmem_limit_bytes=24 << 20),
         cost_estimate=pl.CostEstimate(
             flops=6 * steps, bytes_accessed=2 * delta_parts.size // calls + 4 * toks * wide, transcendentals=steps
         ),
@@ -368,6 +374,7 @@
         out_specs=columns,
         out_shape=jax.ShapeDtypeStruct(gate.shape, jnp.bfloat16),
         input_output_aliases=aliases,
+        compiler_params=pltpu.CompilerParams(vmem_limit_bytes=12 << 20),
         cost_estimate=pl.CostEstimate(
             flops=4 * pieces.size, bytes_accessed=6 * pieces.size, transcendentals=pieces.size
         ),
@@ -430,39 +437,41 @@
         return parts
 
     select_parts = gathered(select_weight)
+    packed = pack(mixer_input[0], ctx, fold, width)
+    packed, delta_weight = lax.optimization_barrier((packed, delta_weight))
     delta_parts = gathered(delta_weight)
 
-    both = jnp.concatenate([keys[0], values[0]], axis=1)
-    blocks = [shifted(both, "ctx", by) for by in range(back, 0, -1)] + [both]
-
-    pieces = exchange(pack(mixer_input[0], ctx, fold, width))
-    pieces, blocks = lax.optimization_barrier((pieces, blocks))
-
-    conv, parts = conv_select(seg_col, pieces, own_part(conv_weight), own_part(conv_bias)[None, :], select_parts)
-
+    same = jnp.concatenate([jnp.zeros((1,), bool), seg[1:] == seg[:-1]])
+    reset_col = jnp.where(same, 0.0, FAR)[:, None]
     seg_pad = jnp.concatenate([jnp.full((back * rows,), -1, jnp.int32), seg])
     seg_k = lax.dynamic_slice_in_dim(seg_pad, place * rows, (back + 1) * rows, 0)
-    seg_q = seg_k[back * rows :, None]
-    parts, blocks = lax.optimization_barrier((parts, blocks))
-    middle = KEY_VALUE_HEADS // 2
-    attended = attention(queries[0], blocks, seg_q, seg_k[None, :], 0, middle)
-    parts, attended = lax.optimization_barrier((exchange(parts), attended))
-    low_own = normalise(parts, rank)
-    low_own, attended = lax.optimization_barrier((low_own, attended))
-    attended = attention(queries[0], blocks, seg_q, seg_k[None, :], middle, KEY_VALUE_HEADS, attended)
-    low, attended = lax.optimization_barrier((exchange(low_own), attended))
-    low = low.reshape(toks, low.shape[2])
+    own = (
+        own_part(delta_bias)[None, :],
+        own_part(jnp.transpose(decay_log)),
+        own_part(skip_gain)[None, :],
+        reset_col,
+        seg_k[back * rows :, None],
+        seg_k[None, :],
+        jnp.concatenate([keys[0], values[0]], axis=1),
+    )
+    pieces, own = lax.optimization_barrier((exchange(packed), own))
+    bias, decay, gain, reset_col, seg_q, seg_k, both = own
+
+    conv, parts = conv_select(seg_col, pieces, own_part(conv_weight), own_part(conv_bias)[None, :], select_parts)
+    low = normalise(exchange(parts), rank)
+
+    low, both = lax.optimization_barrier((low, both))
+    blocks = [shifted(both, "ctx", by) for by in range(back, 0, -1)] + [both]
+    low = exchange(low).reshape(toks, low.shape[2])
 
     calls = 2
-    bias = own_part(delta_bias)[None, :]
-    gain = own_part(skip_gain)[None, :]
-    decay = own_part(jnp.transpose(decay_log))
-    same = jnp.concatenate([jnp.zeros((1,), bool), seg[1:] == seg[:-1]])
-    reset_col = jnp.where(same, 0.0, FAR)[:, None]
-    scanned = [
-        exchange(state_scan(reset_col, low, delta_parts, bias, decay, gain, conv, ctx, call, calls))
-        for call in range(calls)
-    ]
+    scanned = []
+    for call in range(calls):
+        scanned.append(state_scan(reset_col, low, delta_parts, bias, decay, gain, conv, ctx, call, calls))
+    scanned[-1], blocks = lax.optimization_barrier((scanned[-1], blocks))
+    attended = attention(queries[0], blocks, seg_q, seg_k, 0, KEY_VALUE_HEADS)
+    scanned = [exchange(part) for part in scanned]
+    scanned[-1], attended = lax.optimization_barrier((scanned[-1], attended))
     mixed = None
     for call in range(calls):
         mixed = apply_gate(scanned[call], gate_input[0], fold, width, call, mixed)

time: 157 us -> 147 us (0.936)
  waiting for transfers between devices: 36.3 us -> 16.9 us
  local copies, waits for them, and re-layouts: 18.1 us -> 32.3 us
  Pallas kernels: 55.7 us -> 43.3 us
  blocking collectives: 0 us -> 12 us
  starting transfers between devices: 29.9 us -> 23.9 us
    ppermute x2, waiting for transfers between devices: 19.8 us -> 0.01 us  [shifted(): return lax.ppermute(value, axis, pairs)]
    unnamed x26 -> x52, local copies, waits for them, and re-layouts: 8.55 us -> 20.7 us
    all_to_all x0 -> x1, blocking collectives: none -> 12 us  [exchange(): return lax.all_to_all(value, 'ctx', 0, 0, tiled=True)]
    all_to_all x5 -> x4, starting transfers between devices: 21.1 us -> 16.6 us  [exchange(): return lax.all_to_all(value, 'ctx', 0, 0, tiled=True)]
    pallas_call x2, Pallas kernels: 30.5 us -> 26.7 us  [state_scan(): pl.pallas_call(functools.partial(scan_kernel, rank), grid=(1,), in_specs=...]
    pallas_call x1, Pallas kernels: 3.79 us -> 0.33 us  [pack(): pl.pallas_call(functools.partial(pack_kernel, fold, width), grid=(rows //...]
    pallas_call x2 -> x1, Pallas kernels: 6.85 us -> 4.79 us  [attention(): pl.pallas_call(functools.partial(attention_kernel, begin), grid=(end - be...]
    pallas_call x2, Pallas kernels: 7.55 us -> 5.63 us  [apply_gate(): pl.pallas_call(functools.partial(gate_kernel, fold, width), grid=(rows //...]
  transfers between devices with their start and end apart: 9 -> 8, of which waited for: 4 -> 3; matrix products, arithmetic and copies ran while one was open for 7% -> 10% of each run, Pallas kernels for 23% -> 26%
where the time goes in v4:
time: 147 us; the launch traced here: 146 us
  Pallas kernels  43.3 us (29%)
  local copies, waits for them, and re-layouts  32.3 us (22%)
  starting transfers between devices  23.9 us (16%)
  waiting for transfers between devices  16.9 us (11%)
  between operations  14.3 us (10%)
  blocking collectives  12 us (8%)
  other arithmetic  2.72 us (2%)
    pallas_call x2, Pallas kernels, state_scan(): pl.pallas_call(functools.partial(scan_kernel, rank), grid=(1,), in_specs=...  26.7 us
    unnamed x52, local copies, waits for them, and re-layouts  20.7 us
    all_to_all x4, waiting for transfers between devices, exchange(): return lax.all_to_all(value, 'ctx', 0, 0, tiled=True)  16.9 us
    all_to_all x4, starting transfers between devices, exchange(): return lax.all_to_all(value, 'ctx', 0, 0, tiled=True)  16.6 us
    all_to_all x1, blocking collectives, exchange(): return lax.all_to_all(value, 'ctx', 0, 0, tiled=True)  12 us
    ppermute x2, starting transfers between devices, shifted(): return lax.ppermute(value, axis, pairs)  7.27 us
    pallas_call x2, Pallas kernels, apply_gate(): pl.pallas_call(functools.partial(gate_kernel, fold, width), grid=(rows //...  5.63 us
    pallas_call x1, Pallas kernels, conv_select(): pl.pallas_call(conv_select_kernel, grid=(slots // batch,), in_specs=[pl.B...  4.89 us
  transfers between devices with their start and end apart: 8, of which 3 were waited for; matrix products, arithmetic and copies ran while one was open for 10% of the time, Pallas kernels for 26%

profile of v4, /device:TPU:0, one launch (start us, length us, event | category | flops | bytes accessed | tf_op | source)
XLA Modules:
  0.0 145.5 jit_solution(3316584548496626674)
XLA Ops:
  7.2 1.2 copy-done
  9.3 1.6 %copy-done.6 = bf16[1,128,8192]{2,1,0:T(8,128)(2,1)S(1)} copy-done((bf16[1,128,8192]{2,1,0:T(8,128)(2,1)S(1)}, bf16[1,128,8192]{2,1,0:T(8,128)(2,1)}, u32[]{:S(2)}) %copy-start.6) | copy-done | bytes 2097176
  11.2 1.3 copy-done.2
  12.5 1.7 %constant_dynamic-slice_fusion = bf16[512,256]{1,0:T(8,128)(2,1)} fusion(bf16[512,1024]{1,0:T(8,128)(2,1)} %param.22, s32[]{:T(128)S(6)} %select_n.60), kind=kLoop, calls=%fused_computation.7 | loop fusion | bytes 524292 | tf_op jit(solution)/shard_map/dynamic_slice | solution.py:432
  14.3 5.3 %all-to-all-start = ((bf16[4,128,2048]{2,1,0:T(8,128)(2,1)}), bf16[4,128,2048]{2,1,0:T(8,128)(2,1)S(1)}, u32[]{:S(2)}, u32[]{:S(2)}) async-start(bf16[4,128,2048]{2,1,0:T(8,128)(2,1)} %copy-done.2), calls=%async_computation | async-start | bytes 4194304 | tf_op jit(solution)/shard_map/all_to_all | solution.py:392
  23.6 2.2 %reshape.75 = f32[16,8,1,4,256]{4,3,1,0,2:T(4,128)} reshape(f32[16,8192]{1,0:T(8,128)} %bitcast.43) | data formatting | bytes 1048576 | tf_op jit(solution)/shard_map/reshape | solution.py:426
  25.8 1.4 dynamic-slice_reduce_fusion
  29.5 1.0 pad_maximum_fusion.refs_4_.refs_5_
  30.5 1.6 %broadcast_select_fusion.reset_ref = f32[512,1]{1,0:T(8,128)} fusion(pred[512,1]{1,0:T(8,128)(4,1)} %copy.25), kind=kLoop, calls=%fused_computation.1 | loop fusion | flops 512 | bytes 2560 | tf_op jit(solution)/shard_map/jit(_where)/select_n | solution.py:445
  32.1 12.3 %all-to-all-done.x_ref = bf16[4,128,2048]{2,1,0:T(8,128)(2,1)S(1)} async-done(((bf16[4,128,2048]{2,1,0:T(8,128)(2,1)}), bf16[4,128,2048]{2,1,0:T(8,128)(2,1)S(1)}, u32[]{:S(2)}, u32[]{:S(2)}) %all-to-all-start) | async-done | bytes 2097184 | tf_op jit(solution)/shard_map/all_to_all | solution.py:392
  44.4 1.6 %copy-done.5 = bf16[4352,256]{1,0:T(8,128)(2,1)S(1)} copy-done((bf16[4352,256]{1,0:T(8,128)(2,1)S(1)}, bf16[4352,256]{1,0:T(8,128)(2,1)}, u32[]{:S(2)}) %copy-start.5) | copy-done | bytes 2228248
  47.0 4.9 %conv_select.1 = (bf16[512,2048]{1,0:T(8,128)(2,1)S(1)}, bf16[4,128,640]{2,1,0:T(8,128)(2,1)S(1)}) custom-call(s32[512,1]{1,0:T(8,128)S(1)} %copy-done.12, bf16[4,128,2048]{2,1,0:T(8,128)(2,1)S(1)} %all-to-all-done.x_ref, f32[4,2048]{1,0:T(4,128)S(1)} %bitcast.31, f32[1,2048]{1,0:T(1,128)S(1)} %bitcast.34, bf16[8,544,256]{2,1,0:T(8,128)(2,1)S(1)} %bitcast.26), custom_call_target="tpu_custom_call" | custom-call | flops 1140850688 | bytes 6422528 | tf_op jit(solution)/shard_map/conv_select/pallas_call | solution.py:172
  51.9 1.3 copy-done.17
  53.2 12.0 %all_to_all.25.part_ref = bf16[4,128,640]{2,1,0:T(8,128)(2,1)S(1)} all-to-all(bf16[4,128,640]{2,1,0:T(8,128)(2,1)S(1)} %get-tuple-element.25), channel_id=1, replica_groups=mesh['ctx'=4,'rep'=8] {'ctx'}, dimensions={0} | all-to-all | bytes 1310720 | tf_op jit(solution)/shard_map/all_to_all | solution.py:392
  65.3 1.0 normalise.1
  66.3 3.5 %all-to-all-start.2 = ((bf16[4,128,640]{2,1,0:T(8,128)(2,1)}), bf16[4,128,640]{2,1,0:T(8,128)(2,1)S(1)}, u32[]{:S(2)}, u32[]{:S(2)}) async-start(bf16[4,128,640]{2,1,0:T(8,128)(2,1)} %normalise.1), calls=%async_computation.2 | async-start | bytes 1310720 | tf_op jit(solution)/shard_map/all_to_all | solution.py:392
  69.8 3.9 %collective-permute-start.1 = (bf16[128,1024]{1,0:T(8,128)(2,1)S(1)}, bf16[128,1024]{1,0:T(8,128)(2,1)S(1)}, u32[]{:S(2)}, u32[]{:S(2)}) collective-permute-start(bf16[128,1024]{1,0:T(8,128)(2,1)S(1)} %pad_maximum_fusion.refs_4_.refs_5_), channel_id=1, source_target_pairs={{0,8},{8,16},{16,24},{1,9},{9,17},{17,25},{2,10},{10,18},{18,26},{... | collective-permute-start | bytes 786440 | tf_op jit(solution)/shard_map/ppermute | solution.py:388
  73.7 3.4 %collective-permute-start = (bf16[128,1024]{1,0:T(8,128)(2,1)S(1)}, bf16[128,1024]{1,0:T(8,128)(2,1)S(1)}, u32[]{:S(2)}, u32[]{:S(2)}) collective-permute-start(bf16[128,1024]{1,0:T(8,128)(2,1)S(1)} %pad_maximum_fusion.refs_4_.refs_5_), channel_id=1, source_target_pairs={{0,16},{8,24},{1,17},{9,25},{2,18},{10,26},{3,19},{11,27},{4,20},{... | collective-permute-start | bytes 786440 | tf_op jit(solution)/shard_map/ppermute | solution.py:388
  77.1 3.2 %all-to-all-done.2 = bf16[4,128,640]{2,1,0:T(8,128)(2,1)S(1)} async-done(((bf16[4,128,640]{2,1,0:T(8,128)(2,1)}), bf16[4,128,640]{2,1,0:T(8,128)(2,1)S(1)}, u32[]{:S(2)}, u32[]{:S(2)}) %all-to-all-start.2) | async-done | bytes 655392 | tf_op jit(solution)/shard_map/all_to_all | solution.py:392
  80.3 1.6 %copy-done.15 = bf16[4096,256]{1,0:T(8,128)(2,1)S(1)} copy-done((bf16[4096,256]{1,0:T(8,128)(2,1)S(1)}, bf16[4096,256]{1,0:T(8,128)(2,1)}, u32[]{:S(2)}) %copy-start.15) | copy-done | bytes 2097176
  81.9 1.6 %copy-done.18 = bf16[512,2048]{1,0:T(8,128)(2,1)S(1)} copy-done((bf16[512,2048]{1,0:T(8,128)(2,1)S(1)}, bf16[512,2048]{1,0:T(8,128)(2,1)}, u32[]{:S(2)}) %copy-start.18) | copy-done | bytes 2097176
  83.5 13.4 %state_scan_1.1 = bf16[4,128,1024]{2,1,0:T(8,128)(2,1)} custom-call(f32[512,1]{1,0:T(8,128)S(1)} %copy-done.13, bf16[512,640]{1,0:T(8,128)(2,1)S(1)} %bitcast.29, bf16[8,512,256]{2,1,0:T(8,128)(2,1)S(1)} %bitcast.39, f32[1,2048]{1,0:T(1,128)S(1)} %bitcast.35, f32[16,2048]{1,0:T(8,128)S(1)} %bitcast.32, f32[1,2048]{1,0:T(1,128)S(1)} %bitcast.37, ...), custom_call_target="tpu_custom_call" | custom-call | flops 50331648 | bytes 3145728 | tf_op jit(solution)/shard_map/state_scan_1/pallas_call | solution.py:319
  98.3 3.5 %all-to-all-start.3 = ((bf16[4,128,1024]{2,1,0:T(8,128)(2,1)}), bf16[4,128,1024]{2,1,0:T(8,128)(2,1)S(1)}, u32[]{:S(2)}, u32[]{:S(2)}) async-start(bf16[4,128,1024]{2,1,0:T(8,128)(2,1)} %state_scan_1.1), calls=%async_computation.3 | async-start | bytes 2097152 | tf_op jit(solution)/shard_map/all_to_all | solution.py:392
  101.8 1.6 %copy-done.16 = bf16[4096,256]{1,0:T(8,128)(2,1)S(1)} copy-done((bf16[4096,256]{1,0:T(8,128)(2,1)S(1)}, bf16[4096,256]{1,0:T(8,128)(2,1)}, u32[]{:S(2)}) %copy-start.16) | copy-done | bytes 2097176
  103.4 1.6 %copy-done.19 = bf16[512,2048]{1,0:T(8,128)(2,1)S(1)} copy-done((bf16[512,2048]{1,0:T(8,128)(2,1)S(1)}, bf16[512,2048]{1,0:T(8,128)(2,1)}, u32[]{:S(2)}) %copy-start.19) | copy-done | bytes 2097176
  105.0 13.3 %state_scan_0.1 = bf16[4,128,1024]{2,1,0:T(8,128)(2,1)} custom-call(f32[512,1]{1,0:T(8,128)S(1)} %copy-done.13, bf16[512,640]{1,0:T(8,128)(2,1)S(1)} %bitcast.30, bf16[8,512,256]{2,1,0:T(8,128)(2,1)S(1)} %bitcast.40, f32[1,2048]{1,0:T(1,128)S(1)} %bitcast.36, f32[16,2048]{1,0:T(8,128)S(1)} %bitcast.33, f32[1,2048]{1,0:T(1,128)S(1)} %bitcast.38, ...), custom_call_target="tpu_custom_call" | custom-call | flops 50331648 | bytes 3145728 | tf_op jit(solution)/shard_map/state_scan_0/pallas_call | solution.py:319
  119.3 4.2 %all-to-all-start.4 = ((bf16[4,128,1024]{2,1,0:T(8,128)(2,1)}), bf16[4,128,1024]{2,1,0:T(8,128)(2,1)}, u32[]{:S(2)}, u32[]{:S(2)}) async-start(bf16[4,128,1024]{2,1,0:T(8,128)(2,1)} %state_scan_0.1), calls=%async_computation.4 | async-start | bytes 2097152 | tf_op jit(solution)/shard_map/all_to_all | solution.py:392
  123.7 1.3 copy-done.7
  126.9 4.8 %attention_0.1 = bf16[128,4096]{1,0:T(8,128)(2,1)} custom-call(s32[128,1]{1,0:T(8,128)S(1)} %copy.28.seg_q_ref, s32[1,384]{1,0:T(1,128)S(1)} %broadcast_in_dim.25.seg_k_ref, bf16[128,4096]{1,0:T(8,128)(2,1)S(1)} %bitcast.28, bf16[128,1024]{1,0:T(8,128)(2,1)S(1)} %copy-done.11, bf16[128,1024]{1,0:T(8,128)(2,1)S(1)} %copy-done.11, ...), custom_call_target="tpu_custom_call" | custom-call | flops 805306368 | bytes 2097152 | tf_op jit(solution)/shard_map/attention_0/pallas_call | solution.py:72
  131.7 1.3 all-to-all-done.4.y_ref
  133.0 3.7 %gate_0.1.refs_0_ = bf16[128,8192]{1,0:T(8,128)(2,1)} custom-call(bf16[4,128,1024]{2,1,0:T(8,128)(2,1)} %all-to-all-done.4.y_ref, bf16[128,8192]{1,0:T(8,128)(2,1)S(1)} %bitcast.24), custom_call_target="tpu_custom_call" | custom-call | flops 2097152 | bytes 3145728 | tf_op jit(solution)/shard_map/gate_0/pallas_call | solution.py:370
  136.7 1.9 %gate_1.1 = bf16[128,8192]{1,0:T(8,128)(2,1)} custom-call(bf16[4,128,1024]{2,1,0:T(8,128)(2,1)S(1)} %copy-done.4, bf16[128,8192]{1,0:T(8,128)(2,1)S(1)} %bitcast.25, bf16[128,8192]{1,0:T(8,128)(2,1)} %gate_0.1.refs_0_), custom_call_target="tpu_custom_call", output_to_operand_aliasing={{}: (2, {})} | custom-call | flops 2097152 | bytes 3145728 | tf_op jit(solution)/shard_map/gate_1/pallas_call | solution.py:370
  (68 shorter events, 12.9 us)
Async XLA Ops:
  7.2 1.3 copy-start
  7.2 37.3 %all-gather.5.cloned.1.call-start = ((), (), s32[]{:S(2)}) async-start(), calls=%async_computation.5 | async-start | bytes 2506752 | tf_op jit(solution)/shard_map/all_gather | solution.py:433
  9.2 67.9 %all-gather.7.cloned.1.call-start = ((), (), s32[]{:S(2)}) async-start(), calls=%async_computation.6 | async-start | bytes 2359296 | tf_op jit(solution)/shard_map/all_gather | solution.py:433
  9.3 1.6 %copy-start.6 = (bf16[1,128,8192]{2,1,0:T(8,128)(2,1)S(1)}, bf16[1,128,8192]{2,1,0:T(8,128)(2,1)}, u32[]{:S(2)}) copy-start(bf16[1,128,8192]{2,1,0:T(8,128)(2,1)} %param.16) | copy-start | bytes 6291460
  11.2 1.3 copy-start.2
  14.2 5.4 %copy-start.21 = (s32[1,512]{1,0:T(1,128)S(1)}, s32[1,512]{1,0:T(1,128)}, u32[]{:S(2)}) copy-start(s32[1,512]{1,0:T(1,128)} %param.18) | copy-start | bytes 6148
  14.2 5.4 %copy-start.22 = (f32[8192]{0:T(1024)S(1)}, f32[8192]{0:T(1024)}, u32[]{:S(2)}) copy-start(f32[8192]{0:T(1024)} %param.20) | copy-start | bytes 98308
  14.2 6.1 %copy-start.23 = (f32[8192]{0:T(1024)S(1)}, f32[8192]{0:T(1024)}, u32[]{:S(2)}) copy-start(f32[8192]{0:T(1024)} %param.23) | copy-start | bytes 98308
  14.2 6.7 %copy-start.24 = (f32[8192]{0:T(1024)S(1)}, f32[8192]{0:T(1024)}, u32[]{:S(2)}) copy-start(f32[8192]{0:T(1024)} %param.25) | copy-start | bytes 98308
  14.3 8.2 %copy-start.20 = (f32[4,8192]{1,0:T(4,128)S(1)}, f32[4,8192]{1,0:T(4,128)}, u32[]{:S(2)}) copy-start(f32[4,8192]{1,0:T(4,128)} %param.19) | copy-start | bytes 393220
  14.3 30.2 %all-to-all-start = ((bf16[4,128,2048]{2,1,0:T(8,128)(2,1)}), bf16[4,128,2048]{2,1,0:T(8,128)(2,1)S(1)}, u32[]{:S(2)}, u32[]{:S(2)}) async-start(bf16[4,128,2048]{2,1,0:T(8,128)(2,1)} %copy-done.2), calls=%async_computation | async-start | bytes 4194304 | tf_op jit(solution)/shard_map/all_to_all | solution.py:392
  44.4 1.6 %copy-start.5 = (bf16[4352,256]{1,0:T(8,128)(2,1)S(1)}, bf16[4352,256]{1,0:T(8,128)(2,1)}, u32[]{:S(2)}) copy-start(bf16[4352,256]{1,0:T(8,128)(2,1)} %all-gather.5.cloned.1.call-done) | copy-start | bytes 6684676
  46.1 0.9 copy-start.12
  51.9 1.3 copy-start.17
  53.2 27.0 %copy-start.13 = (f32[512,1]{1,0:T(8,128)S(1)}, f32[512,1]{1,0:T(8,128)}, u32[]{:S(2)}) copy-start(f32[512,1]{1,0:T(8,128)} %broadcast_select_fusion.reset_ref) | copy-start | bytes 6148
  53.2 27.0 %copy-start.14 = (f32[2,8,8,256]{3,1,2,0:T(8,128)S(1)}, f32[2,8,8,256]{3,1,2,0:T(8,128)}, u32[]{:S(2)}) copy-start(f32[2,8,8,256]{3,1,2,0:T(8,128)} %copy.31) | copy-start | bytes 393220
  66.3 14.0 %all-to-all-start.2 = ((bf16[4,128,640]{2,1,0:T(8,128)(2,1)}), bf16[4,128,640]{2,1,0:T(8,128)(2,1)S(1)}, u32[]{:S(2)}, u32[]{:S(2)}) async-start(bf16[4,128,640]{2,1,0:T(8,128)(2,1)} %normalise.1), calls=%async_computation.2 | async-start | bytes 1310720 | tf_op jit(solution)/shard_map/all_to_all | solution.py:392
  69.8 27.1 %collective-permute-start.1 = (bf16[128,1024]{1,0:T(8,128)(2,1)S(1)}, bf16[128,1024]{1,0:T(8,128)(2,1)S(1)}, u32[]{:S(2)}, u32[]{:S(2)}) collective-permute-start(bf16[128,1024]{1,0:T(8,128)(2,1)S(1)} %pad_maximum_fusion.refs_4_.refs_5_), channel_id=1, source_target_pairs={{0,8},{8,16},{16,24},{1,9},{9,17},{17,25},{2,10},{10,18},{18,26},{... | collective-permute-start | bytes 786440 | tf_op jit(solution)/shard_map/ppermute | solution.py:388
  73.7 23.9 %collective-permute-start = (bf16[128,1024]{1,0:T(8,128)(2,1)S(1)}, bf16[128,1024]{1,0:T(8,128)(2,1)S(1)}, u32[]{:S(2)}, u32[]{:S(2)}) collective-permute-start(bf16[128,1024]{1,0:T(8,128)(2,1)S(1)} %pad_maximum_fusion.refs_4_.refs_5_), channel_id=1, source_target_pairs={{0,16},{8,24},{1,17},{9,25},{2,18},{10,26},{3,19},{11,27},{4,20},{... | collective-permute-start | bytes 786440 | tf_op jit(solution)/shard_map/ppermute | solution.py:388
  80.3 1.6 %copy-start.15 = (bf16[4096,256]{1,0:T(8,128)(2,1)S(1)}, bf16[4096,256]{1,0:T(8,128)(2,1)}, u32[]{:S(2)}) copy-start(bf16[4096,256]{1,0:T(8,128)(2,1)} %all-gather.7.cloned.1.call-done) | copy-start | bytes 6291460
  81.9 1.6 %copy-start.18 = (bf16[512,2048]{1,0:T(8,128)(2,1)S(1)}, bf16[512,2048]{1,0:T(8,128)(2,1)}, u32[]{:S(2)}) copy-start(bf16[512,2048]{1,0:T(8,128)(2,1)} %copy-done.17) | copy-start | bytes 6291460
  97.6 0.7 copy-start.10
  98.3 20.1 %all-to-all-start.3 = ((bf16[4,128,1024]{2,1,0:T(8,128)(2,1)}), bf16[4,128,1024]{2,1,0:T(8,128)(2,1)S(1)}, u32[]{:S(2)}, u32[]{:S(2)}) async-start(bf16[4,128,1024]{2,1,0:T(8,128)(2,1)} %state_scan_1.1), calls=%async_computation.3 | async-start | bytes 2097152 | tf_op jit(solution)/shard_map/all_to_all | solution.py:392
  101.8 1.6 %copy-start.16 = (bf16[4096,256]{1,0:T(8,128)(2,1)S(1)}, bf16[4096,256]{1,0:T(8,128)(2,1)}, u32[]{:S(2)}) copy-start(bf16[4096,256]{1,0:T(8,128)(2,1)} %all-gather.7.cloned.1.call-done) | copy-start | bytes 6291460
  103.4 1.6 %copy-start.19 = (bf16[512,2048]{1,0:T(8,128)(2,1)S(1)}, bf16[512,2048]{1,0:T(8,128)(2,1)}, u32[]{:S(2)}) copy-start(bf16[512,2048]{1,0:T(8,128)(2,1)} %copy-done.17) | copy-start | bytes 6291460
  118.3 1.0 copy-start.3
  119.3 13.7 %all-to-all-start.4 = ((bf16[4,128,1024]{2,1,0:T(8,128)(2,1)}), bf16[4,128,1024]{2,1,0:T(8,128)(2,1)}, u32[]{:S(2)}, u32[]{:S(2)}) async-start(bf16[4,128,1024]{2,1,0:T(8,128)(2,1)} %state_scan_0.1), calls=%async_computation.4 | async-start | bytes 2097152 | tf_op jit(solution)/shard_map/all_to_all | solution.py:392
  123.5 9.5 %copy-start.1 = (bf16[1,128,8192]{2,1,0:T(8,128)(2,1)S(1)}, bf16[1,128,8192]{2,1,0:T(8,128)(2,1)}, u32[]{:S(2)}) copy-start(bf16[1,128,8192]{2,1,0:T(8,128)(2,1)} %param.17) | copy-start | bytes 6291460
  123.7 1.4 copy-start.7
  125.0 0.9 copy-start.9
  126.0 0.9 copy-start.11
  133.0 3.7 %copy-start.4 = (bf16[4,128,1024]{2,1,0:T(8,128)(2,1)S(1)}, bf16[4,128,1024]{2,1,0:T(8,128)(2,1)}, u32[]{:S(2)}) copy-start(bf16[4,128,1024]{2,1,0:T(8,128)(2,1)} %copy-done.3) | copy-start | bytes 3145732
  (1 other events, 0.7 us)
Sparse Core Ops, SparseCore 0:
  9.7 32.8 all-gather.4
  44.2 28.5 all-gather.6

commit v5 on v4

--- a/solution.py
+++ b/solution.py
@@ -18,7 +18,8 @@
 
 
 def silu(value):
-    return 0.5 * value * (1.0 + jnp.tanh(0.5 * value))
+    half = 0.5 * value
+    return half + half * jnp.tanh(half)
 
 
 def attention_kernel(begin, seg_q_ref, seg_k_ref, q_ref, *refs):
@@ -76,7 +77,7 @@
         out_specs=wide,
         out_shape=jax.ShapeDtypeStruct(queries.shape, jnp.bfloat16),
         input_output_aliases=aliases,
-        compiler_params=pltpu.CompilerParams(vmem_limit_bytes=16 << 20),
+        compiler_params=pltpu.CompilerParams(vmem_limit_bytes=48 << 20),
         cost_estimate=pl.CostEstimate(
             flops=4 * rows * span * group_width * (end - begin),
             bytes_accessed=4 * rows * group_width * (end - begin),
@@ -137,22 +138,17 @@
         for piece in range(pieces):
             first = SUBLANES + piece * rows
             padded[tile, first : first + rows, :] = x_ref[piece, :, lanes].astype(jnp.float32)
-        running = jnp.broadcast_to(bias_ref[0:1, lanes], (toks, LANES))
+        half = jnp.broadcast_to(0.5 * bias_ref[0:1, lanes], (toks, LANES))
         for tap in range(4):
             moved = padded[tile, SUBLANES - 3 + tap : SUBLANES - 3 + tap + toks, :]
-            term = weight_ref[tap : tap + 1, lanes] * moved
-            running = running + (term * masks[tap] if tap < 3 else term)
-        conv = silu(running).astype(jnp.bfloat16)
+            term = (0.5 * weight_ref[tap : tap + 1, lanes]) * moved
+            half = half + (term * masks[tap] if tap < 3 else term)
+        conv = (half + half * jnp.tanh(half)).astype(jnp.bfloat16)
         conv_ref[:, lanes] = conv
         outs.append(conv)
-    per_slot = width // LANES
-    added = total[...]
-    for slot in range(slots):
-        conv = jnp.concatenate(outs[slot * per_slot : (slot + 1) * per_slot], axis=1) if per_slot > 1 else outs[slot]
-        added = added + lax.dot_general(
-            conv, select_ref[slot], (((1,), (1,)), ((), ())), preferred_element_type=jnp.float32
-        )
-    total[...] = added
+    conv = jnp.concatenate(outs, axis=1)
+    select = jnp.concatenate([select_ref[slot] for slot in range(slots)], axis=1)
+    total[...] += lax.dot_general(conv, select, (((1,), (1,)), ((), ())), preferred_element_type=jnp.float32)
 
     @pl.when(step == pl.num_programs(0) - 1)
     def _():
@@ -167,7 +163,7 @@
     ctx, rows, _ = pieces.shape
     toks = ctx * rows
     padded_outputs = -(-outputs // LANES) * LANES
-    batch = 2
+    batch = 4
     wide = batch * width
     return pl.pallas_call(
         conv_select_kernel,
@@ -192,7 +188,7 @@
             jax.ShapeDtypeStruct((toks, slots * width), jnp.bfloat16),
             jax.ShapeDtypeStruct((ctx, rows, padded_outputs), jnp.bfloat16),
         ],
-        compiler_params=pltpu.CompilerParams(vmem_limit_bytes=20 << 20),
+        compiler_params=pltpu.CompilerParams(vmem_limit_bytes=32 << 20),
         cost_estimate=pl.CostEstimate(
             flops=2 * toks * slots * width * outputs,
             bytes_accessed=2 * pieces.size * 2 + 2 * select_parts.size,
@@ -226,7 +222,7 @@
 
 
 def scan_kernel(rank, reset_ref, low_ref, weight_ref, bias_ref, decay_ref, gain_ref, conv_ref, out_ref,
-                in_cols, out_diag, delta_rows, drive_rows, held_even, held_odd):
+                in_cols, out_diag, delta_rows, drive_rows, held_even, held_odd, into_even, into_odd):
     toks = reset_ref.shape[0]
     states = decay_ref.shape[0]
     shards = weight_ref.shape[0]
@@ -263,7 +259,8 @@
             )
             delta = (jnp.maximum(value, 0.0) + log_part).astype(jnp.bfloat16).astype(jnp.float32)
             delta_rows[:, tile] = (delta + reset).reshape(count, block, LANES)
-            drive_rows[:, tile] = (delta * conv_ref[:, lanes].astype(jnp.float32)).reshape(count, block, LANES)
+            drive = delta * conv_ref[:, lanes].astype(jnp.float32)
+            drive_rows[:, :, lanes] = drive.astype(jnp.bfloat16).reshape(toks // LANES, LANES, LANES)
 
     rates = [-LOG2E * jnp.exp(decay_ref[:, tile * LANES : (tile + 1) * LANES]) for tile in range(tiles)]
 
@@ -278,29 +275,48 @@
         place = pl.multiple_of(lax.rem(first, rows), block)
         out_ref[lax.div(first, rows), pl.ds(place, block), lanes] = full.astype(out_ref.dtype)
 
-    def advance(index, held, history, before, before_history):
+    lane_index = lax.broadcasted_iota(jnp.int32, (states, LANES), 1)
+    per_row = LANES // block
+
+    def one_hot(index):
+        columns = in_cols[:, pl.ds(pl.multiple_of(lax.div(index, per_row) * LANES, LANES), LANES)]
+        first = lax.rem(index, per_row) * block
+        return jnp.concatenate(
+            [jnp.where(lane_index == first + inner, columns, 0.0).astype(jnp.bfloat16) for inner in range(block)], axis=0
+        )
+
+    def inject(index, hot, into, part):
+        lanes = slice(part * quarter, (part + 1) * quarter)
+        drive = drive_rows[lax.div(index, per_row), :, lanes]
+        into[:, lanes] = jnp.dot(hot, drive, preferred_element_type=jnp.float32)
+
+    def advance(index, held, history, into, before, before_history, after, after_into):
         held = list(held)
-        per_row = LANES // block
-        columns = in_cols[:, pl.ds(pl.multiple_of(lax.div(index, per_row) * LANES, LANES), LANES)]
-        columns = pltpu.roll(columns, lax.rem(LANES - lax.rem(index, per_row) * block, LANES), 1)
         delta_now = delta_rows.at[index]
-        drive_now = drive_rows.at[index]
+        hot = one_hot(after)
+        stride = block // quarters
         for inner in range(block):
-            into = jnp.broadcast_to(columns[:, inner : inner + 1], (states, LANES))
+            at = slice(inner * states, (inner + 1) * states)
             for tile in range(tiles):
                 lanes = slice(tile * LANES, (tile + 1) * LANES)
                 grow = jnp.exp2(delta_now[tile, inner : inner + 1, :] * rates[tile])
-                held[tile] = grow * held[tile] + into * drive_now[tile, inner : inner + 1, :]
-                history[inner * states : (inner + 1) * states, lanes] = held[tile].astype(jnp.bfloat16)
-            if inner % (block // quarters) == 0:
-                finish(before, before_history, inner // (block // quarters))
+                held[tile] = grow * held[tile] + into[at, lanes]
+                history[at, lanes] = held[tile].astype(jnp.bfloat16)
+            if inner % stride == 0:
+                finish(before, before_history, inner // stride)
+            if inner % stride == stride // 2:
+                inject(after, hot, after_into, inner // stride)
         return tuple(held)
 
     held_odd[...] = jnp.zeros_like(held_odd)
+    first_hot = one_hot(0)
+    for part in range(quarters):
+        inject(0, first_hot, into_even, part)
 
     def pair(index, held):
-        held = advance(2 * index, held, held_even, jnp.maximum(2 * index - 1, 0), held_odd)
-        return advance(2 * index + 1, held, held_odd, 2 * index, held_even)
+        even, odd = 2 * index, 2 * index + 1
+        held = advance(even, held, held_even, into_even, jnp.maximum(even - 1, 0), held_odd, odd, into_odd)
+        return advance(odd, held, held_odd, into_odd, even, held_even, jnp.minimum(odd + 1, count - 1), into_even)
 
     start = tuple(jnp.zeros((states, LANES), jnp.float32) for _ in range(tiles))
     lax.fori_loop(0, count // 2, pair, start)
@@ -334,11 +350,13 @@
             pltpu.VMEM((states, toks), jnp.float32),
             pltpu.VMEM((toks, 16 * states), jnp.bfloat16),
             pltpu.VMEM((toks // 16, wide // LANES, 16, LANES), jnp.float32),
-            pltpu.VMEM((toks // 16, wide // LANES, 16, LANES), jnp.float32),
+            pltpu.VMEM((toks // LANES, LANES, wide), jnp.bfloat16),
             pltpu.VMEM((16 * states, wide), jnp.bfloat16),
             pltpu.VMEM((16 * states, wide), jnp.bfloat16),
+            pltpu.VMEM((16 * states, wide), jnp.float32),
+            pltpu.VMEM((16 * states, wide), jnp.float32),
         ],
-        compiler_params=pltpu.CompilerParams(vmem_limit_bytes=24 << 20),
+        compiler_params=pltpu.CompilerParams(vmem_limit_bytes=60 << 20),
         cost_estimate=pl.CostEstimate(
             flops=6 * steps, bytes_accessed=2 * delta_parts.size // calls + 4 * toks * wide, transcendentals=steps
         ),
@@ -458,22 +476,23 @@
     bias, decay, gain, reset_col, seg_q, seg_k, both = own
 
     conv, parts = conv_select(seg_col, pieces, own_part(conv_weight), own_part(conv_bias)[None, :], select_parts)
+
+    parts, both = lax.optimization_barrier((parts, both))
+    blocks = [shifted(both, "ctx", by) for by in range(back, 0, -1)] + [both]
     low = normalise(exchange(parts), rank)
-
-    low, both = lax.optimization_barrier((low, both))
-    blocks = [shifted(both, "ctx", by) for by in range(back, 0, -1)] + [both]
-    low = exchange(low).reshape(toks, low.shape[2])
+    low, blocks = lax.optimization_barrier((low, blocks))
+    attended = attention(queries[0], blocks, seg_q, seg_k, 0, KEY_VALUE_HEADS)
+    low, attended = lax.optimization_barrier((exchange(low), attended))
+    low = low.reshape(toks, low.shape[2])
 
     calls = 2
     scanned = []
     for call in range(calls):
-        scanned.append(state_scan(reset_col, low, delta_parts, bias, decay, gain, conv, ctx, call, calls))
-    scanned[-1], blocks = lax.optimization_barrier((scanned[-1], blocks))
-    attended = attention(queries[0], blocks, seg_q, seg_k, 0, KEY_VALUE_HEADS)
-    scanned = [exchange(part) for part in scanned]
-    scanned[-1], attended = lax.optimization_barrier((scanned[-1], attended))
+        scanned.append(exchange(state_scan(reset_col, low, delta_parts, bias, decay, gain, conv, ctx, call, calls)))
     mixed = None
     for call in range(calls):
+        if mixed is not None:
+            scanned[call], mixed = lax.optimization_barrier((scanned[call], mixed))
         mixed = apply_gate(scanned[call], gate_input[0], fold, width, call, mixed)
     return (attended[None], mixed[None])
 

time: 147 us -> 160 us (1.088)
  waiting for transfers between devices: 16.9 us -> 36.8 us
  blocking collectives: 12 us -> 0 us
  local copies, waits for them, and re-layouts: 32.3 us -> 20.9 us
  Pallas kernels: 43.3 us -> 54.1 us
  starting transfers between devices: 23.9 us -> 29.8 us
    all_to_all x4 -> x5, waiting for transfers between devices: 16.9 us -> 30.7 us  [exchange(): return lax.all_to_all(value, 'ctx', 0, 0, tiled=True)]
    all_to_all x1 -> x0, blocking collectives: 12 us -> none  [exchange(): return lax.all_to_all(value, 'ctx', 0, 0, tiled=True)]
    unnamed x52 -> x30, local copies, waits for them, and re-layouts: 20.7 us -> 9.57 us
    pallas_call x2, Pallas kernels: 26.7 us -> 35.9 us  [state_scan(): pl.pallas_call(functools.partial(scan_kernel, rank), grid=(1,), in_specs=...]
    ppermute x2, waiting for transfers between devices: 0.01 us -> 6.04 us  [shifted(): return lax.ppermute(value, axis, pairs)]
    all_to_all x4 -> x5, starting transfers between devices: 16.6 us -> 21.7 us  [exchange(): return lax.all_to_all(value, 'ctx', 0, 0, tiled=True)]
  transfers between devices with their start and end apart: 8 -> 9, of which waited for: 3 -> 6; matrix products, arithmetic and copies ran while one was open for 10% -> 9% of each run, Pallas kernels for 26% -> 21%
where the time goes in v5:
time: 160 us; the launch traced here: 159 us
  Pallas kernels  54.1 us (34%)
  waiting for transfers between devices  36.8 us (23%)
  starting transfers between devices  29.8 us (19%)
  local copies, waits for them, and re-layouts  20.9 us (13%)
  between operations  14.2 us (9%)
  other arithmetic  2.74 us (2%)
    pallas_call x2, Pallas kernels, state_scan(): pl.pallas_call(functools.partial(scan_kernel, rank), grid=(1,), in_specs=...  35.9 us
    all_to_all x5, waiting for transfers between devices, exchange(): return lax.all_to_all(value, 'ctx', 0, 0, tiled=True)  30.7 us
    all_to_all x5, starting transfers between devices, exchange(): return lax.all_to_all(value, 'ctx', 0, 0, tiled=True)  21.7 us
    unnamed x30, local copies, waits for them, and re-layouts  9.57 us
    ppermute x2, starting transfers between devices, shifted(): return lax.ppermute(value, axis, pairs)  7.98 us
    pallas_call x2, Pallas kernels, apply_gate(): pl.pallas_call(functools.partial(gate_kernel, fold, width), grid=(rows //...  7.19 us
    ppermute x2, waiting for transfers between devices, shifted(): return lax.ppermute(value, axis, pairs)  6.04 us
    pallas_call x1, Pallas kernels, attention(): pl.pallas_call(functools.partial(attention_kernel, begin), grid=(end - be...  5.4 us
  transfers between devices with their start and end apart: 9, of which 6 were waited for; matrix products, arithmetic and copies ran while one was open for 9% of the time, Pallas kernels for 21%

profile of v5, /device:TPU:0, one launch (start us, length us, event | category | flops | bytes accessed | tf_op | source)
XLA Modules:
  0.0 158.6 jit_solution(6836250831032060636)
XLA Ops:
  7.2 1.2 copy-done
  9.3 1.6 copy-done.4
  11.2 1.3 copy-done.2
  12.5 1.7 %constant_dynamic-slice_fusion = bf16[512,256]{1,0:T(8,128)(2,1)} fusion(bf16[512,1024]{1,0:T(8,128)(2,1)} %param.22, s32[]{:T(128)S(6)} %select_n.60), kind=kLoop, calls=%fused_computation.7 | loop fusion | bytes 524292 | tf_op jit(solution)/shard_map/dynamic_slice | solution.py:450
  14.3 5.3 %all-to-all-start = ((bf16[4,128,2048]{2,1,0:T(8,128)(2,1)}), bf16[4,128,2048]{2,1,0:T(8,128)(2,1)S(1)}, u32[]{:S(2)}, u32[]{:S(2)}) async-start(bf16[4,128,2048]{2,1,0:T(8,128)(2,1)} %copy-done.2), calls=%async_computation | async-start | bytes 4194304 | tf_op jit(solution)/shard_map/all_to_all | solution.py:410
  22.1 0.9 copy.27.seg_ref
  23.0 2.2 %reshape.75 = f32[16,8,1,4,256]{4,3,1,0,2:T(4,128)} reshape(f32[16,8192]{1,0:T(8,128)} %bitcast.33) | data formatting | bytes 1048576 | tf_op jit(solution)/shard_map/reshape | solution.py:444
  25.2 1.4 dynamic-slice_reduce_fusion
  27.9 1.4 constant_dynamic-slice_fusion.2
  29.3 1.0 pad_maximum_fusion.refs_4_.refs_5_
  30.3 1.6 %broadcast_select_fusion.reset_ref = f32[512,1]{1,0:T(8,128)} fusion(pred[512,1]{1,0:T(8,128)(4,1)} %copy.25), kind=kLoop, calls=%fused_computation.1 | loop fusion | flops 512 | bytes 2560 | tf_op jit(solution)/shard_map/jit(_where)/select_n | solution.py:463
  31.9 12.6 %all-to-all-done.x_ref = bf16[4,128,2048]{2,1,0:T(8,128)(2,1)S(1)} async-done(((bf16[4,128,2048]{2,1,0:T(8,128)(2,1)}), bf16[4,128,2048]{2,1,0:T(8,128)(2,1)S(1)}, u32[]{:S(2)}, u32[]{:S(2)}) %all-to-all-start) | async-done | bytes 2097184 | tf_op jit(solution)/shard_map/all_to_all | solution.py:410
  44.5 1.6 %copy-done.3 = bf16[4352,256]{1,0:T(8,128)(2,1)S(1)} copy-done((bf16[4352,256]{1,0:T(8,128)(2,1)S(1)}, bf16[4352,256]{1,0:T(8,128)(2,1)}, u32[]{:S(2)}) %copy-start.3) | copy-done | bytes 2228248
  46.1 0.9 copy-done.6
  47.0 4.3 %conv_select.1 = (bf16[512,2048]{1,0:T(8,128)(2,1)S(1)}, bf16[4,128,640]{2,1,0:T(8,128)(2,1)S(1)}) custom-call(s32[512,1]{1,0:T(8,128)S(1)} %copy-done.6, bf16[4,128,2048]{2,1,0:T(8,128)(2,1)S(1)} %all-to-all-done.x_ref, f32[4,2048]{1,0:T(4,128)S(1)} %bitcast.29, f32[1,2048]{1,0:T(1,128)S(1)} %bitcast.30, bf16[8,544,256]{2,1,0:T(8,128)(2,1)S(1)} %bitcast.26), custom_call_target="tpu_custom_call" | custom-call | flops 1140850688 | bytes 6422528 | tf_op jit(solution)/shard_map/conv_select/pallas_call | solution.py:168
  52.2 1.3 copy-done.8
  53.5 3.6 %all-to-all-start.1 = ((bf16[4,128,640]{2,1,0:T(8,128)(2,1)}), bf16[4,128,640]{2,1,0:T(8,128)(2,1)S(1)}, u32[]{:S(2)}, u32[]{:S(2)}) async-start(bf16[4,128,640]{2,1,0:T(8,128)(2,1)} %copy-done.7), calls=%async_computation.1 | async-start | bytes 1310720 | tf_op jit(solution)/shard_map/all_to_all | solution.py:410
  57.1 3.9 %collective-permute-start.1 = (bf16[128,1024]{1,0:T(8,128)(2,1)S(1)}, bf16[128,1024]{1,0:T(8,128)(2,1)S(1)}, u32[]{:S(2)}, u32[]{:S(2)}) collective-permute-start(bf16[128,1024]{1,0:T(8,128)(2,1)S(1)} %pad_maximum_fusion.refs_4_.refs_5_), channel_id=1, source_target_pairs={{0,8},{8,16},{16,24},{1,9},{9,17},{17,25},{2,10},{10,18},{18,26},{... | collective-permute-start | bytes 786440 | tf_op jit(solution)/shard_map/ppermute | solution.py:406
  61.0 4.1 %collective-permute-start = (bf16[128,1024]{1,0:T(8,128)(2,1)S(1)}, bf16[128,1024]{1,0:T(8,128)(2,1)}, u32[]{:S(2)}, u32[]{:S(2)}) collective-permute-start(bf16[128,1024]{1,0:T(8,128)(2,1)S(1)} %pad_maximum_fusion.refs_4_.refs_5_), channel_id=1, source_target_pairs={{0,16},{8,24},{1,17},{9,25},{2,18},{10,26},{3,19},{11,27},{4,20},{... | collective-permute-start | bytes 786440 | tf_op jit(solution)/shard_map/ppermute | solution.py:406
  65.1 2.8 %all-to-all-done.1.part_ref = bf16[4,128,640]{2,1,0:T(8,128)(2,1)S(1)} async-done(((bf16[4,128,640]{2,1,0:T(8,128)(2,1)}), bf16[4,128,640]{2,1,0:T(8,128)(2,1)S(1)}, u32[]{:S(2)}, u32[]{:S(2)}) %all-to-all-start.1) | async-done | bytes 655392 | tf_op jit(solution)/shard_map/all_to_all | solution.py:410
  67.9 1.0 normalise.1
  69.4 5.6 %collective-permute-done.refs_0_.refs_1_ = bf16[128,1024]{1,0:T(8,128)(2,1)} collective-permute-done((bf16[128,1024]{1,0:T(8,128)(2,1)S(1)}, bf16[128,1024]{1,0:T(8,128)(2,1)}, u32[]{:S(2)}, u32[]{:S(2)}) %collective-permute-start) | collective-permute-done | bytes 262176 | tf_op jit(solution)/shard_map/ppermute | solution.py:406
  75.0 4.2 %all-to-all-start.2 = ((bf16[4,128,640]{2,1,0:T(8,128)(2,1)}), bf16[4,128,640]{2,1,0:T(8,128)(2,1)}, u32[]{:S(2)}, u32[]{:S(2)}) async-start(bf16[4,128,640]{2,1,0:T(8,128)(2,1)} %normalise.1), calls=%async_computation.2 | async-start | bytes 1310720 | tf_op jit(solution)/shard_map/all_to_all | solution.py:410
  79.3 5.4 %attention_0.1 = bf16[128,4096]{1,0:T(8,128)(2,1)} custom-call(s32[128,1]{1,0:T(8,128)S(1)} %copy.28.seg_q_ref, s32[1,384]{1,0:T(1,128)S(1)} %broadcast_in_dim.25.seg_k_ref, bf16[128,4096]{1,0:T(8,128)(2,1)S(1)} %bitcast.28, bf16[128,1024]{1,0:T(8,128)(2,1)} %collective-permute-done.refs_0_.refs_1_, bf16[128,1024]{1,0:T(8,128)(2,1)} %collective-permute-done.refs_0_.refs_1_, ...), custom_call_target="tpu_custom_call" | custom-call | flops 805306368 | bytes 2097152 | tf_op jit(solution)/shard_map/attention_0/pallas_call | solution.py:73
  84.7 4.8 %all-to-all-done.2 = bf16[4,128,640]{2,1,0:T(8,128)(2,1)} async-done(((bf16[4,128,640]{2,1,0:T(8,128)(2,1)}), bf16[4,128,640]{2,1,0:T(8,128)(2,1)}, u32[]{:S(2)}, u32[]{:S(2)}) %all-to-all-start.2) | async-done | bytes 655392 | tf_op jit(solution)/shard_map/all_to_all | solution.py:410
  89.5 18.0 %state_scan_0.1 = bf16[4,128,1024]{2,1,0:T(8,128)(2,1)} custom-call(f32[512,1]{1,0:T(8,128)} %broadcast_select_fusion.reset_ref, bf16[512,640]{1,0:T(8,128)(2,1)} %bitcast.14.low_ref, bf16[8,512,256]{2,1,0:T(8,128)(2,1)} %bitcast.46, f32[1,2048]{1,0:T(1,128)} %bitcast.42, f32[16,2048]{1,0:T(8,128)} %bitcast.35, f32[1,2048]{1,0:T(1,128)} %bitcast.44, ...), custom_call_target="tpu_custom_call" | custom-call | flops 50331648 | bytes 3145728 | tf_op jit(solution)/shard_map/state_scan_0/pallas_call | solution.py:335
  107.5 4.3 %all-to-all-start.4 = ((bf16[4,128,1024]{2,1,0:T(8,128)(2,1)}), bf16[4,128,1024]{2,1,0:T(8,128)(2,1)}, u32[]{:S(2)}, u32[]{:S(2)}) async-start(bf16[4,128,1024]{2,1,0:T(8,128)(2,1)} %state_scan_0.1), calls=%async_computation.4 | async-start | bytes 2097152 | tf_op jit(solution)/shard_map/all_to_all | solution.py:410
  111.8 17.9 %state_scan_1.1 = bf16[4,128,1024]{2,1,0:T(8,128)(2,1)} custom-call(f32[512,1]{1,0:T(8,128)} %broadcast_select_fusion.reset_ref, bf16[512,640]{1,0:T(8,128)(2,1)} %bitcast.14.low_ref, bf16[8,512,256]{2,1,0:T(8,128)(2,1)} %bitcast.47, f32[1,2048]{1,0:T(1,128)} %bitcast.43, f32[16,2048]{1,0:T(8,128)} %bitcast.36, f32[1,2048]{1,0:T(1,128)} %bitcast.45, ...), custom_call_target="tpu_custom_call" | custom-call | flops 50331648 | bytes 3145728 | tf_op jit(solution)/shard_map/state_scan_1/pallas_call | solution.py:335
  129.7 4.4 %all-to-all-start.3 = ((bf16[4,128,1024]{2,1,0:T(8,128)(2,1)}), bf16[4,128,1024]{2,1,0:T(8,128)(2,1)}, u32[]{:S(2)}, u32[]{:S(2)}) async-start(bf16[4,128,1024]{2,1,0:T(8,128)(2,1)} %state_scan_1.1), calls=%async_computation.3 | async-start | bytes 2097152 | tf_op jit(solution)/shard_map/all_to_all | solution.py:410
  134.1 3.6 %gate_0.1.refs_0_ = bf16[128,8192]{1,0:T(8,128)(2,1)} custom-call(bf16[4,128,1024]{2,1,0:T(8,128)(2,1)} %all-to-all-done.4.y_ref, bf16[128,8192]{1,0:T(8,128)(2,1)S(1)} %bitcast.24), custom_call_target="tpu_custom_call" | custom-call | flops 2097152 | bytes 3145728 | tf_op jit(solution)/shard_map/gate_0/pallas_call | solution.py:388
  137.7 10.5 %all-to-all-done.3.y_ref = bf16[4,128,1024]{2,1,0:T(8,128)(2,1)} async-done(((bf16[4,128,1024]{2,1,0:T(8,128)(2,1)}), bf16[4,128,1024]{2,1,0:T(8,128)(2,1)}, u32[]{:S(2)}, u32[]{:S(2)}) %all-to-all-start.3) | async-done | bytes 1048608 | tf_op jit(solution)/shard_map/all_to_all | solution.py:410
  148.2 3.6 %gate_1.1 = bf16[128,8192]{1,0:T(8,128)(2,1)} custom-call(bf16[4,128,1024]{2,1,0:T(8,128)(2,1)} %all-to-all-done.3.y_ref, bf16[128,8192]{1,0:T(8,128)(2,1)S(1)} %bitcast.25, bf16[128,8192]{1,0:T(8,128)(2,1)} %gate_0.1.refs_0_), custom_call_target="tpu_custom_call", output_to_operand_aliasing={{}: (2, {})} | custom-call | flops 2097152 | bytes 3145728 | tf_op jit(solution)/shard_map/gate_1/pallas_call | solution.py:388
  (47 shorter events, 6.4 us)
Async XLA Ops:
  7.2 1.3 copy-start
  7.2 37.3 %all-gather.5.cloned.1.call-start = ((), (), s32[]{:S(2)}) async-start(), calls=%async_computation.5 | async-start | bytes 2506752 | tf_op jit(solution)/shard_map/all_gather | solution.py:451
  9.2 80.3 %all-gather.7.cloned.1.call-start = ((), (), s32[]{:S(2)}) async-start(), calls=%async_computation.6 | async-start | bytes 2359296 | tf_op jit(solution)/shard_map/all_gather | solution.py:451
  9.2 1.6 %copy-start.4 = (bf16[1,128,8192]{2,1,0:T(8,128)(2,1)S(1)}, bf16[1,128,8192]{2,1,0:T(8,128)(2,1)}, u32[]{:S(2)}) copy-start(bf16[1,128,8192]{2,1,0:T(8,128)(2,1)} %param.16) | copy-start | bytes 6291460
  11.2 1.3 copy-start.2
  14.2 5.4 %copy-start.10 = (s32[1,512]{1,0:T(1,128)S(1)}, s32[1,512]{1,0:T(1,128)}, u32[]{:S(2)}) copy-start(s32[1,512]{1,0:T(1,128)} %param.18) | copy-start | bytes 6148
  14.2 5.4 %copy-start.11 = (f32[8192]{0:T(1024)S(1)}, f32[8192]{0:T(1024)}, u32[]{:S(2)}) copy-start(f32[8192]{0:T(1024)} %param.20) | copy-start | bytes 98308
  14.2 6.1 %copy-start.12 = (f32[8192]{0:T(1024)S(1)}, f32[8192]{0:T(1024)}, u32[]{:S(2)}) copy-start(f32[8192]{0:T(1024)} %param.23) | copy-start | bytes 98308
  14.2 6.1 %copy-start.13 = (f32[8192]{0:T(1024)S(1)}, f32[8192]{0:T(1024)}, u32[]{:S(2)}) copy-start(f32[8192]{0:T(1024)} %param.25) | copy-start | bytes 98308
  14.3 7.6 %copy-start.9 = (f32[4,8192]{1,0:T(4,128)S(1)}, f32[4,8192]{1,0:T(4,128)}, u32[]{:S(2)}) copy-start(f32[4,8192]{1,0:T(4,128)} %param.19) | copy-start | bytes 393220
  14.3 30.2 %all-to-all-start = ((bf16[4,128,2048]{2,1,0:T(8,128)(2,1)}), bf16[4,128,2048]{2,1,0:T(8,128)(2,1)S(1)}, u32[]{:S(2)}, u32[]{:S(2)}) async-start(bf16[4,128,2048]{2,1,0:T(8,128)(2,1)} %copy-done.2), calls=%async_computation | async-start | bytes 4194304 | tf_op jit(solution)/shard_map/all_to_all | solution.py:410
  44.4 1.6 %copy-start.3 = (bf16[4352,256]{1,0:T(8,128)(2,1)S(1)}, bf16[4352,256]{1,0:T(8,128)(2,1)}, u32[]{:S(2)}) copy-start(bf16[4352,256]{1,0:T(8,128)(2,1)} %all-gather.5.cloned.1.call-done) | copy-start | bytes 6684676
  46.1 0.9 copy-start.6
  51.3 0.8 copy-start.7
  52.2 1.3 copy-start.8
  53.5 25.8 %copy-start.5 = (bf16[1,128,4096]{2,1,0:T(8,128)(2,1)S(1)}, bf16[1,128,4096]{2,1,0:T(8,128)(2,1)}, u32[]{:S(2)}) copy-start(bf16[1,128,4096]{2,1,0:T(8,128)(2,1)} %param.13) | copy-start | bytes 3145732
  53.5 14.4 %all-to-all-start.1 = ((bf16[4,128,640]{2,1,0:T(8,128)(2,1)}), bf16[4,128,640]{2,1,0:T(8,128)(2,1)S(1)}, u32[]{:S(2)}, u32[]{:S(2)}) async-start(bf16[4,128,640]{2,1,0:T(8,128)(2,1)} %copy-done.7), calls=%async_computation.1 | async-start | bytes 1310720 | tf_op jit(solution)/shard_map/all_to_all | solution.py:410
  57.1 12.2 %collective-permute-start.1 = (bf16[128,1024]{1,0:T(8,128)(2,1)S(1)}, bf16[128,1024]{1,0:T(8,128)(2,1)S(1)}, u32[]{:S(2)}, u32[]{:S(2)}) collective-permute-start(bf16[128,1024]{1,0:T(8,128)(2,1)S(1)} %pad_maximum_fusion.refs_4_.refs_5_), channel_id=1, source_target_pairs={{0,8},{8,16},{16,24},{1,9},{9,17},{17,25},{2,10},{10,18},{18,26},{... | collective-permute-start | bytes 786440 | tf_op jit(solution)/shard_map/ppermute | solution.py:406
  61.0 14.0 %collective-permute-start = (bf16[128,1024]{1,0:T(8,128)(2,1)S(1)}, bf16[128,1024]{1,0:T(8,128)(2,1)}, u32[]{:S(2)}, u32[]{:S(2)}) collective-permute-start(bf16[128,1024]{1,0:T(8,128)(2,1)S(1)} %pad_maximum_fusion.refs_4_.refs_5_), channel_id=1, source_target_pairs={{0,16},{8,24},{1,17},{9,25},{2,18},{10,26},{3,19},{11,27},{4,20},{... | collective-permute-start | bytes 786440 | tf_op jit(solution)/shard_map/ppermute | solution.py:406
  75.0 14.5 %all-to-all-start.2 = ((bf16[4,128,640]{2,1,0:T(8,128)(2,1)}), bf16[4,128,640]{2,1,0:T(8,128)(2,1)}, u32[]{:S(2)}, u32[]{:S(2)}) async-start(bf16[4,128,640]{2,1,0:T(8,128)(2,1)} %normalise.1), calls=%async_computation.2 | async-start | bytes 1310720 | tf_op jit(solution)/shard_map/all_to_all | solution.py:410
  107.5 22.2 %all-to-all-start.4 = ((bf16[4,128,1024]{2,1,0:T(8,128)(2,1)}), bf16[4,128,1024]{2,1,0:T(8,128)(2,1)}, u32[]{:S(2)}, u32[]{:S(2)}) async-start(bf16[4,128,1024]{2,1,0:T(8,128)(2,1)} %state_scan_0.1), calls=%async_computation.4 | async-start | bytes 2097152 | tf_op jit(solution)/shard_map/all_to_all | solution.py:410
  129.7 4.4 %copy-start.1 = (bf16[1,128,8192]{2,1,0:T(8,128)(2,1)S(1)}, bf16[1,128,8192]{2,1,0:T(8,128)(2,1)}, u32[]{:S(2)}) copy-start(bf16[1,128,8192]{2,1,0:T(8,128)(2,1)} %param.17) | copy-start | bytes 6291460
  129.7 18.5 %all-to-all-start.3 = ((bf16[4,128,1024]{2,1,0:T(8,128)(2,1)}), bf16[4,128,1024]{2,1,0:T(8,128)(2,1)}, u32[]{:S(2)}, u32[]{:S(2)}) async-start(bf16[4,128,1024]{2,1,0:T(8,128)(2,1)} %state_scan_1.1), calls=%async_computation.3 | async-start | bytes 2097152 | tf_op jit(solution)/shard_map/all_to_all | solution.py:410
Sparse Core Ops, SparseCore 0:
  9.7 32.8 all-gather.4
  44.2 28.5 all-gather.6

commit v6 on v4

--- a/solution.py
+++ b/solution.py
@@ -18,7 +18,8 @@
 
 
 def silu(value):
-    return 0.5 * value * (1.0 + jnp.tanh(0.5 * value))
+    half = 0.5 * value
+    return half + half * jnp.tanh(half)
 
 
 def attention_kernel(begin, seg_q_ref, seg_k_ref, q_ref, *refs):
@@ -137,22 +138,17 @@
         for piece in range(pieces):
             first = SUBLANES + piece * rows
             padded[tile, first : first + rows, :] = x_ref[piece, :, lanes].astype(jnp.float32)
-        running = jnp.broadcast_to(bias_ref[0:1, lanes], (toks, LANES))
+        half = jnp.broadcast_to(0.5 * bias_ref[0:1, lanes], (toks, LANES))
         for tap in range(4):
             moved = padded[tile, SUBLANES - 3 + tap : SUBLANES - 3 + tap + toks, :]
-            term = weight_ref[tap : tap + 1, lanes] * moved
-            running = running + (term * masks[tap] if tap < 3 else term)
-        conv = silu(running).astype(jnp.bfloat16)
+            term = (0.5 * weight_ref[tap : tap + 1, lanes]) * moved
+            half = half + (term * masks[tap] if tap < 3 else term)
+        conv = (half + half * jnp.tanh(half)).astype(jnp.bfloat16)
         conv_ref[:, lanes] = conv
         outs.append(conv)
-    per_slot = width // LANES
-    added = total[...]
-    for slot in range(slots):
-        conv = jnp.concatenate(outs[slot * per_slot : (slot + 1) * per_slot], axis=1) if per_slot > 1 else outs[slot]
-        added = added + lax.dot_general(
-            conv, select_ref[slot], (((1,), (1,)), ((), ())), preferred_element_type=jnp.float32
-        )
-    total[...] = added
+    conv = jnp.concatenate(outs, axis=1)
+    select = jnp.concatenate([select_ref[slot] for slot in range(slots)], axis=1)
+    total[...] += lax.dot_general(conv, select, (((1,), (1,)), ((), ())), preferred_element_type=jnp.float32)
 
     @pl.when(step == pl.num_programs(0) - 1)
     def _():
@@ -167,7 +163,7 @@
     ctx, rows, _ = pieces.shape
     toks = ctx * rows
     padded_outputs = -(-outputs // LANES) * LANES
-    batch = 2
+    batch = 4
     wide = batch * width
     return pl.pallas_call(
         conv_select_kernel,
@@ -192,7 +188,7 @@
             jax.ShapeDtypeStruct((toks, slots * width), jnp.bfloat16),
             jax.ShapeDtypeStruct((ctx, rows, padded_outputs), jnp.bfloat16),
         ],
-        compiler_params=pltpu.CompilerParams(vmem_limit_bytes=20 << 20),
+        compiler_params=pltpu.CompilerParams(vmem_limit_bytes=32 << 20),
         cost_estimate=pl.CostEstimate(
             flops=2 * toks * slots * width * outputs,
             bytes_accessed=2 * pieces.size * 2 + 2 * select_parts.size,
@@ -225,13 +221,18 @@
     )(parts)
 
 
-def scan_kernel(rank, reset_ref, low_ref, weight_ref, bias_ref, decay_ref, gain_ref, conv_ref, out_ref,
-                in_cols, out_diag, delta_rows, drive_rows, held_even, held_odd):
+def scan_kernel(rank, first_shard, reset_ref, low_ref, weight_hbm, bias_ref, decay_ref, gain_ref, conv_hbm, out_ref,
+                weight_ref, conv_ref, sems, in_cols, out_diag, delta_rows, drive_rows, held_even, held_odd):
     toks = reset_ref.shape[0]
     states = decay_ref.shape[0]
     shards = weight_ref.shape[0]
     width = weight_ref.shape[2]
     tiles = shards * width // LANES
+    column = first_shard * width
+    weight_copy = pltpu.make_async_copy(weight_hbm.at[pl.ds(first_shard, shards)], weight_ref, sems.at[0])
+    conv_copy = pltpu.make_async_copy(conv_hbm.at[:, pl.ds(column, shards * width)], conv_ref, sems.at[1])
+    weight_copy.start()
+    conv_copy.start()
     rows = out_ref.shape[1]
     block = 16
     span = block * states
@@ -249,12 +250,15 @@
 
     reset = jnp.broadcast_to(reset_ref[...], (toks, LANES))
     low = low_ref[:, 0:rank]
+    weight_copy.wait()
+    conv_copy.wait()
     for shard in range(shards):
         pre = jnp.dot(low, weight_ref[shard], preferred_element_type=jnp.float32)
         for part in range(width // LANES):
             tile = shard * (width // LANES) + part
             lanes = slice(tile * LANES, (tile + 1) * LANES)
-            value = pre[:, part * LANES : (part + 1) * LANES] + bias_ref[:, lanes]
+            value = pre[:, part * LANES : (part + 1) * LANES]
+            value = value + bias_ref[:, column + tile * LANES : column + (tile + 1) * LANES]
             raised = jnp.exp(-jnp.abs(value))
             log_part = jnp.where(
                 raised < 0.01,
@@ -265,16 +269,20 @@
             delta_rows[:, tile] = (delta + reset).reshape(count, block, LANES)
             drive_rows[:, tile] = (delta * conv_ref[:, lanes].astype(jnp.float32)).reshape(count, block, LANES)
 
-    rates = [-LOG2E * jnp.exp(decay_ref[:, tile * LANES : (tile + 1) * LANES]) for tile in range(tiles)]
-
-    quarter = min(2 * LANES, tiles * LANES)
-    quarters = tiles * LANES // quarter
+    rates = [
+        -LOG2E * jnp.exp(decay_ref[:, column + tile * LANES : column + (tile + 1) * LANES]) for tile in range(tiles)
+    ]
+
+    wide = tiles * LANES
+    cut = 2 * LANES
+    cuts = -(-wide // cut)
 
     def finish(index, history, part):
         first = pl.multiple_of(index * block, block)
-        lanes = slice(part * quarter, (part + 1) * quarter)
+        lanes = slice(part * cut, min((part + 1) * cut, wide))
         mixed = jnp.dot(out_diag[pl.ds(first, block), :], history[:, lanes], preferred_element_type=jnp.float32)
-        full = mixed + gain_ref[:, lanes] * conv_ref[pl.ds(first, block), lanes].astype(jnp.float32)
+        gain = gain_ref[:, column + lanes.start : column + lanes.stop]
+        full = mixed + gain * conv_ref[pl.ds(first, block), lanes].astype(jnp.float32)
         place = pl.multiple_of(lax.rem(first, rows), block)
         out_ref[lax.div(first, rows), pl.ds(place, block), lanes] = full.astype(out_ref.dtype)
 
@@ -292,8 +300,8 @@
                 grow = jnp.exp2(delta_now[tile, inner : inner + 1, :] * rates[tile])
                 held[tile] = grow * held[tile] + into * drive_now[tile, inner : inner + 1, :]
                 history[inner * states : (inner + 1) * states, lanes] = held[tile].astype(jnp.bfloat16)
-            if inner % (block // quarters) == 0:
-                finish(before, before_history, inner // (block // quarters))
+            if inner % (block // cuts) == 0 and inner // (block // cuts) < cuts:
+                finish(before, before_history, inner // (block // cuts))
         return tuple(held)
 
     held_odd[...] = jnp.zeros_like(held_odd)
@@ -304,33 +312,35 @@
 
     start = tuple(jnp.zeros((states, LANES), jnp.float32) for _ in range(tiles))
     lax.fori_loop(0, count // 2, pair, start)
-    for part in range(quarters):
+    for part in range(cuts):
         finish(count - 1, held_odd, part)
 
 
-def state_scan(reset_col, low, delta_parts, bias, decay, gain, conv, ctx, call, calls):
+def state_scan(reset_col, low, delta_parts, bias, decay, gain, conv, ctx, first_shard, shards):
     toks = low.shape[0]
-    shards, rank, width = delta_parts.shape
-    shards = shards // calls
+    rank, width = delta_parts.shape[1:]
     states = decay.shape[0]
     rows = toks // ctx
     wide = shards * width
     steps = toks * wide * states
+    whole = pl.BlockSpec(memory_space=pltpu.VMEM)
     return pl.pallas_call(
-        functools.partial(scan_kernel, rank),
-        grid=(1,),
+        functools.partial(scan_kernel, rank, first_shard),
         in_specs=[
-            pl.BlockSpec((toks, 1), lambda g: (0, 0)),
-            pl.BlockSpec(low.shape, lambda g: (0, 0)),
-            pl.BlockSpec((shards, rank, width), lambda g: (call, 0, 0)),
-            pl.BlockSpec((1, wide), lambda g: (0, call)),
-            pl.BlockSpec((states, wide), lambda g: (0, call)),
-            pl.BlockSpec((1, wide), lambda g: (0, call)),
-            pl.BlockSpec((toks, wide), lambda g: (0, call)),
+            whole,
+            whole,
+            pl.BlockSpec(memory_space=pl.ANY),
+            whole,
+            whole,
+            whole,
+            pl.BlockSpec(memory_space=pl.ANY),
         ],
-        out_specs=pl.BlockSpec((ctx, rows, wide), lambda g: (0, 0, 0)),
+        out_specs=whole,
         out_shape=jax.ShapeDtypeStruct((ctx, rows, wide), jnp.bfloat16),
         scratch_shapes=[
+            pltpu.VMEM((shards, rank, width), jnp.bfloat16),
+            pltpu.VMEM((toks, wide), jnp.bfloat16),
+            pltpu.SemaphoreType.DMA((2,)),
             pltpu.VMEM((states, toks), jnp.float32),
             pltpu.VMEM((toks, 16 * states), jnp.bfloat16),
             pltpu.VMEM((toks // 16, wide // LANES, 16, LANES), jnp.float32),
@@ -338,48 +348,42 @@
             pltpu.VMEM((16 * states, wide), jnp.bfloat16),
             pltpu.VMEM((16 * states, wide), jnp.bfloat16),
         ],
-        compiler_params=pltpu.CompilerParams(vmem_limit_bytes=24 << 20),
+        compiler_params=pltpu.CompilerParams(vmem_limit_bytes=60 << 20),
         cost_estimate=pl.CostEstimate(
-            flops=6 * steps, bytes_accessed=2 * delta_parts.size // calls + 4 * toks * wide, transcendentals=steps
+            flops=6 * steps, bytes_accessed=2 * shards * rank * width + 4 * toks * wide, transcendentals=steps
         ),
-        name=f"state_scan_{call}",
+        name=f"state_scan_{first_shard}",
     )(reset_col, low, delta_parts, bias, decay, gain, conv)
 
 
-def gate_kernel(fold, width, y_ref, gate_ref, *refs):
+def gate_kernel(fold, width, gate_ref, *refs):
     out_ref = refs[-1]
-    ctx, _, wide = y_ref.shape
-    for slot in range(wide // width):
-        for piece in range(ctx):
-            lanes = piece_lanes(slot, piece, ctx, fold, width)
-            value = y_ref[piece, :, slot * width : (slot + 1) * width].astype(jnp.float32)
-            out_ref[:, lanes] = (value * silu(gate_ref[:, lanes].astype(jnp.float32))).astype(out_ref.dtype)
-
-
-def apply_gate(pieces, gate, fold, width, call, before=None):
-    ctx, rows, wide = pieces.shape
+    slot = 0
+    for y_ref in refs[:-1]:
+        ctx, _, wide = y_ref.shape
+        for place in range(wide // width):
+            for piece in range(ctx):
+                lanes = piece_lanes(slot, piece, ctx, fold, width)
+                value = y_ref[piece, :, place * width : (place + 1) * width].astype(jnp.float32)
+                out_ref[:, lanes] = (value * silu(gate_ref[:, lanes].astype(jnp.float32))).astype(out_ref.dtype)
+            slot += 1
+
+
+def apply_gate(parts, gate, fold, width):
+    rows, channels = gate.shape
+    ctx = parts[0].shape[0]
     part = min(rows, 32)
-    columns = pl.BlockSpec((part, ctx * wide), lambda r: (r, call))
-    operands = [pieces, gate]
-    in_specs = [pl.BlockSpec((ctx, part, wide), lambda r: (0, r, 0)), columns]
-    aliases = {}
-    if before is not None:
-        aliases = {2: 0}
-        operands.append(before)
-        in_specs.append(pl.BlockSpec(memory_space=pl.ANY))
+    columns = pl.BlockSpec((part, channels), lambda r: (r, 0))
     return pl.pallas_call(
         functools.partial(gate_kernel, fold, width),
         grid=(rows // part,),
-        in_specs=in_specs,
+        in_specs=[columns] + [pl.BlockSpec((ctx, part, array.shape[2]), lambda r: (0, r, 0)) for array in parts],
         out_specs=columns,
         out_shape=jax.ShapeDtypeStruct(gate.shape, jnp.bfloat16),
-        input_output_aliases=aliases,
-        compiler_params=pltpu.CompilerParams(vmem_limit_bytes=12 << 20),
-        cost_estimate=pl.CostEstimate(
-            flops=4 * pieces.size, bytes_accessed=6 * pieces.size, transcendentals=pieces.size
-        ),
-        name=f"gate_{call}",
-    )(*operands)
+        compiler_params=pltpu.CompilerParams(vmem_limit_bytes=16 << 20),
+        cost_estimate=pl.CostEstimate(flops=4 * gate.size, bytes_accessed=6 * gate.size, transcendentals=gate.size),
+        name="gate",
+    )(gate, *parts)
 
 
 def shifted(value, axis, by):
@@ -438,8 +442,6 @@
 
     select_parts = gathered(select_weight)
     packed = pack(mixer_input[0], ctx, fold, width)
-    packed, delta_weight = lax.optimization_barrier((packed, delta_weight))
-    delta_parts = gathered(delta_weight)
 
     same = jnp.concatenate([jnp.zeros((1,), bool), seg[1:] == seg[:-1]])
     reset_col = jnp.where(same, 0.0, FAR)[:, None]
@@ -454,7 +456,8 @@
         seg_k[None, :],
         jnp.concatenate([keys[0], values[0]], axis=1),
     )
-    pieces, own = lax.optimization_barrier((exchange(packed), own))
+    pieces, own, delta_weight = lax.optimization_barrier((exchange(packed), own, delta_weight))
+    delta_parts = gathered(delta_weight)
     bias, decay, gain, reset_col, seg_q, seg_k, both = own
 
     conv, parts = conv_select(seg_col, pieces, own_part(conv_weight), own_part(conv_bias)[None, :], select_parts)
@@ -464,17 +467,15 @@
     blocks = [shifted(both, "ctx", by) for by in range(back, 0, -1)] + [both]
     low = exchange(low).reshape(toks, low.shape[2])
 
-    calls = 2
+    early = slots * 5 // 8
     scanned = []
-    for call in range(calls):
-        scanned.append(state_scan(reset_col, low, delta_parts, bias, decay, gain, conv, ctx, call, calls))
+    for first, count in ((0, early), (early, slots - early)):
+        scanned.append(state_scan(reset_col, low, delta_parts, bias, decay, gain, conv, ctx, first, count))
     scanned[-1], blocks = lax.optimization_barrier((scanned[-1], blocks))
     attended = attention(queries[0], blocks, seg_q, seg_k, 0, KEY_VALUE_HEADS)
     scanned = [exchange(part) for part in scanned]
     scanned[-1], attended = lax.optimization_barrier((scanned[-1], attended))
-    mixed = None
-    for call in range(calls):
-        mixed = apply_gate(scanned[call], gate_input[0], fold, width, call, mixed)
+    mixed = apply_gate(scanned, gate_input[0], fold, width)
     return (attended[None], mixed[None])
 
 

time: 147 us -> 151 us (1.027)
  waiting for transfers between devices: 16.9 us -> 23.1 us
  local copies, waits for them, and re-layouts: 32.3 us -> 27.1 us
  starting transfers between devices: 23.9 us -> 26.5 us
  Pallas kernels: 43.3 us -> 44.9 us
    unnamed x52 -> x34, local copies, waits for them, and re-layouts: 20.7 us -> 14.3 us
    all_to_all x4, waiting for transfers between devices: 16.9 us -> 23 us  [exchange(): return lax.all_to_all(value, 'ctx', 0, 0, tiled=True)]
    pallas_call x2, Pallas kernels: 26.7 us -> 32 us  [state_scan(): pl.pallas_call(functools.partial(scan_kernel, rank, first_shard), in_spec...]
    pallas_call x2 -> x1, Pallas kernels: 5.63 us -> 2.52 us  [apply_gate(): pl.pallas_call(functools.partial(gate_kernel, fold, width), grid=(rows //...]
    all_to_all x4, starting transfers between devices: 16.6 us -> 19.2 us  [exchange(): return lax.all_to_all(value, 'ctx', 0, 0, tiled=True)]
  transfers between devices with their start and end apart: 8 -> 8, of which waited for: 3 -> 3; matrix products, arithmetic and copies ran while one was open for 10% -> 10% of each run, Pallas kernels for 26% -> 28%
where the time goes in v6:
time: 151 us; the launch traced here: 149 us
  Pallas kernels  44.9 us (30%)
  local copies, waits for them, and re-layouts  27.1 us (18%)
  starting transfers between devices  26.5 us (18%)
  waiting for transfers between devices  23.1 us (15%)
  between operations  14.3 us (9%)
  blocking collectives  11.7 us (8%)
  other arithmetic  1.88 us (1%)
    pallas_call x2, Pallas kernels, state_scan(): pl.pallas_call(functools.partial(scan_kernel, rank, first_shard), in_spec...  32 us
    all_to_all x4, waiting for transfers between devices, exchange(): return lax.all_to_all(value, 'ctx', 0, 0, tiled=True)  23 us
    all_to_all x4, starting transfers between devices, exchange(): return lax.all_to_all(value, 'ctx', 0, 0, tiled=True)  19.2 us
    unnamed x34, local copies, waits for them, and re-layouts  14.3 us
    all_to_all x1, blocking collectives, exchange(): return lax.all_to_all(value, 'ctx', 0, 0, tiled=True)  11.7 us
    ppermute x2, starting transfers between devices, shifted(): return lax.ppermute(value, axis, pairs)  7.28 us
    reshape x5, local copies, waits for them, and re-layouts, own_part(): cut = array.reshape(array.shape[:-1] + (slots, fold, ctx // fold, width))  5.31 us
    pallas_call x1, Pallas kernels, attention(): pl.pallas_call(functools.partial(attention_kernel, begin), grid=(end - be...  4.76 us
  transfers between devices with their start and end apart: 8, of which 3 were waited for; matrix products, arithmetic and copies ran while one was open for 10% of the time, Pallas kernels for 28%

profile of v6, /device:TPU:0, one launch (start us, length us, event | category | flops | bytes accessed | tf_op | source)
XLA Modules:
  0.0 149.5 jit_solution(6347169218428330886)
XLA Ops:
  7.2 1.2 copy-done
  9.2 1.6 %copy-done.4 = bf16[1,128,8192]{2,1,0:T(8,128)(2,1)S(1)} copy-done((bf16[1,128,8192]{2,1,0:T(8,128)(2,1)S(1)}, bf16[1,128,8192]{2,1,0:T(8,128)(2,1)}, u32[]{:S(2)}) %copy-start.4) | copy-done | bytes 2097176
  11.1 1.3 copy-done.1
  12.5 5.3 %all-to-all-start = ((bf16[4,128,2048]{2,1,0:T(8,128)(2,1)}), bf16[4,128,2048]{2,1,0:T(8,128)(2,1)S(1)}, u32[]{:S(2)}, u32[]{:S(2)}) async-start(bf16[4,128,2048]{2,1,0:T(8,128)(2,1)} %copy-done.1), calls=%async_computation | async-start | bytes 4194304 | tf_op jit(solution)/shard_map/all_to_all | solution.py:396
  17.9 2.2 %reshape.75 = f32[16,8,1,4,256]{4,3,1,0,2:T(4,128)} reshape(f32[16,8192]{1,0:T(8,128)} %bitcast.34) | data formatting | bytes 1048576 | tf_op jit(solution)/shard_map/reshape | solution.py:430
  20.1 1.4 dynamic-slice_reduce_fusion
  23.2 1.0 pad_maximum_fusion.refs_4_.refs_5_
  25.0 17.7 %all-to-all-done.x_ref = bf16[4,128,2048]{2,1,0:T(8,128)(2,1)S(1)} async-done(((bf16[4,128,2048]{2,1,0:T(8,128)(2,1)}), bf16[4,128,2048]{2,1,0:T(8,128)(2,1)S(1)}, u32[]{:S(2)}, u32[]{:S(2)}) %all-to-all-start) | async-done | bytes 2097184 | tf_op jit(solution)/shard_map/all_to_all | solution.py:396
  42.6 1.7 %constant_dynamic-slice_fusion = bf16[512,256]{1,0:T(8,128)(2,1)} fusion(bf16[512,1024]{1,0:T(8,128)(2,1)} %param.22, s32[]{:T(128)S(6)} %select_n.60), kind=kLoop, calls=%fused_computation.7 | loop fusion | bytes 524292 | tf_op jit(solution)/shard_map/dynamic_slice | solution.py:436
  44.3 1.7 %reshape.78 = f32[4,8,1,4,256]{4,3,1,0,2:T(4,128)} reshape(f32[4,8192]{1,0:T(4,128)} %param.19) | data formatting | bytes 262144 | tf_op jit(solution)/shard_map/reshape | solution.py:430
  46.0 1.0 dynamic-slice_reduce_fusion.1
  47.0 1.4 reshape.80
  50.1 1.7 %copy-done.2 = bf16[4352,256]{1,0:T(8,128)(2,1)S(1)} copy-done((bf16[4352,256]{1,0:T(8,128)(2,1)S(1)}, bf16[4352,256]{1,0:T(8,128)(2,1)}, u32[]{:S(2)}) %copy-start.2) | copy-done | bytes 2228248
  51.7 1.0 copy-done.10
  52.7 4.3 %conv_select.1 = (bf16[512,2048]{1,0:T(8,128)(2,1)S(1)}, bf16[4,128,640]{2,1,0:T(8,128)(2,1)S(1)}) custom-call(s32[512,1]{1,0:T(8,128)S(1)} %copy-done.10, bf16[4,128,2048]{2,1,0:T(8,128)(2,1)S(1)} %all-to-all-done.x_ref, f32[4,2048]{1,0:T(4,128)S(1)} %bitcast.28, f32[1,2048]{1,0:T(1,128)S(1)} %bitcast.29, bf16[8,544,256]{2,1,0:T(8,128)(2,1)S(1)} %bitcast.24), custom_call_target="tpu_custom_call" | custom-call | flops 1140850688 | bytes 6422528 | tf_op jit(solution)/shard_map/conv_select/pallas_call | solution.py:168
  57.0 1.3 copy-done.11
  58.3 11.7 %all_to_all.25.part_ref = bf16[4,128,640]{2,1,0:T(8,128)(2,1)S(1)} all-to-all(bf16[4,128,640]{2,1,0:T(8,128)(2,1)S(1)} %get-tuple-element.23), channel_id=1, replica_groups=mesh['ctx'=4,'rep'=8] {'ctx'}, dimensions={0} | all-to-all | bytes 1310720 | tf_op jit(solution)/shard_map/all_to_all | solution.py:396
  70.1 1.0 normalise.1
  71.1 3.5 %all-to-all-start.2 = ((bf16[4,128,640]{2,1,0:T(8,128)(2,1)}), bf16[4,128,640]{2,1,0:T(8,128)(2,1)S(1)}, u32[]{:S(2)}, u32[]{:S(2)}) async-start(bf16[4,128,640]{2,1,0:T(8,128)(2,1)} %normalise.1), calls=%async_computation.2 | async-start | bytes 1310720 | tf_op jit(solution)/shard_map/all_to_all | solution.py:396
  74.5 3.9 %collective-permute-start = (bf16[128,1024]{1,0:T(8,128)(2,1)S(1)}, bf16[128,1024]{1,0:T(8,128)(2,1)S(1)}, u32[]{:S(2)}, u32[]{:S(2)}) collective-permute-start(bf16[128,1024]{1,0:T(8,128)(2,1)S(1)} %pad_maximum_fusion.refs_4_.refs_5_), channel_id=1, source_target_pairs={{0,16},{8,24},{1,17},{9,25},{2,18},{10,26},{3,19},{11,27},{4,20},{... | collective-permute-start | bytes 786440 | tf_op jit(solution)/shard_map/ppermute | solution.py:392
  78.4 3.4 %collective-permute-start.1 = (bf16[128,1024]{1,0:T(8,128)(2,1)S(1)}, bf16[128,1024]{1,0:T(8,128)(2,1)S(1)}, u32[]{:S(2)}, u32[]{:S(2)}) collective-permute-start(bf16[128,1024]{1,0:T(8,128)(2,1)S(1)} %pad_maximum_fusion.refs_4_.refs_5_), channel_id=1, source_target_pairs={{0,8},{8,16},{16,24},{1,9},{9,17},{17,25},{2,10},{10,18},{18,26},{... | collective-permute-start | bytes 786440 | tf_op jit(solution)/shard_map/ppermute | solution.py:392
  81.8 2.5 %all-to-all-done.2 = bf16[4,128,640]{2,1,0:T(8,128)(2,1)S(1)} async-done(((bf16[4,128,640]{2,1,0:T(8,128)(2,1)}), bf16[4,128,640]{2,1,0:T(8,128)(2,1)S(1)}, u32[]{:S(2)}, u32[]{:S(2)}) %all-to-all-start.2) | async-done | bytes 655392 | tf_op jit(solution)/shard_map/all_to_all | solution.py:396
  85.2 13.0 %state_scan_5.1 = bf16[4,128,768]{2,1,0:T(8,128)(2,1)} custom-call(f32[512,1]{1,0:T(8,128)} %broadcast_select_fusion.reset_ref, bf16[512,640]{1,0:T(8,128)(2,1)} %bitcast.32, bf16[8,512,256]{2,1,0:T(8,128)(2,1)} %bitcast.47, f32[1,2048]{1,0:T(1,128)} %bitcast.45, f32[16,2048]{1,0:T(8,128)} %bitcast.36, f32[1,2048]{1,0:T(1,128)} %bitcast.43, ...), custom_call_target="tpu_custom_call" | custom-call | flops 37748736 | bytes 2359296 | tf_op jit(solution)/shard_map/state_scan_5/pallas_call | solution.py:327
  98.3 6.2 %all-to-all-start.3 = ((bf16[4,128,768]{2,1,0:T(8,128)(2,1)}), bf16[4,128,768]{2,1,0:T(8,128)(2,1)S(1)}, u32[]{:S(2)}, u32[]{:S(2)}) async-start(bf16[4,128,768]{2,1,0:T(8,128)(2,1)} %state_scan_5.1), calls=%async_computation.3 | async-start | bytes 1572864 | tf_op jit(solution)/shard_map/all_to_all | solution.py:396
  104.4 19.0 %state_scan_0.1 = bf16[4,128,1280]{2,1,0:T(8,128)(2,1)} custom-call(f32[512,1]{1,0:T(8,128)} %broadcast_select_fusion.reset_ref, bf16[512,640]{1,0:T(8,128)(2,1)} %bitcast.33, bf16[8,512,256]{2,1,0:T(8,128)(2,1)} %bitcast.48, f32[1,2048]{1,0:T(1,128)} %bitcast.46, f32[16,2048]{1,0:T(8,128)} %bitcast.37, f32[1,2048]{1,0:T(1,128)} %bitcast.44, ...), custom_call_target="tpu_custom_call" | custom-call | flops 62914560 | bytes 3932160 | tf_op jit(solution)/shard_map/state_scan_0/pallas_call | solution.py:327
  123.5 4.2 %all-to-all-start.4 = ((bf16[4,128,1280]{2,1,0:T(8,128)(2,1)}), bf16[4,128,1280]{2,1,0:T(8,128)(2,1)S(1)}, u32[]{:S(2)}, u32[]{:S(2)}) async-start(bf16[4,128,1280]{2,1,0:T(8,128)(2,1)} %state_scan_0.1), calls=%async_computation.4 | async-start | bytes 2621440 | tf_op jit(solution)/shard_map/all_to_all | solution.py:396
  127.8 1.2 copy-done.5
  129.1 0.9 copy-done.7
  131.0 4.8 %attention_0.1 = bf16[128,4096]{1,0:T(8,128)(2,1)} custom-call(s32[128,1]{1,0:T(8,128)S(1)} %copy.27.seg_q_ref, s32[1,384]{1,0:T(1,128)S(1)} %broadcast_in_dim.25.seg_k_ref, bf16[128,4096]{1,0:T(8,128)(2,1)S(1)} %bitcast.27, bf16[128,1024]{1,0:T(8,128)(2,1)S(1)} %copy-done.7, bf16[128,1024]{1,0:T(8,128)(2,1)S(1)} %copy-done.7, ...), custom_call_target="tpu_custom_call" | custom-call | flops 805306368 | bytes 2097152 | tf_op jit(solution)/shard_map/attention_0/pallas_call | solution.py:73
  135.7 2.8 %all-to-all-done.4.refs_0_ = bf16[4,128,1280]{2,1,0:T(8,128)(2,1)S(1)} async-done(((bf16[4,128,1280]{2,1,0:T(8,128)(2,1)}), bf16[4,128,1280]{2,1,0:T(8,128)(2,1)S(1)}, u32[]{:S(2)}, u32[]{:S(2)}) %all-to-all-start.4) | async-done | bytes 1310752 | tf_op jit(solution)/shard_map/all_to_all | solution.py:396
  138.6 1.6 %copy-done.3 = bf16[1,128,8192]{2,1,0:T(8,128)(2,1)S(1)} copy-done((bf16[1,128,8192]{2,1,0:T(8,128)(2,1)S(1)}, bf16[1,128,8192]{2,1,0:T(8,128)(2,1)}, u32[]{:S(2)}) %copy-start.3) | copy-done | bytes 2097176
  140.1 2.5 %gate.1 = bf16[128,8192]{1,0:T(8,128)(2,1)} custom-call(bf16[128,8192]{1,0:T(8,128)(2,1)S(1)} %bitcast.25, bf16[4,128,1280]{2,1,0:T(8,128)(2,1)S(1)} %all-to-all-done.4.refs_0_, bf16[4,128,768]{2,1,0:T(8,128)(2,1)S(1)} %all-to-all-done.3.refs_1_), custom_call_target="tpu_custom_call" | custom-call | flops 4194304 | bytes 6291456 | tf_op jit(solution)/shard_map/gate/pallas_call | solution.py:377
  (49 shorter events, 7.3 us)
Async XLA Ops:
  7.2 1.3 copy-start
  7.2 42.9 %all-gather.5.cloned.1.call-start = ((), (), s32[]{:S(2)}) async-start(), calls=%async_computation.5 | async-start | bytes 2506752 | tf_op jit(solution)/shard_map/all_gather | solution.py:437
  9.2 1.6 %copy-start.4 = (bf16[1,128,8192]{2,1,0:T(8,128)(2,1)S(1)}, bf16[1,128,8192]{2,1,0:T(8,128)(2,1)}, u32[]{:S(2)}) copy-start(bf16[1,128,8192]{2,1,0:T(8,128)(2,1)} %param.16) | copy-start | bytes 6291460
  11.1 1.3 copy-start.1
  12.5 5.3 %copy-start.13 = (s32[1,512]{1,0:T(1,128)S(1)}, s32[1,512]{1,0:T(1,128)}, u32[]{:S(2)}) copy-start(s32[1,512]{1,0:T(1,128)} %param.18) | copy-start | bytes 6148
  12.5 5.4 %copy-start.14 = (f32[8192]{0:T(1024)S(1)}, f32[8192]{0:T(1024)}, u32[]{:S(2)}) copy-start(f32[8192]{0:T(1024)} %param.23) | copy-start | bytes 98308
  12.5 5.4 %copy-start.15 = (f32[8192]{0:T(1024)S(1)}, f32[8192]{0:T(1024)}, u32[]{:S(2)}) copy-start(f32[8192]{0:T(1024)} %param.25) | copy-start | bytes 98308
  12.5 30.2 %all-to-all-start = ((bf16[4,128,2048]{2,1,0:T(8,128)(2,1)}), bf16[4,128,2048]{2,1,0:T(8,128)(2,1)S(1)}, u32[]{:S(2)}, u32[]{:S(2)}) async-start(bf16[4,128,2048]{2,1,0:T(8,128)(2,1)} %copy-done.1), calls=%async_computation | async-start | bytes 4194304 | tf_op jit(solution)/shard_map/all_to_all | solution.py:396
  17.8 66.6 %all-gather.7.cloned.1.call-start = ((), (), s32[]{:S(2)}) async-start(), calls=%async_computation.6 | async-start | bytes 2359296 | tf_op jit(solution)/shard_map/all_gather | solution.py:437
  50.1 1.7 %copy-start.2 = (bf16[4352,256]{1,0:T(8,128)(2,1)S(1)}, bf16[4352,256]{1,0:T(8,128)(2,1)}, u32[]{:S(2)}) copy-start(bf16[4352,256]{1,0:T(8,128)(2,1)} %all-gather.5.cloned.1.call-done) | copy-start | bytes 6684676
  51.7 1.0 copy-start.10
  57.0 1.3 copy-start.11
  71.1 13.3 %all-to-all-start.2 = ((bf16[4,128,640]{2,1,0:T(8,128)(2,1)}), bf16[4,128,640]{2,1,0:T(8,128)(2,1)S(1)}, u32[]{:S(2)}, u32[]{:S(2)}) async-start(bf16[4,128,640]{2,1,0:T(8,128)(2,1)} %normalise.1), calls=%async_computation.2 | async-start | bytes 1310720 | tf_op jit(solution)/shard_map/all_to_all | solution.py:396
  74.5 23.7 %collective-permute-start = (bf16[128,1024]{1,0:T(8,128)(2,1)S(1)}, bf16[128,1024]{1,0:T(8,128)(2,1)S(1)}, u32[]{:S(2)}, u32[]{:S(2)}) collective-permute-start(bf16[128,1024]{1,0:T(8,128)(2,1)S(1)} %pad_maximum_fusion.refs_4_.refs_5_), channel_id=1, source_target_pairs={{0,16},{8,24},{1,17},{9,25},{2,18},{10,26},{3,19},{11,27},{4,20},{... | collective-permute-start | bytes 786440 | tf_op jit(solution)/shard_map/ppermute | solution.py:392
  78.4 19.8 %collective-permute-start.1 = (bf16[128,1024]{1,0:T(8,128)(2,1)S(1)}, bf16[128,1024]{1,0:T(8,128)(2,1)S(1)}, u32[]{:S(2)}, u32[]{:S(2)}) collective-permute-start(bf16[128,1024]{1,0:T(8,128)(2,1)S(1)} %pad_maximum_fusion.refs_4_.refs_5_), channel_id=1, source_target_pairs={{0,8},{8,16},{16,24},{1,9},{9,17},{17,25},{2,10},{10,18},{18,26},{... | collective-permute-start | bytes 786440 | tf_op jit(solution)/shard_map/ppermute | solution.py:392
  84.4 0.9 copy-start.12
  98.2 25.3 %copy-start.6 = (bf16[128,1024]{1,0:T(8,128)(2,1)}, bf16[128,1024]{1,0:T(8,128)(2,1)S(1)}, u32[]{:S(2)}) copy-start(bf16[128,1024]{1,0:T(8,128)(2,1)S(1)} %collective-permute-done.refs_0_.refs_1_) | copy-start | bytes 786436
  98.2 25.2 %copy-start.8 = (bf16[128,1024]{1,0:T(8,128)(2,1)}, bf16[128,1024]{1,0:T(8,128)(2,1)S(1)}, u32[]{:S(2)}) copy-start(bf16[128,1024]{1,0:T(8,128)(2,1)S(1)} %collective-permute-done.1.refs_2_.refs_3_) | copy-start | bytes 786436
  98.3 25.2 %all-to-all-start.3 = ((bf16[4,128,768]{2,1,0:T(8,128)(2,1)}), bf16[4,128,768]{2,1,0:T(8,128)(2,1)S(1)}, u32[]{:S(2)}, u32[]{:S(2)}) async-start(bf16[4,128,768]{2,1,0:T(8,128)(2,1)} %state_scan_5.1), calls=%async_computation.3 | async-start | bytes 1572864 | tf_op jit(solution)/shard_map/all_to_all | solution.py:396
  123.5 15.0 %all-to-all-start.4 = ((bf16[4,128,1280]{2,1,0:T(8,128)(2,1)}), bf16[4,128,1280]{2,1,0:T(8,128)(2,1)S(1)}, u32[]{:S(2)}, u32[]{:S(2)}) async-start(bf16[4,128,1280]{2,1,0:T(8,128)(2,1)} %state_scan_0.1), calls=%async_computation.4 | async-start | bytes 2621440 | tf_op jit(solution)/shard_map/all_to_all | solution.py:396
  127.8 1.2 copy-start.5
  129.0 0.9 copy-start.7
  130.0 0.9 copy-start.9
  138.5 1.6 %copy-start.3 = (bf16[1,128,8192]{2,1,0:T(8,128)(2,1)S(1)}, bf16[1,128,8192]{2,1,0:T(8,128)(2,1)}, u32[]{:S(2)}) copy-start(bf16[1,128,8192]{2,1,0:T(8,128)(2,1)} %param.17) | copy-start | bytes 6291460
Sparse Core Ops, SparseCore 0:
  9.7 32.9 all-gather.4
  44.4 29.5 all-gather.6

commit v7 on v6

--- a/solution.py
+++ b/solution.py
@@ -239,14 +239,16 @@
     count = toks // block
 
     in_cols[...] = jnp.transpose(low_ref[:, rank : rank + LANES].astype(jnp.float32))[0:states, :]
+    bits = states.bit_length() - 1
     lane = lax.broadcasted_iota(jnp.int32, (states, span), 1)
-    spread = jnp.where(lane % states == lax.broadcasted_iota(jnp.int32, (states, span), 0), 1.0, 0.0)
+    spread = jnp.where((lane & (states - 1)) == lax.broadcasted_iota(jnp.int32, (states, span), 0), 1.0, 0.0)
     copies = jnp.dot(
         low_ref[:, rank + states : rank + 2 * states], spread.astype(jnp.bfloat16), preferred_element_type=jnp.float32
     )
-    here = lax.broadcasted_iota(jnp.int32, (toks, span), 1) // states
-    there = lax.broadcasted_iota(jnp.int32, (toks, span), 0) % block
-    out_diag[...] = jnp.where(here == there, copies, 0.0).astype(jnp.bfloat16)
+    here = lax.shift_right_logical(lax.broadcasted_iota(jnp.int32, (block, span), 1), bits)
+    there = lax.broadcasted_iota(jnp.int32, (block, span), 0)
+    keep = jnp.where(here == there, 1.0, 0.0)
+    out_diag[...] = (copies.reshape(count, block, span) * keep[None]).reshape(toks, span).astype(jnp.bfloat16)
 
     reset = jnp.broadcast_to(reset_ref[...], (toks, LANES))
     low = low_ref[:, 0:rank]
@@ -259,13 +261,9 @@
             lanes = slice(tile * LANES, (tile + 1) * LANES)
             value = pre[:, part * LANES : (part + 1) * LANES]
             value = value + bias_ref[:, column + tile * LANES : column + (tile + 1) * LANES]
-            raised = jnp.exp(-jnp.abs(value))
-            log_part = jnp.where(
-                raised < 0.01,
-                raised * (1.0 - raised * (0.5 - raised * (1.0 / 3.0))),
-                jnp.log(1.0 + raised),
-            )
-            delta = (jnp.maximum(value, 0.0) + log_part).astype(jnp.bfloat16).astype(jnp.float32)
+            raised = jnp.exp2(jnp.minimum(value, 80.0) * LOG2E)
+            small = raised - 0.5 * raised * raised
+            delta = jnp.maximum(value, jnp.where(raised < 0.01, small, jnp.log(1.0 + raised)))
             delta_rows[:, tile] = (delta + reset).reshape(count, block, LANES)
             drive_rows[:, tile] = (delta * conv_ref[:, lanes].astype(jnp.float32)).reshape(count, block, LANES)
 
@@ -432,15 +430,17 @@
         cut = lax.dynamic_index_in_dim(cut, place % fold, cut.ndim - 2, keepdims=False)
         return cut.reshape(array.shape[:-1] + (slots * width,))
 
-    def gathered(weight):
-        own = lax.dynamic_slice_in_dim(weight, place // fold * width, width, 1)
+    def own_columns(weight):
+        return lax.dynamic_slice_in_dim(weight, place // fold * width, width, 1)
+
+    def gathered(own):
         parts = lax.all_gather(own, "rep", axis=0)
         if fold > 1:
             parts = parts.reshape((slots, fold) + own.shape)
             parts = lax.dynamic_index_in_dim(parts, place % fold, 1, keepdims=False)
         return parts
 
-    select_parts = gathered(select_weight)
+    select_parts = gathered(own_columns(select_weight))
     packed = pack(mixer_input[0], ctx, fold, width)
 
     same = jnp.concatenate([jnp.zeros((1,), bool), seg[1:] == seg[:-1]])
@@ -455,12 +455,16 @@
         seg_k[back * rows :, None],
         seg_k[None, :],
         jnp.concatenate([keys[0], values[0]], axis=1),
+        own_part(conv_weight),
+        own_part(conv_bias)[None, :],
+        seg_col,
+        own_columns(delta_weight),
     )
-    pieces, own, delta_weight = lax.optimization_barrier((exchange(packed), own, delta_weight))
-    delta_parts = gathered(delta_weight)
-    bias, decay, gain, reset_col, seg_q, seg_k, both = own
-
-    conv, parts = conv_select(seg_col, pieces, own_part(conv_weight), own_part(conv_bias)[None, :], select_parts)
+    pieces, own = lax.optimization_barrier((exchange(packed), own))
+    bias, decay, gain, reset_col, seg_q, seg_k, both, conv_weight, conv_bias, seg_col, delta_own = own
+    delta_parts = gathered(delta_own)
+
+    conv, parts = conv_select(seg_col, pieces, conv_weight, conv_bias, select_parts)
     low = normalise(exchange(parts), rank)
 
     low, both = lax.optimization_barrier((low, both))
@@ -470,6 +474,8 @@
     early = slots * 5 // 8
     scanned = []
     for first, count in ((0, early), (early, slots - early)):
+        if scanned:
+            low, scanned[-1] = lax.optimization_barrier((low, scanned[-1]))
         scanned.append(state_scan(reset_col, low, delta_parts, bias, decay, gain, conv, ctx, first, count))
     scanned[-1], blocks = lax.optimization_barrier((scanned[-1], blocks))
     attended = attention(queries[0], blocks, seg_q, seg_k, 0, KEY_VALUE_HEADS)

time: 151 us -> 154 us (1.020)
  blocking collectives: 11.7 us -> 28.3 us
  starting transfers between devices: 26.5 us -> 19.7 us
  waiting for transfers between devices: 23.1 us -> 17.3 us
    all_to_all x1 -> x2, blocking collectives: 11.7 us -> 28.3 us  [exchange(): return lax.all_to_all(value, 'ctx', 0, 0, tiled=True)]
    all_to_all x4 -> x3, starting transfers between devices: 19.2 us -> 12.3 us  [exchange(): return lax.all_to_all(value, 'ctx', 0, 0, tiled=True)]
    all_to_all x4 -> x3, waiting for transfers between devices: 23 us -> 17.3 us  [exchange(): return lax.all_to_all(value, 'ctx', 0, 0, tiled=True)]
    unnamed x34 -> x36, local copies, waits for them, and re-layouts: 14.3 us -> 14.3 us
  transfers between devices with their start and end apart: 8 -> 7, of which waited for: 3 -> 3; matrix products, arithmetic and copies ran while one was open for 10% -> 10% of each run, Pallas kernels for 28% -> 27%
where the time goes in v7:
time: 154 us; the launch traced here: 153 us
  Pallas kernels  44.2 us (29%)
  blocking collectives  28.3 us (18%)
  local copies, waits for them, and re-layouts  26.4 us (17%)
  starting transfers between devices  19.7 us (13%)
  waiting for transfers between devices  17.3 us (11%)
  between operations  14.2 us (9%)
  other arithmetic  2.74 us (2%)
    pallas_call x2, Pallas kernels, state_scan(): pl.pallas_call(functools.partial(scan_kernel, rank, first_shard), in_spec...  31.2 us
    all_to_all x2, blocking collectives, exchange(): return lax.all_to_all(value, 'ctx', 0, 0, tiled=True)  28.3 us
    all_to_all x3, waiting for transfers between devices, exchange(): return lax.all_to_all(value, 'ctx', 0, 0, tiled=True)  17.3 us
    unnamed x36, local copies, waits for them, and re-layouts  14.3 us
    all_to_all x3, starting transfers between devices, exchange(): return lax.all_to_all(value, 'ctx', 0, 0, tiled=True)  12.3 us
    ppermute x2, starting transfers between devices, shifted(): return lax.ppermute(value, axis, pairs)  7.28 us
    pallas_call x1, Pallas kernels, attention(): pl.pallas_call(functools.partial(attention_kernel, begin), grid=(end - be...  4.76 us
    reshape x5, local copies, waits for them, and re-layouts, own_part(): cut = array.reshape(array.shape[:-1] + (slots, fold, ctx // fold, width))  4.34 us
  transfers between devices with their start and end apart: 7, of which 3 were waited for; matrix products, arithmetic and copies ran while one was open for 10% of the time, Pallas kernels for 27%

profile of v7, /device:TPU:0, one launch (start us, length us, event | category | flops | bytes accessed | tf_op | source)
XLA Modules:
  0.0 152.8 jit_solution(242131339435933361)
XLA Ops:
  7.2 1.2 copy-done
  9.2 1.6 %copy-done.4 = bf16[1,128,8192]{2,1,0:T(8,128)(2,1)S(1)} copy-done((bf16[1,128,8192]{2,1,0:T(8,128)(2,1)S(1)}, bf16[1,128,8192]{2,1,0:T(8,128)(2,1)}, u32[]{:S(2)}) %copy-start.4) | copy-done | bytes 2097176
  11.1 1.3 copy-done.1
  12.5 5.3 %all-to-all-start = ((bf16[4,128,2048]{2,1,0:T(8,128)(2,1)}), bf16[4,128,2048]{2,1,0:T(8,128)(2,1)S(1)}, u32[]{:S(2)}, u32[]{:S(2)}) async-start(bf16[4,128,2048]{2,1,0:T(8,128)(2,1)} %copy-done.1), calls=%async_computation | async-start | bytes 4194304 | tf_op jit(solution)/shard_map/all_to_all | solution.py:394
  19.1 2.2 %reshape.75 = f32[16,8,1,4,256]{4,3,1,0,2:T(4,128)} reshape(f32[16,8192]{1,0:T(8,128)} %bitcast.34) | data formatting | bytes 1048576 | tf_op jit(solution)/shard_map/reshape | solution.py:428
  21.3 1.4 dynamic-slice_reduce_fusion
  26.0 1.4 constant_dynamic-slice_fusion.2
  27.4 1.7 %constant_dynamic-slice_fusion.1 = bf16[512,256]{1,0:T(8,128)(2,1)} fusion(bf16[512,1024]{1,0:T(8,128)(2,1)} %param.22, s32[]{:T(128)S(6)} %select_n.60), kind=kLoop, calls=%fused_computation.8 | loop fusion | bytes 524292 | tf_op jit(solution)/shard_map/dynamic_slice | solution.py:434
  29.1 1.0 pad_maximum_fusion.refs_4_.refs_5_
  30.1 1.6 %broadcast_select_fusion.reset_ref = f32[512,1]{1,0:T(8,128)} fusion(pred[512,1]{1,0:T(8,128)(4,1)} %copy.24), kind=kLoop, calls=%fused_computation.1 | loop fusion | flops 512 | bytes 2560 | tf_op jit(solution)/shard_map/jit(_where)/select_n | solution.py:447
  31.7 11.0 %all-to-all-done.x_ref = bf16[4,128,2048]{2,1,0:T(8,128)(2,1)S(1)} async-done(((bf16[4,128,2048]{2,1,0:T(8,128)(2,1)}), bf16[4,128,2048]{2,1,0:T(8,128)(2,1)S(1)}, u32[]{:S(2)}, u32[]{:S(2)}) %all-to-all-start) | async-done | bytes 2097184 | tf_op jit(solution)/shard_map/all_to_all | solution.py:394
  43.5 1.6 %copy-done.2 = bf16[4352,256]{1,0:T(8,128)(2,1)S(1)} copy-done((bf16[4352,256]{1,0:T(8,128)(2,1)S(1)}, bf16[4352,256]{1,0:T(8,128)(2,1)}, u32[]{:S(2)}) %copy-start.2) | copy-done | bytes 2228248
  45.2 0.9 copy-done.10
  46.1 4.3 %conv_select.1 = (bf16[512,2048]{1,0:T(8,128)(2,1)S(1)}, bf16[4,128,640]{2,1,0:T(8,128)(2,1)S(1)}) custom-call(s32[512,1]{1,0:T(8,128)S(1)} %copy-done.10, bf16[4,128,2048]{2,1,0:T(8,128)(2,1)S(1)} %all-to-all-done.x_ref, f32[4,2048]{1,0:T(4,128)S(1)} %bitcast.28, f32[1,2048]{1,0:T(1,128)S(1)} %bitcast.29, bf16[8,544,256]{2,1,0:T(8,128)(2,1)S(1)} %bitcast.24), custom_call_target="tpu_custom_call" | custom-call | flops 1140850688 | bytes 6422528 | tf_op jit(solution)/shard_map/conv_select/pallas_call | solution.py:168
  50.4 1.3 copy-done.11
  51.8 12.8 %all_to_all.25.part_ref = bf16[4,128,640]{2,1,0:T(8,128)(2,1)S(1)} all-to-all(bf16[4,128,640]{2,1,0:T(8,128)(2,1)S(1)} %get-tuple-element.31), channel_id=1, replica_groups=mesh['ctx'=4,'rep'=8] {'ctx'}, dimensions={0} | all-to-all | bytes 1310720 | tf_op jit(solution)/shard_map/all_to_all | solution.py:394
  64.6 1.0 normalise.1
  65.6 3.5 %all-to-all-start.2 = ((bf16[4,128,640]{2,1,0:T(8,128)(2,1)}), bf16[4,128,640]{2,1,0:T(8,128)(2,1)S(1)}, u32[]{:S(2)}, u32[]{:S(2)}) async-start(bf16[4,128,640]{2,1,0:T(8,128)(2,1)} %normalise.1), calls=%async_computation.2 | async-start | bytes 1310720 | tf_op jit(solution)/shard_map/all_to_all | solution.py:394
  69.1 3.9 %collective-permute-start = (bf16[128,1024]{1,0:T(8,128)(2,1)S(1)}, bf16[128,1024]{1,0:T(8,128)(2,1)S(1)}, u32[]{:S(2)}, u32[]{:S(2)}) collective-permute-start(bf16[128,1024]{1,0:T(8,128)(2,1)S(1)} %pad_maximum_fusion.refs_4_.refs_5_), channel_id=1, source_target_pairs={{0,16},{8,24},{1,17},{9,25},{2,18},{10,26},{3,19},{11,27},{4,20},{... | collective-permute-start | bytes 786440 | tf_op jit(solution)/shard_map/ppermute | solution.py:390
  73.0 3.4 %collective-permute-start.1 = (bf16[128,1024]{1,0:T(8,128)(2,1)S(1)}, bf16[128,1024]{1,0:T(8,128)(2,1)S(1)}, u32[]{:S(2)}, u32[]{:S(2)}) collective-permute-start(bf16[128,1024]{1,0:T(8,128)(2,1)S(1)} %pad_maximum_fusion.refs_4_.refs_5_), channel_id=1, source_target_pairs={{0,8},{8,16},{16,24},{1,9},{9,17},{17,25},{2,10},{10,18},{18,26},{... | collective-permute-start | bytes 786440 | tf_op jit(solution)/shard_map/ppermute | solution.py:390
  76.4 3.5 %all-to-all-done.2 = bf16[4,128,640]{2,1,0:T(8,128)(2,1)S(1)} async-done(((bf16[4,128,640]{2,1,0:T(8,128)(2,1)}), bf16[4,128,640]{2,1,0:T(8,128)(2,1)S(1)}, u32[]{:S(2)}, u32[]{:S(2)}) %all-to-all-start.2) | async-done | bytes 655392 | tf_op jit(solution)/shard_map/all_to_all | solution.py:394
  80.8 18.5 %state_scan_0.1 = bf16[4,128,1280]{2,1,0:T(8,128)(2,1)} custom-call(f32[512,1]{1,0:T(8,128)} %broadcast_select_fusion.reset_ref, bf16[512,640]{1,0:T(8,128)(2,1)} %bitcast.32, bf16[8,512,256]{2,1,0:T(8,128)(2,1)} %bitcast.47, f32[1,2048]{1,0:T(1,128)} %bitcast.43, f32[16,2048]{1,0:T(8,128)} %bitcast.36, f32[1,2048]{1,0:T(1,128)} %bitcast.45, ...), custom_call_target="tpu_custom_call" | custom-call | flops 62914560 | bytes 3932160 | tf_op jit(solution)/shard_map/state_scan_0/pallas_call | solution.py:325
  99.3 12.7 %state_scan_5.1 = bf16[4,128,768]{2,1,0:T(8,128)(2,1)} custom-call(f32[512,1]{1,0:T(8,128)} %broadcast_select_fusion.reset_ref, bf16[512,640]{1,0:T(8,128)(2,1)} %bitcast.33, bf16[8,512,256]{2,1,0:T(8,128)(2,1)} %bitcast.48, f32[1,2048]{1,0:T(1,128)} %bitcast.44, f32[16,2048]{1,0:T(8,128)} %bitcast.37, f32[1,2048]{1,0:T(1,128)} %bitcast.46, ...), custom_call_target="tpu_custom_call" | custom-call | flops 37748736 | bytes 2359296 | tf_op jit(solution)/shard_map/state_scan_5/pallas_call | solution.py:325
  112.1 15.4 %all_to_all.26.refs_1_ = bf16[4,128,768]{2,1,0:T(8,128)(2,1)S(1)} all-to-all(bf16[4,128,768]{2,1,0:T(8,128)(2,1)} %state_scan_5.1), channel_id=1, replica_groups=mesh['ctx'=4,'rep'=8] {'ctx'}, dimensions={0} | all-to-all | bytes 1572864 | tf_op jit(solution)/shard_map/all_to_all | solution.py:394
  127.5 3.5 %all-to-all-start.4 = ((bf16[4,128,1280]{2,1,0:T(8,128)(2,1)}), bf16[4,128,1280]{2,1,0:T(8,128)(2,1)S(1)}, u32[]{:S(2)}, u32[]{:S(2)}) async-start(bf16[4,128,1280]{2,1,0:T(8,128)(2,1)} %state_scan_0.1), calls=%async_computation.4 | async-start | bytes 2621440 | tf_op jit(solution)/shard_map/all_to_all | solution.py:394
  131.2 1.2 copy-done.5
  132.4 0.9 copy-done.7
  133.3 0.9 copy-done.9
  134.3 4.8 %attention_0.1 = bf16[128,4096]{1,0:T(8,128)(2,1)} custom-call(s32[128,1]{1,0:T(8,128)S(1)} %copy.27.seg_q_ref, s32[1,384]{1,0:T(1,128)S(1)} %broadcast_in_dim.25.seg_k_ref, bf16[128,4096]{1,0:T(8,128)(2,1)S(1)} %bitcast.27, bf16[128,1024]{1,0:T(8,128)(2,1)S(1)} %copy-done.7, bf16[128,1024]{1,0:T(8,128)(2,1)S(1)} %copy-done.7, ...), custom_call_target="tpu_custom_call" | custom-call | flops 805306368 | bytes 2097152 | tf_op jit(solution)/shard_map/attention_0/pallas_call | solution.py:73
  139.0 2.8 %all-to-all-done.4.refs_0_ = bf16[4,128,1280]{2,1,0:T(8,128)(2,1)S(1)} async-done(((bf16[4,128,1280]{2,1,0:T(8,128)(2,1)}), bf16[4,128,1280]{2,1,0:T(8,128)(2,1)S(1)}, u32[]{:S(2)}, u32[]{:S(2)}) %all-to-all-start.4) | async-done | bytes 1310752 | tf_op jit(solution)/shard_map/all_to_all | solution.py:394
  141.8 1.6 %copy-done.3 = bf16[1,128,8192]{2,1,0:T(8,128)(2,1)S(1)} copy-done((bf16[1,128,8192]{2,1,0:T(8,128)(2,1)S(1)}, bf16[1,128,8192]{2,1,0:T(8,128)(2,1)}, u32[]{:S(2)}) %copy-start.3) | copy-done | bytes 2097176
  143.4 2.5 %gate.1 = bf16[128,8192]{1,0:T(8,128)(2,1)} custom-call(bf16[128,8192]{1,0:T(8,128)(2,1)S(1)} %bitcast.25, bf16[4,128,1280]{2,1,0:T(8,128)(2,1)S(1)} %all-to-all-done.4.refs_0_, bf16[4,128,768]{2,1,0:T(8,128)(2,1)S(1)} %all_to_all.26.refs_1_), custom_call_target="tpu_custom_call" | custom-call | flops 4194304 | bytes 6291456 | tf_op jit(solution)/shard_map/gate/pallas_call | solution.py:375
  (50 shorter events, 7.7 us)
Async XLA Ops:
  7.2 1.3 copy-start
  7.2 36.4 %all-gather.5.cloned.1.call-start = ((), (), s32[]{:S(2)}) async-start(), calls=%async_computation.5 | async-start | bytes 2506752 | tf_op jit(solution)/shard_map/all_gather | solution.py:437
  9.2 1.6 %copy-start.4 = (bf16[1,128,8192]{2,1,0:T(8,128)(2,1)S(1)}, bf16[1,128,8192]{2,1,0:T(8,128)(2,1)}, u32[]{:S(2)}) copy-start(bf16[1,128,8192]{2,1,0:T(8,128)(2,1)} %param.16) | copy-start | bytes 6291460
  11.1 1.3 copy-start.1
  12.5 5.3 %copy-start.14 = (s32[1,512]{1,0:T(1,128)S(1)}, s32[1,512]{1,0:T(1,128)}, u32[]{:S(2)}) copy-start(s32[1,512]{1,0:T(1,128)} %param.18) | copy-start | bytes 6148
  12.5 5.4 %copy-start.15 = (f32[8192]{0:T(1024)S(1)}, f32[8192]{0:T(1024)}, u32[]{:S(2)}) copy-start(f32[8192]{0:T(1024)} %param.25) | copy-start | bytes 98308
  12.5 6.0 %copy-start.16 = (f32[8192]{0:T(1024)S(1)}, f32[8192]{0:T(1024)}, u32[]{:S(2)}) copy-start(f32[8192]{0:T(1024)} %param.20) | copy-start | bytes 98308
  12.5 11.0 %copy-start.13 = (f32[4,8192]{1,0:T(4,128)S(1)}, f32[4,8192]{1,0:T(4,128)}, u32[]{:S(2)}) copy-start(f32[4,8192]{1,0:T(4,128)} %param.19) | copy-start | bytes 393220
  12.5 30.2 %all-to-all-start = ((bf16[4,128,2048]{2,1,0:T(8,128)(2,1)}), bf16[4,128,2048]{2,1,0:T(8,128)(2,1)S(1)}, u32[]{:S(2)}, u32[]{:S(2)}) async-start(bf16[4,128,2048]{2,1,0:T(8,128)(2,1)} %copy-done.1), calls=%async_computation | async-start | bytes 4194304 | tf_op jit(solution)/shard_map/all_to_all | solution.py:394
  17.8 62.1 %all-gather.7.cloned.1.call-start = ((), (), s32[]{:S(2)}) async-start(), calls=%async_computation.6 | async-start | bytes 2359296 | tf_op jit(solution)/shard_map/all_gather | solution.py:437
  43.5 1.6 %copy-start.2 = (bf16[4352,256]{1,0:T(8,128)(2,1)S(1)}, bf16[4352,256]{1,0:T(8,128)(2,1)}, u32[]{:S(2)}) copy-start(bf16[4352,256]{1,0:T(8,128)(2,1)} %all-gather.5.cloned.1.call-done) | copy-start | bytes 6684676
  45.2 0.9 copy-start.10
  50.4 1.3 copy-start.11
  65.6 14.3 %all-to-all-start.2 = ((bf16[4,128,640]{2,1,0:T(8,128)(2,1)}), bf16[4,128,640]{2,1,0:T(8,128)(2,1)S(1)}, u32[]{:S(2)}, u32[]{:S(2)}) async-start(bf16[4,128,640]{2,1,0:T(8,128)(2,1)} %normalise.1), calls=%async_computation.2 | async-start | bytes 1310720 | tf_op jit(solution)/shard_map/all_to_all | solution.py:394
  69.1 42.9 %collective-permute-start = (bf16[128,1024]{1,0:T(8,128)(2,1)S(1)}, bf16[128,1024]{1,0:T(8,128)(2,1)S(1)}, u32[]{:S(2)}, u32[]{:S(2)}) collective-permute-start(bf16[128,1024]{1,0:T(8,128)(2,1)S(1)} %pad_maximum_fusion.refs_4_.refs_5_), channel_id=1, source_target_pairs={{0,16},{8,24},{1,17},{9,25},{2,18},{10,26},{3,19},{11,27},{4,20},{... | collective-permute-start | bytes 786440 | tf_op jit(solution)/shard_map/ppermute | solution.py:390
  73.0 39.1 %collective-permute-start.1 = (bf16[128,1024]{1,0:T(8,128)(2,1)S(1)}, bf16[128,1024]{1,0:T(8,128)(2,1)S(1)}, u32[]{:S(2)}, u32[]{:S(2)}) collective-permute-start(bf16[128,1024]{1,0:T(8,128)(2,1)S(1)} %pad_maximum_fusion.refs_4_.refs_5_), channel_id=1, source_target_pairs={{0,8},{8,16},{16,24},{1,9},{9,17},{17,25},{2,10},{10,18},{18,26},{... | collective-permute-start | bytes 786440 | tf_op jit(solution)/shard_map/ppermute | solution.py:390
  79.9 0.9 copy-start.12
  112.0 15.4 %copy-start.6 = (bf16[128,1024]{1,0:T(8,128)(2,1)}, bf16[128,1024]{1,0:T(8,128)(2,1)S(1)}, u32[]{:S(2)}) copy-start(bf16[128,1024]{1,0:T(8,128)(2,1)S(1)} %collective-permute-done.refs_0_.refs_1_) | copy-start | bytes 786436
  112.1 15.4 %copy-start.8 = (bf16[128,1024]{1,0:T(8,128)(2,1)}, bf16[128,1024]{1,0:T(8,128)(2,1)S(1)}, u32[]{:S(2)}) copy-start(bf16[128,1024]{1,0:T(8,128)(2,1)S(1)} %collective-permute-done.1.refs_2_.refs_3_) | copy-start | bytes 786436
  127.5 14.3 %all-to-all-start.4 = ((bf16[4,128,1280]{2,1,0:T(8,128)(2,1)}), bf16[4,128,1280]{2,1,0:T(8,128)(2,1)S(1)}, u32[]{:S(2)}, u32[]{:S(2)}) async-start(bf16[4,128,1280]{2,1,0:T(8,128)(2,1)} %state_scan_0.1), calls=%async_computation.4 | async-start | bytes 2621440 | tf_op jit(solution)/shard_map/all_to_all | solution.py:394
  131.2 1.2 copy-start.5
  132.4 0.9 copy-start.7
  133.3 0.9 copy-start.9
  141.8 1.6 %copy-start.3 = (bf16[1,128,8192]{2,1,0:T(8,128)(2,1)S(1)}, bf16[1,128,8192]{2,1,0:T(8,128)(2,1)}, u32[]{:S(2)}) copy-start(bf16[1,128,8192]{2,1,0:T(8,128)(2,1)} %param.17) | copy-start | bytes 6291460
Sparse Core Ops, SparseCore 0:
  9.7 32.9 all-gather.4
  44.2 28.5 all-gather.6

commit v8 on v7

--- a/solution.py
+++ b/solution.py
@@ -99,28 +99,27 @@
             out_ref[piece, :, slot * width : (slot + 1) * width] = x_ref[:, piece_lanes(slot, piece, ctx, fold, width)]
 
 
-def pack(value, ctx, fold, width):
+def pack(value, ctx, fold, width, half):
     rows, channels = value.shape
-    part = min(rows, 32)
+    channels = channels // 2
+    part = min(rows, 64)
     return pl.pallas_call(
         functools.partial(pack_kernel, fold, width),
         grid=(rows // part,),
-        in_specs=[pl.BlockSpec((part, channels), lambda r: (r, 0))],
+        in_specs=[pl.BlockSpec((part, channels), lambda r: (r, half))],
         out_specs=pl.BlockSpec((ctx, part, channels // ctx), lambda r: (0, r, 0)),
         out_shape=jax.ShapeDtypeStruct((ctx, rows, channels // ctx), value.dtype),
         compiler_params=pltpu.CompilerParams(vmem_limit_bytes=12 << 20),
-        name="pack",
+        name=f"pack_{half}",
     )(value)
 
 
-def conv_select_kernel(seg_ref, x_ref, weight_ref, bias_ref, select_ref, conv_ref, part_ref, masks, padded, total):
-    step = pl.program_id(0)
+def convolve(seg_ref, x_ref, weight_ref, bias_ref, masks, padded):
     toks = seg_ref.shape[0]
     pieces, rows, wide = x_ref.shape
     tiles = wide // LANES
-    slots, outputs, width = select_ref.shape
-
-    @pl.when(step == 0)
+
+    @pl.when(pl.program_id(0) == 0)
     def _():
         wide_seg = jnp.broadcast_to(seg_ref[...], (toks, LANES)).astype(jnp.float32)
         padded[0, 0:SUBLANES, :] = jnp.full((SUBLANES, LANES), -1.0, jnp.float32)
@@ -130,7 +129,6 @@
             masks[tap] = jnp.where(before == wide_seg, 1.0, 0.0)
         for tile in range(tiles):
             padded[tile, 0:SUBLANES, :] = jnp.zeros((SUBLANES, LANES), jnp.float32)
-        total[...] = jnp.zeros_like(total)
 
     outs = []
     for tile in range(tiles):
@@ -143,12 +141,39 @@
             moved = padded[tile, SUBLANES - 3 + tap : SUBLANES - 3 + tap + toks, :]
             term = (0.5 * weight_ref[tap : tap + 1, lanes]) * moved
             half = half + (term * masks[tap] if tap < 3 else term)
-        conv = (half + half * jnp.tanh(half)).astype(jnp.bfloat16)
-        conv_ref[:, lanes] = conv
-        outs.append(conv)
-    conv = jnp.concatenate(outs, axis=1)
-    select = jnp.concatenate([select_ref[slot] for slot in range(slots)], axis=1)
-    total[...] += lax.dot_general(conv, select, (((1,), (1,)), ((), ())), preferred_element_type=jnp.float32)
+        outs.append((half + half * jnp.tanh(half)).astype(jnp.bfloat16))
+    return outs
+
+
+def conv_kernel(seg_ref, x_ref, weight_ref, bias_ref, conv_ref, masks, padded):
+    for tile, conv in enumerate(convolve(seg_ref, x_ref, weight_ref, bias_ref, masks, padded)):
+        conv_ref[:, tile * LANES : (tile + 1) * LANES] = conv
+
+
+def conv_select_kernel(seg_ref, x_ref, weight_ref, bias_ref, early_ref, early_select_ref, select_ref,
+                       conv_ref, part_ref, masks, padded, total):
+    step = pl.program_id(0)
+    pieces, rows, _ = x_ref.shape
+    slots, outputs, _ = select_ref.shape
+
+    def product(conv, select_ref):
+        select = jnp.concatenate([select_ref[slot] for slot in range(slots)], axis=1)
+        return lax.dot_general(conv, select, (((1,), (1,)), ((), ())), preferred_element_type=jnp.float32)
+
+    early = product(early_ref[...], early_select_ref)
+
+    @pl.when(step == 0)
+    def _():
+        total[...] = early
+
+    @pl.when(step > 0)
+    def _():
+        total[...] += early
+
+    outs = convolve(seg_ref, x_ref, weight_ref, bias_ref, masks, padded)
+    for tile, conv in enumerate(outs):
+        conv_ref[:, tile * LANES : (tile + 1) * LANES] = conv
+    total[...] += product(jnp.concatenate(outs, axis=1), select_ref)
 
     @pl.when(step == pl.num_programs(0) - 1)
     def _():
@@ -158,44 +183,76 @@
             part_ref[piece, :, outputs:] = jnp.zeros((rows, spare), part_ref.dtype)
 
 
-def conv_select(seg_col, pieces, conv_weight, conv_bias, select_parts):
+CONV_BATCH = 2
+
+
+def conv_specs(seg_col, pieces, width, half, steps):
+    ctx, rows, _ = pieces.shape
+    wide = CONV_BATCH * width
+    toks = ctx * rows
+    in_specs = [
+        pl.BlockSpec(seg_col.shape, lambda s: (0, 0)),
+        pl.BlockSpec((ctx, rows, wide), lambda s: (0, 0, s)),
+        pl.BlockSpec((4, wide), lambda s: (0, half * steps + s)),
+        pl.BlockSpec((1, wide), lambda s: (0, half * steps + s)),
+    ]
+    scratch = [
+        pltpu.VMEM((3, toks, LANES), jnp.float32),
+        pltpu.VMEM((wide // LANES, SUBLANES + toks, LANES), jnp.float32),
+    ]
+    return in_specs, pl.BlockSpec((toks, wide), lambda s: (0, s)), scratch
+
+
+def conv_early(seg_col, pieces, conv_weight, conv_bias, width):
+    toks = seg_col.shape[0]
+    columns = pieces.shape[2]
+    steps = columns // (CONV_BATCH * width)
+    in_specs, out_spec, scratch = conv_specs(seg_col, pieces, width, 0, steps)
+    return pl.pallas_call(
+        conv_kernel,
+        grid=(steps,),
+        in_specs=in_specs,
+        out_specs=out_spec,
+        scratch_shapes=scratch,
+        out_shape=jax.ShapeDtypeStruct((toks, columns), jnp.bfloat16),
+        compiler_params=pltpu.CompilerParams(vmem_limit_bytes=24 << 20),
+        cost_estimate=pl.CostEstimate(
+            flops=16 * pieces.size, bytes_accessed=4 * pieces.size, transcendentals=pieces.size
+        ),
+        name="conv_early",
+    )(seg_col, pieces, conv_weight, conv_bias)
+
+
+def conv_select(seg_col, pieces, conv_weight, conv_bias, early, select_parts):
     slots, outputs, width = select_parts.shape
-    ctx, rows, _ = pieces.shape
+    ctx, rows, columns = pieces.shape
     toks = ctx * rows
     padded_outputs = -(-outputs // LANES) * LANES
-    batch = 4
-    wide = batch * width
+    steps = columns // (CONV_BATCH * width)
+    in_specs, out_spec, scratch = conv_specs(seg_col, pieces, width, 1, steps)
     return pl.pallas_call(
         conv_select_kernel,
-        grid=(slots // batch,),
-        in_specs=[
-            pl.BlockSpec((toks, 1), lambda s: (0, 0)),
-            pl.BlockSpec((ctx, rows, wide), lambda s: (0, 0, s)),
-            pl.BlockSpec((4, wide), lambda s: (0, s)),
-            pl.BlockSpec((1, wide), lambda s: (0, s)),
-            pl.BlockSpec((batch, outputs, width), lambda s: (s, 0, 0)),
+        grid=(steps,),
+        in_specs=in_specs
+        + [
+            pl.BlockSpec((toks, CONV_BATCH * width), lambda s: (0, s)),
+            pl.BlockSpec((CONV_BATCH, outputs, width), lambda s: (s, 0, 0)),
+            pl.BlockSpec((CONV_BATCH, outputs, width), lambda s: (steps + s, 0, 0)),
         ],
-        out_specs=[
-            pl.BlockSpec((toks, wide), lambda s: (0, s)),
-            pl.BlockSpec((ctx, rows, padded_outputs), lambda s: (0, 0, 0)),
-        ],
-        scratch_shapes=[
-            pltpu.VMEM((3, toks, LANES), jnp.float32),
-            pltpu.VMEM((wide // LANES, SUBLANES + toks, LANES), jnp.float32),
-            pltpu.VMEM((toks, outputs), jnp.float32),
-        ],
+        out_specs=[out_spec, pl.BlockSpec((ctx, rows, padded_outputs), lambda s: (0, 0, 0))],
+        scratch_shapes=scratch + [pltpu.VMEM((toks, outputs), jnp.float32)],
         out_shape=[
-            jax.ShapeDtypeStruct((toks, slots * width), jnp.bfloat16),
+            jax.ShapeDtypeStruct((toks, columns), jnp.bfloat16),
             jax.ShapeDtypeStruct((ctx, rows, padded_outputs), jnp.bfloat16),
         ],
-        compiler_params=pltpu.CompilerParams(vmem_limit_bytes=32 << 20),
+        compiler_params=pltpu.CompilerParams(vmem_limit_bytes=24 << 20),
         cost_estimate=pl.CostEstimate(
             flops=2 * toks * slots * width * outputs,
-            bytes_accessed=2 * pieces.size * 2 + 2 * select_parts.size,
+            bytes_accessed=6 * pieces.size + 2 * select_parts.size,
             transcendentals=pieces.size,
         ),
         name="conv_select",
-    )(seg_col, pieces, conv_weight, conv_bias, select_parts)
+    )(seg_col, pieces, conv_weight, conv_bias, early, select_parts, select_parts)
 
 
 def normalise_kernel(rank, part_ref, out_ref):
@@ -221,18 +278,38 @@
     )(parts)
 
 
-def scan_kernel(rank, first_shard, reset_ref, low_ref, weight_hbm, bias_ref, decay_ref, gain_ref, conv_hbm, out_ref,
-                weight_ref, conv_ref, sems, in_cols, out_diag, delta_rows, drive_rows, held_even, held_odd):
-    toks = reset_ref.shape[0]
+def scan_kernel(rank, first_shard, reset_hbm, low_hbm, weight_hbm, bias_ref, decay_ref, gain_ref,
+                conv_early_hbm, conv_late_hbm, out_ref, reset_ref, low_ref, weight_ref, conv_ref, sems, in_cols, out_diag, delta_rows, drive_rows, held_even, held_odd):
+    toks = low_ref.shape[0]
     states = decay_ref.shape[0]
     shards = weight_ref.shape[0]
     width = weight_ref.shape[2]
     tiles = shards * width // LANES
     column = first_shard * width
-    weight_copy = pltpu.make_async_copy(weight_hbm.at[pl.ds(first_shard, shards)], weight_ref, sems.at[0])
-    conv_copy = pltpu.make_async_copy(conv_hbm.at[:, pl.ds(column, shards * width)], conv_ref, sems.at[1])
-    weight_copy.start()
-    conv_copy.start()
+    low_copy = pltpu.make_async_copy(low_hbm, low_ref, sems.at[0])
+    low_copy.start()
+    copies = [
+        pltpu.make_async_copy(weight_hbm.at[pl.ds(first_shard, shards)], weight_ref, sems.at[1]),
+        pltpu.make_async_copy(reset_hbm, reset_ref, sems.at[2]),
+    ]
+    middle = conv_early_hbm.shape[1]
+    end = column + shards * width
+    for source, start, low_end, high_end in (
+        (conv_early_hbm, 0, column, min(end, middle)),
+        (conv_late_hbm, middle, max(column, middle), end),
+    ):
+        if low_end < high_end:
+            size = high_end - low_end
+            copies.append(
+                pltpu.make_async_copy(
+                    source.at[:, pl.ds(low_end - start, size)],
+                    conv_ref.at[:, pl.ds(low_end - column, size)],
+                    sems.at[1 + len(copies)],
+                )
+            )
+    for copy in copies:
+        copy.start()
+    low_copy.wait()
     rows = out_ref.shape[1]
     block = 16
     span = block * states
@@ -242,18 +319,18 @@
     bits = states.bit_length() - 1
     lane = lax.broadcasted_iota(jnp.int32, (states, span), 1)
     spread = jnp.where((lane & (states - 1)) == lax.broadcasted_iota(jnp.int32, (states, span), 0), 1.0, 0.0)
-    copies = jnp.dot(
+    spread_out = jnp.dot(
         low_ref[:, rank + states : rank + 2 * states], spread.astype(jnp.bfloat16), preferred_element_type=jnp.float32
     )
     here = lax.shift_right_logical(lax.broadcasted_iota(jnp.int32, (block, span), 1), bits)
     there = lax.broadcasted_iota(jnp.int32, (block, span), 0)
     keep = jnp.where(here == there, 1.0, 0.0)
-    out_diag[...] = (copies.reshape(count, block, span) * keep[None]).reshape(toks, span).astype(jnp.bfloat16)
-
+    out_diag[...] = (spread_out.reshape(count, block, span) * keep[None]).reshape(toks, span).astype(jnp.bfloat16)
+
+    for copy in copies:
+        copy.wait()
     reset = jnp.broadcast_to(reset_ref[...], (toks, LANES))
     low = low_ref[:, 0:rank]
-    weight_copy.wait()
-    conv_copy.wait()
     for shard in range(shards):
         pre = jnp.dot(low, weight_ref[shard], preferred_element_type=jnp.float32)
         for part in range(width // LANES):
@@ -314,7 +391,7 @@
         finish(count - 1, held_odd, part)
 
 
-def state_scan(reset_col, low, delta_parts, bias, decay, gain, conv, ctx, first_shard, shards):
+def state_scan(reset_col, low, delta_parts, bias, decay, gain, convs, ctx, first_shard, shards):
     toks = low.shape[0]
     rank, width = delta_parts.shape[1:]
     states = decay.shape[0]
@@ -322,23 +399,18 @@
     wide = shards * width
     steps = toks * wide * states
     whole = pl.BlockSpec(memory_space=pltpu.VMEM)
+    left = pl.BlockSpec(memory_space=pl.ANY)
     return pl.pallas_call(
         functools.partial(scan_kernel, rank, first_shard),
-        in_specs=[
-            whole,
-            whole,
-            pl.BlockSpec(memory_space=pl.ANY),
-            whole,
-            whole,
-            whole,
-            pl.BlockSpec(memory_space=pl.ANY),
-        ],
+        in_specs=[left, left, left, whole, whole, whole, left, left],
         out_specs=whole,
         out_shape=jax.ShapeDtypeStruct((ctx, rows, wide), jnp.bfloat16),
         scratch_shapes=[
+            pltpu.VMEM(reset_col.shape, reset_col.dtype),
+            pltpu.VMEM(low.shape, low.dtype),
             pltpu.VMEM((shards, rank, width), jnp.bfloat16),
             pltpu.VMEM((toks, wide), jnp.bfloat16),
-            pltpu.SemaphoreType.DMA((2,)),
+            pltpu.SemaphoreType.DMA((5,)),
             pltpu.VMEM((states, toks), jnp.float32),
             pltpu.VMEM((toks, 16 * states), jnp.bfloat16),
             pltpu.VMEM((toks // 16, wide // LANES, 16, LANES), jnp.float32),
@@ -351,7 +423,7 @@
             flops=6 * steps, bytes_accessed=2 * shards * rank * width + 4 * toks * wide, transcendentals=steps
         ),
         name=f"state_scan_{first_shard}",
-    )(reset_col, low, delta_parts, bias, decay, gain, conv)
+    )(reset_col, low, delta_parts, bias, decay, gain, *convs)
 
 
 def gate_kernel(fold, width, gate_ref, *refs):
@@ -441,7 +513,7 @@
         return parts
 
     select_parts = gathered(own_columns(select_weight))
-    packed = pack(mixer_input[0], ctx, fold, width)
+    packed = [pack(mixer_input[0], ctx, fold, width, half) for half in range(2)]
 
     same = jnp.concatenate([jnp.zeros((1,), bool), seg[1:] == seg[:-1]])
     reset_col = jnp.where(same, 0.0, FAR)[:, None]
@@ -460,27 +532,28 @@
         seg_col,
         own_columns(delta_weight),
     )
-    pieces, own = lax.optimization_barrier((exchange(packed), own))
+    early_pieces, own = lax.optimization_barrier((exchange(packed[0]), own))
+    late_pieces = exchange(packed[1])
     bias, decay, gain, reset_col, seg_q, seg_k, both, conv_weight, conv_bias, seg_col, delta_own = own
     delta_parts = gathered(delta_own)
 
-    conv, parts = conv_select(seg_col, pieces, conv_weight, conv_bias, select_parts)
+    early = conv_early(seg_col, early_pieces, conv_weight, conv_bias, width)
+    late, parts = conv_select(seg_col, late_pieces, conv_weight, conv_bias, early, select_parts)
     low = normalise(exchange(parts), rank)
 
     low, both = lax.optimization_barrier((low, both))
     blocks = [shifted(both, "ctx", by) for by in range(back, 0, -1)] + [both]
     low = exchange(low).reshape(toks, low.shape[2])
 
-    early = slots * 5 // 8
-    scanned = []
-    for first, count in ((0, early), (early, slots - early)):
-        if scanned:
-            low, scanned[-1] = lax.optimization_barrier((low, scanned[-1]))
-        scanned.append(state_scan(reset_col, low, delta_parts, bias, decay, gain, conv, ctx, first, count))
-    scanned[-1], blocks = lax.optimization_barrier((scanned[-1], blocks))
+    split = slots * 5 // 8
+    scanned = [
+        state_scan(reset_col, low, delta_parts, bias, decay, gain, (early, late), ctx, first, count)
+        for first, count in ((0, split), (split, slots - split))
+    ]
+    scanned[0], blocks = lax.optimization_barrier((scanned[0], blocks))
     attended = attention(queries[0], blocks, seg_q, seg_k, 0, KEY_VALUE_HEADS)
     scanned = [exchange(part) for part in scanned]
-    scanned[-1], attended = lax.optimization_barrier((scanned[-1], attended))
+    scanned[0], attended = lax.optimization_barrier((scanned[0], attended))
     mixed = apply_gate(scanned, gate_input[0], fold, width)
     return (attended[None], mixed[None])
 

time: 154 us -> 147 us (0.955)
  blocking collectives: 28.3 us -> 11.8 us
  starting transfers between devices: 19.7 us -> 30.1 us
  Pallas kernels: 44.2 us -> 49.2 us
  local copies, waits for them, and re-layouts: 26.4 us -> 22.1 us
  waiting for transfers between devices: 17.3 us -> 15.6 us
    all_to_all x2 -> x1, blocking collectives: 28.3 us -> 11.8 us  [exchange(): return lax.all_to_all(value, 'ctx', 0, 0, tiled=True)]
    all_to_all x3 -> x5, starting transfers between devices: 12.3 us -> 22.8 us  [exchange(): return lax.all_to_all(value, 'ctx', 0, 0, tiled=True)]
    pallas_call x1 -> x2, Pallas kernels: 4.31 us -> 7.44 us  [the longest x1 4.33 us: conv_select(): pl.pallas_call(conv_select_kernel, grid=(steps,), in_specs=in_specs + [pl...]
    all_to_all x3 -> x5, waiting for transfers between devices: 17.3 us -> 15.5 us  [exchange(): return lax.all_to_all(value, 'ctx', 0, 0, tiled=True)]
    unnamed x36 -> x42, local copies, waits for them, and re-layouts: 14.3 us -> 13.2 us
  transfers between devices with their start and end apart: 7 -> 9, of which waited for: 3 -> 3; matrix products, arithmetic and copies ran while one was open for 10% -> 8% of each run, Pallas kernels for 27% -> 32%
where the time goes in v8:
time: 147 us; the launch traced here: 146 us
  Pallas kernels  49.2 us (33%)
  starting transfers between devices  30.1 us (20%)
  local copies, waits for them, and re-layouts  22.1 us (15%)
  waiting for transfers between devices  15.6 us (11%)
  between operations  14.3 us (10%)
  blocking collectives  11.8 us (8%)
  other arithmetic  2.57 us (2%)
    pallas_call x2, Pallas kernels, state_scan(): pl.pallas_call(functools.partial(scan_kernel, rank, first_shard), in_spec...  32.1 us
    all_to_all x5, starting transfers between devices, exchange(): return lax.all_to_all(value, 'ctx', 0, 0, tiled=True)  22.8 us
    all_to_all x5, waiting for transfers between devices, exchange(): return lax.all_to_all(value, 'ctx', 0, 0, tiled=True)  15.5 us
    unnamed x42, local copies, waits for them, and re-layouts  13.2 us
    all_to_all x1, blocking collectives, exchange(): return lax.all_to_all(value, 'ctx', 0, 0, tiled=True)  11.8 us
    ppermute x2, starting transfers between devices, shifted(): return lax.ppermute(value, axis, pairs)  7.27 us
    pallas_call x1, Pallas kernels, attention(): pl.pallas_call(functools.partial(attention_kernel, begin), grid=(end - be...  4.77 us
    pallas_call x1, Pallas kernels, conv_select(): pl.pallas_call(conv_select_kernel, grid=(steps,), in_specs=in_specs + [pl...  4.33 us
  transfers between devices with their start and end apart: 9, of which 3 were waited for; matrix products, arithmetic and copies ran while one was open for 8% of the time, Pallas kernels for 32%

profile of v8, /device:TPU:0, one launch (start us, length us, event | category | flops | bytes accessed | tf_op | source)
XLA Modules:
  0.0 145.7 jit_solution(13423175707399517918)
XLA Ops:
  7.2 1.2 copy-done
  9.2 1.6 %copy-done.2 = bf16[1,128,8192]{2,1,0:T(8,128)(2,1)S(1)} copy-done((bf16[1,128,8192]{2,1,0:T(8,128)(2,1)S(1)}, bf16[1,128,8192]{2,1,0:T(8,128)(2,1)}, u32[]{:S(2)}) %copy-start.2) | copy-done | bytes 2097176
  10.8 1.1 pack_0.1
  11.9 5.3 %all-to-all-start = ((bf16[4,128,1024]{2,1,0:T(8,128)(2,1)}), bf16[4,128,1024]{2,1,0:T(8,128)(2,1)}, u32[]{:S(2)}, u32[]{:S(2)}) async-start(bf16[4,128,1024]{2,1,0:T(8,128)(2,1)} %pack_0.1), calls=%async_computation | async-start | bytes 2097152 | tf_op jit(solution)/shard_map/all_to_all | solution.py:466
  17.4 2.3 %reshape.75 = f32[16,8,1,4,256]{4,3,1,0,2:T(4,128)} reshape(f32[16,8192]{1,0:T(8,128)} %bitcast.38) | data formatting | bytes 1048576 | tf_op jit(solution)/shard_map/reshape | solution.py:500
  19.7 1.4 dynamic-slice_reduce_fusion
  24.3 1.7 %constant_dynamic-slice_fusion.1 = bf16[512,256]{1,0:T(8,128)(2,1)} fusion(bf16[512,1024]{1,0:T(8,128)(2,1)} %param.22, s32[]{:T(128)S(6)} %select_n.60), kind=kLoop, calls=%fused_computation.8 | loop fusion | bytes 524292 | tf_op jit(solution)/shard_map/dynamic_slice | solution.py:506
  26.0 1.7 %pad_maximum_fusion.refs_4_.refs_5_ = bf16[128,1024]{1,0:T(8,128)(2,1)} fusion(bf16[128,512]{1,0:T(8,128)(2,1)} %bitcast.43, bf16[128,512]{1,0:T(8,128)(2,1)} %bitcast.44), kind=kLoop, calls=%fused_computation | loop fusion | flops 524288 | bytes 524288 | tf_op jit(solution)/shard_map/concatenate | solution.py:529
  28.4 3.1 %all-to-all-done.x_ref = bf16[4,128,1024]{2,1,0:T(8,128)(2,1)} async-done(((bf16[4,128,1024]{2,1,0:T(8,128)(2,1)}), bf16[4,128,1024]{2,1,0:T(8,128)(2,1)}, u32[]{:S(2)}, u32[]{:S(2)}) %all-to-all-start) | async-done | bytes 1048608 | tf_op jit(solution)/shard_map/all_to_all | solution.py:466
  31.9 1.0 copy-done.4
  32.8 3.5 %all-to-all-start.1 = ((bf16[4,128,1024]{2,1,0:T(8,128)(2,1)}), bf16[4,128,1024]{2,1,0:T(8,128)(2,1)S(1)}, u32[]{:S(2)}, u32[]{:S(2)}) async-start(bf16[4,128,1024]{2,1,0:T(8,128)(2,1)} %copy-done.4), calls=%async_computation.1 | async-start | bytes 2097152 | tf_op jit(solution)/shard_map/all_to_all | solution.py:466
  36.5 3.1 %conv_early.1.early_ref.conv_early_hbm = bf16[512,1024]{1,0:T(8,128)(2,1)S(1)} custom-call(s32[512,1]{1,0:T(8,128)S(1)} %copy.28.seg_ref, bf16[4,128,1024]{2,1,0:T(8,128)(2,1)} %all-to-all-done.x_ref, f32[4,2048]{1,0:T(4,128)S(1)} %bitcast.30, f32[1,2048]{1,0:T(1,128)S(1)} %bitcast.32), custom_call_target="tpu_custom_call" | custom-call | flops 8388608 | bytes 2097152 | tf_op jit(solution)/shard_map/conv_early/pallas_call | solution.py:211
  39.7 10.0 %all-to-all-done.1.x_ref = bf16[4,128,1024]{2,1,0:T(8,128)(2,1)S(1)} async-done(((bf16[4,128,1024]{2,1,0:T(8,128)(2,1)}), bf16[4,128,1024]{2,1,0:T(8,128)(2,1)S(1)}, u32[]{:S(2)}, u32[]{:S(2)}) %all-to-all-start.1) | async-done | bytes 1048608 | tf_op jit(solution)/shard_map/all_to_all | solution.py:466
  49.7 1.7 %copy-done.1 = bf16[4352,256]{1,0:T(8,128)(2,1)S(1)} copy-done((bf16[4352,256]{1,0:T(8,128)(2,1)S(1)}, bf16[4352,256]{1,0:T(8,128)(2,1)}, u32[]{:S(2)}) %copy-start.1) | copy-done | bytes 2228248
  51.4 4.3 %conv_select.1 = (bf16[512,1024]{1,0:T(8,128)(2,1)S(1)}, bf16[4,128,640]{2,1,0:T(8,128)(2,1)S(1)}) custom-call(s32[512,1]{1,0:T(8,128)S(1)} %copy.28.seg_ref, bf16[4,128,1024]{2,1,0:T(8,128)(2,1)S(1)} %all-to-all-done.1.x_ref, f32[4,2048]{1,0:T(4,128)S(1)} %bitcast.31, f32[1,2048]{1,0:T(1,128)S(1)} %bitcast.33, ...), custom_call_target="tpu_custom_call" | custom-call | flops 1140850688 | bytes 5373952 | tf_op jit(solution)/shard_map/conv_select/pallas_call | solution.py:233
  55.8 11.8 %all_to_all.30.part_ref = bf16[4,128,640]{2,1,0:T(8,128)(2,1)S(1)} all-to-all(bf16[4,128,640]{2,1,0:T(8,128)(2,1)S(1)} %get-tuple-element.29), channel_id=1, replica_groups=mesh['ctx'=4,'rep'=8] {'ctx'}, dimensions={0} | all-to-all | bytes 1310720 | tf_op jit(solution)/shard_map/all_to_all | solution.py:466
  67.6 1.0 normalise.1
  68.6 3.5 %all-to-all-start.3 = ((bf16[4,128,640]{2,1,0:T(8,128)(2,1)}), bf16[4,128,640]{2,1,0:T(8,128)(2,1)S(1)}, u32[]{:S(2)}, u32[]{:S(2)}) async-start(bf16[4,128,640]{2,1,0:T(8,128)(2,1)} %normalise.1), calls=%async_computation.3 | async-start | bytes 1310720 | tf_op jit(solution)/shard_map/all_to_all | solution.py:466
  72.1 3.9 %collective-permute-start = (bf16[128,1024]{1,0:T(8,128)(2,1)S(1)}, bf16[128,1024]{1,0:T(8,128)(2,1)S(1)}, u32[]{:S(2)}, u32[]{:S(2)}) collective-permute-start(bf16[128,1024]{1,0:T(8,128)(2,1)S(1)} %copy-done.6), channel_id=1, source_target_pairs={{0,16},{8,24},{1,17},{9,25},{2,18},{10,26},{3,19},{11,27},{4,20},{... | collective-permute-start | bytes 786440 | tf_op jit(solution)/shard_map/ppermute | solution.py:462
  76.0 3.4 %collective-permute-start.1 = (bf16[128,1024]{1,0:T(8,128)(2,1)S(1)}, bf16[128,1024]{1,0:T(8,128)(2,1)S(1)}, u32[]{:S(2)}, u32[]{:S(2)}) collective-permute-start(bf16[128,1024]{1,0:T(8,128)(2,1)S(1)} %copy-done.6), channel_id=1, source_target_pairs={{0,8},{8,16},{16,24},{1,9},{9,17},{17,25},{2,10},{10,18},{18,26},{... | collective-permute-start | bytes 786440 | tf_op jit(solution)/shard_map/ppermute | solution.py:462
  79.4 2.4 %all-to-all-done.3 = bf16[4,128,640]{2,1,0:T(8,128)(2,1)S(1)} async-done(((bf16[4,128,640]{2,1,0:T(8,128)(2,1)}), bf16[4,128,640]{2,1,0:T(8,128)(2,1)S(1)}, u32[]{:S(2)}, u32[]{:S(2)}) %all-to-all-start.3) | async-done | bytes 655392 | tf_op jit(solution)/shard_map/all_to_all | solution.py:466
  81.8 0.9 copy-done.15
  82.7 19.2 %state_scan_0.1 = bf16[4,128,1280]{2,1,0:T(8,128)(2,1)} custom-call(f32[512,1]{1,0:T(8,128)} %broadcast_select_fusion.reset_hbm, bf16[512,640]{1,0:T(8,128)(2,1)} %bitcast.36, bf16[8,512,256]{2,1,0:T(8,128)(2,1)} %bitcast.51, f32[1,2048]{1,0:T(1,128)} %bitcast.47, f32[16,2048]{1,0:T(8,128)} %bitcast.40, f32[1,2048]{1,0:T(1,128)} %bitcast.49, ...), custom_call_target="tpu_custom_call" | custom-call | flops 62914560 | bytes 3932160 | tf_op jit(solution)/shard_map/state_scan_0/pallas_call | solution.py:403
  103.3 6.2 %all-to-all-start.4 = ((bf16[4,128,1280]{2,1,0:T(8,128)(2,1)}), bf16[4,128,1280]{2,1,0:T(8,128)(2,1)S(1)}, u32[]{:S(2)}, u32[]{:S(2)}) async-start(bf16[4,128,1280]{2,1,0:T(8,128)(2,1)} %state_scan_0.1), calls=%async_computation.4 | async-start | bytes 2621440 | tf_op jit(solution)/shard_map/all_to_all | solution.py:466
  109.6 12.9 %state_scan_5.1 = bf16[4,128,768]{2,1,0:T(8,128)(2,1)} custom-call(f32[512,1]{1,0:T(8,128)} %broadcast_select_fusion.reset_hbm, bf16[512,640]{1,0:T(8,128)(2,1)} %bitcast.37, bf16[8,512,256]{2,1,0:T(8,128)(2,1)} %bitcast.52, f32[1,2048]{1,0:T(1,128)} %bitcast.48, f32[16,2048]{1,0:T(8,128)} %bitcast.41, f32[1,2048]{1,0:T(1,128)} %bitcast.50, ...), custom_call_target="tpu_custom_call" | custom-call | flops 37748736 | bytes 2359296 | tf_op jit(solution)/shard_map/state_scan_5/pallas_call | solution.py:403
  122.5 4.2 %all-to-all-start.5 = ((bf16[4,128,768]{2,1,0:T(8,128)(2,1)}), bf16[4,128,768]{2,1,0:T(8,128)(2,1)S(1)}, u32[]{:S(2)}, u32[]{:S(2)}) async-start(bf16[4,128,768]{2,1,0:T(8,128)(2,1)} %state_scan_5.1), calls=%async_computation.5 | async-start | bytes 1572864 | tf_op jit(solution)/shard_map/all_to_all | solution.py:466
  126.8 1.2 copy-done.9
  128.0 0.9 copy-done.11
  129.0 0.9 copy-done.13
  129.9 4.8 %attention_0.1 = bf16[128,4096]{1,0:T(8,128)(2,1)} custom-call(s32[128,1]{1,0:T(8,128)S(1)} %copy.29.seg_q_ref, s32[1,384]{1,0:T(1,128)S(1)} %broadcast_in_dim.25.seg_k_ref, bf16[128,4096]{1,0:T(8,128)(2,1)S(1)} %bitcast.29, bf16[128,1024]{1,0:T(8,128)(2,1)S(1)} %copy-done.11, bf16[128,1024]{1,0:T(8,128)(2,1)S(1)} %copy-done.11, ...), custom_call_target="tpu_custom_call" | custom-call | flops 805306368 | bytes 2097152 | tf_op jit(solution)/shard_map/attention_0/pallas_call | solution.py:73
  134.7 1.6 %copy-done.8 = bf16[1,128,8192]{2,1,0:T(8,128)(2,1)S(1)} copy-done((bf16[1,128,8192]{2,1,0:T(8,128)(2,1)S(1)}, bf16[1,128,8192]{2,1,0:T(8,128)(2,1)}, u32[]{:S(2)}) %copy-start.8) | copy-done | bytes 2097176
  136.3 2.5 %gate.1 = bf16[128,8192]{1,0:T(8,128)(2,1)} custom-call(bf16[128,8192]{1,0:T(8,128)(2,1)S(1)} %bitcast.28, bf16[4,128,1280]{2,1,0:T(8,128)(2,1)S(1)} %all-to-all-done.4.refs_0_, bf16[4,128,768]{2,1,0:T(8,128)(2,1)S(1)} %all-to-all-done.5.refs_1_), custom_call_target="tpu_custom_call" | custom-call | flops 4194304 | bytes 6291456 | tf_op jit(solution)/shard_map/gate/pallas_call | solution.py:447
  (61 shorter events, 7.0 us)
Async XLA Ops:
  7.2 1.3 copy-start
  7.2 42.5 %all-gather.5.cloned.1.call-start = ((), (), s32[]{:S(2)}) async-start(), calls=%async_computation.6 | async-start | bytes 2506752 | tf_op jit(solution)/shard_map/all_gather | solution.py:509
  9.2 1.6 %copy-start.2 = (bf16[1,128,8192]{2,1,0:T(8,128)(2,1)S(1)}, bf16[1,128,8192]{2,1,0:T(8,128)(2,1)}, u32[]{:S(2)}) copy-start(bf16[1,128,8192]{2,1,0:T(8,128)(2,1)} %param.16) | copy-start | bytes 6291460
  10.8 6.4 %copy-start.17 = (s32[1,512]{1,0:T(1,128)S(1)}, s32[1,512]{1,0:T(1,128)}, u32[]{:S(2)}) copy-start(s32[1,512]{1,0:T(1,128)} %param.18) | copy-start | bytes 6148
  10.8 6.5 %copy-start.18 = (f32[8192]{0:T(1024)S(1)}, f32[8192]{0:T(1024)}, u32[]{:S(2)}) copy-start(f32[8192]{0:T(1024)} %param.25) | copy-start | bytes 98308
  10.8 6.5 %copy-start.19 = (f32[8192]{0:T(1024)S(1)}, f32[8192]{0:T(1024)}, u32[]{:S(2)}) copy-start(f32[8192]{0:T(1024)} %param.20) | copy-start | bytes 98308
  11.9 9.9 %copy-start.16 = (f32[4,8192]{1,0:T(4,128)S(1)}, f32[4,8192]{1,0:T(4,128)}, u32[]{:S(2)}) copy-start(f32[4,8192]{1,0:T(4,128)} %param.19) | copy-start | bytes 393220
  11.9 19.6 %all-to-all-start = ((bf16[4,128,1024]{2,1,0:T(8,128)(2,1)}), bf16[4,128,1024]{2,1,0:T(8,128)(2,1)}, u32[]{:S(2)}, u32[]{:S(2)}) async-start(bf16[4,128,1024]{2,1,0:T(8,128)(2,1)} %pack_0.1), calls=%async_computation | async-start | bytes 2097152 | tf_op jit(solution)/shard_map/all_to_all | solution.py:466
  17.2 14.3 %copy-start.3 = (bf16[1,128,8192]{2,1,0:T(8,128)(2,1)S(1)}, bf16[1,128,8192]{2,1,0:T(8,128)(2,1)}, u32[]{:S(2)}) copy-start(bf16[1,128,8192]{2,1,0:T(8,128)(2,1)} %param.16) | copy-start | bytes 6291460
  17.2 62.2 %all-gather.7.cloned.1.call-start = ((), (), s32[]{:S(2)}) async-start(), calls=%async_computation.7 | async-start | bytes 2359296 | tf_op jit(solution)/shard_map/all_gather | solution.py:509
  31.8 1.0 copy-start.4
  32.8 16.9 %all-to-all-start.1 = ((bf16[4,128,1024]{2,1,0:T(8,128)(2,1)}), bf16[4,128,1024]{2,1,0:T(8,128)(2,1)S(1)}, u32[]{:S(2)}, u32[]{:S(2)}) async-start(bf16[4,128,1024]{2,1,0:T(8,128)(2,1)} %copy-done.4), calls=%async_computation.1 | async-start | bytes 2097152 | tf_op jit(solution)/shard_map/all_to_all | solution.py:466
  39.6 16.1 %copy-start.5 = (bf16[512,1024]{1,0:T(8,128)(2,1)}, bf16[512,1024]{1,0:T(8,128)(2,1)S(1)}, u32[]{:S(2)}) copy-start(bf16[512,1024]{1,0:T(8,128)(2,1)S(1)} %conv_early.1.early_ref.conv_early_hbm) | copy-start | bytes 3145732
  49.7 1.7 %copy-start.1 = (bf16[4352,256]{1,0:T(8,128)(2,1)S(1)}, bf16[4352,256]{1,0:T(8,128)(2,1)}, u32[]{:S(2)}) copy-start(bf16[4352,256]{1,0:T(8,128)(2,1)} %all-gather.5.cloned.1.call-done) | copy-start | bytes 6684676
  55.7 11.9 %copy-start.14 = (bf16[512,1024]{1,0:T(8,128)(2,1)}, bf16[512,1024]{1,0:T(8,128)(2,1)S(1)}, u32[]{:S(2)}) copy-start(bf16[512,1024]{1,0:T(8,128)(2,1)S(1)} %get-tuple-element.36.conv_late_hbm) | copy-start | bytes 3145732
  55.7 16.3 %copy-start.6 = (bf16[128,1024]{1,0:T(8,128)(2,1)S(1)}, bf16[128,1024]{1,0:T(8,128)(2,1)}, u32[]{:S(2)}) copy-start(bf16[128,1024]{1,0:T(8,128)(2,1)} %pad_maximum_fusion.refs_4_.refs_5_) | copy-start | bytes 786436
  68.6 13.2 %all-to-all-start.3 = ((bf16[4,128,640]{2,1,0:T(8,128)(2,1)}), bf16[4,128,640]{2,1,0:T(8,128)(2,1)S(1)}, u32[]{:S(2)}, u32[]{:S(2)}) async-start(bf16[4,128,640]{2,1,0:T(8,128)(2,1)} %normalise.1), calls=%async_computation.3 | async-start | bytes 1310720 | tf_op jit(solution)/shard_map/all_to_all | solution.py:466
  72.1 29.8 %collective-permute-start = (bf16[128,1024]{1,0:T(8,128)(2,1)S(1)}, bf16[128,1024]{1,0:T(8,128)(2,1)S(1)}, u32[]{:S(2)}, u32[]{:S(2)}) collective-permute-start(bf16[128,1024]{1,0:T(8,128)(2,1)S(1)} %copy-done.6), channel_id=1, source_target_pairs={{0,16},{8,24},{1,17},{9,25},{2,18},{10,26},{3,19},{11,27},{4,20},{... | collective-permute-start | bytes 786440 | tf_op jit(solution)/shard_map/ppermute | solution.py:462
  76.0 26.6 %collective-permute-start.1 = (bf16[128,1024]{1,0:T(8,128)(2,1)S(1)}, bf16[128,1024]{1,0:T(8,128)(2,1)S(1)}, u32[]{:S(2)}, u32[]{:S(2)}) collective-permute-start(bf16[128,1024]{1,0:T(8,128)(2,1)S(1)} %copy-done.6), channel_id=1, source_target_pairs={{0,8},{8,16},{16,24},{1,9},{9,17},{17,25},{2,10},{10,18},{18,26},{... | collective-permute-start | bytes 786440 | tf_op jit(solution)/shard_map/ppermute | solution.py:462
  81.8 0.9 copy-start.15
  101.9 0.7 copy-start.10
  102.6 0.7 copy-start.12
  103.3 19.1 %all-to-all-start.4 = ((bf16[4,128,1280]{2,1,0:T(8,128)(2,1)}), bf16[4,128,1280]{2,1,0:T(8,128)(2,1)S(1)}, u32[]{:S(2)}, u32[]{:S(2)}) async-start(bf16[4,128,1280]{2,1,0:T(8,128)(2,1)} %state_scan_0.1), calls=%async_computation.4 | async-start | bytes 2621440 | tf_op jit(solution)/shard_map/all_to_all | solution.py:466
  109.6 17.2 %copy-start.7 = (bf16[128,1024]{1,0:T(8,128)(2,1)S(1)}, bf16[128,1024]{1,0:T(8,128)(2,1)}, u32[]{:S(2)}) copy-start(bf16[128,1024]{1,0:T(8,128)(2,1)} %pad_maximum_fusion.refs_4_.refs_5_) | copy-start | bytes 786436
  122.5 12.2 %all-to-all-start.5 = ((bf16[4,128,768]{2,1,0:T(8,128)(2,1)}), bf16[4,128,768]{2,1,0:T(8,128)(2,1)S(1)}, u32[]{:S(2)}, u32[]{:S(2)}) async-start(bf16[4,128,768]{2,1,0:T(8,128)(2,1)} %state_scan_5.1), calls=%async_computation.5 | async-start | bytes 1572864 | tf_op jit(solution)/shard_map/all_to_all | solution.py:466
  126.8 1.2 copy-start.9
  128.0 0.9 copy-start.11
  129.0 0.9 copy-start.13
  134.7 1.6 %copy-start.8 = (bf16[1,128,8192]{2,1,0:T(8,128)(2,1)S(1)}, bf16[1,128,8192]{2,1,0:T(8,128)(2,1)}, u32[]{:S(2)}) copy-start(bf16[1,128,8192]{2,1,0:T(8,128)(2,1)} %param.17) | copy-start | bytes 6291460
Sparse Core Ops, SparseCore 0:
  9.7 32.8 all-gather.4
  44.2 28.5 all-gather.6

commit v9 on v7

--- a/solution.py
+++ b/solution.py
@@ -77,7 +77,7 @@
         out_specs=wide,
         out_shape=jax.ShapeDtypeStruct(queries.shape, jnp.bfloat16),
         input_output_aliases=aliases,
-        compiler_params=pltpu.CompilerParams(vmem_limit_bytes=16 << 20),
+        compiler_params=pltpu.CompilerParams(vmem_limit_bytes=40 << 20),
         cost_estimate=pl.CostEstimate(
             flops=4 * rows * span * group_width * (end - begin),
             bytes_accessed=4 * rows * group_width * (end - begin),
@@ -221,18 +221,30 @@
     )(parts)
 
 
-def scan_kernel(rank, first_shard, reset_ref, low_ref, weight_hbm, bias_ref, decay_ref, gain_ref, conv_hbm, out_ref,
-                weight_ref, conv_ref, sems, in_cols, out_diag, delta_rows, drive_rows, held_even, held_odd):
-    toks = reset_ref.shape[0]
+def scan_kernel(rank, first_shard, reset_hbm, low_hbm, weight_hbm, bias_ref, decay_ref, gain_ref,
+                conv_hbm, out_ref, reset_ref, low_ref, weight_ref, conv_ref, sems, in_cols, out_diag, delta_rows, drive_rows, held_even, held_odd):
+    toks = low_ref.shape[0]
     states = decay_ref.shape[0]
     shards = weight_ref.shape[0]
     width = weight_ref.shape[2]
     tiles = shards * width // LANES
     column = first_shard * width
-    weight_copy = pltpu.make_async_copy(weight_hbm.at[pl.ds(first_shard, shards)], weight_ref, sems.at[0])
-    conv_copy = pltpu.make_async_copy(conv_hbm.at[:, pl.ds(column, shards * width)], conv_ref, sems.at[1])
-    weight_copy.start()
-    conv_copy.start()
+    low_copy = pltpu.make_async_copy(low_hbm, low_ref, sems.at[0])
+    reset_copy = pltpu.make_async_copy(reset_hbm, reset_ref, sems.at[1])
+    low_copy.start()
+    reset_copy.start()
+    shard_copies = []
+    for shard in range(shards):
+        at = shard * width
+        shard_copies += [
+            pltpu.make_async_copy(weight_hbm.at[first_shard + shard], weight_ref.at[shard], sems.at[2 + 2 * shard]),
+            pltpu.make_async_copy(
+                conv_hbm.at[:, pl.ds(column + at, width)], conv_ref.at[:, pl.ds(at, width)], sems.at[3 + 2 * shard]
+            ),
+        ]
+    for copy in shard_copies:
+        copy.start()
+    low_copy.wait()
     rows = out_ref.shape[1]
     block = 16
     span = block * states
@@ -242,19 +254,20 @@
     bits = states.bit_length() - 1
     lane = lax.broadcasted_iota(jnp.int32, (states, span), 1)
     spread = jnp.where((lane & (states - 1)) == lax.broadcasted_iota(jnp.int32, (states, span), 0), 1.0, 0.0)
-    copies = jnp.dot(
+    spread_out = jnp.dot(
         low_ref[:, rank + states : rank + 2 * states], spread.astype(jnp.bfloat16), preferred_element_type=jnp.float32
     )
     here = lax.shift_right_logical(lax.broadcasted_iota(jnp.int32, (block, span), 1), bits)
     there = lax.broadcasted_iota(jnp.int32, (block, span), 0)
     keep = jnp.where(here == there, 1.0, 0.0)
-    out_diag[...] = (copies.reshape(count, block, span) * keep[None]).reshape(toks, span).astype(jnp.bfloat16)
-
+    out_diag[...] = (spread_out.reshape(count, block, span) * keep[None]).reshape(toks, span).astype(jnp.bfloat16)
+
+    reset_copy.wait()
     reset = jnp.broadcast_to(reset_ref[...], (toks, LANES))
     low = low_ref[:, 0:rank]
-    weight_copy.wait()
-    conv_copy.wait()
     for shard in range(shards):
+        shard_copies[2 * shard].wait()
+        shard_copies[2 * shard + 1].wait()
         pre = jnp.dot(low, weight_ref[shard], preferred_element_type=jnp.float32)
         for part in range(width // LANES):
             tile = shard * (width // LANES) + part
@@ -322,23 +335,18 @@
     wide = shards * width
     steps = toks * wide * states
     whole = pl.BlockSpec(memory_space=pltpu.VMEM)
+    left = pl.BlockSpec(memory_space=pl.ANY)
     return pl.pallas_call(
         functools.partial(scan_kernel, rank, first_shard),
-        in_specs=[
-            whole,
-            whole,
-            pl.BlockSpec(memory_space=pl.ANY),
-            whole,
-            whole,
-            whole,
-            pl.BlockSpec(memory_space=pl.ANY),
-        ],
+        in_specs=[left, left, left, whole, whole, whole, left],
         out_specs=whole,
         out_shape=jax.ShapeDtypeStruct((ctx, rows, wide), jnp.bfloat16),
         scratch_shapes=[
+            pltpu.VMEM(reset_col.shape, reset_col.dtype),
+            pltpu.VMEM(low.shape, low.dtype),
             pltpu.VMEM((shards, rank, width), jnp.bfloat16),
             pltpu.VMEM((toks, wide), jnp.bfloat16),
-            pltpu.SemaphoreType.DMA((2,)),
+            pltpu.SemaphoreType.DMA((2 + 2 * shards,)),
             pltpu.VMEM((states, toks), jnp.float32),
             pltpu.VMEM((toks, 16 * states), jnp.bfloat16),
             pltpu.VMEM((toks // 16, wide // LANES, 16, LANES), jnp.float32),
@@ -469,18 +477,18 @@
 
     low, both = lax.optimization_barrier((low, both))
     blocks = [shifted(both, "ctx", by) for by in range(back, 0, -1)] + [both]
-    low = exchange(low).reshape(toks, low.shape[2])
-
-    early = slots * 5 // 8
-    scanned = []
-    for first, count in ((0, early), (early, slots - early)):
-        if scanned:
-            low, scanned[-1] = lax.optimization_barrier((low, scanned[-1]))
-        scanned.append(state_scan(reset_col, low, delta_parts, bias, decay, gain, conv, ctx, first, count))
-    scanned[-1], blocks = lax.optimization_barrier((scanned[-1], blocks))
+    low, blocks = lax.optimization_barrier((exchange(low), blocks))
+    low = low.reshape(toks, low.shape[2])
+
+    split = slots * 3 // 4
+    scanned = [
+        state_scan(reset_col, low, delta_parts, bias, decay, gain, conv, ctx, first, count)
+        for first, count in ((0, split), (split, slots - split))
+    ]
+    scanned[0], blocks = lax.optimization_barrier((scanned[0], blocks))
     attended = attention(queries[0], blocks, seg_q, seg_k, 0, KEY_VALUE_HEADS)
     scanned = [exchange(part) for part in scanned]
-    scanned[-1], attended = lax.optimization_barrier((scanned[-1], attended))
+    scanned[0], attended = lax.optimization_barrier((scanned[0], attended))
     mixed = apply_gate(scanned, gate_input[0], fold, width)
     return (attended[None], mixed[None])
 

time: 154 us -> 159 us (1.032)
  blocking collectives: 28.3 us -> 12.8 us
  waiting for transfers between devices: 17.3 us -> 29.8 us
  starting transfers between devices: 19.7 us -> 23.3 us
  Pallas kernels: 44.2 us -> 47.2 us
    all_to_all x2 -> x1, blocking collectives: 28.3 us -> 12.8 us  [exchange(): return lax.all_to_all(value, 'ctx', 0, 0, tiled=True)]
    ppermute x2, waiting for transfers between devices: 0.01 us -> 10.4 us  [shifted(): return lax.ppermute(value, axis, pairs)]
    all_to_all x3 -> x4, starting transfers between devices: 12.3 us -> 16 us  [exchange(): return lax.all_to_all(value, 'ctx', 0, 0, tiled=True)]
    pallas_call x2, Pallas kernels: 31.2 us -> 34.2 us  [state_scan(): pl.pallas_call(functools.partial(scan_kernel, rank, first_shard), in_spec...]
    all_to_all x3 -> x4, waiting for transfers between devices: 17.3 us -> 19.3 us  [exchange(): return lax.all_to_all(value, 'ctx', 0, 0, tiled=True)]
    unnamed x36 -> x38, local copies, waits for them, and re-layouts: 14.3 us -> 15.7 us
  transfers between devices with their start and end apart: 7 -> 8, of which waited for: 3 -> 4; matrix products, arithmetic and copies ran while one was open for 10% -> 9% of each run, Pallas kernels for 27% -> 14%
where the time goes in v9:
time: 159 us; the launch traced here: 158 us
  Pallas kernels  47.2 us (30%)
  waiting for transfers between devices  29.8 us (19%)
  local copies, waits for them, and re-layouts  27.9 us (18%)
  starting transfers between devices  23.3 us (15%)
  between operations  14.2 us (9%)
  blocking collectives  12.8 us (8%)
  other arithmetic  2.71 us (2%)
    pallas_call x2, Pallas kernels, state_scan(): pl.pallas_call(functools.partial(scan_kernel, rank, first_shard), in_spec...  34.2 us
    all_to_all x4, waiting for transfers between devices, exchange(): return lax.all_to_all(value, 'ctx', 0, 0, tiled=True)  19.3 us
    all_to_all x4, starting transfers between devices, exchange(): return lax.all_to_all(value, 'ctx', 0, 0, tiled=True)  16 us
    unnamed x38, local copies, waits for them, and re-layouts  15.7 us
    all_to_all x1, blocking collectives, exchange(): return lax.all_to_all(value, 'ctx', 0, 0, tiled=True)  12.8 us
    ppermute x2, waiting for transfers between devices, shifted(): return lax.ppermute(value, axis, pairs)  10.4 us
    ppermute x2, starting transfers between devices, shifted(): return lax.ppermute(value, axis, pairs)  7.28 us
    pallas_call x1, Pallas kernels, attention(): pl.pallas_call(functools.partial(attention_kernel, begin), grid=(end - be...  4.78 us
  transfers between devices with their start and end apart: 8, of which 4 were waited for; matrix products, arithmetic and copies ran while one was open for 9% of the time, Pallas kernels for 14%

profile of v9, /device:TPU:0, one launch (start us, length us, event | category | flops | bytes accessed | tf_op | source)
XLA Modules:
  0.0 157.9 jit_solution(18093665999188703674)
XLA Ops:
  7.2 1.2 copy-done
  9.2 1.6 %copy-done.4 = bf16[1,128,8192]{2,1,0:T(8,128)(2,1)S(1)} copy-done((bf16[1,128,8192]{2,1,0:T(8,128)(2,1)S(1)}, bf16[1,128,8192]{2,1,0:T(8,128)(2,1)}, u32[]{:S(2)}) %copy-start.4) | copy-done | bytes 2097176
  11.2 1.3 copy-done.1
  12.5 5.3 %all-to-all-start = ((bf16[4,128,2048]{2,1,0:T(8,128)(2,1)}), bf16[4,128,2048]{2,1,0:T(8,128)(2,1)S(1)}, u32[]{:S(2)}, u32[]{:S(2)}) async-start(bf16[4,128,2048]{2,1,0:T(8,128)(2,1)} %copy-done.1), calls=%async_computation | async-start | bytes 4194304 | tf_op jit(solution)/shard_map/all_to_all | solution.py:402
  18.5 2.2 %reshape.75 = f32[16,8,1,4,256]{4,3,1,0,2:T(4,128)} reshape(f32[16,8192]{1,0:T(8,128)} %bitcast.34) | data formatting | bytes 1048576 | tf_op jit(solution)/shard_map/reshape | solution.py:436
  20.7 1.4 dynamic-slice_reduce_fusion
  25.4 1.4 constant_dynamic-slice_fusion.2
  26.8 1.7 %constant_dynamic-slice_fusion.1 = bf16[512,256]{1,0:T(8,128)(2,1)} fusion(bf16[512,1024]{1,0:T(8,128)(2,1)} %param.22, s32[]{:T(128)S(6)} %select_n.60), kind=kLoop, calls=%fused_computation.8 | loop fusion | bytes 524292 | tf_op jit(solution)/shard_map/dynamic_slice | solution.py:442
  28.5 1.0 pad_maximum_fusion.refs_4_.refs_5_
  30.1 1.6 broadcast_select_fusion.reset_hbm
  31.7 11.0 %all-to-all-done.x_ref = bf16[4,128,2048]{2,1,0:T(8,128)(2,1)S(1)} async-done(((bf16[4,128,2048]{2,1,0:T(8,128)(2,1)}), bf16[4,128,2048]{2,1,0:T(8,128)(2,1)S(1)}, u32[]{:S(2)}, u32[]{:S(2)}) %all-to-all-start) | async-done | bytes 2097184 | tf_op jit(solution)/shard_map/all_to_all | solution.py:402
  43.5 1.6 %copy-done.2 = bf16[4352,256]{1,0:T(8,128)(2,1)S(1)} copy-done((bf16[4352,256]{1,0:T(8,128)(2,1)S(1)}, bf16[4352,256]{1,0:T(8,128)(2,1)}, u32[]{:S(2)}) %copy-start.2) | copy-done | bytes 2228248
  45.2 0.9 copy-done.10
  46.1 4.4 %conv_select.1 = (bf16[512,2048]{1,0:T(8,128)(2,1)S(1)}, bf16[4,128,640]{2,1,0:T(8,128)(2,1)S(1)}) custom-call(s32[512,1]{1,0:T(8,128)S(1)} %copy-done.10, bf16[4,128,2048]{2,1,0:T(8,128)(2,1)S(1)} %all-to-all-done.x_ref, f32[4,2048]{1,0:T(4,128)S(1)} %bitcast.28, f32[1,2048]{1,0:T(1,128)S(1)} %bitcast.29, bf16[8,544,256]{2,1,0:T(8,128)(2,1)S(1)} %bitcast.24), custom_call_target="tpu_custom_call" | custom-call | flops 1140850688 | bytes 6422528 | tf_op jit(solution)/shard_map/conv_select/pallas_call | solution.py:168
  50.5 1.3 copy-done.11
  51.8 12.8 %all_to_all.25.part_ref = bf16[4,128,640]{2,1,0:T(8,128)(2,1)S(1)} all-to-all(bf16[4,128,640]{2,1,0:T(8,128)(2,1)S(1)} %get-tuple-element.33), channel_id=1, replica_groups=mesh['ctx'=4,'rep'=8] {'ctx'}, dimensions={0} | all-to-all | bytes 1310720 | tf_op jit(solution)/shard_map/all_to_all | solution.py:402
  64.7 1.0 normalise.1
  65.7 3.5 %all-to-all-start.2 = ((bf16[4,128,640]{2,1,0:T(8,128)(2,1)}), bf16[4,128,640]{2,1,0:T(8,128)(2,1)S(1)}, u32[]{:S(2)}, u32[]{:S(2)}) async-start(bf16[4,128,640]{2,1,0:T(8,128)(2,1)} %normalise.1), calls=%async_computation.2 | async-start | bytes 1310720 | tf_op jit(solution)/shard_map/all_to_all | solution.py:402
  69.2 3.9 %collective-permute-start = (bf16[128,1024]{1,0:T(8,128)(2,1)S(1)}, bf16[128,1024]{1,0:T(8,128)(2,1)S(1)}, u32[]{:S(2)}, u32[]{:S(2)}) collective-permute-start(bf16[128,1024]{1,0:T(8,128)(2,1)S(1)} %pad_maximum_fusion.refs_4_.refs_5_), channel_id=1, source_target_pairs={{0,16},{8,24},{1,17},{9,25},{2,18},{10,26},{3,19},{11,27},{4,20},{... | collective-permute-start | bytes 786440 | tf_op jit(solution)/shard_map/ppermute | solution.py:398
  73.1 3.4 %collective-permute-start.1 = (bf16[128,1024]{1,0:T(8,128)(2,1)S(1)}, bf16[128,1024]{1,0:T(8,128)(2,1)S(1)}, u32[]{:S(2)}, u32[]{:S(2)}) collective-permute-start(bf16[128,1024]{1,0:T(8,128)(2,1)S(1)} %pad_maximum_fusion.refs_4_.refs_5_), channel_id=1, source_target_pairs={{0,8},{8,16},{16,24},{1,9},{9,17},{17,25},{2,10},{10,18},{18,26},{... | collective-permute-start | bytes 786440 | tf_op jit(solution)/shard_map/ppermute | solution.py:398
  76.5 10.4 %collective-permute-done.refs_0_.refs_1_ = bf16[128,1024]{1,0:T(8,128)(2,1)S(1)} collective-permute-done((bf16[128,1024]{1,0:T(8,128)(2,1)S(1)}, bf16[128,1024]{1,0:T(8,128)(2,1)S(1)}, u32[]{:S(2)}, u32[]{:S(2)}) %collective-permute-start) | collective-permute-done | bytes 262176 | tf_op jit(solution)/shard_map/ppermute | solution.py:398
  89.1 23.3 %state_scan_0.1 = bf16[4,128,1536]{2,1,0:T(8,128)(2,1)} custom-call(f32[512,1]{1,0:T(8,128)} %broadcast_select_fusion.reset_hbm, bf16[512,640]{1,0:T(8,128)(2,1)} %bitcast.32, bf16[8,512,256]{2,1,0:T(8,128)(2,1)} %bitcast.47, f32[1,2048]{1,0:T(1,128)} %bitcast.43, f32[16,2048]{1,0:T(8,128)} %bitcast.36, f32[1,2048]{1,0:T(1,128)} %bitcast.45, ...), custom_call_target="tpu_custom_call" | custom-call | flops 75497472 | bytes 4718592 | tf_op jit(solution)/shard_map/state_scan_0/pallas_call | solution.py:339
  112.4 3.8 %all-to-all-start.3 = ((bf16[4,128,1536]{2,1,0:T(8,128)(2,1)}), bf16[4,128,1536]{2,1,0:T(8,128)(2,1)S(1)}, u32[]{:S(2)}, u32[]{:S(2)}) async-start(bf16[4,128,1536]{2,1,0:T(8,128)(2,1)} %state_scan_0.1), calls=%async_computation.3 | async-start | bytes 3145728 | tf_op jit(solution)/shard_map/all_to_all | solution.py:402
  116.2 10.9 %state_scan_6.1 = bf16[4,128,512]{2,1,0:T(8,128)(2,1)} custom-call(f32[512,1]{1,0:T(8,128)} %broadcast_select_fusion.reset_hbm, bf16[512,640]{1,0:T(8,128)(2,1)} %bitcast.33, bf16[8,512,256]{2,1,0:T(8,128)(2,1)} %bitcast.48, f32[1,2048]{1,0:T(1,128)} %bitcast.44, f32[16,2048]{1,0:T(8,128)} %bitcast.37, f32[1,2048]{1,0:T(1,128)} %bitcast.46, ...), custom_call_target="tpu_custom_call" | custom-call | flops 25165824 | bytes 1572864 | tf_op jit(solution)/shard_map/state_scan_6/pallas_call | solution.py:339
  127.1 8.1 %all-to-all-done.3.refs_0_ = bf16[4,128,1536]{2,1,0:T(8,128)(2,1)S(1)} async-done(((bf16[4,128,1536]{2,1,0:T(8,128)(2,1)}), bf16[4,128,1536]{2,1,0:T(8,128)(2,1)S(1)}, u32[]{:S(2)}, u32[]{:S(2)}) %all-to-all-start.3) | async-done | bytes 1572896 | tf_op jit(solution)/shard_map/all_to_all | solution.py:402
  135.2 3.5 %all-to-all-start.4 = ((bf16[4,128,512]{2,1,0:T(8,128)(2,1)}), bf16[4,128,512]{2,1,0:T(8,128)(2,1)S(1)}, u32[]{:S(2)}, u32[]{:S(2)}) async-start(bf16[4,128,512]{2,1,0:T(8,128)(2,1)} %state_scan_6.1), calls=%async_computation.4 | async-start | bytes 1048576 | tf_op jit(solution)/shard_map/all_to_all | solution.py:402
  138.8 1.2 copy-done.5
  140.0 0.9 copy-done.7
  141.0 0.9 copy-done.9
  141.9 4.8 %attention_0.1 = bf16[128,4096]{1,0:T(8,128)(2,1)} custom-call(s32[128,1]{1,0:T(8,128)S(1)} %copy.27.seg_q_ref, s32[1,384]{1,0:T(1,128)S(1)} %broadcast_in_dim.25.seg_k_ref, bf16[128,4096]{1,0:T(8,128)(2,1)S(1)} %bitcast.27, bf16[128,1024]{1,0:T(8,128)(2,1)S(1)} %copy-done.7, bf16[128,1024]{1,0:T(8,128)(2,1)S(1)} %copy-done.7, ...), custom_call_target="tpu_custom_call" | custom-call | flops 805306368 | bytes 2097152 | tf_op jit(solution)/shard_map/attention_0/pallas_call | solution.py:73
  147.0 1.6 %copy-done.3 = bf16[1,128,8192]{2,1,0:T(8,128)(2,1)S(1)} copy-done((bf16[1,128,8192]{2,1,0:T(8,128)(2,1)S(1)}, bf16[1,128,8192]{2,1,0:T(8,128)(2,1)}, u32[]{:S(2)}) %copy-start.3) | copy-done | bytes 2097176
  148.6 2.5 %gate.1 = bf16[128,8192]{1,0:T(8,128)(2,1)} custom-call(bf16[128,8192]{1,0:T(8,128)(2,1)S(1)} %bitcast.25, bf16[4,128,1536]{2,1,0:T(8,128)(2,1)S(1)} %all-to-all-done.3.refs_0_, bf16[4,128,512]{2,1,0:T(8,128)(2,1)S(1)} %all-to-all-done.4.refs_1_), custom_call_target="tpu_custom_call" | custom-call | flops 4194304 | bytes 6291456 | tf_op jit(solution)/shard_map/gate/pallas_call | solution.py:383
  (53 shorter events, 9.4 us)
Async XLA Ops:
  7.2 1.3 copy-start
  7.2 36.4 %all-gather.5.cloned.1.call-start = ((), (), s32[]{:S(2)}) async-start(), calls=%async_computation.5 | async-start | bytes 2506752 | tf_op jit(solution)/shard_map/all_gather | solution.py:445
  9.2 1.6 %copy-start.4 = (bf16[1,128,8192]{2,1,0:T(8,128)(2,1)S(1)}, bf16[1,128,8192]{2,1,0:T(8,128)(2,1)}, u32[]{:S(2)}) copy-start(bf16[1,128,8192]{2,1,0:T(8,128)(2,1)} %param.16) | copy-start | bytes 6291460
  11.1 1.3 copy-start.1
  12.5 5.3 %copy-start.14 = (s32[1,512]{1,0:T(1,128)S(1)}, s32[1,512]{1,0:T(1,128)}, u32[]{:S(2)}) copy-start(s32[1,512]{1,0:T(1,128)} %param.18) | copy-start | bytes 6148
  12.5 5.4 %copy-start.15 = (f32[8192]{0:T(1024)S(1)}, f32[8192]{0:T(1024)}, u32[]{:S(2)}) copy-start(f32[8192]{0:T(1024)} %param.25) | copy-start | bytes 98308
  12.5 5.4 %copy-start.16 = (f32[8192]{0:T(1024)S(1)}, f32[8192]{0:T(1024)}, u32[]{:S(2)}) copy-start(f32[8192]{0:T(1024)} %param.20) | copy-start | bytes 98308
  12.5 10.4 %copy-start.13 = (f32[4,8192]{1,0:T(4,128)S(1)}, f32[4,8192]{1,0:T(4,128)}, u32[]{:S(2)}) copy-start(f32[4,8192]{1,0:T(4,128)} %param.19) | copy-start | bytes 393220
  12.5 30.2 %all-to-all-start = ((bf16[4,128,2048]{2,1,0:T(8,128)(2,1)}), bf16[4,128,2048]{2,1,0:T(8,128)(2,1)S(1)}, u32[]{:S(2)}, u32[]{:S(2)}) async-start(bf16[4,128,2048]{2,1,0:T(8,128)(2,1)} %copy-done.1), calls=%async_computation | async-start | bytes 4194304 | tf_op jit(solution)/shard_map/all_to_all | solution.py:402
  17.8 70.5 %all-gather.7.cloned.1.call-start = ((), (), s32[]{:S(2)}) async-start(), calls=%async_computation.6 | async-start | bytes 2359296 | tf_op jit(solution)/shard_map/all_gather | solution.py:445
  17.9 6.0 %copy-start.17 = (s32[384]{0:T(512)}, s32[384]{0:T(512)S(1)}, u32[]{:S(2)}) copy-start(s32[384]{0:T(512)S(1)} %pad_dynamic-slice_fusion) | copy-start | bytes 4612
  43.5 1.6 %copy-start.2 = (bf16[4352,256]{1,0:T(8,128)(2,1)S(1)}, bf16[4352,256]{1,0:T(8,128)(2,1)}, u32[]{:S(2)}) copy-start(bf16[4352,256]{1,0:T(8,128)(2,1)} %all-gather.5.cloned.1.call-done) | copy-start | bytes 6684676
  45.2 0.9 copy-start.10
  50.5 1.3 copy-start.11
  65.7 22.6 %all-to-all-start.2 = ((bf16[4,128,640]{2,1,0:T(8,128)(2,1)}), bf16[4,128,640]{2,1,0:T(8,128)(2,1)S(1)}, u32[]{:S(2)}, u32[]{:S(2)}) async-start(bf16[4,128,640]{2,1,0:T(8,128)(2,1)} %normalise.1), calls=%async_computation.2 | async-start | bytes 1310720 | tf_op jit(solution)/shard_map/all_to_all | solution.py:402
  69.2 17.7 %collective-permute-start = (bf16[128,1024]{1,0:T(8,128)(2,1)S(1)}, bf16[128,1024]{1,0:T(8,128)(2,1)S(1)}, u32[]{:S(2)}, u32[]{:S(2)}) collective-permute-start(bf16[128,1024]{1,0:T(8,128)(2,1)S(1)} %pad_maximum_fusion.refs_4_.refs_5_), channel_id=1, source_target_pairs={{0,16},{8,24},{1,17},{9,25},{2,18},{10,26},{3,19},{11,27},{4,20},{... | collective-permute-start | bytes 786440 | tf_op jit(solution)/shard_map/ppermute | solution.py:398
  73.1 14.5 %collective-permute-start.1 = (bf16[128,1024]{1,0:T(8,128)(2,1)S(1)}, bf16[128,1024]{1,0:T(8,128)(2,1)S(1)}, u32[]{:S(2)}, u32[]{:S(2)}) collective-permute-start(bf16[128,1024]{1,0:T(8,128)(2,1)S(1)} %pad_maximum_fusion.refs_4_.refs_5_), channel_id=1, source_target_pairs={{0,8},{8,16},{16,24},{1,9},{9,17},{17,25},{2,10},{10,18},{18,26},{... | collective-permute-start | bytes 786440 | tf_op jit(solution)/shard_map/ppermute | solution.py:398
  86.9 0.7 copy-start.6
  87.6 0.7 copy-start.8
  88.3 0.8 copy-start.12
  112.4 22.8 %all-to-all-start.3 = ((bf16[4,128,1536]{2,1,0:T(8,128)(2,1)}), bf16[4,128,1536]{2,1,0:T(8,128)(2,1)S(1)}, u32[]{:S(2)}, u32[]{:S(2)}) async-start(bf16[4,128,1536]{2,1,0:T(8,128)(2,1)} %state_scan_0.1), calls=%async_computation.3 | async-start | bytes 3145728 | tf_op jit(solution)/shard_map/all_to_all | solution.py:402
  135.2 11.8 %all-to-all-start.4 = ((bf16[4,128,512]{2,1,0:T(8,128)(2,1)}), bf16[4,128,512]{2,1,0:T(8,128)(2,1)S(1)}, u32[]{:S(2)}, u32[]{:S(2)}) async-start(bf16[4,128,512]{2,1,0:T(8,128)(2,1)} %state_scan_6.1), calls=%async_computation.4 | async-start | bytes 1048576 | tf_op jit(solution)/shard_map/all_to_all | solution.py:402
  138.8 1.2 copy-start.5
  140.0 0.9 copy-start.7
  141.0 0.9 copy-start.9
  147.0 1.6 %copy-start.3 = (bf16[1,128,8192]{2,1,0:T(8,128)(2,1)S(1)}, bf16[1,128,8192]{2,1,0:T(8,128)(2,1)}, u32[]{:S(2)}) copy-start(bf16[1,128,8192]{2,1,0:T(8,128)(2,1)} %param.17) | copy-start | bytes 6291460
Sparse Core Ops, SparseCore 0:
  9.7 32.9 all-gather.4
  44.3 28.5 all-gather.6

commit v10 on v9

--- a/solution.py
+++ b/solution.py
@@ -77,7 +77,7 @@
         out_specs=wide,
         out_shape=jax.ShapeDtypeStruct(queries.shape, jnp.bfloat16),
         input_output_aliases=aliases,
-        compiler_params=pltpu.CompilerParams(vmem_limit_bytes=40 << 20),
+        compiler_params=pltpu.CompilerParams(vmem_limit_bytes=54 << 20),
         cost_estimate=pl.CostEstimate(
             flops=4 * rows * span * group_width * (end - begin),
             bytes_accessed=4 * rows * group_width * (end - begin),
@@ -113,24 +113,19 @@
     )(value)
 
 
-def conv_select_kernel(seg_ref, x_ref, weight_ref, bias_ref, select_ref, conv_ref, part_ref, masks, padded, total):
+def conv_select_kernel(match_ref, x_ref, weight_ref, bias_ref, select_ref, early_ref, late_ref, part_ref, masks, padded, total):
     step = pl.program_id(0)
-    toks = seg_ref.shape[0]
     pieces, rows, wide = x_ref.shape
+    toks = pieces * rows
     tiles = wide // LANES
-    slots, outputs, width = select_ref.shape
+    slots, outputs, _ = select_ref.shape
 
     @pl.when(step == 0)
     def _():
-        wide_seg = jnp.broadcast_to(seg_ref[...], (toks, LANES)).astype(jnp.float32)
-        padded[0, 0:SUBLANES, :] = jnp.full((SUBLANES, LANES), -1.0, jnp.float32)
-        padded[0, SUBLANES : SUBLANES + toks, :] = wide_seg
         for tap in range(3):
-            before = padded[0, SUBLANES - 3 + tap : SUBLANES - 3 + tap + toks, :]
-            masks[tap] = jnp.where(before == wide_seg, 1.0, 0.0)
+            masks[tap] = jnp.broadcast_to(match_ref[:, tap : tap + 1], (toks, LANES))
         for tile in range(tiles):
             padded[tile, 0:SUBLANES, :] = jnp.zeros((SUBLANES, LANES), jnp.float32)
-        total[...] = jnp.zeros_like(total)
 
     outs = []
     for tile in range(tiles):
@@ -143,49 +138,52 @@
             moved = padded[tile, SUBLANES - 3 + tap : SUBLANES - 3 + tap + toks, :]
             term = (0.5 * weight_ref[tap : tap + 1, lanes]) * moved
             half = half + (term * masks[tap] if tap < 3 else term)
-        conv = (half + half * jnp.tanh(half)).astype(jnp.bfloat16)
-        conv_ref[:, lanes] = conv
-        outs.append(conv)
+        outs.append((half + half * jnp.tanh(half)).astype(jnp.bfloat16))
     conv = jnp.concatenate(outs, axis=1)
     select = jnp.concatenate([select_ref[slot] for slot in range(slots)], axis=1)
-    total[...] += lax.dot_general(conv, select, (((1,), (1,)), ((), ())), preferred_element_type=jnp.float32)
-
-    @pl.when(step == pl.num_programs(0) - 1)
+    added = lax.dot_general(conv, select, (((1,), (1,)), ((), ())), preferred_element_type=jnp.float32)
+
+    @pl.when(step == 0)
     def _():
+        early_ref[...] = conv
+        total[...] = added
+
+    @pl.when(step == 1)
+    def _():
+        late_ref[...] = conv
         spare = part_ref.shape[2] - outputs
+        full = (total[...] + added).astype(part_ref.dtype)
         for piece in range(pieces):
-            part_ref[piece, :, 0:outputs] = total[piece * rows : (piece + 1) * rows, :].astype(part_ref.dtype)
+            part_ref[piece, :, 0:outputs] = full[piece * rows : (piece + 1) * rows, :]
             part_ref[piece, :, outputs:] = jnp.zeros((rows, spare), part_ref.dtype)
 
 
-def conv_select(seg_col, pieces, conv_weight, conv_bias, select_parts):
+def conv_select(match, pieces, conv_weight, conv_bias, select_parts):
     slots, outputs, width = select_parts.shape
-    ctx, rows, _ = pieces.shape
+    ctx, rows, columns = pieces.shape
     toks = ctx * rows
     padded_outputs = -(-outputs // LANES) * LANES
-    batch = 4
-    wide = batch * width
+    wide = columns // 2
+    half = pl.BlockSpec((toks, wide), lambda s: (0, 0))
     return pl.pallas_call(
         conv_select_kernel,
-        grid=(slots // batch,),
+        grid=(2,),
         in_specs=[
-            pl.BlockSpec((toks, 1), lambda s: (0, 0)),
+            pl.BlockSpec(match.shape, lambda s: (0, 0)),
             pl.BlockSpec((ctx, rows, wide), lambda s: (0, 0, s)),
             pl.BlockSpec((4, wide), lambda s: (0, s)),
             pl.BlockSpec((1, wide), lambda s: (0, s)),
-            pl.BlockSpec((batch, outputs, width), lambda s: (s, 0, 0)),
+            pl.BlockSpec((slots // 2, outputs, width), lambda s: (s, 0, 0)),
         ],
-        out_specs=[
-            pl.BlockSpec((toks, wide), lambda s: (0, s)),
-            pl.BlockSpec((ctx, rows, padded_outputs), lambda s: (0, 0, 0)),
-        ],
+        out_specs=[half, half, pl.BlockSpec((ctx, rows, padded_outputs), lambda s: (0, 0, 0))],
         scratch_shapes=[
             pltpu.VMEM((3, toks, LANES), jnp.float32),
             pltpu.VMEM((wide // LANES, SUBLANES + toks, LANES), jnp.float32),
             pltpu.VMEM((toks, outputs), jnp.float32),
         ],
         out_shape=[
-            jax.ShapeDtypeStruct((toks, slots * width), jnp.bfloat16),
+            jax.ShapeDtypeStruct((toks, wide), jnp.bfloat16),
+            jax.ShapeDtypeStruct((toks, wide), jnp.bfloat16),
             jax.ShapeDtypeStruct((ctx, rows, padded_outputs), jnp.bfloat16),
         ],
         compiler_params=pltpu.CompilerParams(vmem_limit_bytes=32 << 20),
@@ -195,7 +193,7 @@
             transcendentals=pieces.size,
         ),
         name="conv_select",
-    )(seg_col, pieces, conv_weight, conv_bias, select_parts)
+    )(match, pieces, conv_weight, conv_bias, select_parts)
 
 
 def normalise_kernel(rank, part_ref, out_ref):
@@ -222,7 +220,7 @@
 
 
 def scan_kernel(rank, first_shard, reset_hbm, low_hbm, weight_hbm, bias_ref, decay_ref, gain_ref,
-                conv_hbm, out_ref, reset_ref, low_ref, weight_ref, conv_ref, sems, in_cols, out_diag, delta_rows, drive_rows, held_even, held_odd):
+                early_hbm, late_hbm, out_ref, reset_ref, low_ref, weight_ref, conv_ref, sems, in_cols, out_diag, delta_rows, drive_rows, held_even, held_odd):
     toks = low_ref.shape[0]
     states = decay_ref.shape[0]
     shards = weight_ref.shape[0]
@@ -236,11 +234,12 @@
     shard_copies = []
     for shard in range(shards):
         at = shard * width
+        start = column + at
+        middle = early_hbm.shape[1]
+        source = early_hbm.at[:, pl.ds(start, width)] if start < middle else late_hbm.at[:, pl.ds(start - middle, width)]
         shard_copies += [
             pltpu.make_async_copy(weight_hbm.at[first_shard + shard], weight_ref.at[shard], sems.at[2 + 2 * shard]),
-            pltpu.make_async_copy(
-                conv_hbm.at[:, pl.ds(column + at, width)], conv_ref.at[:, pl.ds(at, width)], sems.at[3 + 2 * shard]
-            ),
+            pltpu.make_async_copy(source, conv_ref.at[:, pl.ds(at, width)], sems.at[3 + 2 * shard]),
         ]
     for copy in shard_copies:
         copy.start()
@@ -327,7 +326,7 @@
         finish(count - 1, held_odd, part)
 
 
-def state_scan(reset_col, low, delta_parts, bias, decay, gain, conv, ctx, first_shard, shards):
+def state_scan(reset_col, low, delta_parts, bias, decay, gain, convs, ctx, first_shard, shards):
     toks = low.shape[0]
     rank, width = delta_parts.shape[1:]
     states = decay.shape[0]
@@ -338,7 +337,7 @@
     left = pl.BlockSpec(memory_space=pl.ANY)
     return pl.pallas_call(
         functools.partial(scan_kernel, rank, first_shard),
-        in_specs=[left, left, left, whole, whole, whole, left],
+        in_specs=[left, left, left, whole, whole, whole, left, left],
         out_specs=whole,
         out_shape=jax.ShapeDtypeStruct((ctx, rows, wide), jnp.bfloat16),
         scratch_shapes=[
@@ -354,12 +353,12 @@
             pltpu.VMEM((16 * states, wide), jnp.bfloat16),
             pltpu.VMEM((16 * states, wide), jnp.bfloat16),
         ],
-        compiler_params=pltpu.CompilerParams(vmem_limit_bytes=60 << 20),
+        compiler_params=pltpu.CompilerParams(vmem_limit_bytes=54 << 20),
         cost_estimate=pl.CostEstimate(
             flops=6 * steps, bytes_accessed=2 * shards * rank * width + 4 * toks * wide, transcendentals=steps
         ),
         name=f"state_scan_{first_shard}",
-    )(reset_col, low, delta_parts, bias, decay, gain, conv)
+    )(reset_col, low, delta_parts, bias, decay, gain, *convs)
 
 
 def gate_kernel(fold, width, gate_ref, *refs):
@@ -427,7 +426,6 @@
     fold = width * shards * ctx // channels
     seg = segment_ids[0]
     toks = seg.shape[0]
-    seg_col = seg[:, None]
     back = min(ctx - 1, -(-(toks // 2 - 1) // rows))
 
     slots = shards // fold
@@ -453,6 +451,8 @@
 
     same = jnp.concatenate([jnp.zeros((1,), bool), seg[1:] == seg[:-1]])
     reset_col = jnp.where(same, 0.0, FAR)[:, None]
+    seg_before = jnp.concatenate([jnp.full((3,), -1, jnp.int32), seg])
+    match = jnp.stack([(seg_before[tap : tap + toks] == seg) for tap in range(3)], axis=1).astype(jnp.float32)
     seg_pad = jnp.concatenate([jnp.full((back * rows,), -1, jnp.int32), seg])
     seg_k = lax.dynamic_slice_in_dim(seg_pad, place * rows, (back + 1) * rows, 0)
     own = (
@@ -465,24 +465,23 @@
         jnp.concatenate([keys[0], values[0]], axis=1),
         own_part(conv_weight),
         own_part(conv_bias)[None, :],
-        seg_col,
+        match,
         own_columns(delta_weight),
     )
     pieces, own = lax.optimization_barrier((exchange(packed), own))
-    bias, decay, gain, reset_col, seg_q, seg_k, both, conv_weight, conv_bias, seg_col, delta_own = own
+    bias, decay, gain, reset_col, seg_q, seg_k, both, conv_weight, conv_bias, match, delta_own = own
     delta_parts = gathered(delta_own)
 
-    conv, parts = conv_select(seg_col, pieces, conv_weight, conv_bias, select_parts)
+    *convs, parts = conv_select(match, pieces, conv_weight, conv_bias, select_parts)
     low = normalise(exchange(parts), rank)
 
     low, both = lax.optimization_barrier((low, both))
     blocks = [shifted(both, "ctx", by) for by in range(back, 0, -1)] + [both]
-    low, blocks = lax.optimization_barrier((exchange(low), blocks))
-    low = low.reshape(toks, low.shape[2])
-
-    split = slots * 3 // 4
+    low = exchange(low).reshape(toks, low.shape[2])
+
+    split = slots * 5 // 8
     scanned = [
-        state_scan(reset_col, low, delta_parts, bias, decay, gain, conv, ctx, first, count)
+        state_scan(reset_col, low, delta_parts, bias, decay, gain, convs, ctx, first, count)
         for first, count in ((0, split), (split, slots - split))
     ]
     scanned[0], blocks = lax.optimization_barrier((scanned[0], blocks))

time: 159 us -> 142 us (0.89)
  waiting for transfers between devices: 29.8 us -> 14.9 us
  local copies, waits for them, and re-layouts: 27.9 us -> 23.1 us
  other arithmetic: 2.71 us -> 4.39 us
    ppermute x2, waiting for transfers between devices: 10.4 us -> 0.01 us  [shifted(): return lax.ppermute(value, axis, pairs)]
    unnamed x38 -> x34, local copies, waits for them, and re-layouts: 15.7 us -> 10.6 us
    all_to_all x4, waiting for transfers between devices: 19.3 us -> 14.8 us  [exchange(): return lax.all_to_all(value, 'ctx', 0, 0, tiled=True)]
    pallas_call x2, Pallas kernels: 34.2 us -> 32.6 us  [state_scan(): pl.pallas_call(functools.partial(scan_kernel, rank, first_shard), in_spec...]
  transfers between devices with their start and end apart: 8 -> 8, of which waited for: 4 -> 3; matrix products, arithmetic and copies ran while one was open for 9% -> 12% of each run, Pallas kernels for 14% -> 31%
where the time goes in v10:
time: 142 us; the launch traced here: 141 us
  Pallas kernels  46.9 us (33%)
  starting transfers between devices  23.8 us (17%)
  local copies, waits for them, and re-layouts  23.1 us (16%)
  waiting for transfers between devices  14.9 us (10%)
  between operations  14.3 us (10%)
  blocking collectives  13.8 us (10%)
  other arithmetic  4.39 us (3%)
    pallas_call x2, Pallas kernels, state_scan(): pl.pallas_call(functools.partial(scan_kernel, rank, first_shard), in_spec...  32.6 us
    all_to_all x4, starting transfers between devices, exchange(): return lax.all_to_all(value, 'ctx', 0, 0, tiled=True)  16.5 us
    all_to_all x4, waiting for transfers between devices, exchange(): return lax.all_to_all(value, 'ctx', 0, 0, tiled=True)  14.8 us
    all_to_all x1, blocking collectives, exchange(): return lax.all_to_all(value, 'ctx', 0, 0, tiled=True)  13.8 us
    unnamed x34, local copies, waits for them, and re-layouts  10.6 us
    ppermute x2, starting transfers between devices, shifted(): return lax.ppermute(value, axis, pairs)  7.26 us
    pallas_call x1, Pallas kernels, attention(): pl.pallas_call(functools.partial(attention_kernel, begin), grid=(end - be...  5.76 us
    pallas_call x1, Pallas kernels, conv_select(): pl.pallas_call(conv_select_kernel, grid=(2,), in_specs=[pl.BlockSpec(matc...  4.78 us
  transfers between devices with their start and end apart: 8, of which 3 were waited for; matrix products, arithmetic and copies ran while one was open for 12% of the time, Pallas kernels for 31%

profile of v10, /device:TPU:0, one launch (start us, length us, event | category | flops | bytes accessed | tf_op | source)
XLA Modules:
  0.0 141.2 jit_solution(5598514941001750249)
XLA Ops:
  7.2 1.2 copy-done
  9.2 1.6 %copy-done.4 = bf16[1,128,8192]{2,1,0:T(8,128)(2,1)S(1)} copy-done((bf16[1,128,8192]{2,1,0:T(8,128)(2,1)S(1)}, bf16[1,128,8192]{2,1,0:T(8,128)(2,1)}, u32[]{:S(2)}) %copy-start.4) | copy-done | bytes 2097176
  11.2 1.3 copy-done.1
  12.5 5.3 %all-to-all-start = ((bf16[4,128,2048]{2,1,0:T(8,128)(2,1)}), bf16[4,128,2048]{2,1,0:T(8,128)(2,1)S(1)}, u32[]{:S(2)}, u32[]{:S(2)}) async-start(bf16[4,128,2048]{2,1,0:T(8,128)(2,1)} %copy-done.1), calls=%async_computation | async-start | bytes 4194304 | tf_op jit(solution)/shard_map/all_to_all | solution.py:401
  20.0 0.8 copy.26
  20.8 0.8 copy.28
  21.8 0.9 convert_element_type.3.match_ref
  22.7 2.2 %reshape.75 = f32[16,8,1,4,256]{4,3,1,0,2:T(4,128)} reshape(f32[16,8192]{1,0:T(8,128)} %bitcast.33) | data formatting | bytes 1048576 | tf_op jit(solution)/shard_map/reshape | solution.py:434
  24.9 1.4 dynamic-slice_reduce_fusion
  27.6 1.4 constant_dynamic-slice_fusion.2
  29.0 1.7 %constant_dynamic-slice_fusion.1 = bf16[512,256]{1,0:T(8,128)(2,1)} fusion(bf16[512,1024]{1,0:T(8,128)(2,1)} %param.22, s32[]{:T(128)S(6)} %select_n.60), kind=kLoop, calls=%fused_computation.15 | loop fusion | bytes 524292 | tf_op jit(solution)/shard_map/dynamic_slice | solution.py:440
  30.7 1.7 %pad_maximum_fusion.refs_4_.refs_5_ = bf16[128,1024]{1,0:T(8,128)(2,1)} fusion(bf16[128,512]{1,0:T(8,128)(2,1)} %bitcast.38, bf16[128,512]{1,0:T(8,128)(2,1)} %bitcast.39), kind=kLoop, calls=%fused_computation | loop fusion | flops 524288 | bytes 524288 | tf_op jit(solution)/shard_map/concatenate | solution.py:465
  32.4 1.6 %broadcast_select_fusion.reset_hbm = f32[512,1]{1,0:T(8,128)} fusion(pred[512,1]{1,0:T(8,128)(4,1)} %copy.26), kind=kLoop, calls=%fused_computation.1 | loop fusion | flops 512 | bytes 2560 | tf_op jit(solution)/shard_map/jit(_where)/select_n | solution.py:453
  33.9 8.7 %all-to-all-done.x_ref = bf16[4,128,2048]{2,1,0:T(8,128)(2,1)S(1)} async-done(((bf16[4,128,2048]{2,1,0:T(8,128)(2,1)}), bf16[4,128,2048]{2,1,0:T(8,128)(2,1)S(1)}, u32[]{:S(2)}, u32[]{:S(2)}) %all-to-all-start) | async-done | bytes 2097184 | tf_op jit(solution)/shard_map/all_to_all | solution.py:401
  42.7 1.6 %copy-done.2 = bf16[4352,256]{1,0:T(8,128)(2,1)S(1)} copy-done((bf16[4352,256]{1,0:T(8,128)(2,1)S(1)}, bf16[4352,256]{1,0:T(8,128)(2,1)}, u32[]{:S(2)}) %copy-start.2) | copy-done | bytes 2228248
  44.4 4.8 %conv_select.1 = (bf16[512,1024]{1,0:T(8,128)(2,1)S(1)}, bf16[512,1024]{1,0:T(8,128)(2,1)S(1)}, bf16[4,128,640]{2,1,0:T(8,128)(2,1)S(1)}) custom-call(f32[512,3]{1,0:T(8,128)S(1)} %convert_element_type.3.match_ref, bf16[4,128,2048]{2,1,0:T(8,128)(2,1)S(1)} %all-to-all-done.x_ref, f32[4,2048]{1,0:T(4,128)S(1)} %bitcast.26, f32[1,2048]{1,0:T(1,128)S(1)} %bitcast.27, ...), custom_call_target="tpu_custom_call" | custom-call | flops 1140850688 | bytes 6422528 | tf_op jit(solution)/shard_map/conv_select/pallas_call | solution.py:168
  49.1 1.0 copy-done.6
  50.1 13.8 %all_to_all.25.part_ref = bf16[4,128,640]{2,1,0:T(8,128)(2,1)S(1)} all-to-all(bf16[4,128,640]{2,1,0:T(8,128)(2,1)S(1)} %get-tuple-element.30), channel_id=1, replica_groups=mesh['ctx'=4,'rep'=8] {'ctx'}, dimensions={0} | all-to-all | bytes 1310720 | tf_op jit(solution)/shard_map/all_to_all | solution.py:401
  63.9 1.0 normalise.1
  64.9 3.5 %all-to-all-start.2 = ((bf16[4,128,640]{2,1,0:T(8,128)(2,1)}), bf16[4,128,640]{2,1,0:T(8,128)(2,1)S(1)}, u32[]{:S(2)}, u32[]{:S(2)}) async-start(bf16[4,128,640]{2,1,0:T(8,128)(2,1)} %normalise.1), calls=%async_computation.2 | async-start | bytes 1310720 | tf_op jit(solution)/shard_map/all_to_all | solution.py:401
  68.4 3.9 %collective-permute-start.1 = (bf16[128,1024]{1,0:T(8,128)(2,1)S(1)}, bf16[128,1024]{1,0:T(8,128)(2,1)S(1)}, u32[]{:S(2)}, u32[]{:S(2)}) collective-permute-start(bf16[128,1024]{1,0:T(8,128)(2,1)S(1)} %copy-done.7), channel_id=1, source_target_pairs={{0,8},{8,16},{16,24},{1,9},{9,17},{17,25},{2,10},{10,18},{18,26},{... | collective-permute-start | bytes 786440 | tf_op jit(solution)/shard_map/ppermute | solution.py:397
  72.3 3.4 %collective-permute-start = (bf16[128,1024]{1,0:T(8,128)(2,1)S(1)}, bf16[128,1024]{1,0:T(8,128)(2,1)S(1)}, u32[]{:S(2)}, u32[]{:S(2)}) collective-permute-start(bf16[128,1024]{1,0:T(8,128)(2,1)S(1)} %copy-done.7), channel_id=1, source_target_pairs={{0,16},{8,24},{1,17},{9,25},{2,18},{10,26},{3,19},{11,27},{4,20},{... | collective-permute-start | bytes 786440 | tf_op jit(solution)/shard_map/ppermute | solution.py:397
  75.7 3.5 %all-to-all-done.2 = bf16[4,128,640]{2,1,0:T(8,128)(2,1)S(1)} async-done(((bf16[4,128,640]{2,1,0:T(8,128)(2,1)}), bf16[4,128,640]{2,1,0:T(8,128)(2,1)S(1)}, u32[]{:S(2)}, u32[]{:S(2)}) %all-to-all-start.2) | async-done | bytes 655392 | tf_op jit(solution)/shard_map/all_to_all | solution.py:401
  79.2 0.8 copy-done.10
  80.1 19.3 %state_scan_0.1 = bf16[4,128,1280]{2,1,0:T(8,128)(2,1)} custom-call(f32[512,1]{1,0:T(8,128)} %broadcast_select_fusion.reset_hbm, bf16[512,640]{1,0:T(8,128)(2,1)} %bitcast.31, bf16[8,512,256]{2,1,0:T(8,128)(2,1)} %bitcast.46, f32[1,2048]{1,0:T(1,128)} %bitcast.42, f32[16,2048]{1,0:T(8,128)} %bitcast.35, f32[1,2048]{1,0:T(1,128)} %bitcast.44, ...), custom_call_target="tpu_custom_call" | custom-call | flops 62914560 | bytes 3932160 | tf_op jit(solution)/shard_map/state_scan_0/pallas_call | solution.py:338
  100.2 3.5 %all-to-all-start.3 = ((bf16[4,128,1280]{2,1,0:T(8,128)(2,1)}), bf16[4,128,1280]{2,1,0:T(8,128)(2,1)S(1)}, u32[]{:S(2)}, u32[]{:S(2)}) async-start(bf16[4,128,1280]{2,1,0:T(8,128)(2,1)} %state_scan_0.1), calls=%async_computation.3 | async-start | bytes 2621440 | tf_op jit(solution)/shard_map/all_to_all | solution.py:401
  103.7 13.2 %state_scan_5.1 = bf16[4,128,768]{2,1,0:T(8,128)(2,1)} custom-call(f32[512,1]{1,0:T(8,128)} %broadcast_select_fusion.reset_hbm, bf16[512,640]{1,0:T(8,128)(2,1)} %bitcast.32, bf16[8,512,256]{2,1,0:T(8,128)(2,1)} %bitcast.47, f32[1,2048]{1,0:T(1,128)} %bitcast.43, f32[16,2048]{1,0:T(8,128)} %bitcast.36, f32[1,2048]{1,0:T(1,128)} %bitcast.45, ...), custom_call_target="tpu_custom_call" | custom-call | flops 37748736 | bytes 2359296 | tf_op jit(solution)/shard_map/state_scan_5/pallas_call | solution.py:338
  117.0 4.2 %all-to-all-start.4 = ((bf16[4,128,768]{2,1,0:T(8,128)(2,1)}), bf16[4,128,768]{2,1,0:T(8,128)(2,1)S(1)}, u32[]{:S(2)}, u32[]{:S(2)}) async-start(bf16[4,128,768]{2,1,0:T(8,128)(2,1)} %state_scan_5.1), calls=%async_computation.4 | async-start | bytes 1572864 | tf_op jit(solution)/shard_map/all_to_all | solution.py:401
  121.9 5.8 %attention_0.1 = bf16[128,4096]{1,0:T(8,128)(2,1)} custom-call(s32[128,1]{1,0:T(8,128)} %copy.29.seg_q_ref, s32[1,384]{1,0:T(1,128)} %broadcast_in_dim.25.seg_k_ref, bf16[128,4096]{1,0:T(8,128)(2,1)} %bitcast.29, bf16[128,1024]{1,0:T(8,128)(2,1)} %copy-done.9, bf16[128,1024]{1,0:T(8,128)(2,1)} %copy-done.9, bf16[128,1024]{1,0:T(8,128)(2,1)} %copy-done.8, ...), custom_call_target="tpu_custom_call" | custom-call | flops 805306368 | bytes 2097152 | tf_op jit(solution)/shard_map/attention_0/pallas_call | solution.py:73
  127.7 2.6 %all-to-all-done.4.refs_1_ = bf16[4,128,768]{2,1,0:T(8,128)(2,1)S(1)} async-done(((bf16[4,128,768]{2,1,0:T(8,128)(2,1)}), bf16[4,128,768]{2,1,0:T(8,128)(2,1)S(1)}, u32[]{:S(2)}, u32[]{:S(2)}) %all-to-all-start.4) | async-done | bytes 786464 | tf_op jit(solution)/shard_map/all_to_all | solution.py:401
  130.2 1.6 %copy-done.3 = bf16[1,128,8192]{2,1,0:T(8,128)(2,1)S(1)} copy-done((bf16[1,128,8192]{2,1,0:T(8,128)(2,1)S(1)}, bf16[1,128,8192]{2,1,0:T(8,128)(2,1)}, u32[]{:S(2)}) %copy-start.3) | copy-done | bytes 2097176
  131.8 2.5 %gate.1 = bf16[128,8192]{1,0:T(8,128)(2,1)} custom-call(bf16[128,8192]{1,0:T(8,128)(2,1)S(1)} %bitcast.24, bf16[4,128,1280]{2,1,0:T(8,128)(2,1)S(1)} %all-to-all-done.3.refs_0_, bf16[4,128,768]{2,1,0:T(8,128)(2,1)S(1)} %all-to-all-done.4.refs_1_), custom_call_target="tpu_custom_call" | custom-call | flops 4194304 | bytes 6291456 | tf_op jit(solution)/shard_map/gate/pallas_call | solution.py:382
  (55 shorter events, 6.4 us)
Async XLA Ops:
  7.2 1.3 copy-start
  7.2 35.5 %all-gather.5.cloned.1.call-start = ((), (), s32[]{:S(2)}) async-start(), calls=%async_computation.5 | async-start | bytes 2506752 | tf_op jit(solution)/shard_map/all_gather | solution.py:443
  9.2 1.6 %copy-start.4 = (bf16[1,128,8192]{2,1,0:T(8,128)(2,1)S(1)}, bf16[1,128,8192]{2,1,0:T(8,128)(2,1)}, u32[]{:S(2)}) copy-start(bf16[1,128,8192]{2,1,0:T(8,128)(2,1)} %param.16) | copy-start | bytes 6291460
  11.1 1.3 copy-start.1
  12.5 5.3 %copy-start.12 = (s32[1,512]{1,0:T(1,128)S(1)}, s32[1,512]{1,0:T(1,128)}, u32[]{:S(2)}) copy-start(s32[1,512]{1,0:T(1,128)} %param.18) | copy-start | bytes 6148
  12.5 6.0 %copy-start.13 = (f32[8192]{0:T(1024)S(1)}, f32[8192]{0:T(1024)}, u32[]{:S(2)}) copy-start(f32[8192]{0:T(1024)} %param.20) | copy-start | bytes 98308
  12.5 6.7 %copy-start.14 = (f32[8192]{0:T(1024)S(1)}, f32[8192]{0:T(1024)}, u32[]{:S(2)}) copy-start(f32[8192]{0:T(1024)} %param.23) | copy-start | bytes 98308
  12.5 6.7 %copy-start.15 = (f32[8192]{0:T(1024)S(1)}, f32[8192]{0:T(1024)}, u32[]{:S(2)}) copy-start(f32[8192]{0:T(1024)} %param.25) | copy-start | bytes 98308
  12.5 9.1 %copy-start.11 = (f32[4,8192]{1,0:T(4,128)S(1)}, f32[4,8192]{1,0:T(4,128)}, u32[]{:S(2)}) copy-start(f32[4,8192]{1,0:T(4,128)} %param.19) | copy-start | bytes 393220
  12.5 30.2 %all-to-all-start = ((bf16[4,128,2048]{2,1,0:T(8,128)(2,1)}), bf16[4,128,2048]{2,1,0:T(8,128)(2,1)S(1)}, u32[]{:S(2)}, u32[]{:S(2)}) async-start(bf16[4,128,2048]{2,1,0:T(8,128)(2,1)} %copy-done.1), calls=%async_computation | async-start | bytes 4194304 | tf_op jit(solution)/shard_map/all_to_all | solution.py:401
  17.8 61.4 %all-gather.7.cloned.1.call-start = ((), (), s32[]{:S(2)}) async-start(), calls=%async_computation.6 | async-start | bytes 2359296 | tf_op jit(solution)/shard_map/all_gather | solution.py:443
  42.7 1.6 %copy-start.2 = (bf16[4352,256]{1,0:T(8,128)(2,1)S(1)}, bf16[4352,256]{1,0:T(8,128)(2,1)}, u32[]{:S(2)}) copy-start(bf16[4352,256]{1,0:T(8,128)(2,1)} %all-gather.5.cloned.1.call-done) | copy-start | bytes 6684676
  49.1 1.0 copy-start.6
  50.1 13.8 %copy-start.5 = (bf16[512,1024]{1,0:T(8,128)(2,1)}, bf16[512,1024]{1,0:T(8,128)(2,1)S(1)}, u32[]{:S(2)}) copy-start(bf16[512,1024]{1,0:T(8,128)(2,1)S(1)} %get-tuple-element.37.early_hbm) | copy-start | bytes 3145732
  50.1 18.3 %copy-start.7 = (bf16[128,1024]{1,0:T(8,128)(2,1)S(1)}, bf16[128,1024]{1,0:T(8,128)(2,1)}, u32[]{:S(2)}) copy-start(bf16[128,1024]{1,0:T(8,128)(2,1)} %pad_maximum_fusion.refs_4_.refs_5_) | copy-start | bytes 786436
  64.9 14.3 %all-to-all-start.2 = ((bf16[4,128,640]{2,1,0:T(8,128)(2,1)}), bf16[4,128,640]{2,1,0:T(8,128)(2,1)S(1)}, u32[]{:S(2)}, u32[]{:S(2)}) async-start(bf16[4,128,640]{2,1,0:T(8,128)(2,1)} %normalise.1), calls=%async_computation.2 | async-start | bytes 1310720 | tf_op jit(solution)/shard_map/all_to_all | solution.py:401
  68.4 31.0 %collective-permute-start.1 = (bf16[128,1024]{1,0:T(8,128)(2,1)S(1)}, bf16[128,1024]{1,0:T(8,128)(2,1)S(1)}, u32[]{:S(2)}, u32[]{:S(2)}) collective-permute-start(bf16[128,1024]{1,0:T(8,128)(2,1)S(1)} %copy-done.7), channel_id=1, source_target_pairs={{0,8},{8,16},{16,24},{1,9},{9,17},{17,25},{2,10},{10,18},{18,26},{... | collective-permute-start | bytes 786440 | tf_op jit(solution)/shard_map/ppermute | solution.py:397
  72.3 27.1 %collective-permute-start = (bf16[128,1024]{1,0:T(8,128)(2,1)S(1)}, bf16[128,1024]{1,0:T(8,128)(2,1)S(1)}, u32[]{:S(2)}, u32[]{:S(2)}) collective-permute-start(bf16[128,1024]{1,0:T(8,128)(2,1)S(1)} %copy-done.7), channel_id=1, source_target_pairs={{0,16},{8,24},{1,17},{9,25},{2,18},{10,26},{3,19},{11,27},{4,20},{... | collective-permute-start | bytes 786440 | tf_op jit(solution)/shard_map/ppermute | solution.py:397
  79.2 0.8 copy-start.10
  99.4 17.5 %copy-start.8 = (bf16[128,1024]{1,0:T(8,128)(2,1)}, bf16[128,1024]{1,0:T(8,128)(2,1)S(1)}, u32[]{:S(2)}) copy-start(bf16[128,1024]{1,0:T(8,128)(2,1)S(1)} %collective-permute-done.1.refs_2_.refs_3_) | copy-start | bytes 786436
  99.5 0.7 copy-start.9
  100.2 16.8 %all-to-all-start.3 = ((bf16[4,128,1280]{2,1,0:T(8,128)(2,1)}), bf16[4,128,1280]{2,1,0:T(8,128)(2,1)S(1)}, u32[]{:S(2)}, u32[]{:S(2)}) async-start(bf16[4,128,1280]{2,1,0:T(8,128)(2,1)} %state_scan_0.1), calls=%async_computation.3 | async-start | bytes 2621440 | tf_op jit(solution)/shard_map/all_to_all | solution.py:401
  117.0 13.2 %all-to-all-start.4 = ((bf16[4,128,768]{2,1,0:T(8,128)(2,1)}), bf16[4,128,768]{2,1,0:T(8,128)(2,1)S(1)}, u32[]{:S(2)}, u32[]{:S(2)}) async-start(bf16[4,128,768]{2,1,0:T(8,128)(2,1)} %state_scan_5.1), calls=%async_computation.4 | async-start | bytes 1572864 | tf_op jit(solution)/shard_map/all_to_all | solution.py:401
  130.2 1.6 %copy-start.3 = (bf16[1,128,8192]{2,1,0:T(8,128)(2,1)S(1)}, bf16[1,128,8192]{2,1,0:T(8,128)(2,1)}, u32[]{:S(2)}) copy-start(bf16[1,128,8192]{2,1,0:T(8,128)(2,1)} %param.17) | copy-start | bytes 6291460
Sparse Core Ops, SparseCore 0:
  9.7 32.9 all-gather.4
  44.2 28.5 all-gather.6

commit v11 on v10

--- a/solution.py
+++ b/solution.py
@@ -22,9 +22,8 @@
     return half + half * jnp.tanh(half)
 
 
-def attention_kernel(begin, seg_q_ref, seg_k_ref, q_ref, *refs):
-    out_ref = refs[-1]
-    refs = refs[: -1 if begin == 0 else -2]
+def attention_kernel(place_ref, seg_q_ref, seg_k_ref, q_ref, *refs):
+    key_refs, value_refs, out_ref = refs[0:-1:2], refs[1:-1:2], refs[-1]
     rows = q_ref.shape[0]
     span = seg_k_ref.shape[1]
     groups = QUERY_HEADS // KEY_VALUE_HEADS
@@ -32,8 +31,8 @@
     col = lax.broadcasted_iota(jnp.int32, (rows, span), 1)
     allowed = (col <= row) & (seg_q_ref[...] == seg_k_ref[...])
     shift = jnp.where(allowed, 0.0, -FAR)
-    keys = jnp.concatenate([ref[...] for ref in refs[0::2]], axis=0)
-    vals = jnp.concatenate([ref[...] for ref in refs[1::2]], axis=0)
+    keys = jnp.concatenate([ref[0] for ref in key_refs], axis=0)
+    vals = jnp.concatenate([ref[0] for ref in value_refs], axis=0)
     factor = LOG2E / math.sqrt(HEAD_WIDTH)
     batch = 4
     for first in range(0, groups, batch):
@@ -51,40 +50,38 @@
             out_ref[:, cut] = (total / norm).astype(out_ref.dtype)
 
 
-def attention(queries, blocks, seg_q, seg_k, begin, end, before=None):
+def attention(queries, blocks, seg_q, seg_k, place, back):
     rows = queries.shape[0]
     span = seg_k.shape[1]
     group_width = QUERY_HEADS // KEY_VALUE_HEADS * HEAD_WIDTH
-    key_spec = pl.BlockSpec((rows, HEAD_WIDTH), lambda h: (0, begin + h))
-    value_spec = pl.BlockSpec((rows, HEAD_WIDTH), lambda h: (0, KEY_VALUE_HEADS + begin + h))
-    wide = pl.BlockSpec((rows, group_width), lambda h: (0, begin + h))
-    operands = [seg_q, seg_k, queries] + [block for block in blocks for _ in range(2)]
+    wide = pl.BlockSpec((rows, group_width), lambda h, p: (0, h))
     in_specs = [
-        pl.BlockSpec((rows, 1), lambda h: (0, 0)),
-        pl.BlockSpec((1, span), lambda h: (0, 0)),
+        pl.BlockSpec((rows, 1), lambda h, p: (0, 0)),
+        pl.BlockSpec((1, span), lambda h, p: (0, 0)),
         wide,
-        *([key_spec, value_spec] * len(blocks)),
     ]
-    aliases = {}
-    if before is not None:
-        aliases = {len(operands): 0}
-        operands.append(before)
-        in_specs.append(pl.BlockSpec(memory_space=pl.ANY))
-    return pl.pallas_call(
-        functools.partial(attention_kernel, begin),
-        grid=(end - begin,),
-        in_specs=in_specs,
-        out_specs=wide,
+    for by in range(back, -1, -1):
+        for first in (0, KEY_VALUE_HEADS):
+            in_specs.append(
+                pl.BlockSpec(
+                    (1, rows, HEAD_WIDTH),
+                    lambda h, p, by=by, first=first: (jnp.maximum(p[0] - by, 0), 0, first + h),
+                )
+            )
+    return pl.pallas_call(
+        attention_kernel,
+        grid_spec=pltpu.PrefetchScalarGridSpec(
+            num_scalar_prefetch=1, grid=(KEY_VALUE_HEADS,), in_specs=in_specs, out_specs=wide
+        ),
         out_shape=jax.ShapeDtypeStruct(queries.shape, jnp.bfloat16),
-        input_output_aliases=aliases,
         compiler_params=pltpu.CompilerParams(vmem_limit_bytes=54 << 20),
         cost_estimate=pl.CostEstimate(
-            flops=4 * rows * span * group_width * (end - begin),
-            bytes_accessed=4 * rows * group_width * (end - begin),
-            transcendentals=rows * span * group_width // HEAD_WIDTH * (end - begin),
+            flops=4 * rows * span * QUERY_HEADS * HEAD_WIDTH,
+            bytes_accessed=4 * queries.size,
+            transcendentals=rows * span * QUERY_HEADS,
         ),
-        name=f"attention_{begin}",
-    )(*operands)
+        name="attention",
+    )(place, seg_q, seg_k, queries, *([blocks] * (2 * back + 2)))
 
 
 def piece_lanes(slot, piece, ctx, fold, width):
@@ -151,11 +148,9 @@
     @pl.when(step == 1)
     def _():
         late_ref[...] = conv
-        spare = part_ref.shape[2] - outputs
-        full = (total[...] + added).astype(part_ref.dtype)
-        for piece in range(pieces):
-            part_ref[piece, :, 0:outputs] = full[piece * rows : (piece + 1) * rows, :]
-            part_ref[piece, :, outputs:] = jnp.zeros((rows, spare), part_ref.dtype)
+        spare = part_ref.shape[1] - outputs
+        part_ref[:, 0:outputs] = (total[...] + added).astype(part_ref.dtype)
+        part_ref[:, outputs:] = jnp.zeros((toks, spare), part_ref.dtype)
 
 
 def conv_select(match, pieces, conv_weight, conv_bias, select_parts):
@@ -175,7 +170,7 @@
             pl.BlockSpec((1, wide), lambda s: (0, s)),
             pl.BlockSpec((slots // 2, outputs, width), lambda s: (s, 0, 0)),
         ],
-        out_specs=[half, half, pl.BlockSpec((ctx, rows, padded_outputs), lambda s: (0, 0, 0))],
+        out_specs=[half, half, pl.BlockSpec((toks, padded_outputs), lambda s: (0, 0))],
         scratch_shapes=[
             pltpu.VMEM((3, toks, LANES), jnp.float32),
             pltpu.VMEM((wide // LANES, SUBLANES + toks, LANES), jnp.float32),
@@ -184,7 +179,7 @@
         out_shape=[
             jax.ShapeDtypeStruct((toks, wide), jnp.bfloat16),
             jax.ShapeDtypeStruct((toks, wide), jnp.bfloat16),
-            jax.ShapeDtypeStruct((ctx, rows, padded_outputs), jnp.bfloat16),
+            jax.ShapeDtypeStruct((toks, padded_outputs), jnp.bfloat16),
         ],
         compiler_params=pltpu.CompilerParams(vmem_limit_bytes=32 << 20),
         cost_estimate=pl.CostEstimate(
@@ -196,27 +191,20 @@
     )(match, pieces, conv_weight, conv_bias, select_parts)
 
 
-def normalise_kernel(rank, part_ref, out_ref):
-    pieces = part_ref.shape[0]
-    total = part_ref[0].astype(jnp.float32)
-    for piece in range(1, pieces):
-        total = total + part_ref[piece].astype(jnp.float32)
-    low = total[:, :rank]
+def normalise_kernel(rank, select_ref, out_ref):
+    low = select_ref[:, :rank].astype(jnp.float32)
     scale = lax.rsqrt(jnp.mean(low * low, axis=-1, keepdims=True) + 1e-06)
-    low = (low * scale).astype(out_ref.dtype)
-    maps = total[:, rank:].astype(out_ref.dtype)
-    for piece in range(pieces):
-        out_ref[piece, :, :rank] = low
-        out_ref[piece, :, rank:] = maps
-
-
-def normalise(parts, rank):
+    out_ref[:, :rank] = (low * scale).astype(out_ref.dtype)
+    out_ref[:, rank:] = select_ref[:, rank:]
+
+
+def normalise(select, rank):
     return pl.pallas_call(
         functools.partial(normalise_kernel, rank),
-        out_shape=jax.ShapeDtypeStruct(parts.shape, jnp.bfloat16),
+        out_shape=jax.ShapeDtypeStruct(select.shape, jnp.bfloat16),
         compiler_params=pltpu.CompilerParams(vmem_limit_bytes=12 << 20),
         name="normalise",
-    )(parts)
+    )(select)
 
 
 def scan_kernel(rank, first_shard, reset_hbm, low_hbm, weight_hbm, bias_ref, decay_ref, gain_ref,
@@ -385,16 +373,10 @@
         in_specs=[columns] + [pl.BlockSpec((ctx, part, array.shape[2]), lambda r: (0, r, 0)) for array in parts],
         out_specs=columns,
         out_shape=jax.ShapeDtypeStruct(gate.shape, jnp.bfloat16),
-        compiler_params=pltpu.CompilerParams(vmem_limit_bytes=16 << 20),
+        compiler_params=pltpu.CompilerParams(vmem_limit_bytes=60 << 20),
         cost_estimate=pl.CostEstimate(flops=4 * gate.size, bytes_accessed=6 * gate.size, transcendentals=gate.size),
         name="gate",
     )(gate, *parts)
-
-
-def shifted(value, axis, by):
-    size = lax.axis_size(axis)
-    pairs = [(i, i + by) for i in range(size) if 0 <= i + by < size]
-    return lax.ppermute(value, axis, pairs)
 
 
 def exchange(value):
@@ -462,7 +444,7 @@
         reset_col,
         seg_k[back * rows :, None],
         seg_k[None, :],
-        jnp.concatenate([keys[0], values[0]], axis=1),
+        jnp.broadcast_to(jnp.concatenate([keys[0], values[0]], axis=1), (ctx, rows, keys.shape[2] + values.shape[2])),
         own_part(conv_weight),
         own_part(conv_bias)[None, :],
         match,
@@ -473,11 +455,10 @@
     delta_parts = gathered(delta_own)
 
     *convs, parts = conv_select(match, pieces, conv_weight, conv_bias, select_parts)
-    low = normalise(exchange(parts), rank)
+    low = normalise(lax.psum(parts, "ctx"), rank)
 
     low, both = lax.optimization_barrier((low, both))
-    blocks = [shifted(both, "ctx", by) for by in range(back, 0, -1)] + [both]
-    low = exchange(low).reshape(toks, low.shape[2])
+    blocks = exchange(both)
 
     split = slots * 5 // 8
     scanned = [
@@ -485,7 +466,7 @@
         for first, count in ((0, split), (split, slots - split))
     ]
     scanned[0], blocks = lax.optimization_barrier((scanned[0], blocks))
-    attended = attention(queries[0], blocks, seg_q, seg_k, 0, KEY_VALUE_HEADS)
+    attended = attention(queries[0], blocks, seg_q, seg_k, jnp.reshape(place, (1,)).astype(jnp.int32), back)
     scanned = [exchange(part) for part in scanned]
     scanned[0], attended = lax.optimization_barrier((scanned[0], attended))
     mixed = apply_gate(scanned, gate_input[0], fold, width)

time: 142 us -> 199 us (1.40)
  waiting for transfers between devices: 14.9 us -> 88.9 us
  blocking collectives: 13.8 us -> 0 us
  starting transfers between devices: 23.8 us -> 16.1 us
  local copies, waits for them, and re-layouts: 23.1 us -> 26.6 us
    psum x0 -> x1, waiting for transfers between devices: none -> 46.7 us  [local(): low = normalise(lax.psum(parts, 'ctx'), rank)]
    all_gather x2, waiting for transfers between devices: 0.02 us -> 25.1 us  [gathered(): parts = lax.all_gather(own, 'rep', axis=0)]
    all_to_all x1 -> x0, blocking collectives: 13.8 us -> none  [exchange(): return lax.all_to_all(value, 'ctx', 0, 0, tiled=True)]
    ppermute x2 -> x0, starting transfers between devices: 7.26 us -> none  [shifted(): return lax.ppermute(value, axis, pairs)]
    broadcast_in_dim x0 -> x1, local copies, waits for them, and re-layouts: none -> 2.05 us  [local(): jnp.broadcast_to(jnp.concatenate([keys[0], values[0]], axis=1), (ctx, row...]
    pallas_call x1, Pallas kernels: 2.52 us -> 4.55 us  [apply_gate(): pl.pallas_call(functools.partial(gate_kernel, fold, width), grid=(rows //...]
    unnamed x34 -> x36, local copies, waits for them, and re-layouts: 10.6 us -> 12.1 us
  transfers between devices with their start and end apart: 8 -> 7, of which waited for: 3 -> 5; matrix products, arithmetic and copies ran while one was open for 12% -> 10% of each run, Pallas kernels for 31% -> 20%
where the time goes in v11:
time: 199 us; the launch traced here: 198 us
  waiting for transfers between devices  88.9 us (45%)
  Pallas kernels  48.2 us (24%)
  local copies, waits for them, and re-layouts  26.6 us (13%)
  starting transfers between devices  16.1 us (8%)
  between operations  13.9 us (7%)
  other arithmetic  4.38 us (2%)
    psum x1, waiting for transfers between devices, local(): low = normalise(lax.psum(parts, 'ctx'), rank)  46.7 us
    pallas_call x2, Pallas kernels, state_scan(): pl.pallas_call(functools.partial(scan_kernel, rank, first_shard), in_spec...  32.5 us
    all_gather x2, waiting for transfers between devices, gathered(): parts = lax.all_gather(own, 'rep', axis=0)  25.1 us
    all_to_all x4, waiting for transfers between devices, exchange(): return lax.all_to_all(value, 'ctx', 0, 0, tiled=True)  16.4 us
    all_to_all x4, starting transfers between devices, exchange(): return lax.all_to_all(value, 'ctx', 0, 0, tiled=True)  16 us
    unnamed x36, local copies, waits for them, and re-layouts  12.1 us
    pallas_call x1, Pallas kernels, attention(): pl.pallas_call(attention_kernel, grid_spec=pltpu.PrefetchScalarGridSpec(n...  5.81 us
    pallas_call x1, Pallas kernels, conv_select(): pl.pallas_call(conv_select_kernel, grid=(2,), in_specs=[pl.BlockSpec(matc...  4.76 us
  transfers between devices with their start and end apart: 7, of which 5 were waited for; matrix products, arithmetic and copies ran while one was open for 10% of the time, Pallas kernels for 20%

profile of v11, /device:TPU:0, one launch (start us, length us, event | category | flops | bytes accessed | tf_op | source)
XLA Modules:
  0.0 198.1 jit_solution(15322794223452916314)
XLA Ops:
  7.2 1.2 copy-done
  9.2 1.6 copy-done.3
  11.1 1.3 copy-done.1
  12.5 5.3 %all-to-all-start = ((bf16[4,128,2048]{2,1,0:T(8,128)(2,1)}), bf16[4,128,2048]{2,1,0:T(8,128)(2,1)S(1)}, u32[]{:S(2)}, u32[]{:S(2)}) async-start(bf16[4,128,2048]{2,1,0:T(8,128)(2,1)} %copy-done.1), calls=%async_computation | async-start | bytes 4194304 | tf_op jit(solution)/shard_map/all_to_all | solution.py:383
  21.9 0.9 convert_element_type.3.match_ref
  22.7 2.2 %reshape.75 = f32[16,8,1,4,256]{4,3,1,0,2:T(4,128)} reshape(f32[16,8192]{1,0:T(8,128)} %bitcast.31) | data formatting | bytes 1048576 | tf_op jit(solution)/shard_map/reshape | solution.py:416
  24.9 1.4 dynamic-slice_reduce_fusion
  27.6 1.4 constant_dynamic-slice_fusion.2
  29.0 1.7 constant_dynamic-slice_fusion.1
  30.7 1.7 pad_maximum_fusion
  32.4 1.6 broadcast_select_fusion.reset_hbm
  33.9 8.7 %all-to-all-done.x_ref = bf16[4,128,2048]{2,1,0:T(8,128)(2,1)S(1)} async-done(((bf16[4,128,2048]{2,1,0:T(8,128)(2,1)}), bf16[4,128,2048]{2,1,0:T(8,128)(2,1)S(1)}, u32[]{:S(2)}, u32[]{:S(2)}) %all-to-all-start) | async-done | bytes 2097184 | tf_op jit(solution)/shard_map/all_to_all | solution.py:383
  42.6 2.0 %broadcast_in_dim.29 = bf16[4,128,1024]{2,1,0:T(8,128)(2,1)} broadcast(bf16[128,1024]{1,0:T(8,128)(2,1)} %pad_maximum_fusion), dimensions={1,2} | broadcast | bytes 1310720 | tf_op jit(solution)/shard_map/broadcast_in_dim | solution.py:447
  44.7 1.6 copy-done.2
  46.3 4.8 %conv_select.1 = (bf16[512,1024]{1,0:T(8,128)(2,1)S(1)}, bf16[512,1024]{1,0:T(8,128)(2,1)S(1)}, bf16[512,640]{1,0:T(8,128)(2,1)S(1)}) custom-call(f32[512,3]{1,0:T(8,128)S(1)} %convert_element_type.3.match_ref, bf16[4,128,2048]{2,1,0:T(8,128)(2,1)S(1)} %all-to-all-done.x_ref, f32[4,2048]{1,0:T(4,128)S(1)} %bitcast.25, f32[1,2048]{1,0:T(1,128)S(1)} %bitcast.26, ...), custom_call_target="tpu_custom_call" | custom-call | flops 1140850688 | bytes 6422528 | tf_op jit(solution)/shard_map/conv_select/pallas_call | solution.py:163
  51.1 0.8 copy-done.5
  51.9 1.0 copy-done.7
  52.9 1.0 copy-done.8
  54.7 46.7 %all-reduce.4.cloned.1.call-done.select_ref = bf16[512,640]{1,0:T(8,128)(2,1)} async-done(((bf16[512,640]{1,0:T(8,128)(2,1)}), bf16[512,640]{1,0:T(8,128)(2,1)}) %all-reduce.4.cloned.1.call-update) | async-done | bytes 655376 | tf_op jit(solution)/shard_map/psum | solution.py:458
  101.4 1.1 copy-done.6
  102.7 0.8 copy-done.4
  103.5 3.5 %all-to-all-start.1 = ((bf16[4,128,1024]{2,1,0:T(8,128)(2,1)}), bf16[4,128,1024]{2,1,0:T(8,128)(2,1)S(1)}, u32[]{:S(2)}, u32[]{:S(2)}) async-start(bf16[4,128,1024]{2,1,0:T(8,128)(2,1)} %broadcast_in_dim.29), calls=%async_computation.1 | async-start | bytes 2097152 | tf_op jit(solution)/shard_map/all_to_all | solution.py:383
  107.0 25.1 %all-gather.7.cloned.1.call-done = bf16[4096,256]{1,0:T(8,128)(2,1)} async-done(((bf16[512,256]{1,0:T(8,128)(2,1)}), bf16[4096,256]{1,0:T(8,128)(2,1)}) %all-gather.7.cloned.1.call-update) | async-done | bytes 2097168 | tf_op jit(solution)/shard_map/all_gather | solution.py:425
  132.1 19.3 %state_scan_0.1 = bf16[4,128,1280]{2,1,0:T(8,128)(2,1)} custom-call(f32[512,1]{1,0:T(8,128)} %broadcast_select_fusion.reset_hbm, bf16[512,640]{1,0:T(8,128)(2,1)} %copy-done.4, bf16[8,512,256]{2,1,0:T(8,128)(2,1)} %bitcast.44, f32[1,2048]{1,0:T(1,128)} %bitcast.40, f32[16,2048]{1,0:T(8,128)} %bitcast.33, f32[1,2048]{1,0:T(1,128)} %bitcast.42, ...), custom_call_target="tpu_custom_call" | custom-call | flops 62914560 | bytes 3932160 | tf_op jit(solution)/shard_map/state_scan_0/pallas_call | solution.py:326
  151.5 3.7 %all-to-all-start.2 = ((bf16[4,128,1280]{2,1,0:T(8,128)(2,1)}), bf16[4,128,1280]{2,1,0:T(8,128)(2,1)S(1)}, u32[]{:S(2)}, u32[]{:S(2)}) async-start(bf16[4,128,1280]{2,1,0:T(8,128)(2,1)} %state_scan_0.1), calls=%async_computation.2 | async-start | bytes 2621440 | tf_op jit(solution)/shard_map/all_to_all | solution.py:383
  155.1 13.2 %state_scan_5.1 = bf16[4,128,768]{2,1,0:T(8,128)(2,1)} custom-call(f32[512,1]{1,0:T(8,128)} %broadcast_select_fusion.reset_hbm, bf16[512,640]{1,0:T(8,128)(2,1)} %copy-done.4, bf16[8,512,256]{2,1,0:T(8,128)(2,1)} %bitcast.45, f32[1,2048]{1,0:T(1,128)} %bitcast.41, f32[16,2048]{1,0:T(8,128)} %bitcast.34, f32[1,2048]{1,0:T(1,128)} %bitcast.43, ...), custom_call_target="tpu_custom_call" | custom-call | flops 37748736 | bytes 2359296 | tf_op jit(solution)/shard_map/state_scan_5/pallas_call | solution.py:326
  168.4 3.8 %all-to-all-done.2.refs_0_ = bf16[4,128,1280]{2,1,0:T(8,128)(2,1)S(1)} async-done(((bf16[4,128,1280]{2,1,0:T(8,128)(2,1)}), bf16[4,128,1280]{2,1,0:T(8,128)(2,1)S(1)}, u32[]{:S(2)}, u32[]{:S(2)}) %all-to-all-start.2) | async-done | bytes 1310752 | tf_op jit(solution)/shard_map/all_to_all | solution.py:383
  172.1 3.5 %all-to-all-start.3 = ((bf16[4,128,768]{2,1,0:T(8,128)(2,1)}), bf16[4,128,768]{2,1,0:T(8,128)(2,1)S(1)}, u32[]{:S(2)}, u32[]{:S(2)}) async-start(bf16[4,128,768]{2,1,0:T(8,128)(2,1)} %state_scan_5.1), calls=%async_computation.3 | async-start | bytes 1572864 | tf_op jit(solution)/shard_map/all_to_all | solution.py:383
  176.4 5.8 %attention.1 = bf16[128,4096]{1,0:T(8,128)(2,1)} custom-call(s32[1]{0:T(128)} %bitcast.12.place_ref, s32[128,1]{1,0:T(8,128)} %copy.29.seg_q_ref, s32[1,384]{1,0:T(1,128)} %broadcast_in_dim.28.seg_k_ref, bf16[128,4096]{1,0:T(8,128)(2,1)} %bitcast.29, bf16[4,128,1024]{2,1,0:T(8,128)(2,1)} %copy-done.9, bf16[4,128,1024]{2,1,0:T(8,128)(2,1)} %copy-done.9, ...), custom_call_target="tpu_custom_call" | custom-call | flops 805306368 | bytes 2097152 | tf_op jit(solution)/shard_map/attention/pallas_call | solution.py:71
  182.2 3.9 %all-to-all-done.3.refs_1_ = bf16[4,128,768]{2,1,0:T(8,128)(2,1)S(1)} async-done(((bf16[4,128,768]{2,1,0:T(8,128)(2,1)}), bf16[4,128,768]{2,1,0:T(8,128)(2,1)S(1)}, u32[]{:S(2)}, u32[]{:S(2)}) %all-to-all-start.3) | async-done | bytes 786464 | tf_op jit(solution)/shard_map/all_to_all | solution.py:383
  186.1 0.9 copy-done.11
  187.0 4.6 %gate.1 = bf16[128,8192]{1,0:T(8,128)(2,1)} custom-call(bf16[128,8192]{1,0:T(8,128)(2,1)} %bitcast.27, bf16[4,128,1280]{2,1,0:T(8,128)(2,1)} %copy-done.10, bf16[4,128,768]{2,1,0:T(8,128)(2,1)} %copy-done.11), custom_call_target="tpu_custom_call" | custom-call | flops 4194304 | bytes 6291456 | tf_op jit(solution)/shard_map/gate/pallas_call | solution.py:370
  (56 shorter events, 8.2 us)
Async XLA Ops:
  7.2 1.3 copy-start
  7.2 37.5 %all-gather.5.cloned.1.call-start = ((), (), s32[]{:S(2)}) async-start(), calls=%async_computation.5 | async-start | bytes 2506752 | tf_op jit(solution)/shard_map/all_gather | solution.py:425
  9.2 1.6 copy-start.3
  11.1 1.3 copy-start.1
  12.4 5.3 %copy-start.13 = (s32[1,512]{1,0:T(1,128)S(1)}, s32[1,512]{1,0:T(1,128)}, u32[]{:S(2)}) copy-start(s32[1,512]{1,0:T(1,128)} %param.18) | copy-start | bytes 6148
  12.4 6.1 %copy-start.14 = (f32[8192]{0:T(1024)S(1)}, f32[8192]{0:T(1024)}, u32[]{:S(2)}) copy-start(f32[8192]{0:T(1024)} %param.20) | copy-start | bytes 98308
  12.5 6.8 %copy-start.15 = (f32[8192]{0:T(1024)S(1)}, f32[8192]{0:T(1024)}, u32[]{:S(2)}) copy-start(f32[8192]{0:T(1024)} %param.23) | copy-start | bytes 98308
  12.5 6.8 %copy-start.16 = (f32[8192]{0:T(1024)S(1)}, f32[8192]{0:T(1024)}, u32[]{:S(2)}) copy-start(f32[8192]{0:T(1024)} %param.25) | copy-start | bytes 98308
  12.5 9.2 %copy-start.12 = (f32[4,8192]{1,0:T(4,128)S(1)}, f32[4,8192]{1,0:T(4,128)}, u32[]{:S(2)}) copy-start(f32[4,8192]{1,0:T(4,128)} %param.19) | copy-start | bytes 393220
  12.5 30.2 %all-to-all-start = ((bf16[4,128,2048]{2,1,0:T(8,128)(2,1)}), bf16[4,128,2048]{2,1,0:T(8,128)(2,1)S(1)}, u32[]{:S(2)}, u32[]{:S(2)}) async-start(bf16[4,128,2048]{2,1,0:T(8,128)(2,1)} %copy-done.1), calls=%async_computation | async-start | bytes 4194304 | tf_op jit(solution)/shard_map/all_to_all | solution.py:383
  17.8 83.6 %all-reduce.4.cloned.1.call-start = ((), (), s32[]{:S(2)}) async-start(), calls=%async_computation.4 | async-start | bytes 1310720 | tf_op jit(solution)/shard_map/psum | solution.py:458
  44.7 1.6 copy-start.2
  51.1 0.8 copy-start.5
  51.9 1.0 copy-start.7
  52.9 1.0 copy-start.8
  53.9 78.2 %all-gather.7.cloned.1.call-start = ((), (), s32[]{:S(2)}) async-start(), calls=%async_computation.6 | async-start | bytes 2359296 | tf_op jit(solution)/shard_map/all_gather | solution.py:425
  101.4 1.1 copy-start.6
  102.7 0.8 copy-start.4
  103.5 48.0 %all-to-all-start.1 = ((bf16[4,128,1024]{2,1,0:T(8,128)(2,1)}), bf16[4,128,1024]{2,1,0:T(8,128)(2,1)S(1)}, u32[]{:S(2)}, u32[]{:S(2)}) async-start(bf16[4,128,1024]{2,1,0:T(8,128)(2,1)} %broadcast_in_dim.29), calls=%async_computation.1 | async-start | bytes 2097152 | tf_op jit(solution)/shard_map/all_to_all | solution.py:383
  151.5 16.9 %copy-start.9 = (bf16[4,128,1024]{2,1,0:T(8,128)(2,1)}, bf16[4,128,1024]{2,1,0:T(8,128)(2,1)S(1)}, u32[]{:S(2)}) copy-start(bf16[4,128,1024]{2,1,0:T(8,128)(2,1)S(1)} %all-to-all-done.1.refs_0_.refs_1_.refs_2_.refs_3_.refs_4_.refs_5_) | copy-start | bytes 3145732
  151.5 20.6 %all-to-all-start.2 = ((bf16[4,128,1280]{2,1,0:T(8,128)(2,1)}), bf16[4,128,1280]{2,1,0:T(8,128)(2,1)S(1)}, u32[]{:S(2)}, u32[]{:S(2)}) async-start(bf16[4,128,1280]{2,1,0:T(8,128)(2,1)} %state_scan_0.1), calls=%async_computation.2 | async-start | bytes 2621440 | tf_op jit(solution)/shard_map/all_to_all | solution.py:383
  172.1 10.1 %copy-start.10 = (bf16[4,128,1280]{2,1,0:T(8,128)(2,1)}, bf16[4,128,1280]{2,1,0:T(8,128)(2,1)S(1)}, u32[]{:S(2)}) copy-start(bf16[4,128,1280]{2,1,0:T(8,128)(2,1)S(1)} %all-to-all-done.2.refs_0_) | copy-start | bytes 3932164
  172.1 14.0 %all-to-all-start.3 = ((bf16[4,128,768]{2,1,0:T(8,128)(2,1)}), bf16[4,128,768]{2,1,0:T(8,128)(2,1)S(1)}, u32[]{:S(2)}, u32[]{:S(2)}) async-start(bf16[4,128,768]{2,1,0:T(8,128)(2,1)} %state_scan_5.1), calls=%async_computation.3 | async-start | bytes 1572864 | tf_op jit(solution)/shard_map/all_to_all | solution.py:383
  186.1 0.9 copy-start.11
Sparse Core Ops, SparseCore 0:
  9.7 32.9 all-gather.4
  54.1 47.2 all-reduce.3
  103.0 29.0 all-gather.6

commit v12 on v10

--- a/solution.py
+++ b/solution.py
@@ -92,42 +92,54 @@
     return slice(start, start + width)
 
 
-def pack_kernel(fold, width, x_ref, out_ref):
-    ctx = out_ref.shape[0]
-    for piece in range(ctx):
-        for slot in range(out_ref.shape[2] // width):
-            out_ref[piece, :, slot * width : (slot + 1) * width] = x_ref[:, piece_lanes(slot, piece, ctx, fold, width)]
-
-
-def pack(value, ctx, fold, width):
+def cut_kernel(fold, width, start_ref, x_hbm, weight_hbm, out_hbm, own_hbm, sems):
+    ctx, _, columns = out_hbm.shape
+    start = pl.multiple_of(start_ref[0], LANES)
+    copies = [pltpu.make_async_copy(weight_hbm.at[:, pl.ds(start, width)], own_hbm, sems.at[0])]
+    for slot in range(columns // width):
+        for piece in range(ctx):
+            source = x_hbm.at[:, piece_lanes(slot, piece, ctx, fold, width)]
+            target = out_hbm.at[piece, :, slot * width : (slot + 1) * width]
+            copies.append(pltpu.make_async_copy(source, target, sems.at[len(copies)]))
+    for copy in copies:
+        copy.start()
+    for copy in copies:
+        copy.wait()
+
+
+def cut(start, value, weight, ctx, fold, width):
     rows, channels = value.shape
-    part = min(rows, 32)
-    return pl.pallas_call(
-        functools.partial(pack_kernel, fold, width),
-        grid=(rows // part,),
-        in_specs=[pl.BlockSpec((part, channels), lambda r: (r, 0))],
-        out_specs=pl.BlockSpec((ctx, part, channels // ctx), lambda r: (0, r, 0)),
-        out_shape=jax.ShapeDtypeStruct((ctx, rows, channels // ctx), value.dtype),
-        compiler_params=pltpu.CompilerParams(vmem_limit_bytes=12 << 20),
-        name="pack",
-    )(value)
-
-
-def conv_select_kernel(match_ref, x_ref, weight_ref, bias_ref, select_ref, early_ref, late_ref, part_ref, masks, padded, total):
-    step = pl.program_id(0)
+    left = pl.BlockSpec(memory_space=pl.ANY)
+    return pl.pallas_call(
+        functools.partial(cut_kernel, fold, width),
+        grid_spec=pltpu.PrefetchScalarGridSpec(
+            num_scalar_prefetch=1,
+            grid=(1,),
+            in_specs=[left, left],
+            out_specs=[left, left],
+            scratch_shapes=[pltpu.SemaphoreType.DMA((1 + channels // width,))],
+        ),
+        out_shape=[
+            jax.ShapeDtypeStruct((ctx, rows, channels // ctx), value.dtype),
+            jax.ShapeDtypeStruct((weight.shape[0], width), weight.dtype),
+        ],
+        compiler_params=pltpu.CompilerParams(vmem_limit_bytes=60 << 20),
+        name="cut",
+    )(start, value, weight)
+
+
+def conv_kernel(match_ref, x_ref, weight_ref, bias_ref, conv_ref, masks, padded):
     pieces, rows, wide = x_ref.shape
     toks = pieces * rows
     tiles = wide // LANES
-    slots, outputs, _ = select_ref.shape
-
-    @pl.when(step == 0)
+
+    @pl.when(pl.program_id(0) == 0)
     def _():
         for tap in range(3):
             masks[tap] = jnp.broadcast_to(match_ref[:, tap : tap + 1], (toks, LANES))
         for tile in range(tiles):
             padded[tile, 0:SUBLANES, :] = jnp.zeros((SUBLANES, LANES), jnp.float32)
 
-    outs = []
     for tile in range(tiles):
         lanes = slice(tile * LANES, (tile + 1) * LANES)
         for piece in range(pieces):
@@ -138,62 +150,76 @@
             moved = padded[tile, SUBLANES - 3 + tap : SUBLANES - 3 + tap + toks, :]
             term = (0.5 * weight_ref[tap : tap + 1, lanes]) * moved
             half = half + (term * masks[tap] if tap < 3 else term)
-        outs.append((half + half * jnp.tanh(half)).astype(jnp.bfloat16))
-    conv = jnp.concatenate(outs, axis=1)
-    select = jnp.concatenate([select_ref[slot] for slot in range(slots)], axis=1)
-    added = lax.dot_general(conv, select, (((1,), (1,)), ((), ())), preferred_element_type=jnp.float32)
-
-    @pl.when(step == 0)
-    def _():
-        early_ref[...] = conv
-        total[...] = added
-
-    @pl.when(step == 1)
-    def _():
-        late_ref[...] = conv
-        spare = part_ref.shape[2] - outputs
-        full = (total[...] + added).astype(part_ref.dtype)
-        for piece in range(pieces):
-            part_ref[piece, :, 0:outputs] = full[piece * rows : (piece + 1) * rows, :]
-            part_ref[piece, :, outputs:] = jnp.zeros((rows, spare), part_ref.dtype)
-
-
-def conv_select(match, pieces, conv_weight, conv_bias, select_parts):
-    slots, outputs, width = select_parts.shape
+        conv_ref[0, :, lanes] = (half + half * jnp.tanh(half)).astype(jnp.bfloat16)
+
+
+def convolve(match, pieces, conv_weight, conv_bias):
     ctx, rows, columns = pieces.shape
     toks = ctx * rows
-    padded_outputs = -(-outputs // LANES) * LANES
     wide = columns // 2
-    half = pl.BlockSpec((toks, wide), lambda s: (0, 0))
-    return pl.pallas_call(
-        conv_select_kernel,
+    return pl.pallas_call(
+        conv_kernel,
         grid=(2,),
         in_specs=[
             pl.BlockSpec(match.shape, lambda s: (0, 0)),
             pl.BlockSpec((ctx, rows, wide), lambda s: (0, 0, s)),
             pl.BlockSpec((4, wide), lambda s: (0, s)),
             pl.BlockSpec((1, wide), lambda s: (0, s)),
-            pl.BlockSpec((slots // 2, outputs, width), lambda s: (s, 0, 0)),
         ],
-        out_specs=[half, half, pl.BlockSpec((ctx, rows, padded_outputs), lambda s: (0, 0, 0))],
+        out_specs=pl.BlockSpec((1, toks, wide), lambda s: (s, 0, 0)),
         scratch_shapes=[
             pltpu.VMEM((3, toks, LANES), jnp.float32),
             pltpu.VMEM((wide // LANES, SUBLANES + toks, LANES), jnp.float32),
-            pltpu.VMEM((toks, outputs), jnp.float32),
         ],
-        out_shape=[
-            jax.ShapeDtypeStruct((toks, wide), jnp.bfloat16),
-            jax.ShapeDtypeStruct((toks, wide), jnp.bfloat16),
-            jax.ShapeDtypeStruct((ctx, rows, padded_outputs), jnp.bfloat16),
+        out_shape=jax.ShapeDtypeStruct((2, toks, wide), jnp.bfloat16),
+        compiler_params=pltpu.CompilerParams(vmem_limit_bytes=28 << 20),
+        cost_estimate=pl.CostEstimate(
+            flops=16 * pieces.size, bytes_accessed=4 * pieces.size, transcendentals=pieces.size
+        ),
+        name="convolve",
+    )(match, pieces, conv_weight, conv_bias)
+
+
+def select_kernel(conv_ref, select_ref, part_ref, total):
+    step = pl.program_id(0)
+    pieces, rows, _ = part_ref.shape
+    slots, outputs, _ = select_ref.shape
+    select = jnp.concatenate([select_ref[slot] for slot in range(slots)], axis=1)
+    added = lax.dot_general(conv_ref[0], select, (((1,), (1,)), ((), ())), preferred_element_type=jnp.float32)
+
+    @pl.when(step == 0)
+    def _():
+        total[...] = added
+
+    @pl.when(step == 1)
+    def _():
+        spare = part_ref.shape[2] - outputs
+        full = (total[...] + added).astype(part_ref.dtype)
+        for piece in range(pieces):
+            part_ref[piece, :, 0:outputs] = full[piece * rows : (piece + 1) * rows, :]
+            part_ref[piece, :, outputs:] = jnp.zeros((rows, spare), part_ref.dtype)
+
+
+def select_part(conv, select_parts, ctx):
+    slots, outputs, width = select_parts.shape
+    _, toks, wide = conv.shape
+    shape = (ctx, toks // ctx, -(-outputs // LANES) * LANES)
+    return pl.pallas_call(
+        select_kernel,
+        grid=(2,),
+        in_specs=[
+            pl.BlockSpec((1, toks, wide), lambda s: (s, 0, 0)),
+            pl.BlockSpec((slots // 2, outputs, width), lambda s: (s, 0, 0)),
         ],
-        compiler_params=pltpu.CompilerParams(vmem_limit_bytes=32 << 20),
+        out_specs=pl.BlockSpec(shape, lambda s: (0, 0, 0)),
+        scratch_shapes=[pltpu.VMEM((toks, outputs), jnp.float32)],
+        out_shape=jax.ShapeDtypeStruct(shape, jnp.bfloat16),
+        compiler_params=pltpu.CompilerParams(vmem_limit_bytes=28 << 20),
         cost_estimate=pl.CostEstimate(
-            flops=2 * toks * slots * width * outputs,
-            bytes_accessed=2 * pieces.size * 2 + 2 * select_parts.size,
-            transcendentals=pieces.size,
+            flops=2 * conv.size * outputs, bytes_accessed=2 * conv.size + 2 * select_parts.size, transcendentals=0
         ),
-        name="conv_select",
-    )(match, pieces, conv_weight, conv_bias, select_parts)
+        name="select",
+    )(conv, select_parts)
 
 
 def normalise_kernel(rank, part_ref, out_ref):
@@ -219,31 +245,28 @@
     )(parts)
 
 
-def scan_kernel(rank, first_shard, reset_hbm, low_hbm, weight_hbm, bias_ref, decay_ref, gain_ref,
-                early_hbm, late_hbm, out_ref, reset_ref, low_ref, weight_ref, conv_ref, sems, in_cols, out_diag, delta_rows, drive_rows, held_even, held_odd):
+def scan_kernel(rank, first_shard, reset_hbm, low_ref, weight_hbm, bias_ref, decay_ref, gain_ref,
+                conv_hbm, out_ref, reset_ref, weight_ref, conv_ref, sems, in_cols, out_diag, delta_rows, drive_rows, held_even, held_odd):
     toks = low_ref.shape[0]
     states = decay_ref.shape[0]
     shards = weight_ref.shape[0]
     width = weight_ref.shape[2]
     tiles = shards * width // LANES
     column = first_shard * width
-    low_copy = pltpu.make_async_copy(low_hbm, low_ref, sems.at[0])
-    reset_copy = pltpu.make_async_copy(reset_hbm, reset_ref, sems.at[1])
-    low_copy.start()
+    reset_copy = pltpu.make_async_copy(reset_hbm, reset_ref, sems.at[0])
     reset_copy.start()
     shard_copies = []
     for shard in range(shards):
         at = shard * width
         start = column + at
-        middle = early_hbm.shape[1]
-        source = early_hbm.at[:, pl.ds(start, width)] if start < middle else late_hbm.at[:, pl.ds(start - middle, width)]
+        middle = conv_hbm.shape[2]
+        source = conv_hbm.at[start // middle, :, pl.ds(start % middle, width)]
         shard_copies += [
-            pltpu.make_async_copy(weight_hbm.at[first_shard + shard], weight_ref.at[shard], sems.at[2 + 2 * shard]),
-            pltpu.make_async_copy(source, conv_ref.at[:, pl.ds(at, width)], sems.at[3 + 2 * shard]),
+            pltpu.make_async_copy(weight_hbm.at[first_shard + shard], weight_ref.at[shard], sems.at[1 + 2 * shard]),
+            pltpu.make_async_copy(source, conv_ref.at[:, pl.ds(at, width)], sems.at[2 + 2 * shard]),
         ]
     for copy in shard_copies:
         copy.start()
-    low_copy.wait()
     rows = out_ref.shape[1]
     block = 16
     span = block * states
@@ -326,7 +349,7 @@
         finish(count - 1, held_odd, part)
 
 
-def state_scan(reset_col, low, delta_parts, bias, decay, gain, convs, ctx, first_shard, shards):
+def state_scan(reset_col, low, delta_parts, bias, decay, gain, conv, ctx, first_shard, shards):
     toks = low.shape[0]
     rank, width = delta_parts.shape[1:]
     states = decay.shape[0]
@@ -337,15 +360,14 @@
     left = pl.BlockSpec(memory_space=pl.ANY)
     return pl.pallas_call(
         functools.partial(scan_kernel, rank, first_shard),
-        in_specs=[left, left, left, whole, whole, whole, left, left],
+        in_specs=[left, whole, left, whole, whole, whole, left],
         out_specs=whole,
         out_shape=jax.ShapeDtypeStruct((ctx, rows, wide), jnp.bfloat16),
         scratch_shapes=[
             pltpu.VMEM(reset_col.shape, reset_col.dtype),
-            pltpu.VMEM(low.shape, low.dtype),
             pltpu.VMEM((shards, rank, width), jnp.bfloat16),
             pltpu.VMEM((toks, wide), jnp.bfloat16),
-            pltpu.SemaphoreType.DMA((2 + 2 * shards,)),
+            pltpu.SemaphoreType.DMA((1 + 2 * shards,)),
             pltpu.VMEM((states, toks), jnp.float32),
             pltpu.VMEM((toks, 16 * states), jnp.bfloat16),
             pltpu.VMEM((toks // 16, wide // LANES, 16, LANES), jnp.float32),
@@ -358,7 +380,7 @@
             flops=6 * steps, bytes_accessed=2 * shards * rank * width + 4 * toks * wide, transcendentals=steps
         ),
         name=f"state_scan_{first_shard}",
-    )(reset_col, low, delta_parts, bias, decay, gain, *convs)
+    )(reset_col, low, delta_parts, bias, decay, gain, conv)
 
 
 def gate_kernel(fold, width, gate_ref, *refs):
@@ -446,8 +468,9 @@
             parts = lax.dynamic_index_in_dim(parts, place % fold, 1, keepdims=False)
         return parts
 
-    select_parts = gathered(own_columns(select_weight))
-    packed = pack(mixer_input[0], ctx, fold, width)
+    start = jnp.reshape(place // fold * width, (1,)).astype(jnp.int32)
+    packed, select_own = cut(start, mixer_input[0], select_weight, ctx, fold, width)
+    select_parts = gathered(select_own)
 
     same = jnp.concatenate([jnp.zeros((1,), bool), seg[1:] == seg[:-1]])
     reset_col = jnp.where(same, 0.0, FAR)[:, None]
@@ -472,7 +495,8 @@
     bias, decay, gain, reset_col, seg_q, seg_k, both, conv_weight, conv_bias, match, delta_own = own
     delta_parts = gathered(delta_own)
 
-    *convs, parts = conv_select(match, pieces, conv_weight, conv_bias, select_parts)
+    conv = convolve(match, pieces, conv_weight, conv_bias)
+    parts = select_part(conv, select_parts, ctx)
     low = normalise(exchange(parts), rank)
 
     low, both = lax.optimization_barrier((low, both))
@@ -481,7 +505,7 @@
 
     split = slots * 5 // 8
     scanned = [
-        state_scan(reset_col, low, delta_parts, bias, decay, gain, convs, ctx, first, count)
+        state_scan(reset_col, low, delta_parts, bias, decay, gain, conv, ctx, first, count)
         for first, count in ((0, split), (split, slots - split))
     ]
     scanned[0], blocks = lax.optimization_barrier((scanned[0], blocks))

time: 142 us -> 212 us (1.49)
  Pallas kernels: 46.9 us -> 121 us
  local copies, waits for them, and re-layouts: 23.1 us -> 18.1 us
  starting transfers between devices: 23.8 us -> 26.5 us
    pallas_call x2 -> x3, Pallas kernels: 5.11 us -> 79.7 us  [the longest x1 73.4 us: cut(): pl.pallas_call(functools.partial(cut_kernel, fold, width), grid_spec=pltp...]
    all_to_all x4, starting transfers between devices: 16.5 us -> 19.2 us  [exchange(): return lax.all_to_all(value, 'ctx', 0, 0, tiled=True)]
    unnamed x34 -> x30, local copies, waits for them, and re-layouts: 10.6 us -> 8.48 us
  transfers between devices with their start and end apart: 8 -> 8, of which waited for: 3 -> 3; matrix products, arithmetic and copies ran while one was open for 12% -> 6% of each run, Pallas kernels for 31% -> 21%
where the time goes in v12:
time: 212 us; the launch traced here: 211 us
  Pallas kernels  121 us (57%)
  starting transfers between devices  26.5 us (12%)
  local copies, waits for them, and re-layouts  18.1 us (9%)
  waiting for transfers between devices  16.7 us (8%)
  between operations  14.3 us (7%)
  blocking collectives  12 us (6%)
  other arithmetic  2.7 us (1%)
    pallas_call x1, Pallas kernels, cut(): pl.pallas_call(functools.partial(cut_kernel, fold, width), grid_spec=pltp...  73.4 us
    pallas_call x2, Pallas kernels, state_scan(): pl.pallas_call(functools.partial(scan_kernel, rank, first_shard), in_spec...  32.1 us
    all_to_all x4, starting transfers between devices, exchange(): return lax.all_to_all(value, 'ctx', 0, 0, tiled=True)  19.2 us
    all_to_all x4, waiting for transfers between devices, exchange(): return lax.all_to_all(value, 'ctx', 0, 0, tiled=True)  16.6 us
    all_to_all x1, blocking collectives, exchange(): return lax.all_to_all(value, 'ctx', 0, 0, tiled=True)  12 us
    unnamed x30, local copies, waits for them, and re-layouts  8.48 us
    ppermute x2, starting transfers between devices, shifted(): return lax.ppermute(value, axis, pairs)  7.27 us
    pallas_call x1, Pallas kernels, attention(): pl.pallas_call(functools.partial(attention_kernel, begin), grid=(end - be...  5.77 us
  transfers between devices with their start and end apart: 8, of which 3 were waited for; matrix products, arithmetic and copies ran while one was open for 6% of the time, Pallas kernels for 21%

profile of v12, /device:TPU:0, one launch (start us, length us, event | category | flops | bytes accessed | tf_op | source)
XLA Modules:
  0.0 211.3 jit_solution(11099809497163304957)
XLA Ops:
  7.2 73.4 %cut.1 = (bf16[4,128,2048]{2,1,0:T(8,128)(2,1)}, bf16[544,256]{1,0:T(8,128)(2,1)}) custom-call(s32[1]{0:T(128)} %bitcast.start_ref, bf16[128,8192]{1,0:T(8,128)(2,1)} %bitcast.29, bf16[544,1024]{1,0:T(8,128)(2,1)} %weight_hbm.1), custom_call_target="tpu_custom_call" | custom-call | tf_op jit(solution)/shard_map/cut/pallas_call | solution.py:113
  80.7 5.3 %all-to-all-start = ((bf16[4,128,2048]{2,1,0:T(8,128)(2,1)}), bf16[4,128,2048]{2,1,0:T(8,128)(2,1)S(1)}, u32[]{:S(2)}, u32[]{:S(2)}) async-start(bf16[4,128,2048]{2,1,0:T(8,128)(2,1)} %get-tuple-element.24), calls=%async_computation | async-start | bytes 4194304 | tf_op jit(solution)/shard_map/all_to_all | solution.py:423
  87.9 2.2 %reshape.79 = f32[16,8,1,4,256]{4,3,1,0,2:T(4,128)} reshape(f32[16,8192]{1,0:T(8,128)} %bitcast.34) | data formatting | bytes 1048576 | tf_op jit(solution)/shard_map/reshape | solution.py:456
  90.1 1.4 dynamic-slice_reduce_fusion
  91.5 0.7 copy.32
  93.8 1.4 constant_dynamic-slice_fusion.1
  95.2 0.7 constant_dynamic-slice_fusion
  95.9 1.7 pad_maximum_fusion.refs_4_.refs_5_
  97.6 0.7 broadcast_select_fusion.reset_hbm
  98.4 12.5 %all-to-all-done.x_ref = bf16[4,128,2048]{2,1,0:T(8,128)(2,1)S(1)} async-done(((bf16[4,128,2048]{2,1,0:T(8,128)(2,1)}), bf16[4,128,2048]{2,1,0:T(8,128)(2,1)S(1)}, u32[]{:S(2)}, u32[]{:S(2)}) %all-to-all-start) | async-done | bytes 2097184 | tf_op jit(solution)/shard_map/all_to_all | solution.py:423
  110.9 4.1 %convolve.1.conv_ref.conv_hbm = bf16[2,512,1024]{2,1,0:T(8,128)(2,1)S(1)} custom-call(f32[512,3]{1,0:T(8,128)S(1)} %convert_element_type.3.match_ref, bf16[4,128,2048]{2,1,0:T(8,128)(2,1)S(1)} %all-to-all-done.x_ref, f32[4,2048]{1,0:T(4,128)S(1)} %bitcast.26, f32[1,2048]{1,0:T(1,128)S(1)} %bitcast.27), custom_call_target="tpu_custom_call" | custom-call | flops 16777216 | bytes 4194304 | tf_op jit(solution)/shard_map/convolve/pallas_call | solution.py:160
  115.0 1.3 copy-done.1
  116.3 1.6 copy-done.2
  117.9 1.6 copy-done.3
  119.5 2.2 %select.7 = bf16[4,128,640]{2,1,0:T(8,128)(2,1)S(1)} custom-call(bf16[2,512,1024]{2,1,0:T(8,128)(2,1)S(1)} %copy-done.2, bf16[8,544,256]{2,1,0:T(8,128)(2,1)S(1)} %bitcast.24), custom_call_target="tpu_custom_call" | custom-call | flops 1140850688 | bytes 4325376 | tf_op jit(solution)/shard_map/select/pallas_call | solution.py:207
  121.8 12.0 %all_to_all.25.part_ref = bf16[4,128,640]{2,1,0:T(8,128)(2,1)S(1)} all-to-all(bf16[4,128,640]{2,1,0:T(8,128)(2,1)S(1)} %select.7), channel_id=1, replica_groups=mesh['ctx'=4,'rep'=8] {'ctx'}, dimensions={0} | all-to-all | bytes 1310720 | tf_op jit(solution)/shard_map/all_to_all | solution.py:423
  133.8 1.0 normalise.1
  134.8 3.5 %all-to-all-start.2 = ((bf16[4,128,640]{2,1,0:T(8,128)(2,1)}), bf16[4,128,640]{2,1,0:T(8,128)(2,1)S(1)}, u32[]{:S(2)}, u32[]{:S(2)}) async-start(bf16[4,128,640]{2,1,0:T(8,128)(2,1)} %normalise.1), calls=%async_computation.2 | async-start | bytes 1310720 | tf_op jit(solution)/shard_map/all_to_all | solution.py:423
  138.3 3.9 %collective-permute-start = (bf16[128,1024]{1,0:T(8,128)(2,1)S(1)}, bf16[128,1024]{1,0:T(8,128)(2,1)S(1)}, u32[]{:S(2)}, u32[]{:S(2)}) collective-permute-start(bf16[128,1024]{1,0:T(8,128)(2,1)S(1)} %copy-done.5), channel_id=1, source_target_pairs={{0,16},{8,24},{1,17},{9,25},{2,18},{10,26},{3,19},{11,27},{4,20},{... | collective-permute-start | bytes 786440 | tf_op jit(solution)/shard_map/ppermute | solution.py:419
  142.2 3.4 %collective-permute-start.1 = (bf16[128,1024]{1,0:T(8,128)(2,1)S(1)}, bf16[128,1024]{1,0:T(8,128)(2,1)S(1)}, u32[]{:S(2)}, u32[]{:S(2)}) collective-permute-start(bf16[128,1024]{1,0:T(8,128)(2,1)S(1)} %copy-done.5), channel_id=1, source_target_pairs={{0,8},{8,16},{16,24},{1,9},{9,17},{17,25},{2,10},{10,18},{18,26},{... | collective-permute-start | bytes 786440 | tf_op jit(solution)/shard_map/ppermute | solution.py:419
  145.6 2.6 %all-to-all-done.2 = bf16[4,128,640]{2,1,0:T(8,128)(2,1)S(1)} async-done(((bf16[4,128,640]{2,1,0:T(8,128)(2,1)}), bf16[4,128,640]{2,1,0:T(8,128)(2,1)S(1)}, u32[]{:S(2)}, u32[]{:S(2)}) %all-to-all-start.2) | async-done | bytes 655392 | tf_op jit(solution)/shard_map/all_to_all | solution.py:423
  148.2 0.8 copy-done.8
  149.0 19.1 %state_scan_0.1 = bf16[4,128,1280]{2,1,0:T(8,128)(2,1)} custom-call(f32[512,1]{1,0:T(8,128)} %broadcast_select_fusion.reset_hbm, bf16[512,640]{1,0:T(8,128)(2,1)} %bitcast.32, bf16[8,512,256]{2,1,0:T(8,128)(2,1)} %bitcast.47, f32[1,2048]{1,0:T(1,128)} %bitcast.43, f32[16,2048]{1,0:T(8,128)} %bitcast.36, f32[1,2048]{1,0:T(1,128)} %bitcast.45, ...), custom_call_target="tpu_custom_call" | custom-call | flops 62914560 | bytes 3932160 | tf_op jit(solution)/shard_map/state_scan_0/pallas_call | solution.py:361
  168.2 0.8 copy-done.7
  168.9 6.2 %all-to-all-start.3 = ((bf16[4,128,1280]{2,1,0:T(8,128)(2,1)}), bf16[4,128,1280]{2,1,0:T(8,128)(2,1)S(1)}, u32[]{:S(2)}, u32[]{:S(2)}) async-start(bf16[4,128,1280]{2,1,0:T(8,128)(2,1)} %state_scan_0.1), calls=%async_computation.3 | async-start | bytes 2621440 | tf_op jit(solution)/shard_map/all_to_all | solution.py:423
  175.2 13.0 %state_scan_5.1 = bf16[4,128,768]{2,1,0:T(8,128)(2,1)} custom-call(f32[512,1]{1,0:T(8,128)} %broadcast_select_fusion.reset_hbm, bf16[512,640]{1,0:T(8,128)(2,1)} %bitcast.33, bf16[8,512,256]{2,1,0:T(8,128)(2,1)} %bitcast.48, f32[1,2048]{1,0:T(1,128)} %bitcast.44, f32[16,2048]{1,0:T(8,128)} %bitcast.37, f32[1,2048]{1,0:T(1,128)} %bitcast.46, ...), custom_call_target="tpu_custom_call" | custom-call | flops 37748736 | bytes 2359296 | tf_op jit(solution)/shard_map/state_scan_5/pallas_call | solution.py:361
  188.1 4.2 %all-to-all-start.4 = ((bf16[4,128,768]{2,1,0:T(8,128)(2,1)}), bf16[4,128,768]{2,1,0:T(8,128)(2,1)S(1)}, u32[]{:S(2)}, u32[]{:S(2)}) async-start(bf16[4,128,768]{2,1,0:T(8,128)(2,1)} %state_scan_5.1), calls=%async_computation.4 | async-start | bytes 1572864 | tf_op jit(solution)/shard_map/all_to_all | solution.py:423
  192.3 0.7 copy.29.seg_q_ref
  193.1 5.8 %attention_0.1 = bf16[128,4096]{1,0:T(8,128)(2,1)} custom-call(s32[128,1]{1,0:T(8,128)} %copy.29.seg_q_ref, s32[1,384]{1,0:T(1,128)} %broadcast_in_dim.25.seg_k_ref, bf16[128,4096]{1,0:T(8,128)(2,1)} %bitcast.30, bf16[128,1024]{1,0:T(8,128)(2,1)} %copy-done.6, bf16[128,1024]{1,0:T(8,128)(2,1)} %copy-done.6, bf16[128,1024]{1,0:T(8,128)(2,1)} %copy-done.7, ...), custom_call_target="tpu_custom_call" | custom-call | flops 805306368 | bytes 2097152 | tf_op jit(solution)/shard_map/attention_0/pallas_call | solution.py:73
  198.9 1.5 all-to-all-done.4.refs_1_
  200.4 1.6 copy-done.4
  202.0 2.5 %gate.1 = bf16[128,8192]{1,0:T(8,128)(2,1)} custom-call(bf16[128,8192]{1,0:T(8,128)(2,1)S(1)} %bitcast.25, bf16[4,128,1280]{2,1,0:T(8,128)(2,1)S(1)} %all-to-all-done.3.refs_0_, bf16[4,128,768]{2,1,0:T(8,128)(2,1)S(1)} %all-to-all-done.4.refs_1_), custom_call_target="tpu_custom_call" | custom-call | flops 4194304 | bytes 6291456 | tf_op jit(solution)/shard_map/gate/pallas_call | solution.py:404
  (51 shorter events, 3.6 us)
Async XLA Ops:
  7.2 88.0 %copy-start = (bf16[512,1024]{1,0:T(8,128)(2,1)S(1)}, bf16[512,1024]{1,0:T(8,128)(2,1)}, u32[]{:S(2)}) copy-start(bf16[512,1024]{1,0:T(8,128)(2,1)} %param.22) | copy-start | bytes 3145732
  7.2 109.1 %all-gather.5.cloned.1.call-start = ((), (), s32[]{:S(2)}) async-start(), calls=%async_computation.5 | async-start | bytes 2506752 | tf_op jit(solution)/shard_map/all_gather | solution.py:465
  80.6 5.4 %copy-start.10 = (s32[1,512]{1,0:T(1,128)S(1)}, s32[1,512]{1,0:T(1,128)}, u32[]{:S(2)}) copy-start(s32[1,512]{1,0:T(1,128)} %param.18) | copy-start | bytes 6148
  80.6 6.0 %copy-start.11 = (f32[8192]{0:T(1024)S(1)}, f32[8192]{0:T(1024)}, u32[]{:S(2)}) copy-start(f32[8192]{0:T(1024)} %param.25) | copy-start | bytes 98308
  80.7 6.6 %copy-start.12 = (f32[8192]{0:T(1024)S(1)}, f32[8192]{0:T(1024)}, u32[]{:S(2)}) copy-start(f32[8192]{0:T(1024)} %param.20) | copy-start | bytes 98308
  80.7 11.5 %copy-start.9 = (f32[4,8192]{1,0:T(4,128)S(1)}, f32[4,8192]{1,0:T(4,128)}, u32[]{:S(2)}) copy-start(f32[4,8192]{1,0:T(4,128)} %param.19) | copy-start | bytes 393220
  80.7 30.2 %all-to-all-start = ((bf16[4,128,2048]{2,1,0:T(8,128)(2,1)}), bf16[4,128,2048]{2,1,0:T(8,128)(2,1)S(1)}, u32[]{:S(2)}, u32[]{:S(2)}) async-start(bf16[4,128,2048]{2,1,0:T(8,128)(2,1)} %get-tuple-element.24), calls=%async_computation | async-start | bytes 4194304 | tf_op jit(solution)/shard_map/all_to_all | solution.py:423
  86.0 6.5 %copy-start.13 = (f32[8192]{0:T(1024)S(1)}, f32[8192]{0:T(1024)}, u32[]{:S(2)}) copy-start(f32[8192]{0:T(1024)} %param.23) | copy-start | bytes 98308
  86.0 62.2 %all-gather.7.cloned.1.call-start = ((), (), s32[]{:S(2)}) async-start(), calls=%async_computation.6 | async-start | bytes 2359296 | tf_op jit(solution)/shard_map/all_gather | solution.py:465
  115.0 1.3 copy-start.1
  116.3 1.6 copy-start.2
  117.9 1.6 copy-start.3
  121.8 16.5 %copy-start.5 = (bf16[128,1024]{1,0:T(8,128)(2,1)S(1)}, bf16[128,1024]{1,0:T(8,128)(2,1)}, u32[]{:S(2)}) copy-start(bf16[128,1024]{1,0:T(8,128)(2,1)} %pad_maximum_fusion.refs_4_.refs_5_) | copy-start | bytes 786436
  134.8 13.4 %all-to-all-start.2 = ((bf16[4,128,640]{2,1,0:T(8,128)(2,1)}), bf16[4,128,640]{2,1,0:T(8,128)(2,1)S(1)}, u32[]{:S(2)}, u32[]{:S(2)}) async-start(bf16[4,128,640]{2,1,0:T(8,128)(2,1)} %normalise.1), calls=%async_computation.2 | async-start | bytes 1310720 | tf_op jit(solution)/shard_map/all_to_all | solution.py:423
  138.3 29.8 %collective-permute-start = (bf16[128,1024]{1,0:T(8,128)(2,1)S(1)}, bf16[128,1024]{1,0:T(8,128)(2,1)S(1)}, u32[]{:S(2)}, u32[]{:S(2)}) collective-permute-start(bf16[128,1024]{1,0:T(8,128)(2,1)S(1)} %copy-done.5), channel_id=1, source_target_pairs={{0,16},{8,24},{1,17},{9,25},{2,18},{10,26},{3,19},{11,27},{4,20},{... | collective-permute-start | bytes 786440 | tf_op jit(solution)/shard_map/ppermute | solution.py:419
  142.2 26.0 %collective-permute-start.1 = (bf16[128,1024]{1,0:T(8,128)(2,1)S(1)}, bf16[128,1024]{1,0:T(8,128)(2,1)S(1)}, u32[]{:S(2)}, u32[]{:S(2)}) collective-permute-start(bf16[128,1024]{1,0:T(8,128)(2,1)S(1)} %copy-done.5), channel_id=1, source_target_pairs={{0,8},{8,16},{16,24},{1,9},{9,17},{17,25},{2,10},{10,18},{18,26},{... | collective-permute-start | bytes 786440 | tf_op jit(solution)/shard_map/ppermute | solution.py:419
  148.2 0.8 copy-start.8
  168.2 20.0 %copy-start.6 = (bf16[128,1024]{1,0:T(8,128)(2,1)}, bf16[128,1024]{1,0:T(8,128)(2,1)S(1)}, u32[]{:S(2)}) copy-start(bf16[128,1024]{1,0:T(8,128)(2,1)S(1)} %collective-permute-done.refs_0_.refs_1_) | copy-start | bytes 786436
  168.2 0.8 copy-start.7
  168.9 19.2 %all-to-all-start.3 = ((bf16[4,128,1280]{2,1,0:T(8,128)(2,1)}), bf16[4,128,1280]{2,1,0:T(8,128)(2,1)S(1)}, u32[]{:S(2)}, u32[]{:S(2)}) async-start(bf16[4,128,1280]{2,1,0:T(8,128)(2,1)} %state_scan_0.1), calls=%async_computation.3 | async-start | bytes 2621440 | tf_op jit(solution)/shard_map/all_to_all | solution.py:423
  188.1 12.2 %all-to-all-start.4 = ((bf16[4,128,768]{2,1,0:T(8,128)(2,1)}), bf16[4,128,768]{2,1,0:T(8,128)(2,1)S(1)}, u32[]{:S(2)}, u32[]{:S(2)}) async-start(bf16[4,128,768]{2,1,0:T(8,128)(2,1)} %state_scan_5.1), calls=%async_computation.4 | async-start | bytes 1572864 | tf_op jit(solution)/shard_map/all_to_all | solution.py:423
  200.4 1.6 copy-start.4
Sparse Core Ops, SparseCore 0:
  80.7 32.8 all-gather.4
  115.3 28.5 all-gather.6

commit v13 on v10

--- a/solution.py
+++ b/solution.py
@@ -113,15 +113,22 @@
     )(value)
 
 
-def conv_select_kernel(match_ref, x_ref, weight_ref, bias_ref, select_ref, early_ref, late_ref, part_ref, masks, padded, total):
+def conv_select_kernel(match_ref, x_ref, weight_ref, bias_ref, select_hbm, early_ref, late_ref, part_ref,
+                       masks, padded, total, select_ref, sems):
     step = pl.program_id(0)
     pieces, rows, wide = x_ref.shape
     toks = pieces * rows
     tiles = wide // LANES
-    slots, outputs, _ = select_ref.shape
+    _, slots, outputs, _ = select_ref.shape
+    copies = [
+        pltpu.make_async_copy(select_hbm.at[pl.ds(half * slots, slots)], select_ref.at[half], sems.at[half])
+        for half in range(2)
+    ]
 
     @pl.when(step == 0)
     def _():
+        for copy in copies:
+            copy.start()
         for tap in range(3):
             masks[tap] = jnp.broadcast_to(match_ref[:, tap : tap + 1], (toks, LANES))
         for tile in range(tiles):
@@ -140,17 +147,21 @@
             half = half + (term * masks[tap] if tap < 3 else term)
         outs.append((half + half * jnp.tanh(half)).astype(jnp.bfloat16))
     conv = jnp.concatenate(outs, axis=1)
-    select = jnp.concatenate([select_ref[slot] for slot in range(slots)], axis=1)
-    added = lax.dot_general(conv, select, (((1,), (1,)), ((), ())), preferred_element_type=jnp.float32)
+
+    def product(half):
+        copies[half].wait()
+        select = jnp.concatenate([select_ref[half, slot] for slot in range(slots)], axis=1)
+        return lax.dot_general(conv, select, (((1,), (1,)), ((), ())), preferred_element_type=jnp.float32)
 
     @pl.when(step == 0)
     def _():
         early_ref[...] = conv
-        total[...] = added
+        total[...] = product(0)
 
     @pl.when(step == 1)
     def _():
         late_ref[...] = conv
+        added = product(1)
         spare = part_ref.shape[2] - outputs
         full = (total[...] + added).astype(part_ref.dtype)
         for piece in range(pieces):
@@ -173,20 +184,22 @@
             pl.BlockSpec((ctx, rows, wide), lambda s: (0, 0, s)),
             pl.BlockSpec((4, wide), lambda s: (0, s)),
             pl.BlockSpec((1, wide), lambda s: (0, s)),
-            pl.BlockSpec((slots // 2, outputs, width), lambda s: (s, 0, 0)),
+            pl.BlockSpec(memory_space=pl.ANY),
         ],
         out_specs=[half, half, pl.BlockSpec((ctx, rows, padded_outputs), lambda s: (0, 0, 0))],
         scratch_shapes=[
             pltpu.VMEM((3, toks, LANES), jnp.float32),
             pltpu.VMEM((wide // LANES, SUBLANES + toks, LANES), jnp.float32),
             pltpu.VMEM((toks, outputs), jnp.float32),
+            pltpu.VMEM((2, slots // 2, outputs, width), jnp.bfloat16),
+            pltpu.SemaphoreType.DMA((2,)),
         ],
         out_shape=[
             jax.ShapeDtypeStruct((toks, wide), jnp.bfloat16),
             jax.ShapeDtypeStruct((toks, wide), jnp.bfloat16),
             jax.ShapeDtypeStruct((ctx, rows, padded_outputs), jnp.bfloat16),
         ],
-        compiler_params=pltpu.CompilerParams(vmem_limit_bytes=32 << 20),
+        compiler_params=pltpu.CompilerParams(vmem_limit_bytes=54 << 20),
         cost_estimate=pl.CostEstimate(
             flops=2 * toks * slots * width * outputs,
             bytes_accessed=2 * pieces.size * 2 + 2 * select_parts.size,
@@ -361,34 +374,52 @@
     )(reset_col, low, delta_parts, bias, decay, gain, *convs)
 
 
-def gate_kernel(fold, width, gate_ref, *refs):
-    out_ref = refs[-1]
-    slot = 0
-    for y_ref in refs[:-1]:
-        ctx, _, wide = y_ref.shape
-        for place in range(wide // width):
-            for piece in range(ctx):
-                lanes = piece_lanes(slot, piece, ctx, fold, width)
-                value = y_ref[piece, :, place * width : (place + 1) * width].astype(jnp.float32)
-                out_ref[:, lanes] = (value * silu(gate_ref[:, lanes].astype(jnp.float32))).astype(out_ref.dtype)
-            slot += 1
-
-
-def apply_gate(parts, gate, fold, width):
-    rows, channels = gate.shape
-    ctx = parts[0].shape[0]
-    part = min(rows, 32)
-    columns = pl.BlockSpec((part, channels), lambda r: (r, 0))
+def gate_kernel(fold, width, first_slot, y_ref, gate_hbm, *refs):
+    out_hbm, gate_ref, mixed_ref, in_sems, out_sems = refs[-5:]
+    ctx, _, wide = y_ref.shape
+    slots = wide // width
+    column = first_slot * ctx * width
+    ins, outs = [], []
+    for slot in range(slots):
+        here = pl.ds(slot * ctx * width, ctx * width)
+        there = pl.ds(column + slot * ctx * width, ctx * width)
+        ins.append(pltpu.make_async_copy(gate_hbm.at[:, there], gate_ref.at[:, here], in_sems.at[slot]))
+        outs.append(pltpu.make_async_copy(mixed_ref.at[:, here], out_hbm.at[:, there], out_sems.at[slot]))
+        ins[slot].start()
+    for slot in range(slots):
+        ins[slot].wait()
+        for piece in range(ctx):
+            lanes = piece_lanes(slot, piece, ctx, fold, width)
+            value = y_ref[piece, :, slot * width : (slot + 1) * width].astype(jnp.float32)
+            mixed_ref[:, lanes] = (value * silu(gate_ref[:, lanes].astype(jnp.float32))).astype(mixed_ref.dtype)
+        outs[slot].start()
+    for copy in outs:
+        copy.wait()
+
+
+def apply_gate(pieces, gate, fold, width, first_slot, before=None):
+    rows = gate.shape[0]
+    ctx, _, wide = pieces.shape
+    left = pl.BlockSpec(memory_space=pl.ANY)
+    operands = [pieces, gate] + ([] if before is None else [before])
     return pl.pallas_call(
-        functools.partial(gate_kernel, fold, width),
-        grid=(rows // part,),
-        in_specs=[columns] + [pl.BlockSpec((ctx, part, array.shape[2]), lambda r: (0, r, 0)) for array in parts],
-        out_specs=columns,
+        functools.partial(gate_kernel, fold, width, first_slot),
+        in_specs=[pl.BlockSpec(memory_space=pltpu.VMEM)] + [left] * (len(operands) - 1),
+        out_specs=left,
         out_shape=jax.ShapeDtypeStruct(gate.shape, jnp.bfloat16),
-        compiler_params=pltpu.CompilerParams(vmem_limit_bytes=16 << 20),
-        cost_estimate=pl.CostEstimate(flops=4 * gate.size, bytes_accessed=6 * gate.size, transcendentals=gate.size),
-        name="gate",
-    )(gate, *parts)
+        scratch_shapes=[
+            pltpu.VMEM((rows, ctx * wide), gate.dtype),
+            pltpu.VMEM((rows, ctx * wide), gate.dtype),
+            pltpu.SemaphoreType.DMA((wide // width,)),
+            pltpu.SemaphoreType.DMA((wide // width,)),
+        ],
+        input_output_aliases={} if before is None else {2: 0},
+        compiler_params=pltpu.CompilerParams(vmem_limit_bytes=54 << 20),
+        cost_estimate=pl.CostEstimate(
+            flops=4 * pieces.size, bytes_accessed=6 * pieces.size, transcendentals=pieces.size
+        ),
+        name=f"gate_{first_slot}",
+    )(*operands)
 
 
 def shifted(value, axis, by):
@@ -488,7 +519,9 @@
     attended = attention(queries[0], blocks, seg_q, seg_k, 0, KEY_VALUE_HEADS)
     scanned = [exchange(part) for part in scanned]
     scanned[0], attended = lax.optimization_barrier((scanned[0], attended))
-    mixed = apply_gate(scanned, gate_input[0], fold, width)
+    mixed = apply_gate(scanned[0], gate_input[0], fold, width, 0)
+    scanned[1], mixed = lax.optimization_barrier((scanned[1], mixed))
+    mixed = apply_gate(scanned[1], gate_input[0], fold, width, split, mixed)
     return (attended[None], mixed[None])
 
 

time: 142 us -> 145 us (1.021)
  Pallas kernels: 46.9 us -> 57 us
  local copies, waits for them, and re-layouts: 23.1 us -> 20.1 us
  other arithmetic: 4.39 us -> 2.75 us
  waiting for transfers between devices: 14.9 us -> 13.3 us
    pallas_call x1 -> x2, Pallas kernels: 2.52 us -> 6.97 us  [apply_gate(): pl.pallas_call(functools.partial(gate_kernel, fold, width, first_slot), i...]
    pallas_call x1, Pallas kernels: 4.78 us -> 8.92 us  [conv_select(): pl.pallas_call(conv_select_kernel, grid=(2,), in_specs=[pl.BlockSpec(matc...]
    unnamed x34 -> x28, local copies, waits for them, and re-layouts: 10.6 us -> 7.9 us
    all_to_all x4, waiting for transfers between devices: 14.8 us -> 13.2 us  [exchange(): return lax.all_to_all(value, 'ctx', 0, 0, tiled=True)]
    pallas_call x1, Pallas kernels: 0.33 us -> 1.83 us  [pack(): pl.pallas_call(functools.partial(pack_kernel, fold, width), grid=(rows //...]
  transfers between devices with their start and end apart: 8 -> 8, of which waited for: 3 -> 2; matrix products, arithmetic and copies ran while one was open for 12% -> 11% of each run, Pallas kernels for 31% -> 37%
where the time goes in v13:
time: 145 us; the launch traced here: 144 us
  Pallas kernels  57 us (39%)
  starting transfers between devices  23.8 us (16%)
  local copies, waits for them, and re-layouts  20.1 us (14%)
  between operations  14.3 us (10%)
  waiting for transfers between devices  13.3 us (9%)
  blocking collectives  12.9 us (9%)
  other arithmetic  2.75 us (2%)
    pallas_call x2, Pallas kernels, state_scan(): pl.pallas_call(functools.partial(scan_kernel, rank, first_shard), in_spec...  32.5 us
    all_to_all x4, starting transfers between devices, exchange(): return lax.all_to_all(value, 'ctx', 0, 0, tiled=True)  16.5 us
    all_to_all x4, waiting for transfers between devices, exchange(): return lax.all_to_all(value, 'ctx', 0, 0, tiled=True)  13.2 us
    all_to_all x1, blocking collectives, exchange(): return lax.all_to_all(value, 'ctx', 0, 0, tiled=True)  12.9 us
    pallas_call x1, Pallas kernels, conv_select(): pl.pallas_call(conv_select_kernel, grid=(2,), in_specs=[pl.BlockSpec(matc...  8.92 us
    unnamed x28, local copies, waits for them, and re-layouts  7.9 us
    ppermute x2, starting transfers between devices, shifted(): return lax.ppermute(value, axis, pairs)  7.27 us
    pallas_call x2, Pallas kernels, apply_gate(): pl.pallas_call(functools.partial(gate_kernel, fold, width, first_slot), i...  6.97 us
  transfers between devices with their start and end apart: 8, of which 2 were waited for; matrix products, arithmetic and copies ran while one was open for 11% of the time, Pallas kernels for 37%

profile of v13, /device:TPU:0, one launch (start us, length us, event | category | flops | bytes accessed | tf_op | source)
XLA Modules:
  0.0 144.1 jit_solution(8294359395429852501)
XLA Ops:
  7.2 1.2 copy-done
  8.4 0.7 constant_dynamic-slice_fusion
  9.2 1.6 %copy-done.1 = bf16[1,128,8192]{2,1,0:T(8,128)(2,1)S(1)} copy-done((bf16[1,128,8192]{2,1,0:T(8,128)(2,1)S(1)}, bf16[1,128,8192]{2,1,0:T(8,128)(2,1)}, u32[]{:S(2)}) %copy-start.1) | copy-done | bytes 2097176
  10.8 1.8 %pack.1 = bf16[4,128,2048]{2,1,0:T(8,128)(2,1)} custom-call(bf16[128,8192]{1,0:T(8,128)(2,1)S(1)} %bitcast.23), custom_call_target="tpu_custom_call" | custom-call | tf_op jit(solution)/shard_map/pack/pallas_call | solution.py:105
  12.6 5.3 %all-to-all-start = ((bf16[4,128,2048]{2,1,0:T(8,128)(2,1)}), bf16[4,128,2048]{2,1,0:T(8,128)(2,1)S(1)}, u32[]{:S(2)}, u32[]{:S(2)}) async-start(bf16[4,128,2048]{2,1,0:T(8,128)(2,1)} %pack.1), calls=%async_computation | async-start | bytes 4194304 | tf_op jit(solution)/shard_map/all_to_all | solution.py:432
  20.6 1.0 reshape.78
  22.4 0.7 convert_element_type.3.match_ref
  23.1 2.2 %reshape.75 = f32[16,8,1,4,256]{4,3,1,0,2:T(4,128)} reshape(f32[16,8192]{1,0:T(8,128)} %bitcast.32) | data formatting | bytes 1048576 | tf_op jit(solution)/shard_map/reshape | solution.py:465
  25.3 1.4 dynamic-slice_reduce_fusion
  28.0 1.4 constant_dynamic-slice_fusion.2
  29.3 1.7 %constant_dynamic-slice_fusion.1 = bf16[512,256]{1,0:T(8,128)(2,1)} fusion(bf16[512,1024]{1,0:T(8,128)(2,1)} %param.22, s32[]{:T(128)S(6)} %select_n.60), kind=kLoop, calls=%fused_computation.15 | loop fusion | bytes 524292 | tf_op jit(solution)/shard_map/dynamic_slice | solution.py:471
  31.0 1.0 pad_maximum_fusion.refs_4_.refs_5_
  32.0 0.8 broadcast_select_fusion.reset_hbm
  32.8 10.0 %all-to-all-done.x_ref = bf16[4,128,2048]{2,1,0:T(8,128)(2,1)S(1)} async-done(((bf16[4,128,2048]{2,1,0:T(8,128)(2,1)}), bf16[4,128,2048]{2,1,0:T(8,128)(2,1)S(1)}, u32[]{:S(2)}, u32[]{:S(2)}) %all-to-all-start) | async-done | bytes 2097184 | tf_op jit(solution)/shard_map/all_to_all | solution.py:432
  42.9 1.3 copy-done.2
  44.1 8.9 %conv_select.1 = (bf16[512,1024]{1,0:T(8,128)(2,1)}, bf16[512,1024]{1,0:T(8,128)(2,1)}, bf16[4,128,640]{2,1,0:T(8,128)(2,1)}) custom-call(f32[512,3]{1,0:T(8,128)} %convert_element_type.3.match_ref, bf16[4,128,2048]{2,1,0:T(8,128)(2,1)} %copy-done.2, f32[4,2048]{1,0:T(4,128)} %bitcast.34, f32[1,2048]{1,0:T(1,128)} %bitcast.40, bf16[8,544,256]{2,1,0:T(8,128)(2,1)} %bitcast.27), custom_call_target="tpu_custom_call" | custom-call | flops 1140850688 | bytes 6422528 | tf_op jit(solution)/shard_map/conv_select/pallas_call | solution.py:179
  53.1 12.9 %all_to_all.25.part_ref = bf16[4,128,640]{2,1,0:T(8,128)(2,1)S(1)} all-to-all(bf16[4,128,640]{2,1,0:T(8,128)(2,1)} %get-tuple-element.32), channel_id=1, replica_groups=mesh['ctx'=4,'rep'=8] {'ctx'}, dimensions={0} | all-to-all | bytes 1310720 | tf_op jit(solution)/shard_map/all_to_all | solution.py:432
  65.9 1.0 normalise.1
  66.9 3.5 %all-to-all-start.2 = ((bf16[4,128,640]{2,1,0:T(8,128)(2,1)}), bf16[4,128,640]{2,1,0:T(8,128)(2,1)S(1)}, u32[]{:S(2)}, u32[]{:S(2)}) async-start(bf16[4,128,640]{2,1,0:T(8,128)(2,1)} %normalise.1), calls=%async_computation.2 | async-start | bytes 1310720 | tf_op jit(solution)/shard_map/all_to_all | solution.py:432
  70.4 3.9 %collective-permute-start.1 = (bf16[128,1024]{1,0:T(8,128)(2,1)S(1)}, bf16[128,1024]{1,0:T(8,128)(2,1)S(1)}, u32[]{:S(2)}, u32[]{:S(2)}) collective-permute-start(bf16[128,1024]{1,0:T(8,128)(2,1)S(1)} %pad_maximum_fusion.refs_4_.refs_5_), channel_id=1, source_target_pairs={{0,8},{8,16},{16,24},{1,9},{9,17},{17,25},{2,10},{10,18},{18,26},{... | collective-permute-start | bytes 786440 | tf_op jit(solution)/shard_map/ppermute | solution.py:428
  74.3 3.4 %collective-permute-start = (bf16[128,1024]{1,0:T(8,128)(2,1)S(1)}, bf16[128,1024]{1,0:T(8,128)(2,1)S(1)}, u32[]{:S(2)}, u32[]{:S(2)}) collective-permute-start(bf16[128,1024]{1,0:T(8,128)(2,1)S(1)} %pad_maximum_fusion.refs_4_.refs_5_), channel_id=1, source_target_pairs={{0,16},{8,24},{1,17},{9,25},{2,18},{10,26},{3,19},{11,27},{4,20},{... | collective-permute-start | bytes 786440 | tf_op jit(solution)/shard_map/ppermute | solution.py:428
  77.7 3.2 %all-to-all-done.2 = bf16[4,128,640]{2,1,0:T(8,128)(2,1)S(1)} async-done(((bf16[4,128,640]{2,1,0:T(8,128)(2,1)}), bf16[4,128,640]{2,1,0:T(8,128)(2,1)S(1)}, u32[]{:S(2)}, u32[]{:S(2)}) %all-to-all-start.2) | async-done | bytes 655392 | tf_op jit(solution)/shard_map/all_to_all | solution.py:432
  80.9 0.8 copy-done.8
  81.8 19.3 %state_scan_0.1 = bf16[4,128,1280]{2,1,0:T(8,128)(2,1)} custom-call(f32[512,1]{1,0:T(8,128)} %broadcast_select_fusion.reset_hbm, bf16[512,640]{1,0:T(8,128)(2,1)} %bitcast.30, bf16[8,512,256]{2,1,0:T(8,128)(2,1)} %bitcast.47, f32[1,2048]{1,0:T(1,128)} %bitcast.43, f32[16,2048]{1,0:T(8,128)} %bitcast.35, f32[1,2048]{1,0:T(1,128)} %bitcast.45, ...), custom_call_target="tpu_custom_call" | custom-call | flops 62914560 | bytes 3932160 | tf_op jit(solution)/shard_map/state_scan_0/pallas_call | solution.py:351
  101.9 3.7 %all-to-all-start.3 = ((bf16[4,128,1280]{2,1,0:T(8,128)(2,1)}), bf16[4,128,1280]{2,1,0:T(8,128)(2,1)S(1)}, u32[]{:S(2)}, u32[]{:S(2)}) async-start(bf16[4,128,1280]{2,1,0:T(8,128)(2,1)} %state_scan_0.1), calls=%async_computation.3 | async-start | bytes 2621440 | tf_op jit(solution)/shard_map/all_to_all | solution.py:432
  105.7 13.2 %state_scan_5.1 = bf16[4,128,768]{2,1,0:T(8,128)(2,1)} custom-call(f32[512,1]{1,0:T(8,128)} %broadcast_select_fusion.reset_hbm, bf16[512,640]{1,0:T(8,128)(2,1)} %bitcast.31, bf16[8,512,256]{2,1,0:T(8,128)(2,1)} %bitcast.48, f32[1,2048]{1,0:T(1,128)} %bitcast.44, f32[16,2048]{1,0:T(8,128)} %bitcast.36, f32[1,2048]{1,0:T(1,128)} %bitcast.46, ...), custom_call_target="tpu_custom_call" | custom-call | flops 37748736 | bytes 2359296 | tf_op jit(solution)/shard_map/state_scan_5/pallas_call | solution.py:351
  118.9 4.0 %all-to-all-start.4 = ((bf16[4,128,768]{2,1,0:T(8,128)(2,1)}), bf16[4,128,768]{2,1,0:T(8,128)(2,1)S(1)}, u32[]{:S(2)}, u32[]{:S(2)}) async-start(bf16[4,128,768]{2,1,0:T(8,128)(2,1)} %state_scan_5.1), calls=%async_computation.4 | async-start | bytes 1572864 | tf_op jit(solution)/shard_map/all_to_all | solution.py:432
  122.9 0.7 copy.30.seg_q_ref
  123.6 5.8 %attention_0.1 = bf16[128,4096]{1,0:T(8,128)(2,1)} custom-call(s32[128,1]{1,0:T(8,128)} %copy.30.seg_q_ref, s32[1,384]{1,0:T(1,128)} %broadcast_in_dim.25.seg_k_ref, bf16[128,4096]{1,0:T(8,128)(2,1)} %bitcast.28, bf16[128,1024]{1,0:T(8,128)(2,1)} %copy-done.7, bf16[128,1024]{1,0:T(8,128)(2,1)} %copy-done.7, bf16[128,1024]{1,0:T(8,128)(2,1)} %copy-done.6, ...), custom_call_target="tpu_custom_call" | custom-call | flops 805306368 | bytes 2097152 | tf_op jit(solution)/shard_map/attention_0/pallas_call | solution.py:73
  129.4 3.7 %gate_0.1.refs_0_ = bf16[128,8192]{1,0:T(8,128)(2,1)} custom-call(bf16[4,128,1280]{2,1,0:T(8,128)(2,1)} %copy-done.3, bf16[128,8192]{1,0:T(8,128)(2,1)} %bitcast.24), custom_call_target="tpu_custom_call" | custom-call | flops 2621440 | bytes 3932160 | tf_op jit(solution)/shard_map/gate_0/pallas_call | solution.py:405
  133.1 0.9 copy-done.4
  134.0 3.2 %gate_5.1 = bf16[128,8192]{1,0:T(8,128)(2,1)} custom-call(bf16[4,128,768]{2,1,0:T(8,128)(2,1)} %copy-done.4, bf16[128,8192]{1,0:T(8,128)(2,1)} %bitcast.25, bf16[128,8192]{1,0:T(8,128)(2,1)} %gate_0.1.refs_0_), custom_call_target="tpu_custom_call", output_to_operand_aliasing={{}: (2, {})} | custom-call | flops 1572864 | bytes 2359296 | tf_op jit(solution)/shard_map/gate_5/pallas_call | solution.py:405
  (50 shorter events, 5.6 us)
Async XLA Ops:
  7.2 1.3 copy-start
  7.2 35.7 %all-gather.5.cloned.1.call-start = ((), (), s32[]{:S(2)}) async-start(), calls=%async_computation.5 | async-start | bytes 2506752 | tf_op jit(solution)/shard_map/all_gather | solution.py:474
  9.2 1.6 %copy-start.1 = (bf16[1,128,8192]{2,1,0:T(8,128)(2,1)S(1)}, bf16[1,128,8192]{2,1,0:T(8,128)(2,1)}, u32[]{:S(2)}) copy-start(bf16[1,128,8192]{2,1,0:T(8,128)(2,1)} %param.16) | copy-start | bytes 6291460
  12.6 5.3 %copy-start.9 = (s32[1,512]{1,0:T(1,128)S(1)}, s32[1,512]{1,0:T(1,128)}, u32[]{:S(2)}) copy-start(s32[1,512]{1,0:T(1,128)} %param.18) | copy-start | bytes 6148
  12.6 6.1 %copy-start.10 = (f32[8192]{0:T(1024)S(1)}, f32[8192]{0:T(1024)}, u32[]{:S(2)}) copy-start(f32[8192]{0:T(1024)} %param.20) | copy-start | bytes 98308
  12.6 6.7 %copy-start.11 = (f32[8192]{0:T(1024)S(1)}, f32[8192]{0:T(1024)}, u32[]{:S(2)}) copy-start(f32[8192]{0:T(1024)} %param.23) | copy-start | bytes 98308
  12.6 6.8 %copy-start.12 = (f32[8192]{0:T(1024)S(1)}, f32[8192]{0:T(1024)}, u32[]{:S(2)}) copy-start(f32[8192]{0:T(1024)} %param.25) | copy-start | bytes 98308
  12.6 30.2 %all-to-all-start = ((bf16[4,128,2048]{2,1,0:T(8,128)(2,1)}), bf16[4,128,2048]{2,1,0:T(8,128)(2,1)S(1)}, u32[]{:S(2)}, u32[]{:S(2)}) async-start(bf16[4,128,2048]{2,1,0:T(8,128)(2,1)} %pack.1), calls=%async_computation | async-start | bytes 4194304 | tf_op jit(solution)/shard_map/all_to_all | solution.py:432
  17.9 63.0 %all-gather.7.cloned.1.call-start = ((), (), s32[]{:S(2)}) async-start(), calls=%async_computation.6 | async-start | bytes 2359296 | tf_op jit(solution)/shard_map/all_gather | solution.py:474
  32.0 42.3 %copy-start.5 = (bf16[128,1024]{1,0:T(8,128)(2,1)}, bf16[128,1024]{1,0:T(8,128)(2,1)S(1)}, u32[]{:S(2)}) copy-start(bf16[128,1024]{1,0:T(8,128)(2,1)S(1)} %pad_maximum_fusion.refs_4_.refs_5_) | copy-start | bytes 786436
  42.8 1.3 copy-start.2
  66.9 14.0 %all-to-all-start.2 = ((bf16[4,128,640]{2,1,0:T(8,128)(2,1)}), bf16[4,128,640]{2,1,0:T(8,128)(2,1)S(1)}, u32[]{:S(2)}, u32[]{:S(2)}) async-start(bf16[4,128,640]{2,1,0:T(8,128)(2,1)} %normalise.1), calls=%async_computation.2 | async-start | bytes 1310720 | tf_op jit(solution)/shard_map/all_to_all | solution.py:432
  70.4 30.7 %collective-permute-start.1 = (bf16[128,1024]{1,0:T(8,128)(2,1)S(1)}, bf16[128,1024]{1,0:T(8,128)(2,1)S(1)}, u32[]{:S(2)}, u32[]{:S(2)}) collective-permute-start(bf16[128,1024]{1,0:T(8,128)(2,1)S(1)} %pad_maximum_fusion.refs_4_.refs_5_), channel_id=1, source_target_pairs={{0,8},{8,16},{16,24},{1,9},{9,17},{17,25},{2,10},{10,18},{18,26},{... | collective-permute-start | bytes 786440 | tf_op jit(solution)/shard_map/ppermute | solution.py:428
  74.3 26.8 %collective-permute-start = (bf16[128,1024]{1,0:T(8,128)(2,1)S(1)}, bf16[128,1024]{1,0:T(8,128)(2,1)S(1)}, u32[]{:S(2)}, u32[]{:S(2)}) collective-permute-start(bf16[128,1024]{1,0:T(8,128)(2,1)S(1)} %pad_maximum_fusion.refs_4_.refs_5_), channel_id=1, source_target_pairs={{0,16},{8,24},{1,17},{9,25},{2,18},{10,26},{3,19},{11,27},{4,20},{... | collective-permute-start | bytes 786440 | tf_op jit(solution)/shard_map/ppermute | solution.py:428
  80.9 0.9 copy-start.8
  101.1 0.7 copy-start.6
  101.2 0.8 copy-start.7
  101.9 16.9 %all-to-all-start.3 = ((bf16[4,128,1280]{2,1,0:T(8,128)(2,1)}), bf16[4,128,1280]{2,1,0:T(8,128)(2,1)S(1)}, u32[]{:S(2)}, u32[]{:S(2)}) async-start(bf16[4,128,1280]{2,1,0:T(8,128)(2,1)} %state_scan_0.1), calls=%async_computation.3 | async-start | bytes 2621440 | tf_op jit(solution)/shard_map/all_to_all | solution.py:432
  118.9 10.5 %copy-start.3 = (bf16[4,128,1280]{2,1,0:T(8,128)(2,1)}, bf16[4,128,1280]{2,1,0:T(8,128)(2,1)S(1)}, u32[]{:S(2)}) copy-start(bf16[4,128,1280]{2,1,0:T(8,128)(2,1)S(1)} %all-to-all-done.3.y_ref) | copy-start | bytes 3932164
  118.9 14.2 %all-to-all-start.4 = ((bf16[4,128,768]{2,1,0:T(8,128)(2,1)}), bf16[4,128,768]{2,1,0:T(8,128)(2,1)S(1)}, u32[]{:S(2)}, u32[]{:S(2)}) async-start(bf16[4,128,768]{2,1,0:T(8,128)(2,1)} %state_scan_5.1), calls=%async_computation.4 | async-start | bytes 1572864 | tf_op jit(solution)/shard_map/all_to_all | solution.py:432
  133.1 0.9 copy-start.4
Sparse Core Ops, SparseCore 0:
  9.7 32.8 all-gather.4
  44.2 28.6 all-gather.6

commit v14 on v10

--- a/solution.py
+++ b/solution.py
@@ -219,17 +219,15 @@
     )(parts)
 
 
-def scan_kernel(rank, first_shard, reset_hbm, low_hbm, weight_hbm, bias_ref, decay_ref, gain_ref,
-                early_hbm, late_hbm, out_ref, reset_ref, low_ref, weight_ref, conv_ref, sems, in_cols, out_diag, delta_rows, drive_rows, held_even, held_odd):
+def scan_kernel(rank, first_shard, reset_hbm, low_ref, weight_hbm, bias_ref, decay_ref, gain_ref,
+                early_hbm, late_hbm, out_ref, reset_ref, weight_ref, conv_ref, sems, in_cols, out_diag, delta_rows, drive_rows, held_even, held_odd):
     toks = low_ref.shape[0]
     states = decay_ref.shape[0]
     shards = weight_ref.shape[0]
     width = weight_ref.shape[2]
     tiles = shards * width // LANES
     column = first_shard * width
-    low_copy = pltpu.make_async_copy(low_hbm, low_ref, sems.at[0])
-    reset_copy = pltpu.make_async_copy(reset_hbm, reset_ref, sems.at[1])
-    low_copy.start()
+    reset_copy = pltpu.make_async_copy(reset_hbm, reset_ref, sems.at[0])
     reset_copy.start()
     shard_copies = []
     for shard in range(shards):
@@ -238,12 +236,11 @@
         middle = early_hbm.shape[1]
         source = early_hbm.at[:, pl.ds(start, width)] if start < middle else late_hbm.at[:, pl.ds(start - middle, width)]
         shard_copies += [
-            pltpu.make_async_copy(weight_hbm.at[first_shard + shard], weight_ref.at[shard], sems.at[2 + 2 * shard]),
-            pltpu.make_async_copy(source, conv_ref.at[:, pl.ds(at, width)], sems.at[3 + 2 * shard]),
+            pltpu.make_async_copy(weight_hbm.at[first_shard + shard], weight_ref.at[shard], sems.at[1 + 2 * shard]),
+            pltpu.make_async_copy(source, conv_ref.at[:, pl.ds(at, width)], sems.at[2 + 2 * shard]),
         ]
     for copy in shard_copies:
         copy.start()
-    low_copy.wait()
     rows = out_ref.shape[1]
     block = 16
     span = block * states
@@ -337,15 +334,14 @@
     left = pl.BlockSpec(memory_space=pl.ANY)
     return pl.pallas_call(
         functools.partial(scan_kernel, rank, first_shard),
-        in_specs=[left, left, left, whole, whole, whole, left, left],
+        in_specs=[left, whole, left, whole, whole, whole, left, left],
         out_specs=whole,
         out_shape=jax.ShapeDtypeStruct((ctx, rows, wide), jnp.bfloat16),
         scratch_shapes=[
             pltpu.VMEM(reset_col.shape, reset_col.dtype),
-            pltpu.VMEM(low.shape, low.dtype),
             pltpu.VMEM((shards, rank, width), jnp.bfloat16),
             pltpu.VMEM((toks, wide), jnp.bfloat16),
-            pltpu.SemaphoreType.DMA((2 + 2 * shards,)),
+            pltpu.SemaphoreType.DMA((1 + 2 * shards,)),
             pltpu.VMEM((states, toks), jnp.float32),
             pltpu.VMEM((toks, 16 * states), jnp.bfloat16),
             pltpu.VMEM((toks // 16, wide // LANES, 16, LANES), jnp.float32),
@@ -353,12 +349,31 @@
             pltpu.VMEM((16 * states, wide), jnp.bfloat16),
             pltpu.VMEM((16 * states, wide), jnp.bfloat16),
         ],
-        compiler_params=pltpu.CompilerParams(vmem_limit_bytes=54 << 20),
+        compiler_params=pltpu.CompilerParams(vmem_limit_bytes=52 << 20),
         cost_estimate=pl.CostEstimate(
             flops=6 * steps, bytes_accessed=2 * shards * rank * width + 4 * toks * wide, transcendentals=steps
         ),
         name=f"state_scan_{first_shard}",
     )(reset_col, low, delta_parts, bias, decay, gain, *convs)
+
+
+def silu_kernel(gate_ref, out_ref):
+    out_ref[...] = silu(gate_ref[...].astype(jnp.float32)).astype(out_ref.dtype)
+
+
+def silu_rows(gate):
+    rows, channels = gate.shape
+    block = pl.BlockSpec((min(rows, 32), channels), lambda r: (r, 0))
+    return pl.pallas_call(
+        silu_kernel,
+        grid=(rows // min(rows, 32),),
+        in_specs=[block],
+        out_specs=block,
+        out_shape=jax.ShapeDtypeStruct(gate.shape, gate.dtype),
+        compiler_params=pltpu.CompilerParams(vmem_limit_bytes=16 << 20),
+        cost_estimate=pl.CostEstimate(flops=4 * gate.size, bytes_accessed=4 * gate.size, transcendentals=gate.size),
+        name="silu",
+    )(gate)
 
 
 def gate_kernel(fold, width, gate_ref, *refs):
@@ -369,8 +384,7 @@
         for place in range(wide // width):
             for piece in range(ctx):
                 lanes = piece_lanes(slot, piece, ctx, fold, width)
-                value = y_ref[piece, :, place * width : (place + 1) * width].astype(jnp.float32)
-                out_ref[:, lanes] = (value * silu(gate_ref[:, lanes].astype(jnp.float32))).astype(out_ref.dtype)
+                out_ref[:, lanes] = y_ref[piece, :, place * width : (place + 1) * width] * gate_ref[:, lanes]
             slot += 1
 
 
@@ -473,7 +487,9 @@
     delta_parts = gathered(delta_own)
 
     *convs, parts = conv_select(match, pieces, conv_weight, conv_bias, select_parts)
-    low = normalise(exchange(parts), rank)
+    parts, gate = lax.optimization_barrier((parts, gate_input[0]))
+    parts, gate = lax.optimization_barrier((exchange(parts), silu_rows(gate)))
+    low = normalise(parts, rank)
 
     low, both = lax.optimization_barrier((low, both))
     blocks = [shifted(both, "ctx", by) for by in range(back, 0, -1)] + [both]
@@ -488,7 +504,7 @@
     attended = attention(queries[0], blocks, seg_q, seg_k, 0, KEY_VALUE_HEADS)
     scanned = [exchange(part) for part in scanned]
     scanned[0], attended = lax.optimization_barrier((scanned[0], attended))
-    mixed = apply_gate(scanned, gate_input[0], fold, width)
+    mixed = apply_gate(scanned, gate, fold, width)
     return (attended[None], mixed[None])
 
 

time: 142 us -> 148 us (1.042)
  blocking collectives: 13.8 us -> 0 us
  waiting for transfers between devices: 14.9 us -> 22.6 us
  starting transfers between devices: 23.8 us -> 30.8 us
  local copies, waits for them, and re-layouts: 23.1 us -> 27.1 us
    all_to_all x1 -> x0, blocking collectives: 13.8 us -> none  [exchange(): return lax.all_to_all(value, 'ctx', 0, 0, tiled=True)]
    all_to_all x4 -> x5, waiting for transfers between devices: 14.8 us -> 22.5 us  [exchange(): return lax.all_to_all(value, 'ctx', 0, 0, tiled=True)]
    all_to_all x4 -> x5, starting transfers between devices: 16.5 us -> 22.2 us  [exchange(): return lax.all_to_all(value, 'ctx', 0, 0, tiled=True)]
    unnamed x34 -> x38, local copies, waits for them, and re-layouts: 10.6 us -> 14.3 us
    pallas_call x2, Pallas kernels: 32.6 us -> 31 us  [state_scan(): pl.pallas_call(functools.partial(scan_kernel, rank, first_shard), in_spec...]
  transfers between devices with their start and end apart: 8 -> 9, of which waited for: 3 -> 5; matrix products, arithmetic and copies ran while one was open for 12% -> 12% of each run, Pallas kernels for 31% -> 30%
where the time goes in v14:
time: 148 us; the launch traced here: 147 us
  Pallas kernels  47.7 us (32%)
  starting transfers between devices  30.8 us (21%)
  local copies, waits for them, and re-layouts  27.1 us (18%)
  waiting for transfers between devices  22.6 us (15%)
  between operations  14.3 us (10%)
  other arithmetic  4.4 us (3%)
    pallas_call x2, Pallas kernels, state_scan(): pl.pallas_call(functools.partial(scan_kernel, rank, first_shard), in_spec...  31 us
    all_to_all x5, waiting for transfers between devices, exchange(): return lax.all_to_all(value, 'ctx', 0, 0, tiled=True)  22.5 us
    all_to_all x5, starting transfers between devices, exchange(): return lax.all_to_all(value, 'ctx', 0, 0, tiled=True)  22.2 us
    unnamed x38, local copies, waits for them, and re-layouts  14.3 us
    ppermute x2, starting transfers between devices, shifted(): return lax.ppermute(value, axis, pairs)  8.65 us
    pallas_call x1, Pallas kernels, attention(): pl.pallas_call(functools.partial(attention_kernel, begin), grid=(end - be...  5.76 us
    pallas_call x1, Pallas kernels, conv_select(): pl.pallas_call(conv_select_kernel, grid=(2,), in_specs=[pl.BlockSpec(matc...  4.76 us
    reshape x5, local copies, waits for them, and re-layouts, own_part(): cut = array.reshape(array.shape[:-1] + (slots, fold, ctx // fold, width))  4.34 us
  transfers between devices with their start and end apart: 9, of which 5 were waited for; matrix products, arithmetic and copies ran while one was open for 12% of the time, Pallas kernels for 30%

profile of v14, /device:TPU:0, one launch (start us, length us, event | category | flops | bytes accessed | tf_op | source)
XLA Modules:
  0.0 146.9 jit_solution(4437418717156010412)
XLA Ops:
  7.2 1.2 copy-done
  9.2 1.6 %copy-done.4 = bf16[1,128,8192]{2,1,0:T(8,128)(2,1)S(1)} copy-done((bf16[1,128,8192]{2,1,0:T(8,128)(2,1)S(1)}, bf16[1,128,8192]{2,1,0:T(8,128)(2,1)}, u32[]{:S(2)}) %copy-start.4) | copy-done | bytes 2097176
  11.1 1.3 copy-done.1
  12.4 5.3 %all-to-all-start = ((bf16[4,128,2048]{2,1,0:T(8,128)(2,1)}), bf16[4,128,2048]{2,1,0:T(8,128)(2,1)S(1)}, u32[]{:S(2)}, u32[]{:S(2)}) async-start(bf16[4,128,2048]{2,1,0:T(8,128)(2,1)} %copy-done.1), calls=%async_computation | async-start | bytes 4194304 | tf_op jit(solution)/shard_map/all_to_all | solution.py:415
  19.7 2.2 %reshape.75 = f32[16,8,1,4,256]{4,3,1,0,2:T(4,128)} reshape(f32[16,8192]{1,0:T(8,128)} %bitcast.37) | data formatting | bytes 1048576 | tf_op jit(solution)/shard_map/reshape | solution.py:448
  21.9 1.4 dynamic-slice_reduce_fusion
  28.6 1.7 %constant_dynamic-slice_fusion.1 = bf16[512,256]{1,0:T(8,128)(2,1)} fusion(bf16[512,1024]{1,0:T(8,128)(2,1)} %param.22, s32[]{:T(128)S(6)} %select_n.60), kind=kLoop, calls=%fused_computation.15 | loop fusion | bytes 524292 | tf_op jit(solution)/shard_map/dynamic_slice | solution.py:454
  30.3 1.7 %pad_maximum_fusion.refs_4_.refs_5_ = bf16[128,1024]{1,0:T(8,128)(2,1)} fusion(bf16[128,512]{1,0:T(8,128)(2,1)} %bitcast.40, bf16[128,512]{1,0:T(8,128)(2,1)} %bitcast.41), kind=kLoop, calls=%fused_computation | loop fusion | flops 524288 | bytes 524288 | tf_op jit(solution)/shard_map/concatenate | solution.py:479
  32.7 1.6 %broadcast_select_fusion.reset_hbm = f32[512,1]{1,0:T(8,128)} fusion(pred[512,1]{1,0:T(8,128)(4,1)} %copy.26), kind=kLoop, calls=%fused_computation.1 | loop fusion | flops 512 | bytes 2560 | tf_op jit(solution)/shard_map/jit(_where)/select_n | solution.py:467
  34.2 8.4 %all-to-all-done.x_ref = bf16[4,128,2048]{2,1,0:T(8,128)(2,1)S(1)} async-done(((bf16[4,128,2048]{2,1,0:T(8,128)(2,1)}), bf16[4,128,2048]{2,1,0:T(8,128)(2,1)S(1)}, u32[]{:S(2)}, u32[]{:S(2)}) %all-to-all-start) | async-done | bytes 2097184 | tf_op jit(solution)/shard_map/all_to_all | solution.py:415
  42.7 1.6 %copy-done.3 = bf16[4352,256]{1,0:T(8,128)(2,1)S(1)} copy-done((bf16[4352,256]{1,0:T(8,128)(2,1)S(1)}, bf16[4352,256]{1,0:T(8,128)(2,1)}, u32[]{:S(2)}) %copy-start.3) | copy-done | bytes 2228248
  44.3 4.8 %conv_select.1 = (bf16[512,1024]{1,0:T(8,128)(2,1)S(1)}, bf16[512,1024]{1,0:T(8,128)(2,1)S(1)}, bf16[4,128,640]{2,1,0:T(8,128)(2,1)S(1)}) custom-call(f32[512,3]{1,0:T(8,128)S(1)} %convert_element_type.3.match_ref, bf16[4,128,2048]{2,1,0:T(8,128)(2,1)S(1)} %all-to-all-done.x_ref, f32[4,2048]{1,0:T(4,128)S(1)} %bitcast.26, f32[1,2048]{1,0:T(1,128)S(1)} %bitcast.29, ...), custom_call_target="tpu_custom_call" | custom-call | flops 1140850688 | bytes 6422528 | tf_op jit(solution)/shard_map/conv_select/pallas_call | solution.py:168
  49.9 1.0 copy-done.11
  50.9 1.0 copy-done.12
  51.9 4.2 %all-to-all-start.1 = ((bf16[4,128,640]{2,1,0:T(8,128)(2,1)}), bf16[4,128,640]{2,1,0:T(8,128)(2,1)}, u32[]{:S(2)}, u32[]{:S(2)}) async-start(bf16[4,128,640]{2,1,0:T(8,128)(2,1)} %copy-done.7), calls=%async_computation.1 | async-start | bytes 1310720 | tf_op jit(solution)/shard_map/all_to_all | solution.py:415
  56.1 1.6 %copy-done.5 = bf16[1,128,8192]{2,1,0:T(8,128)(2,1)S(1)} copy-done((bf16[1,128,8192]{2,1,0:T(8,128)(2,1)S(1)}, bf16[1,128,8192]{2,1,0:T(8,128)(2,1)}, u32[]{:S(2)}) %copy-start.5) | copy-done | bytes 2097176
  58.5 7.7 %all-to-all-done.1.part_ref = bf16[4,128,640]{2,1,0:T(8,128)(2,1)} async-done(((bf16[4,128,640]{2,1,0:T(8,128)(2,1)}), bf16[4,128,640]{2,1,0:T(8,128)(2,1)}, u32[]{:S(2)}, u32[]{:S(2)}) %all-to-all-start.1) | async-done | bytes 655392 | tf_op jit(solution)/shard_map/all_to_all | solution.py:415
  66.2 1.3 normalise.1
  68.3 4.2 %all-to-all-start.2 = ((bf16[4,128,640]{2,1,0:T(8,128)(2,1)}), bf16[4,128,640]{2,1,0:T(8,128)(2,1)}, u32[]{:S(2)}, u32[]{:S(2)}) async-start(bf16[4,128,640]{2,1,0:T(8,128)(2,1)} %copy-done.2), calls=%async_computation.2 | async-start | bytes 1310720 | tf_op jit(solution)/shard_map/all_to_all | solution.py:415
  72.4 4.6 %collective-permute-start = (bf16[128,1024]{1,0:T(8,128)(2,1)}, bf16[128,1024]{1,0:T(8,128)(2,1)}, u32[]{:S(2)}, u32[]{:S(2)}) collective-permute-start(bf16[128,1024]{1,0:T(8,128)(2,1)} %pad_maximum_fusion.refs_4_.refs_5_), channel_id=1, source_target_pairs={{0,16},{8,24},{1,17},{9,25},{2,18},{10,26},{3,19},{11,27},{4,20},{... | collective-permute-start | bytes 786440 | tf_op jit(solution)/shard_map/ppermute | solution.py:411
  77.0 4.1 %collective-permute-start.1 = (bf16[128,1024]{1,0:T(8,128)(2,1)}, bf16[128,1024]{1,0:T(8,128)(2,1)}, u32[]{:S(2)}, u32[]{:S(2)}) collective-permute-start(bf16[128,1024]{1,0:T(8,128)(2,1)} %pad_maximum_fusion.refs_4_.refs_5_), channel_id=1, source_target_pairs={{0,8},{8,16},{16,24},{1,9},{9,17},{17,25},{2,10},{10,18},{18,26},{... | collective-permute-start | bytes 786440 | tf_op jit(solution)/shard_map/ppermute | solution.py:411
  81.1 2.0 %all-to-all-done.2 = bf16[4,128,640]{2,1,0:T(8,128)(2,1)} async-done(((bf16[4,128,640]{2,1,0:T(8,128)(2,1)}), bf16[4,128,640]{2,1,0:T(8,128)(2,1)}, u32[]{:S(2)}, u32[]{:S(2)}) %all-to-all-start.2) | async-done | bytes 655392 | tf_op jit(solution)/shard_map/all_to_all | solution.py:415
  83.0 0.9 copy-done.9
  83.9 19.0 %state_scan_0.1 = bf16[4,128,1280]{2,1,0:T(8,128)(2,1)} custom-call(f32[512,1]{1,0:T(8,128)S(1)} %copy-done.8, bf16[512,640]{1,0:T(8,128)(2,1)} %bitcast.12.low_ref, bf16[8,512,256]{2,1,0:T(8,128)(2,1)} %bitcast.44, f32[1,2048]{1,0:T(1,128)S(1)} %bitcast.30, f32[16,2048]{1,0:T(8,128)S(1)} %bitcast.27, f32[1,2048]{1,0:T(1,128)S(1)} %bitcast.32, ...), custom_call_target="tpu_custom_call" | custom-call | flops 62914560 | bytes 3932160 | tf_op jit(solution)/shard_map/state_scan_0/pallas_call | solution.py:335
  102.9 4.3 %all-to-all-start.3 = ((bf16[4,128,1280]{2,1,0:T(8,128)(2,1)}), bf16[4,128,1280]{2,1,0:T(8,128)(2,1)}, u32[]{:S(2)}, u32[]{:S(2)}) async-start(bf16[4,128,1280]{2,1,0:T(8,128)(2,1)} %state_scan_0.1), calls=%async_computation.3 | async-start | bytes 2621440 | tf_op jit(solution)/shard_map/all_to_all | solution.py:415
  107.3 0.9 copy-done.10
  108.2 12.0 %state_scan_5.1 = bf16[4,128,768]{2,1,0:T(8,128)(2,1)S(1)} custom-call(f32[512,1]{1,0:T(8,128)S(1)} %copy-done.8, bf16[512,640]{1,0:T(8,128)(2,1)} %bitcast.12.low_ref, bf16[8,512,256]{2,1,0:T(8,128)(2,1)} %bitcast.45, f32[1,2048]{1,0:T(1,128)S(1)} %bitcast.31, f32[16,2048]{1,0:T(8,128)S(1)} %bitcast.28, f32[1,2048]{1,0:T(1,128)S(1)} %bitcast.33, ...), custom_call_target="tpu_custom_call" | custom-call | flops 37748736 | bytes 2359296 | tf_op jit(solution)/shard_map/state_scan_5/pallas_call | solution.py:335
  120.2 0.9 copy-done.6
  121.8 4.2 %all-to-all-start.4 = ((bf16[4,128,768]{2,1,0:T(8,128)(2,1)}), bf16[4,128,768]{2,1,0:T(8,128)(2,1)}, u32[]{:S(2)}, u32[]{:S(2)}) async-start(bf16[4,128,768]{2,1,0:T(8,128)(2,1)} %copy-done.6), calls=%async_computation.4 | async-start | bytes 1572864 | tf_op jit(solution)/shard_map/all_to_all | solution.py:415
  126.7 5.8 %attention_0.1 = bf16[128,4096]{1,0:T(8,128)(2,1)} custom-call(s32[128,1]{1,0:T(8,128)} %copy.29.seg_q_ref, s32[1,384]{1,0:T(1,128)} %broadcast_in_dim.25.seg_k_ref, bf16[128,4096]{1,0:T(8,128)(2,1)} %bitcast.35, bf16[128,1024]{1,0:T(8,128)(2,1)} %collective-permute-done.refs_0_.refs_1_, bf16[128,1024]{1,0:T(8,128)(2,1)} %collective-permute-done.refs_0_.refs_1_, ...), custom_call_target="tpu_custom_call" | custom-call | flops 805306368 | bytes 2097152 | tf_op jit(solution)/shard_map/attention_0/pallas_call | solution.py:73
  132.5 3.8 %all-to-all-done.4.refs_1_ = bf16[4,128,768]{2,1,0:T(8,128)(2,1)} async-done(((bf16[4,128,768]{2,1,0:T(8,128)(2,1)}), bf16[4,128,768]{2,1,0:T(8,128)(2,1)}, u32[]{:S(2)}, u32[]{:S(2)}) %all-to-all-start.4) | async-done | bytes 786464 | tf_op jit(solution)/shard_map/all_to_all | solution.py:415
  136.3 3.8 %gate.1 = bf16[128,8192]{1,0:T(8,128)(2,1)} custom-call(bf16[128,8192]{1,0:T(8,128)(2,1)S(1)} %silu.1.gate_ref, bf16[4,128,1280]{2,1,0:T(8,128)(2,1)} %all-to-all-done.3.refs_0_, bf16[4,128,768]{2,1,0:T(8,128)(2,1)} %all-to-all-done.4.refs_1_), custom_call_target="tpu_custom_call" | custom-call | flops 4194304 | bytes 6291456 | tf_op jit(solution)/shard_map/gate/pallas_call | solution.py:396
  (61 shorter events, 13.0 us)
Async XLA Ops:
  7.2 1.3 copy-start
  7.2 35.5 %all-gather.5.cloned.1.call-start = ((), (), s32[]{:S(2)}) async-start(), calls=%async_computation.5 | async-start | bytes 2506752 | tf_op jit(solution)/shard_map/all_gather | solution.py:457
  9.2 1.6 %copy-start.4 = (bf16[1,128,8192]{2,1,0:T(8,128)(2,1)S(1)}, bf16[1,128,8192]{2,1,0:T(8,128)(2,1)}, u32[]{:S(2)}) copy-start(bf16[1,128,8192]{2,1,0:T(8,128)(2,1)} %param.16) | copy-start | bytes 6291460
  11.1 1.3 copy-start.1
  12.4 5.3 %copy-start.14 = (s32[1,512]{1,0:T(1,128)S(1)}, s32[1,512]{1,0:T(1,128)}, u32[]{:S(2)}) copy-start(s32[1,512]{1,0:T(1,128)} %param.18) | copy-start | bytes 6148
  12.4 6.0 %copy-start.15 = (f32[8192]{0:T(1024)S(1)}, f32[8192]{0:T(1024)}, u32[]{:S(2)}) copy-start(f32[8192]{0:T(1024)} %param.25) | copy-start | bytes 98308
  12.4 6.6 %copy-start.16 = (f32[8192]{0:T(1024)S(1)}, f32[8192]{0:T(1024)}, u32[]{:S(2)}) copy-start(f32[8192]{0:T(1024)} %param.20) | copy-start | bytes 98308
  12.4 11.5 %copy-start.13 = (f32[4,8192]{1,0:T(4,128)S(1)}, f32[4,8192]{1,0:T(4,128)}, u32[]{:S(2)}) copy-start(f32[4,8192]{1,0:T(4,128)} %param.19) | copy-start | bytes 393220
  12.4 30.2 %all-to-all-start = ((bf16[4,128,2048]{2,1,0:T(8,128)(2,1)}), bf16[4,128,2048]{2,1,0:T(8,128)(2,1)S(1)}, u32[]{:S(2)}, u32[]{:S(2)}) async-start(bf16[4,128,2048]{2,1,0:T(8,128)(2,1)} %copy-done.1), calls=%async_computation | async-start | bytes 4194304 | tf_op jit(solution)/shard_map/all_to_all | solution.py:415
  17.7 65.3 %all-gather.7.cloned.1.call-start = ((), (), s32[]{:S(2)}) async-start(), calls=%async_computation.6 | async-start | bytes 2359296 | tf_op jit(solution)/shard_map/all_gather | solution.py:457
  17.8 5.5 %copy-start.17 = (s32[384]{0:T(512)}, s32[384]{0:T(512)S(1)}, u32[]{:S(2)}) copy-start(s32[384]{0:T(512)S(1)} %pad_dynamic-slice_fusion) | copy-start | bytes 4612
  42.7 1.6 %copy-start.3 = (bf16[4352,256]{1,0:T(8,128)(2,1)S(1)}, bf16[4352,256]{1,0:T(8,128)(2,1)}, u32[]{:S(2)}) copy-start(bf16[4352,256]{1,0:T(8,128)(2,1)} %all-gather.5.cloned.1.call-done) | copy-start | bytes 6684676
  49.1 0.8 copy-start.7
  49.9 1.0 copy-start.11
  50.9 1.0 copy-start.12
  51.9 14.3 %all-to-all-start.1 = ((bf16[4,128,640]{2,1,0:T(8,128)(2,1)}), bf16[4,128,640]{2,1,0:T(8,128)(2,1)}, u32[]{:S(2)}, u32[]{:S(2)}) async-start(bf16[4,128,640]{2,1,0:T(8,128)(2,1)} %copy-done.7), calls=%async_computation.1 | async-start | bytes 1310720 | tf_op jit(solution)/shard_map/all_to_all | solution.py:415
  56.0 1.6 %copy-start.5 = (bf16[1,128,8192]{2,1,0:T(8,128)(2,1)S(1)}, bf16[1,128,8192]{2,1,0:T(8,128)(2,1)}, u32[]{:S(2)}) copy-start(bf16[1,128,8192]{2,1,0:T(8,128)(2,1)} %param.17) | copy-start | bytes 6291460
  58.5 24.6 %copy-start.8 = (f32[512,1]{1,0:T(8,128)S(1)}, f32[512,1]{1,0:T(8,128)}, u32[]{:S(2)}) copy-start(f32[512,1]{1,0:T(8,128)} %broadcast_select_fusion.reset_hbm) | copy-start | bytes 6148
  67.4 0.8 copy-start.2
  68.3 14.8 %all-to-all-start.2 = ((bf16[4,128,640]{2,1,0:T(8,128)(2,1)}), bf16[4,128,640]{2,1,0:T(8,128)(2,1)}, u32[]{:S(2)}, u32[]{:S(2)}) async-start(bf16[4,128,640]{2,1,0:T(8,128)(2,1)} %copy-done.2), calls=%async_computation.2 | async-start | bytes 1310720 | tf_op jit(solution)/shard_map/all_to_all | solution.py:415
  72.4 30.5 %collective-permute-start = (bf16[128,1024]{1,0:T(8,128)(2,1)}, bf16[128,1024]{1,0:T(8,128)(2,1)}, u32[]{:S(2)}, u32[]{:S(2)}) collective-permute-start(bf16[128,1024]{1,0:T(8,128)(2,1)} %pad_maximum_fusion.refs_4_.refs_5_), channel_id=1, source_target_pairs={{0,16},{8,24},{1,17},{9,25},{2,18},{10,26},{3,19},{11,27},{4,20},{... | collective-permute-start | bytes 786440 | tf_op jit(solution)/shard_map/ppermute | solution.py:411
  77.0 25.9 %collective-permute-start.1 = (bf16[128,1024]{1,0:T(8,128)(2,1)}, bf16[128,1024]{1,0:T(8,128)(2,1)}, u32[]{:S(2)}, u32[]{:S(2)}) collective-permute-start(bf16[128,1024]{1,0:T(8,128)(2,1)} %pad_maximum_fusion.refs_4_.refs_5_), channel_id=1, source_target_pairs={{0,8},{8,16},{16,24},{1,9},{9,17},{17,25},{2,10},{10,18},{18,26},{... | collective-permute-start | bytes 786440 | tf_op jit(solution)/shard_map/ppermute | solution.py:411
  83.0 0.9 copy-start.9
  102.9 18.8 %all-to-all-start.3 = ((bf16[4,128,1280]{2,1,0:T(8,128)(2,1)}), bf16[4,128,1280]{2,1,0:T(8,128)(2,1)}, u32[]{:S(2)}, u32[]{:S(2)}) async-start(bf16[4,128,1280]{2,1,0:T(8,128)(2,1)} %state_scan_0.1), calls=%async_computation.3 | async-start | bytes 2621440 | tf_op jit(solution)/shard_map/all_to_all | solution.py:415
  107.3 0.9 copy-start.10
  120.2 0.9 copy-start.6
  121.8 14.5 %all-to-all-start.4 = ((bf16[4,128,768]{2,1,0:T(8,128)(2,1)}), bf16[4,128,768]{2,1,0:T(8,128)(2,1)}, u32[]{:S(2)}, u32[]{:S(2)}) async-start(bf16[4,128,768]{2,1,0:T(8,128)(2,1)} %copy-done.6), calls=%async_computation.4 | async-start | bytes 1572864 | tf_op jit(solution)/shard_map/all_to_all | solution.py:415
Sparse Core Ops, SparseCore 0:
  9.7 32.9 all-gather.4
  44.2 28.5 all-gather.6

commit v15 on v10

--- a/solution.py
+++ b/solution.py
@@ -473,10 +473,9 @@
     delta_parts = gathered(delta_own)
 
     *convs, parts = conv_select(match, pieces, conv_weight, conv_bias, select_parts)
+    parts, both = lax.optimization_barrier((parts, both))
+    blocks = [shifted(both, "ctx", by) for by in range(back, 0, -1)] + [both]
     low = normalise(exchange(parts), rank)
-
-    low, both = lax.optimization_barrier((low, both))
-    blocks = [shifted(both, "ctx", by) for by in range(back, 0, -1)] + [both]
     low = exchange(low).reshape(toks, low.shape[2])
 
     split = slots * 5 // 8

time: 142 us -> 142 us (level)
  no operation moved by 1% of the time
where the time goes in v15:
time: 142 us; the launch traced here: 141 us
  Pallas kernels  46.9 us (33%)
  starting transfers between devices  23.8 us (17%)
  local copies, waits for them, and re-layouts  23.1 us (16%)
  waiting for transfers between devices  14.9 us (10%)
  between operations  14.3 us (10%)
  blocking collectives  13.8 us (10%)
  other arithmetic  4.39 us (3%)
    pallas_call x2, Pallas kernels, state_scan(): pl.pallas_call(functools.partial(scan_kernel, rank, first_shard), in_spec...  32.6 us
    all_to_all x4, starting transfers between devices, exchange(): return lax.all_to_all(value, 'ctx', 0, 0, tiled=True)  16.5 us
    all_to_all x4, waiting for transfers between devices, exchange(): return lax.all_to_all(value, 'ctx', 0, 0, tiled=True)  14.8 us
    all_to_all x1, blocking collectives, exchange(): return lax.all_to_all(value, 'ctx', 0, 0, tiled=True)  13.8 us
    unnamed x34, local copies, waits for them, and re-layouts  10.6 us
    ppermute x2, starting transfers between devices, shifted(): return lax.ppermute(value, axis, pairs)  7.26 us
    pallas_call x1, Pallas kernels, attention(): pl.pallas_call(functools.partial(attention_kernel, begin), grid=(end - be...  5.76 us
    pallas_call x1, Pallas kernels, conv_select(): pl.pallas_call(conv_select_kernel, grid=(2,), in_specs=[pl.BlockSpec(matc...  4.78 us
  transfers between devices with their start and end apart: 8, of which 3 were waited for; matrix products, arithmetic and copies ran while one was open for 12% of the time, Pallas kernels for 31%

profile of v15, /device:TPU:0, one launch (start us, length us, event | category | flops | bytes accessed | tf_op | source)
XLA Modules:
  0.0 141.2 jit_solution(5598514941001750249)
XLA Ops:
  7.2 1.2 copy-done
  9.2 1.6 %copy-done.4 = bf16[1,128,8192]{2,1,0:T(8,128)(2,1)S(1)} copy-done((bf16[1,128,8192]{2,1,0:T(8,128)(2,1)S(1)}, bf16[1,128,8192]{2,1,0:T(8,128)(2,1)}, u32[]{:S(2)}) %copy-start.4) | copy-done | bytes 2097176
  11.2 1.3 copy-done.1
  12.5 5.3 %all-to-all-start = ((bf16[4,128,2048]{2,1,0:T(8,128)(2,1)}), bf16[4,128,2048]{2,1,0:T(8,128)(2,1)S(1)}, u32[]{:S(2)}, u32[]{:S(2)}) async-start(bf16[4,128,2048]{2,1,0:T(8,128)(2,1)} %copy-done.1), calls=%async_computation | async-start | bytes 4194304 | tf_op jit(solution)/shard_map/all_to_all | solution.py:401
  20.0 0.8 copy.26
  20.8 0.8 copy.28
  21.8 0.9 convert_element_type.3.match_ref
  22.7 2.2 %reshape.75 = f32[16,8,1,4,256]{4,3,1,0,2:T(4,128)} reshape(f32[16,8192]{1,0:T(8,128)} %bitcast.33) | data formatting | bytes 1048576 | tf_op jit(solution)/shard_map/reshape | solution.py:434
  24.9 1.4 dynamic-slice_reduce_fusion
  27.6 1.4 constant_dynamic-slice_fusion.2
  29.0 1.7 %constant_dynamic-slice_fusion.1 = bf16[512,256]{1,0:T(8,128)(2,1)} fusion(bf16[512,1024]{1,0:T(8,128)(2,1)} %param.22, s32[]{:T(128)S(6)} %select_n.60), kind=kLoop, calls=%fused_computation.15 | loop fusion | bytes 524292 | tf_op jit(solution)/shard_map/dynamic_slice | solution.py:440
  30.7 1.7 %pad_maximum_fusion.refs_4_.refs_5_ = bf16[128,1024]{1,0:T(8,128)(2,1)} fusion(bf16[128,512]{1,0:T(8,128)(2,1)} %bitcast.38, bf16[128,512]{1,0:T(8,128)(2,1)} %bitcast.39), kind=kLoop, calls=%fused_computation | loop fusion | flops 524288 | bytes 524288 | tf_op jit(solution)/shard_map/concatenate | solution.py:465
  32.4 1.6 %broadcast_select_fusion.reset_hbm = f32[512,1]{1,0:T(8,128)} fusion(pred[512,1]{1,0:T(8,128)(4,1)} %copy.26), kind=kLoop, calls=%fused_computation.1 | loop fusion | flops 512 | bytes 2560 | tf_op jit(solution)/shard_map/jit(_where)/select_n | solution.py:453
  33.9 8.7 %all-to-all-done.x_ref = bf16[4,128,2048]{2,1,0:T(8,128)(2,1)S(1)} async-done(((bf16[4,128,2048]{2,1,0:T(8,128)(2,1)}), bf16[4,128,2048]{2,1,0:T(8,128)(2,1)S(1)}, u32[]{:S(2)}, u32[]{:S(2)}) %all-to-all-start) | async-done | bytes 2097184 | tf_op jit(solution)/shard_map/all_to_all | solution.py:401
  42.7 1.6 %copy-done.2 = bf16[4352,256]{1,0:T(8,128)(2,1)S(1)} copy-done((bf16[4352,256]{1,0:T(8,128)(2,1)S(1)}, bf16[4352,256]{1,0:T(8,128)(2,1)}, u32[]{:S(2)}) %copy-start.2) | copy-done | bytes 2228248
  44.4 4.8 %conv_select.1 = (bf16[512,1024]{1,0:T(8,128)(2,1)S(1)}, bf16[512,1024]{1,0:T(8,128)(2,1)S(1)}, bf16[4,128,640]{2,1,0:T(8,128)(2,1)S(1)}) custom-call(f32[512,3]{1,0:T(8,128)S(1)} %convert_element_type.3.match_ref, bf16[4,128,2048]{2,1,0:T(8,128)(2,1)S(1)} %all-to-all-done.x_ref, f32[4,2048]{1,0:T(4,128)S(1)} %bitcast.26, f32[1,2048]{1,0:T(1,128)S(1)} %bitcast.27, ...), custom_call_target="tpu_custom_call" | custom-call | flops 1140850688 | bytes 6422528 | tf_op jit(solution)/shard_map/conv_select/pallas_call | solution.py:168
  49.1 1.0 copy-done.6
  50.1 13.8 %all_to_all.25.part_ref = bf16[4,128,640]{2,1,0:T(8,128)(2,1)S(1)} all-to-all(bf16[4,128,640]{2,1,0:T(8,128)(2,1)S(1)} %get-tuple-element.32), channel_id=1, replica_groups=mesh['ctx'=4,'rep'=8] {'ctx'}, dimensions={0} | all-to-all | bytes 1310720 | tf_op jit(solution)/shard_map/all_to_all | solution.py:401
  63.9 1.0 normalise.1
  64.9 3.5 %all-to-all-start.2 = ((bf16[4,128,640]{2,1,0:T(8,128)(2,1)}), bf16[4,128,640]{2,1,0:T(8,128)(2,1)S(1)}, u32[]{:S(2)}, u32[]{:S(2)}) async-start(bf16[4,128,640]{2,1,0:T(8,128)(2,1)} %normalise.1), calls=%async_computation.2 | async-start | bytes 1310720 | tf_op jit(solution)/shard_map/all_to_all | solution.py:401
  68.4 3.9 %collective-permute-start.1 = (bf16[128,1024]{1,0:T(8,128)(2,1)S(1)}, bf16[128,1024]{1,0:T(8,128)(2,1)S(1)}, u32[]{:S(2)}, u32[]{:S(2)}) collective-permute-start(bf16[128,1024]{1,0:T(8,128)(2,1)S(1)} %copy-done.7), channel_id=1, source_target_pairs={{0,8},{8,16},{16,24},{1,9},{9,17},{17,25},{2,10},{10,18},{18,26},{... | collective-permute-start | bytes 786440 | tf_op jit(solution)/shard_map/ppermute | solution.py:397
  72.3 3.4 %collective-permute-start = (bf16[128,1024]{1,0:T(8,128)(2,1)S(1)}, bf16[128,1024]{1,0:T(8,128)(2,1)S(1)}, u32[]{:S(2)}, u32[]{:S(2)}) collective-permute-start(bf16[128,1024]{1,0:T(8,128)(2,1)S(1)} %copy-done.7), channel_id=1, source_target_pairs={{0,16},{8,24},{1,17},{9,25},{2,18},{10,26},{3,19},{11,27},{4,20},{... | collective-permute-start | bytes 786440 | tf_op jit(solution)/shard_map/ppermute | solution.py:397
  75.7 3.5 %all-to-all-done.2 = bf16[4,128,640]{2,1,0:T(8,128)(2,1)S(1)} async-done(((bf16[4,128,640]{2,1,0:T(8,128)(2,1)}), bf16[4,128,640]{2,1,0:T(8,128)(2,1)S(1)}, u32[]{:S(2)}, u32[]{:S(2)}) %all-to-all-start.2) | async-done | bytes 655392 | tf_op jit(solution)/shard_map/all_to_all | solution.py:401
  79.2 0.8 copy-done.10
  80.1 19.3 %state_scan_0.1 = bf16[4,128,1280]{2,1,0:T(8,128)(2,1)} custom-call(f32[512,1]{1,0:T(8,128)} %broadcast_select_fusion.reset_hbm, bf16[512,640]{1,0:T(8,128)(2,1)} %bitcast.31, bf16[8,512,256]{2,1,0:T(8,128)(2,1)} %bitcast.46, f32[1,2048]{1,0:T(1,128)} %bitcast.42, f32[16,2048]{1,0:T(8,128)} %bitcast.35, f32[1,2048]{1,0:T(1,128)} %bitcast.44, ...), custom_call_target="tpu_custom_call" | custom-call | flops 62914560 | bytes 3932160 | tf_op jit(solution)/shard_map/state_scan_0/pallas_call | solution.py:338
  100.2 3.5 %all-to-all-start.3 = ((bf16[4,128,1280]{2,1,0:T(8,128)(2,1)}), bf16[4,128,1280]{2,1,0:T(8,128)(2,1)S(1)}, u32[]{:S(2)}, u32[]{:S(2)}) async-start(bf16[4,128,1280]{2,1,0:T(8,128)(2,1)} %state_scan_0.1), calls=%async_computation.3 | async-start | bytes 2621440 | tf_op jit(solution)/shard_map/all_to_all | solution.py:401
  103.7 13.2 %state_scan_5.1 = bf16[4,128,768]{2,1,0:T(8,128)(2,1)} custom-call(f32[512,1]{1,0:T(8,128)} %broadcast_select_fusion.reset_hbm, bf16[512,640]{1,0:T(8,128)(2,1)} %bitcast.32, bf16[8,512,256]{2,1,0:T(8,128)(2,1)} %bitcast.47, f32[1,2048]{1,0:T(1,128)} %bitcast.43, f32[16,2048]{1,0:T(8,128)} %bitcast.36, f32[1,2048]{1,0:T(1,128)} %bitcast.45, ...), custom_call_target="tpu_custom_call" | custom-call | flops 37748736 | bytes 2359296 | tf_op jit(solution)/shard_map/state_scan_5/pallas_call | solution.py:338
  117.0 4.2 %all-to-all-start.4 = ((bf16[4,128,768]{2,1,0:T(8,128)(2,1)}), bf16[4,128,768]{2,1,0:T(8,128)(2,1)S(1)}, u32[]{:S(2)}, u32[]{:S(2)}) async-start(bf16[4,128,768]{2,1,0:T(8,128)(2,1)} %state_scan_5.1), calls=%async_computation.4 | async-start | bytes 1572864 | tf_op jit(solution)/shard_map/all_to_all | solution.py:401
  121.9 5.8 %attention_0.1 = bf16[128,4096]{1,0:T(8,128)(2,1)} custom-call(s32[128,1]{1,0:T(8,128)} %copy.29.seg_q_ref, s32[1,384]{1,0:T(1,128)} %broadcast_in_dim.25.seg_k_ref, bf16[128,4096]{1,0:T(8,128)(2,1)} %bitcast.29, bf16[128,1024]{1,0:T(8,128)(2,1)} %copy-done.9, bf16[128,1024]{1,0:T(8,128)(2,1)} %copy-done.9, bf16[128,1024]{1,0:T(8,128)(2,1)} %copy-done.8, ...), custom_call_target="tpu_custom_call" | custom-call | flops 805306368 | bytes 2097152 | tf_op jit(solution)/shard_map/attention_0/pallas_call | solution.py:73
  127.7 2.6 %all-to-all-done.4.refs_1_ = bf16[4,128,768]{2,1,0:T(8,128)(2,1)S(1)} async-done(((bf16[4,128,768]{2,1,0:T(8,128)(2,1)}), bf16[4,128,768]{2,1,0:T(8,128)(2,1)S(1)}, u32[]{:S(2)}, u32[]{:S(2)}) %all-to-all-start.4) | async-done | bytes 786464 | tf_op jit(solution)/shard_map/all_to_all | solution.py:401
  130.2 1.6 %copy-done.3 = bf16[1,128,8192]{2,1,0:T(8,128)(2,1)S(1)} copy-done((bf16[1,128,8192]{2,1,0:T(8,128)(2,1)S(1)}, bf16[1,128,8192]{2,1,0:T(8,128)(2,1)}, u32[]{:S(2)}) %copy-start.3) | copy-done | bytes 2097176
  131.8 2.5 %gate.1 = bf16[128,8192]{1,0:T(8,128)(2,1)} custom-call(bf16[128,8192]{1,0:T(8,128)(2,1)S(1)} %bitcast.24, bf16[4,128,1280]{2,1,0:T(8,128)(2,1)S(1)} %all-to-all-done.3.refs_0_, bf16[4,128,768]{2,1,0:T(8,128)(2,1)S(1)} %all-to-all-done.4.refs_1_), custom_call_target="tpu_custom_call" | custom-call | flops 4194304 | bytes 6291456 | tf_op jit(solution)/shard_map/gate/pallas_call | solution.py:382
  (55 shorter events, 6.4 us)
Async XLA Ops:
  7.2 1.3 copy-start
  7.2 35.5 %all-gather.5.cloned.1.call-start = ((), (), s32[]{:S(2)}) async-start(), calls=%async_computation.5 | async-start | bytes 2506752 | tf_op jit(solution)/shard_map/all_gather | solution.py:443
  9.2 1.6 %copy-start.4 = (bf16[1,128,8192]{2,1,0:T(8,128)(2,1)S(1)}, bf16[1,128,8192]{2,1,0:T(8,128)(2,1)}, u32[]{:S(2)}) copy-start(bf16[1,128,8192]{2,1,0:T(8,128)(2,1)} %param.16) | copy-start | bytes 6291460
  11.1 1.3 copy-start.1
  12.5 5.3 %copy-start.12 = (s32[1,512]{1,0:T(1,128)S(1)}, s32[1,512]{1,0:T(1,128)}, u32[]{:S(2)}) copy-start(s32[1,512]{1,0:T(1,128)} %param.18) | copy-start | bytes 6148
  12.5 6.0 %copy-start.13 = (f32[8192]{0:T(1024)S(1)}, f32[8192]{0:T(1024)}, u32[]{:S(2)}) copy-start(f32[8192]{0:T(1024)} %param.20) | copy-start | bytes 98308
  12.5 6.7 %copy-start.14 = (f32[8192]{0:T(1024)S(1)}, f32[8192]{0:T(1024)}, u32[]{:S(2)}) copy-start(f32[8192]{0:T(1024)} %param.23) | copy-start | bytes 98308
  12.5 6.7 %copy-start.15 = (f32[8192]{0:T(1024)S(1)}, f32[8192]{0:T(1024)}, u32[]{:S(2)}) copy-start(f32[8192]{0:T(1024)} %param.25) | copy-start | bytes 98308
  12.5 9.1 %copy-start.11 = (f32[4,8192]{1,0:T(4,128)S(1)}, f32[4,8192]{1,0:T(4,128)}, u32[]{:S(2)}) copy-start(f32[4,8192]{1,0:T(4,128)} %param.19) | copy-start | bytes 393220
  12.5 30.2 %all-to-all-start = ((bf16[4,128,2048]{2,1,0:T(8,128)(2,1)}), bf16[4,128,2048]{2,1,0:T(8,128)(2,1)S(1)}, u32[]{:S(2)}, u32[]{:S(2)}) async-start(bf16[4,128,2048]{2,1,0:T(8,128)(2,1)} %copy-done.1), calls=%async_computation | async-start | bytes 4194304 | tf_op jit(solution)/shard_map/all_to_all | solution.py:401
  17.8 61.4 %all-gather.7.cloned.1.call-start = ((), (), s32[]{:S(2)}) async-start(), calls=%async_computation.6 | async-start | bytes 2359296 | tf_op jit(solution)/shard_map/all_gather | solution.py:443
  42.7 1.6 %copy-start.2 = (bf16[4352,256]{1,0:T(8,128)(2,1)S(1)}, bf16[4352,256]{1,0:T(8,128)(2,1)}, u32[]{:S(2)}) copy-start(bf16[4352,256]{1,0:T(8,128)(2,1)} %all-gather.5.cloned.1.call-done) | copy-start | bytes 6684676
  49.1 1.0 copy-start.6
  50.1 13.8 %copy-start.5 = (bf16[512,1024]{1,0:T(8,128)(2,1)}, bf16[512,1024]{1,0:T(8,128)(2,1)S(1)}, u32[]{:S(2)}) copy-start(bf16[512,1024]{1,0:T(8,128)(2,1)S(1)} %get-tuple-element.37.early_hbm) | copy-start | bytes 3145732
  50.1 18.3 %copy-start.7 = (bf16[128,1024]{1,0:T(8,128)(2,1)S(1)}, bf16[128,1024]{1,0:T(8,128)(2,1)}, u32[]{:S(2)}) copy-start(bf16[128,1024]{1,0:T(8,128)(2,1)} %pad_maximum_fusion.refs_4_.refs_5_) | copy-start | bytes 786436
  64.9 14.3 %all-to-all-start.2 = ((bf16[4,128,640]{2,1,0:T(8,128)(2,1)}), bf16[4,128,640]{2,1,0:T(8,128)(2,1)S(1)}, u32[]{:S(2)}, u32[]{:S(2)}) async-start(bf16[4,128,640]{2,1,0:T(8,128)(2,1)} %normalise.1), calls=%async_computation.2 | async-start | bytes 1310720 | tf_op jit(solution)/shard_map/all_to_all | solution.py:401
  68.4 31.0 %collective-permute-start.1 = (bf16[128,1024]{1,0:T(8,128)(2,1)S(1)}, bf16[128,1024]{1,0:T(8,128)(2,1)S(1)}, u32[]{:S(2)}, u32[]{:S(2)}) collective-permute-start(bf16[128,1024]{1,0:T(8,128)(2,1)S(1)} %copy-done.7), channel_id=1, source_target_pairs={{0,8},{8,16},{16,24},{1,9},{9,17},{17,25},{2,10},{10,18},{18,26},{... | collective-permute-start | bytes 786440 | tf_op jit(solution)/shard_map/ppermute | solution.py:397
  72.3 27.1 %collective-permute-start = (bf16[128,1024]{1,0:T(8,128)(2,1)S(1)}, bf16[128,1024]{1,0:T(8,128)(2,1)S(1)}, u32[]{:S(2)}, u32[]{:S(2)}) collective-permute-start(bf16[128,1024]{1,0:T(8,128)(2,1)S(1)} %copy-done.7), channel_id=1, source_target_pairs={{0,16},{8,24},{1,17},{9,25},{2,18},{10,26},{3,19},{11,27},{4,20},{... | collective-permute-start | bytes 786440 | tf_op jit(solution)/shard_map/ppermute | solution.py:397
  79.2 0.8 copy-start.10
  99.4 17.5 %copy-start.8 = (bf16[128,1024]{1,0:T(8,128)(2,1)}, bf16[128,1024]{1,0:T(8,128)(2,1)S(1)}, u32[]{:S(2)}) copy-start(bf16[128,1024]{1,0:T(8,128)(2,1)S(1)} %collective-permute-done.1.refs_2_.refs_3_) | copy-start | bytes 786436
  99.5 0.7 copy-start.9
  100.2 16.8 %all-to-all-start.3 = ((bf16[4,128,1280]{2,1,0:T(8,128)(2,1)}), bf16[4,128,1280]{2,1,0:T(8,128)(2,1)S(1)}, u32[]{:S(2)}, u32[]{:S(2)}) async-start(bf16[4,128,1280]{2,1,0:T(8,128)(2,1)} %state_scan_0.1), calls=%async_computation.3 | async-start | bytes 2621440 | tf_op jit(solution)/shard_map/all_to_all | solution.py:401
  117.0 13.2 %all-to-all-start.4 = ((bf16[4,128,768]{2,1,0:T(8,128)(2,1)}), bf16[4,128,768]{2,1,0:T(8,128)(2,1)S(1)}, u32[]{:S(2)}, u32[]{:S(2)}) async-start(bf16[4,128,768]{2,1,0:T(8,128)(2,1)} %state_scan_5.1), calls=%async_computation.4 | async-start | bytes 1572864 | tf_op jit(solution)/shard_map/all_to_all | solution.py:401
  130.2 1.6 %copy-start.3 = (bf16[1,128,8192]{2,1,0:T(8,128)(2,1)S(1)}, bf16[1,128,8192]{2,1,0:T(8,128)(2,1)}, u32[]{:S(2)}) copy-start(bf16[1,128,8192]{2,1,0:T(8,128)(2,1)} %param.17) | copy-start | bytes 6291460
Sparse Core Ops, SparseCore 0:
  9.7 32.9 all-gather.4
  44.2 28.5 all-gather.6
